TPU v7x, 256 devices: a whole 4x4x8 slice. The times are simulated.
256 devices in a mesh: tm: 32 (over x, z), tensor: 4 (over y), dp: 2 (over core).
Axes of the slice: x: 4, y: 4, z: 8, core: 2. Of those that a mesh axis runs over, the one named last changes fastest.
Arguments:
- query_rows: bfloat16 [2, 4096, 1024], P('dp', 'tm', 'tensor'), may hold values from -8 to 8
- key_rows: bfloat16 [2, 4096, 1024], P('dp', 'tm', 'tensor'), may hold values from -8 to 8
- value_rows: bfloat16 [2, 4096, 1024], P('dp', 'tm', 'tensor'), may hold values from -6 to 6
- out_weight: bfloat16 [1024, 2048], P('tensor'), may hold values from -0.1875 to 0.1875
- cotangent: bfloat16 [2, 4096, 2048], P('dp', ('tm', 'tensor')), may hold values from -6 to 6
- tile_mask: int32 [32, 32], replicated, may hold values from 0 to 1, as said below
Outputs:
- mixed: bfloat16 [2, 4096, 2048], P('dp', ('tm', 'tensor'))
- grad_queries: bfloat16 [2, 4096, 1024], P('dp', 'tm', 'tensor')
- grad_keys: bfloat16 [2, 4096, 1024], P('dp', 'tm', 'tensor')
- grad_values: bfloat16 [2, 4096, 1024], P('dp', 'tm', 'tensor')
- grad_weight: float32 [1024, 2048], P('tensor')
Inputs may be any that keep to these rules, and one draw needn't show every extreme that they name: tile_mask[i, j] is 1 exactly when the sweep of tile j (tile index // 2) is not later than that of tile i and the places of the two tiles within their sweeps (tile index % 2) differ by at most a radius of tile i, which lies in 0 to 3; tile_mask[i, i] is 1.
All inputs are finite; a program needn't handle non-finite values.
Results may differ from a plain program's by a relative error of at most 0.03.
Values may be sent and summed in bfloat16 or wider, within the bound.
No kernel may reach another device: no remote copies, remote signals or barrier semaphores. Data moves between devices by JAX's collectives and lax.ppermute only.
A program may use at most 64 MiB of HBM per device.

v0:
```python
import jax
import jax.numpy as jnp
from jax import lax
from jax.sharding import PartitionSpec as P

HD = 128
TILE = 128


def on_device(query_rows, key_rows, value_rows, out_weight, cotangent, tile_mask):
    row_count = query_rows.shape[1]
    feature_width = query_rows.shape[2]
    head_count = feature_width // HD
    scaling = HD ** (-0.5)
    position = lax.axis_index("tm")
    my_tile = position * (row_count // TILE)
    local_query = query_rows[0].reshape(row_count, head_count, HD)
    local_key = key_rows[0].reshape(row_count, head_count, HD)
    local_value = value_rows[0].reshape(row_count, head_count, HD)

    def block_mask(row_tile, col_tile, rows_in, cols_in):
        tiles = lax.dynamic_slice(
            tile_mask, (row_tile, col_tile), (rows_in // TILE, cols_in // TILE)
        )
        return jnp.repeat(jnp.repeat(tiles > 0, TILE, axis=0), TILE, axis=1)

    def keep_same(running):
        return running

    start_state = (
        jnp.full((row_count, head_count), -1e30, jnp.float32),
        jnp.zeros((row_count, head_count), jnp.float32),
        jnp.zeros((row_count, head_count, HD), jnp.float32),
    )
    block_in = (
        lax.all_gather(key_rows, "tm", axis=1, tiled=True),
        lax.all_gather(value_rows, "tm", axis=1, tiled=True),
    )
    key_part = block_in[0][0].reshape(-1, head_count, HD)
    value_part = block_in[1][0].reshape(-1, head_count, HD)
    allowed = block_mask(my_tile, jnp.int32(0) // TILE, row_count, key_part.shape[0])[:, None, :]

    def attend_compute(carried):
        largest, totals, summed = carried
        scores = (
            jnp.einsum("thd,shd->ths", local_query, key_part, preferred_element_type=jnp.float32)
            * scaling
        )
        scores = jnp.where(allowed, scores, -1e30)
        new_largest = jnp.maximum(largest, jnp.max(scores, axis=2))
        weights = jnp.where(allowed, jnp.exp(scores - new_largest[:, :, None]), 0.0)
        totals = jnp.sum(weights, axis=2)
        summed = jnp.einsum(
            "ths,shd->thd",
            weights.astype(jnp.bfloat16),
            value_part,
            preferred_element_type=jnp.float32,
        )
        return (new_largest, totals, summed)

    largest, totals, summed = lax.cond(jnp.any(allowed), attend_compute, keep_same, start_state)
    attended = (summed / totals[:, :, None]).reshape(row_count, feature_width).astype(jnp.bfloat16)
    log_norm = largest + jnp.log(totals)
    mixed = lax.psum_scatter(
        jnp.dot(attended, out_weight, preferred_element_type=jnp.float32).astype(jnp.bfloat16),
        "tensor",
        scatter_dimension=0,
        tiled=True,
    )[None]
    incoming = lax.all_gather(cotangent, "tensor", axis=1, tiled=True)[0]
    back = lax.dot_general(
        incoming, out_weight, (((1,), (1,)), ((), ())), preferred_element_type=jnp.float32
    )
    grad_rows = back
    grad_proj = lax.dot_general(
        attended, incoming, (((0,), (0,)), ((), ())), preferred_element_type=jnp.float32
    )
    grad_rows, grad_proj = (grad_rows, grad_proj)
    grad_attended = grad_rows.astype(jnp.bfloat16)
    grad_weight = lax.psum(grad_proj, ("tm", "dp"))
    grad_heads = grad_attended.reshape(row_count, head_count, HD)
    delta = (
        (grad_attended.astype(jnp.float32) * attended.astype(jnp.float32))
        .reshape(row_count, head_count, HD)
        .sum(axis=2)
    )
    norm_all, delta_all = (
        lax.all_gather(log_norm, "tm", axis=0, tiled=True),
        lax.all_gather(delta, "tm", axis=0, tiled=True),
    )

    def key_side_terms(query_part, grad_part, norm_part, delta_part, allowed):
        scores = (
            jnp.einsum("thd,shd->ths", query_part, local_key, preferred_element_type=jnp.float32)
            * scaling
        )
        probs = jnp.where(
            allowed, jnp.exp(jnp.where(allowed, scores, -1e30) - norm_part[:, :, None]), 0.0
        )
        value_term = jnp.einsum(
            "ths,thd->shd",
            probs.astype(jnp.bfloat16),
            grad_part,
            preferred_element_type=jnp.float32,
        )
        grad_probs = jnp.einsum(
            "thd,shd->ths", grad_part, local_value, preferred_element_type=jnp.float32
        )
        grad_scores = (probs * (grad_probs - delta_part[:, :, None])).astype(jnp.bfloat16)
        key_term = jnp.einsum(
            "ths,thd->shd", grad_scores, query_part, preferred_element_type=jnp.float32
        )
        return (grad_scores, key_term, value_term)

    zero_heads = jnp.zeros((row_count, head_count, HD), jnp.float32)
    block_in = (
        lax.all_gather(key_rows, "tm", axis=1, tiled=True),
        lax.all_gather(value_rows, "tm", axis=1, tiled=True),
    )
    query_key_part = block_in[0][0].reshape(-1, head_count, HD)
    query_value_part = block_in[1][0].reshape(-1, head_count, HD)
    query_allowed = block_mask(my_tile, jnp.int32(0) // TILE, row_count, query_key_part.shape[0])[
        :, None, :
    ]

    def query_compute(grad_acc):
        scores = (
            jnp.einsum(
                "thd,shd->ths", local_query, query_key_part, preferred_element_type=jnp.float32
            )
            * scaling
        )
        probs = jnp.where(
            query_allowed,
            jnp.exp(jnp.where(query_allowed, scores, -1e30) - log_norm[:, :, None]),
            0.0,
        )
        grad_probs = jnp.einsum(
            "thd,shd->ths", grad_heads, query_value_part, preferred_element_type=jnp.float32
        )
        grad_scores = (probs * (grad_probs - delta[:, :, None])).astype(jnp.bfloat16)
        return jnp.einsum(
            "ths,shd->thd", grad_scores, query_key_part, preferred_element_type=jnp.float32
        )

    grad_query = lax.cond(jnp.any(query_allowed), query_compute, keep_same, zero_heads)
    block_in = (
        lax.all_gather(query_rows[0], "tm", axis=0, tiled=True),
        lax.all_gather(grad_attended, "tm", axis=0, tiled=True),
    )
    query_part = block_in[0].reshape(-1, head_count, HD)
    grad_part = block_in[1].reshape(-1, head_count, HD)
    amount = query_part.shape[0]
    norm_part = norm_all
    delta_part = delta_all
    key_allowed = block_mask(jnp.int32(0) // TILE, my_tile, amount, row_count)[:, None, :]

    def key_compute(carried):
        grad_scores, key_term, value_term = key_side_terms(
            query_part, grad_part, norm_part, delta_part, key_allowed
        )
        return (key_term, value_term)

    grad_key, grad_value = lax.cond(
        jnp.any(key_allowed), key_compute, keep_same, (zero_heads, zero_heads)
    )
    grad_queries = (
        (grad_query * scaling).reshape(row_count, feature_width).astype(jnp.bfloat16)[None]
    )
    grad_keys = (grad_key * scaling).reshape(row_count, feature_width).astype(jnp.bfloat16)[None]
    grad_values = grad_value.reshape(row_count, feature_width).astype(jnp.bfloat16)[None]
    return (mixed, grad_queries, grad_keys, grad_values, grad_weight)


def solution(mesh):
    placed = (
        P("dp", "tm", "tensor"),
        P("dp", "tm", "tensor"),
        P("dp", "tm", "tensor"),
        P("tensor", None),
        P("dp", ("tm", "tensor"), None),
        P(),
    )
    return jax.shard_map(
        on_device,
        mesh=mesh,
        in_specs=placed,
        out_specs=(
            P("dp", ("tm", "tensor"), None),
            P("dp", "tm", "tensor"),
            P("dp", "tm", "tensor"),
            P("dp", "tm", "tensor"),
            P("tensor", None),
        ),
        check_vma=False,
    )
```

profile of v0, /device:TPU:1, one launch (start us, length us, event | category | flops | bytes accessed | tf_op | source)
XLA Modules:
  0.0 550.6 jit_solution(11013140794667166835)
XLA Ops:
  7.2 0.0 copy-start
  7.2 0.0 all-gather.6.cloned.1.call-start
  7.2 1.7 copy.72
  8.9 0.0 all-gather.6.cloned.1.call-update
  8.9 0.0 all-gather.8.cloned.1.call-start
  9.0 1.6 copy.74
  10.5 0.0 all-gather.8.cloned.1.call-update
  10.6 0.0 all-gather.12.cloned.1.call-start
  10.6 0.7 all-gather.12.cloned.1.call-update
  11.3 0.0 all-gather.10.cloned.1.call-start
  11.3 1.6 copy.73
  12.9 0.7 compare_bitcast_fusion
  13.6 0.1 broadcast_bitcast_fusion.1
  13.7 2.7 broadcast_reduce_fusion.1
  17.1 12.8 %all_gather.25 = bf16[1,128,2048]{2,1,0:T(8,128)(2,1)S(1)} all-gather(bf16[1,32,2048]{2,1,0:T(8,128)(2,1)} %param.16), channel_id=1, replica_groups=mesh['tm'=32,'tensor'=4,'dp'=2] {'tensor'}, dimensions={1}, use_global_device_ids=true | all-gather | bytes 655360 | tf_op jit(solution)/shard_map/all_gather | solution.py:70
  29.9 56.7 %all-gather.6.cloned.1.call-done = bf16[1,4096,256]{1,2,0:T(8,128)(2,1)} async-done(((bf16[1,128,256]{1,2,0:T(8,128)(2,1)}), bf16[1,4096,256]{1,2,0:T(8,128)(2,1)}) %all-gather.6.cloned.1.call-update) | async-done | bytes 2097168 | tf_op jit(solution)/shard_map/all_gather | solution.py:36
  86.6 77.1 %all-gather.8.cloned.1.call-done = bf16[1,4096,256]{1,2,0:T(8,128)(2,1)} async-done(((bf16[1,128,256]{1,2,0:T(8,128)(2,1)}), bf16[1,4096,256]{1,2,0:T(8,128)(2,1)}) %all-gather.8.cloned.1.call-update) | async-done | bytes 2097168 | tf_op jit(solution)/shard_map/all_gather | solution.py:37
  163.7 2.8 broadcast_in_dim.99
  166.5 9.5 %conditional.3 = (f32[128,2]{0,1:T(2,128)}, f32[128,2]{0,1:T(2,128)}, f32[128,2,128]{2,0,1:T(8,128)S(1)}, f32[128,2]{0,1:T(2,128)S(1)}) conditional(s32[]{:T(128)} %convert_element_type.83, () %tuple.34, (pred[128,1,4096]{0,2,1:T(8,128)(4,1)}, bf16[4096,2,128]{0,2,1:T(8,128)(2,1)}, bf16[128,2,128]{0,2,1:T(8,128)(2,1)}, ...), branch_computations={%region_1.2_spmd, %region_2.5_spmd} | conditional | flops 546307840 | bytes 26943548 | solution.py:61
  166.5 3.2 fusion.60
  169.6 0.6 broadcast_maximum_fusion
  170.2 2.5 fusion.3
  172.7 2.6 fusion.9
  175.3 0.7 log.5
  175.9 0.8 fusion.56
  176.8 0.0 copy-start.7
  176.8 1.1 convert_multiply_fusion
  177.9 0.0 all-gather.10.cloned.1.call-update
  177.9 0.0 reduce-scatter.2.cloned.1.call-start
  178.0 1.1 convolution_convert_fusion
  179.1 0.0 reduce-scatter.2.cloned.1.call-update
  179.1 0.0 all-reduce.2.cloned.1.call-start
  179.2 2.8 fusion.51
  182.0 0.0 all-reduce.2.cloned.1.call-update
  182.0 0.2 fusion.59
  182.2 0.1 broadcast_bitcast_fusion
  182.3 1.2 broadcast_reduce_fusion
  184.2 0.1 reshape.85
  184.3 0.7 add.10
  185.0 0.2 reduce_sum.18
  185.2 0.0 copy-start.5
  185.2 0.0 copy-start.6
  185.2 9.3 %conditional.4 = (f32[128,2,128]{2,0,1:T(8,128)S(1)}) conditional(s32[]{:T(128)} %convert_element_type.83, () %tuple.36, (pred[128,1,4096]{0,2,1:T(8,128)(4,1)}, bf16[4096,2,128]{0,2,1:T(8,128)(2,1)S(1)}, bf16[128,2,128]{0,2,1:T(8,128)(2,1)}, f32[128,2]{0,1:T(2,128)S(1)}, bf16[128,256]{1,0:T(8,128)(2,1)S(1)}, ...), branch_computations={%region_7.8_spmd, %region_8.9_spmd} | conditional | flops 812646400 | bytes 15470600 | solution.py:146
  185.2 4.6 fusion.19
  189.9 0.1 copy.82
  189.9 4.6 fusion.22
  194.6 0.1 copy.83
  194.7 0.7 convert_element_type.91
  195.3 34.1 %all_gather.27 = f32[4096,2]{0,1:T(2,128)S(1)} all-gather(f32[128,2]{0,1:T(2,128)S(1)} %add.10), channel_id=1, replica_groups=mesh['tm'=32,'tensor'=4,'dp'=2] {'tm'}, dimensions={0}, use_global_device_ids=true | all-gather | bytes 33792 | tf_op jit(solution)/shard_map/all_gather | solution.py:88
  229.5 44.6 %all_gather.29 = f32[4096,2]{1,0:T(8,128)} all-gather(f32[128,2]{1,0:T(8,128)S(1)} %reduce_sum.18), channel_id=1, replica_groups=mesh['tm'=32,'tensor'=4,'dp'=2] {'tm'}, dimensions={0}, use_global_device_ids=true | all-gather | bytes 33792 | tf_op jit(solution)/shard_map/all_gather | solution.py:89
  274.1 47.2 %all-gather.10.cloned.1.call-done = bf16[4096,256]{1,0:T(8,128)(2,1)} async-done(((bf16[128,256]{1,0:T(8,128)(2,1)}), bf16[4096,256]{1,0:T(8,128)(2,1)}) %all-gather.10.cloned.1.call-update) | async-done | bytes 2097168 | tf_op jit(solution)/shard_map/all_gather | solution.py:149
  321.3 0.2 broadcast_in_dim.103
  321.5 18.2 %conditional.5 = (f32[128,2,128]{2,0,1:T(8,128)S(1)}, bf16[1,128,256]{2,1,0:T(8,128)(2,1)}) conditional(s32[]{:T(128)} %convert_element_type.92, () %tuple.38, (pred[4096,1,128]{0,2,1:T(8,128)(4,1)S(1)}, bf16[1,128,256]{2,1,0:T(8,128)(2,1)S(1)}, bf16[4096,256]{1,0:T(8,128)(2,1)}, f32[4096,2]{0,1:T(2,128)S(1)}, bf16[1,128,256]{2,1,0:T(8,128)(2,1)S(1)}, ...), branch_computations={%region_10.11_spmd, %region_11.12_spmd} | conditional | flops 1082163200 | bytes 26542096 | solution.py:164
  321.6 5.1 fusion.33
  326.7 2.9 copy.84
  329.6 2.2 copy.85
  331.8 4.1 fusion.42
  335.9 3.0 fusion.45
  338.9 0.7 copy.99
  339.7 0.1 copy.86
  339.8 0.7 convert_element_type.94
  340.5 7.3 %reduce-scatter.2.cloned.1.call-done = bf16[32,2048]{1,0:T(8,128)(2,1)} async-done(((bf16[128,2048]{1,0:T(8,128)(2,1)}), bf16[32,2048]{1,0:T(8,128)(2,1)}) %reduce-scatter.2.cloned.1.call-update) | async-done | bytes 131088 | tf_op jit(solution)/shard_map/reduce_scatter | solution.py:64
  347.7 192.9 %all-reduce.2.cloned.1.call-done = f32[256,2048]{1,0:T(8,128)} async-done(((f32[256,2048]{1,0:T(8,128)}), f32[256,2048]{1,0:T(8,128)}) %all-reduce.2.cloned.1.call-update) | async-done | bytes 2097168 | tf_op jit(solution)/shard_map/psum | solution.py:80
  540.6 3.1 copy.147
  (17 shorter events, 0.1 us)
Async XLA Ops:
  7.2 169.6 %copy-start = (bf16[256,2048]{1,0:T(8,128)(2,1)S(1)}, bf16[256,2048]{1,0:T(8,128)(2,1)}, u32[]{:S(2)}) copy-start(bf16[256,2048]{1,0:T(8,128)(2,1)} %param.15) | copy-start | bytes 3145732
  7.2 79.4 %all-gather.6.cloned.1.call-start = ((), (), s32[]{:S(2)}) async-start(), calls=%async_computation.1 | async-start | bytes 2162688 | tf_op jit(solution)/shard_map/all_gather | solution.py:36
  8.9 154.8 %all-gather.8.cloned.1.call-start = ((), (), s32[]{:S(2)}) async-start(), calls=%async_computation.2 | async-start | bytes 2162688 | tf_op jit(solution)/shard_map/all_gather | solution.py:37
  10.6 263.5 %all-gather.12.cloned.1.call-start = ((), (), s32[]{:S(2)}) async-start(), calls=%async_computation.6 | async-start | bytes 2162688 | tf_op jit(solution)/shard_map/all_gather | solution.py:148
  11.3 310.0 %all-gather.10.cloned.1.call-start = ((), (), s32[]{:S(2)}) async-start(), calls=%async_computation.4 | async-start | bytes 2162688 | tf_op jit(solution)/shard_map/all_gather | solution.py:149
  29.9 146.9 %copy-start.2 = (bf16[1,128,2048]{2,1,0:T(8,128)(2,1)}, bf16[1,128,2048]{2,1,0:T(8,128)(2,1)S(1)}, u32[]{:S(2)}) copy-start(bf16[1,128,2048]{2,1,0:T(8,128)(2,1)S(1)} %all_gather.25) | copy-start | bytes 1572868
  166.5 6.2 %copy-start.3 = (bf16[4096,2,128]{0,2,1:T(8,128)(2,1)S(1)}, bf16[4096,2,128]{0,2,1:T(8,128)(2,1)}, u32[]{:S(2)}) copy-start(bf16[4096,2,128]{0,2,1:T(8,128)(2,1)} %get-tuple-element.146) | copy-start | bytes 6291460 | tf_op jit(solution)/shard_map/cond
  176.8 5.2 copy-start.7
  177.9 7.3 %copy-start.1 = (bf16[1,4096,256]{1,2,0:T(8,128)(2,1)S(1)}, bf16[1,4096,256]{1,2,0:T(8,128)(2,1)}, u32[]{:S(2)}) copy-start(bf16[1,4096,256]{1,2,0:T(8,128)(2,1)} %all-gather.6.cloned.1.call-done) | copy-start | bytes 6291460
  177.9 7.3 %copy-start.4 = (bf16[128,256]{1,0:T(8,128)(2,1)S(1)}, bf16[128,256]{1,0:T(8,128)(2,1)}, u32[]{:S(2)}) copy-start(bf16[128,256]{1,0:T(8,128)(2,1)} %get-tuple-element.170) | copy-start | bytes 196612
  177.9 169.8 %reduce-scatter.2.cloned.1.call-start = ((), (), s32[]{:S(2)}) async-start(), calls=%async_computation.3 | async-start | bytes 655360 | tf_op jit(solution)/shard_map/reduce_scatter | solution.py:64
  179.1 361.5 %all-reduce.2.cloned.1.call-start = ((), (), s32[]{:S(2)}) async-start(), calls=%async_computation.5 | async-start | bytes 4194304 | tf_op jit(solution)/shard_map/psum | solution.py:80
  185.2 136.3 %copy-start.5 = (bf16[1,128,256]{2,1,0:T(8,128)(2,1)S(1)}, bf16[1,128,256]{2,1,0:T(8,128)(2,1)}, u32[]{:S(2)}) copy-start(bf16[1,128,256]{2,1,0:T(8,128)(2,1)} %param.13) | copy-start | bytes 196612
  185.2 136.3 %copy-start.6 = (bf16[1,128,256]{2,1,0:T(8,128)(2,1)S(1)}, bf16[1,128,256]{2,1,0:T(8,128)(2,1)}, u32[]{:S(2)}) copy-start(bf16[1,128,256]{2,1,0:T(8,128)(2,1)} %param.14) | copy-start | bytes 196612
Sparse Core Ops, SparseCore 0:
  11.1 75.4 all-gather.5
  89.6 74.0 all-gather.7
  166.3 76.6 all-gather.11
  246.0 75.2 all-gather.9
  324.2 23.4 reduce-scatter.1
  351.6 188.9 all-reduce.1
where the time goes:
time: 552 us; the launch traced here: 551 us
  waiting for transfers between devices  382 us (69%)
  blocking collectives  91.5 us (17%)
  matrix products  32.2 us (6%)
  local copies, waits for them, and re-layouts  19.3 us (3%)
  between operations  15.6 us (3%)
  other arithmetic  9.58 us (2%)
    psum x1, waiting for transfers between devices, on_device(): grad_weight = lax.psum(grad_proj, ('tm', 'dp'))  193 us
    all_gather x1, waiting for transfers between devices, on_device(): lax.all_gather(value_rows, 'tm', axis=1, tiled=True)  77.1 us
    all_gather x1, waiting for transfers between devices, on_device(): lax.all_gather(key_rows, 'tm', axis=1, tiled=True)  56.7 us
    all_gather x1, waiting for transfers between devices, on_device(): lax.all_gather(grad_attended, 'tm', axis=0, tiled=True)  47.2 us
    all_gather x1, blocking collectives, on_device(): lax.all_gather(delta, 'tm', axis=0, tiled=True)  44.6 us
    all_gather x1, blocking collectives, on_device(): lax.all_gather(log_norm, 'tm', axis=0, tiled=True)  34.1 us
    all_gather x1, blocking collectives, on_device(): incoming = lax.all_gather(cotangent, 'tensor', axis=1, tiled=True)[0]  12.8 us
  transfers between devices with their start and end apart: 6, of which 5 were waited for; matrix products, arithmetic and copies ran while one was open for 10% of the time, Pallas kernels for 0%

commit v1 on v0

v1 whole, which is shorter than its diff:
```python
import functools
import math

import jax
import jax.numpy as jnp
from jax import lax
from jax.experimental import pallas as pl
from jax.experimental.pallas import tpu as pltpu
from jax.sharding import PartitionSpec as P

HD = 128
TILE = 128
BLK = 256
SCALE = HD ** (-0.5)
LOG2E = math.log2(math.e)
LOW = -1e30
F32 = jnp.float32
BF16 = jnp.bfloat16
X, ZH, PAR, Y = 0, 1, 2, 3
NN = (((1,), (0,)), ((), ()))
NT = (((1,), (1,)), ((), ()))


def dot(a, b, dims=NN):
    return lax.dot_general(a, b, dims, preferred_element_type=F32)


def call(body, outs, ins, flops=0, scratch=(), smem=1, vmem=48):
    specs = [pl.BlockSpec(memory_space=pltpu.SMEM)] * smem
    specs += [pl.BlockSpec(memory_space=pltpu.VMEM)] * (len(ins) - smem)
    shapes = [jax.ShapeDtypeStruct(s, d) for s, d in outs]
    moved = sum(math.prod(a.shape) * a.dtype.itemsize for a in list(ins) + shapes)
    return pl.pallas_call(
        body,
        out_shape=shapes,
        in_specs=specs,
        out_specs=[pl.BlockSpec(memory_space=pltpu.VMEM)] * len(outs),
        scratch_shapes=list(scratch),
        compiler_params=pltpu.CompilerParams(vmem_limit_bytes=vmem * 2**20),
        cost_estimate=pl.CostEstimate(flops=flops, bytes_accessed=moved, transcendentals=0),
    )(*ins)


def split_heads(pos, q, k, v, keep, send):
    for n, ref in enumerate((q, k, v)):
        rows = slice(n * TILE, (n + 1) * TILE)

        @pl.when(pos[PAR] == 0)
        def _():
            keep[rows, :] = ref[:, :HD]
            send[rows, :] = ref[:, HD:]

        @pl.when(pos[PAR] != 0)
        def _():
            keep[rows, :] = ref[:, HD:]
            send[rows, :] = ref[:, :HD]


def back_project(pos, w, c0, c1, c2, c3, cot, keep, send):
    for d, ref in enumerate((c0, c1, c2, c3)):
        start = pl.multiple_of(lax.rem(pos[Y] - d + 4, 4) * 32, 32)
        cot[pl.ds(start, 32), :] = ref[...]
    full = cot[...]
    mine = pl.multiple_of(pos[PAR] * HD, HD)
    other = pl.multiple_of((1 - pos[PAR]) * HD, HD)
    keep[...] = dot(w[pl.ds(mine, HD), :], full, NT).astype(BF16)
    send[...] = dot(w[pl.ds(other, HD), :], full, NT).astype(BF16)


def bias_rows(pos, mask, query_x):
    lane = lax.broadcasted_iota(jnp.int32, (1, BLK), 1)
    par = pos[PAR]
    query = (query_x * 4 + pos[ZH]) * 2
    rows = []
    for e in range(4):
        key = (pos[X] * 4 + lax.rem(pos[ZH] - e + 4, 4)) * 2
        for tile in (par, 1 - par):
            near = jnp.where(mask[query + par, key + tile] > 0, 0.0, LOW)
            far = jnp.where(mask[query + 1 - par, key + tile] > 0, 0.0, LOW)
            rows.append(jnp.where(lane < TILE, near, far))
    return rows


def scores_of(keys, queries, rows, e):
    raw = dot(keys, queries, NT) * (SCALE * LOG2E)
    return jnp.concatenate([raw[:TILE] + rows[2 * e], raw[TILE:] + rows[2 * e + 1]], axis=0)


def split3(value):
    high = value.astype(BF16).astype(F32)
    rest = value - high
    middle = rest.astype(BF16).astype(F32)
    low = (rest - middle).astype(BF16).astype(F32)
    return high, middle, low


def forward(pos, mask, kv0, kv1, kv2, kv3, qd0, qd1, qd2, qd3, p0, p1, p2, p3, qd, part, stats):
    kvs = (kv0, kv1, kv2, kv3)
    for d, ref in enumerate((qd0, qd1, qd2, qd3)):
        qd[d] = ref[...]
    values_t = [kv[BLK:, :].astype(F32).T.astype(BF16) for kv in kvs]

    def block(d, carry):
        query_x = lax.rem(pos[X] - d + 4, 4)
        rows = bias_rows(pos, mask, query_x)
        queries = qd[d, :BLK, :]
        scores = [scores_of(kvs[e][:BLK, :], queries, rows, e) for e in range(4)]
        largest = functools.reduce(
            jnp.maximum, [jnp.max(s, axis=0, keepdims=True) for s in scores]
        )
        largest = jnp.maximum(largest, 0.1 * LOW)
        total = jnp.zeros((1, BLK), F32)
        summed = jnp.zeros((HD, BLK), F32)
        for e in range(4):
            weights = jnp.exp2(scores[e] - largest)
            total = total + jnp.sum(weights, axis=0, keepdims=True)
            summed = summed + dot(values_t[e], weights.astype(BF16))
        some = total > 0.0
        safe = jnp.where(some, total, 1.0)
        summed = summed / safe
        lse = jnp.where(some, largest + jnp.log2(safe), LOW)
        grad_t = jnp.concatenate(
            [qd[d, BLK : BLK + TILE, :], qd[d, BLK + TILE :, :]], axis=1
        ).astype(F32)
        delta = jnp.sum(grad_t * summed, axis=0, keepdims=True)
        part[d] = summed.astype(BF16)
        row = lax.broadcasted_iota(jnp.int32, (16, BLK), 0)
        packed = jnp.zeros((16, BLK), F32)
        for n, value in enumerate(split3(lse) + split3(delta)):
            packed = jnp.where(row == n, value, packed)
        stats[pl.ds(pl.multiple_of(query_x * 16, 16), 16), :] = packed.astype(BF16)
        return carry

    lax.fori_loop(0, 4, block, 0)
    for d, ref in enumerate((p0, p1, p2, p3)):
        ref[:HD, :] = part[d]
        ref[HD:, :] = stats[...]


def merge_stats(packs, block):
    lses, deltas = [], []
    for pack in packs:
        s = pack[pl.ds(pl.multiple_of(HD + block * 16, 16), 16), :].astype(F32)
        lses.append(s[0:1] + s[1:2] + s[2:3])
        deltas.append(s[3:4] + s[4:5] + s[5:6])
    largest = functools.reduce(jnp.maximum, lses)
    weights = [jnp.exp2(v - largest) for v in lses]
    total = sum(weights)
    shares = [w / total for w in weights]
    delta = sum(w * v for w, v in zip(shares, deltas))
    return largest + jnp.log2(total), delta, shares


def backward(
    pos, mask, kv0, kv1, kv2, kv3, qd0, qd1, qd2, qd3, p0, p1, p2, p3,
    dkv0, dkv1, dkv2, dkv3, dq0, dq1, dq2, dq3, qd, dq, dkv,
):
    kvs = (kv0, kv1, kv2, kv3)
    for d, ref in enumerate((qd0, qd1, qd2, qd3)):
        qd[d] = ref[...]
    dkv[...] = jnp.zeros_like(dkv)
    keys_t = [kv[:BLK, :].astype(F32).T.astype(BF16) for kv in kvs]

    def block(d, carry):
        query_x = lax.rem(pos[X] - d + 4, 4)
        rows = bias_rows(pos, mask, query_x)
        lse, delta, _ = merge_stats((p0, p1, p2, p3), query_x)
        queries = qd[d, :BLK, :]
        grad_t = jnp.concatenate([qd[d, BLK : BLK + TILE, :], qd[d, BLK + TILE :, :]], axis=1)
        grad_query = jnp.zeros((HD, BLK), F32)
        for e in range(4):
            probs = jnp.exp2(scores_of(kvs[e][:BLK, :], queries, rows, e) - lse)
            grad_probs = dot(kvs[e][BLK:, :], grad_t)
            grad_scores = (probs * (grad_probs - delta)).astype(BF16)
            dkv[e, BLK:, :] += dot(probs.astype(BF16), grad_t, NT)
            dkv[e, :BLK, :] += dot(grad_scores, queries)
            grad_query = grad_query + dot(keys_t[e], grad_scores)
        dq[d] = (grad_query * SCALE).astype(BF16)
        return carry

    lax.fori_loop(0, 4, block, 0)
    for e, ref in enumerate((dkv0, dkv1, dkv2, dkv3)):
        ref[:BLK, :] = (dkv[e, :BLK, :] * SCALE).astype(BF16)
        ref[BLK:, :] = dkv[e, BLK:, :].astype(BF16)
    for d, ref in enumerate((dq0, dq1, dq2, dq3)):
        ref[...] = dq[d]


def attend(pos, p0, p1, p2, p3, att, send):
    packs = (p0, p1, p2, p3)
    _, _, shares = merge_stats(packs, pos[X])
    out = sum(w * p[:HD, :].astype(F32) for w, p in zip(shares, packs)).astype(BF16)
    att[...] = out
    send[...] = out[:, TILE:]


def weight_part(pos, att, near, far, keep, send):
    both = dot(att[:, :TILE], near[...]) + dot(att[:, TILE:], far[...])

    @pl.when(pos[4] == 0)
    def _():
        keep[...] = both[:, :1024]
        send[...] = both[:, 1024:]

    @pl.when(pos[4] != 0)
    def _():
        keep[...] = both[:, 1024:]
        send[...] = both[:, :1024]


def weight_cut(pos, mine, other, b0, b1, b2, b3):
    for d, ref in enumerate((b0, b1, b2, b3)):
        columns = pl.ds(pl.multiple_of(lax.rem(pos[X] + d, 4) * 256, 256), 256)
        ref[...] = (mine[:, columns] + other[:, columns]).astype(BF16)


def sum_four(a, b, c, d, out):
    out[...] = (
        (a[...].astype(F32) + b[...].astype(F32)) + (c[...].astype(F32) + d[...].astype(F32))
    ).astype(out.dtype)


def weight_row(pos, f0, f1, f2, f3, out):
    for d, ref in enumerate((f0, f1, f2, f3)):
        columns = pl.ds(pl.multiple_of(lax.rem(pos[X] - d + 4, 4) * 256, 256), 256)
        out[:, columns] = ref[...]


def weight_out(pos, here, pair, core, both, out):
    par, dp = pos[PAR], pos[4]
    for rows, columns, ref in (
        (par, dp, here), (1 - par, dp, pair), (par, 1 - dp, core), (1 - par, 1 - dp, both),
    ):
        out[
            pl.ds(pl.multiple_of(rows * HD, HD), HD),
            pl.ds(pl.multiple_of(columns * 1024, 1024), 1024),
        ] = ref[...].astype(F32)


def mix(pos, att, other, w, m0, m1, m2, m3, full):
    mine_rows = pl.ds(pl.multiple_of(pos[PAR] * HD, HD), HD)
    other_rows = pl.ds(pl.multiple_of((1 - pos[PAR]) * HD, HD), HD)
    mine_t = att[:, :TILE].astype(F32).T.astype(BF16)
    other_t = other[...].astype(F32).T.astype(BF16)
    full[...] = (dot(mine_t, w[mine_rows, :]) + dot(other_t, w[other_rows, :])).astype(BF16)
    for d, ref in enumerate((m0, m1, m2, m3)):
        ref[...] = full[pl.ds(pl.multiple_of(lax.rem(pos[Y] + d, 4) * 32, 32), 32), :]


def gather_grads(k0, k1, k2, k3, q0, q1, q2, q3, keep, send):
    kv = (k0[...].astype(F32) + k1[...].astype(F32)) + (k2[...].astype(F32) + k3[...].astype(F32))
    q = (q0[...].astype(F32) + q1[...].astype(F32)) + (q2[...].astype(F32) + q3[...].astype(F32))
    keep[:TILE, :] = q[:, :TILE].T.astype(BF16)
    send[:TILE, :] = q[:, TILE:].T.astype(BF16)
    keep[TILE : 2 * TILE, :] = kv[:TILE].astype(BF16)
    send[TILE : 2 * TILE, :] = kv[TILE:BLK].astype(BF16)
    keep[2 * TILE :, :] = kv[BLK : BLK + TILE].astype(BF16)
    send[2 * TILE :, :] = kv[BLK + TILE :].astype(BF16)


def join_heads(pos, mine, other, q, k, v):
    for n, ref in enumerate((q, k, v)):
        rows = slice(n * TILE, (n + 1) * TILE)

        @pl.when(pos[PAR] == 0)
        def _():
            ref[:, :HD] = mine[rows, :]
            ref[:, HD:] = other[rows, :]

        @pl.when(pos[PAR] != 0)
        def _():
            ref[:, HD:] = mine[rows, :]
            ref[:, :HD] = other[rows, :]


def over_x(a, d):
    return lax.ppermute(a, "tm", [(i, (i + 8 * d) % 32) for i in range(32)])


def over_z(a, d):
    return lax.ppermute(a, "tm", [(i, i // 8 * 8 + (i + 2 * d) % 8) for i in range(32)])


def over_pair(a):
    return lax.ppermute(a, "tm", [(i, i ^ 1) for i in range(32)])


def over_y(a, d):
    return lax.ppermute(a, "tensor", [(i, (i + d) % 4) for i in range(4)])


def over_core(a):
    return lax.ppermute(a, "dp", [(0, 1), (1, 0)])


def on_device(query_rows, key_rows, value_rows, out_weight, cotangent, tile_mask):
    tm = lax.axis_index("tm")
    pos = jnp.stack(
        [tm // 8, tm % 8 // 2, tm % 2, lax.axis_index("tensor"), lax.axis_index("dp")]
    ).astype(jnp.int32)
    kv_mm = 2 * 1024 * 1024 * HD

    keep, send = call(
        split_heads,
        [((3 * TILE, HD), BF16)] * 2,
        (pos, query_rows[0], key_rows[0], value_rows[0]),
    )
    recv = over_pair(send)
    cots = [cotangent[0]] + [over_y(cotangent[0], d) for d in (1, 3, 2)]
    cots = [cots[0], cots[1], cots[3], cots[2]]
    cot, grad_keep, grad_send = call(
        back_project,
        [((TILE, 2048), BF16), ((HD, TILE), BF16), ((HD, TILE), BF16)],
        (pos, out_weight, *cots),
        flops=2 * TILE * 256 * 2048,
    )
    kv = jnp.concatenate(
        [keep[TILE : 2 * TILE], recv[TILE : 2 * TILE], keep[2 * TILE :], recv[2 * TILE :]]
    )
    kvs = [kv] + [over_z(kv, d) for d in (1, 2, 3)]
    grad_recv = over_pair(grad_send)
    qd = jnp.concatenate([keep[:TILE], recv[:TILE], grad_keep, grad_recv])
    qds = [qd] + [over_x(qd, d) for d in (1, 2, 3)]
    cot_far = over_pair(cot)

    packs = call(
        forward,
        [((192, BLK), BF16)] * 4,
        (pos, tile_mask, *kvs, *qds),
        flops=2 * kv_mm,
        scratch=[
            pltpu.VMEM((4, 2 * BLK, HD), BF16),
            pltpu.VMEM((4, HD, BLK), BF16),
            pltpu.VMEM((64, BLK), BF16),
        ],
        smem=2,
    )
    packs = [packs[0]] + [over_x(packs[d], -d) for d in (1, 2, 3)]

    att, att_send = call(attend, [((HD, BLK), BF16), ((HD, TILE), BF16)], (pos, *packs))
    gw_keep, gw_send = call(
        weight_part,
        [((HD, 1024), F32)] * 2,
        (pos, att, cot, cot_far),
        flops=2 * HD * BLK * 2048,
    )
    gw_recv = over_core(gw_send)
    cuts = call(weight_cut, [((HD, 256), BF16)] * 4, (pos, gw_keep, gw_recv))
    cuts = [cuts[0]] + [over_x(cuts[d], d) for d in (1, 2, 3)]
    (share,) = call(sum_four, [((HD, 256), BF16)], cuts, smem=0)
    shares = [share] + [over_z(share, d) for d in (1, 2, 3)]
    (done,) = call(sum_four, [((HD, 256), BF16)], shares, smem=0)
    dones = [done] + [over_x(done, d) for d in (1, 2, 3)]
    (here,) = call(weight_row, [((HD, 1024), BF16)], (pos, *dones))
    pair = over_pair(here)
    core, both = over_core(here), over_core(pair)
    (grad_weight,) = call(weight_out, [((256, 2048), F32)], (pos, here, pair, core, both))

    att_recv = over_pair(att_send)
    mixes = call(
        mix,
        [((32, 2048), BF16)] * 4,
        (pos, att, att_recv, out_weight),
        flops=2 * TILE * 256 * 2048,
        scratch=[pltpu.VMEM((TILE, 2048), BF16)],
    )
    mixes = [mixes[0]] + [over_y(mixes[d], d) for d in (1, 2, 3)]
    (mixed,) = call(sum_four, [((32, 2048), BF16)], mixes, smem=0)

    grads = call(
        backward,
        [((2 * BLK, HD), BF16)] * 4 + [((HD, BLK), BF16)] * 4,
        (pos, tile_mask, *kvs, *qds, *packs),
        flops=5 * kv_mm,
        scratch=[
            pltpu.VMEM((4, 2 * BLK, HD), BF16),
            pltpu.VMEM((4, HD, BLK), BF16),
            pltpu.VMEM((4, 2 * BLK, HD), F32),
        ],
        smem=2,
    )
    dkvs = [grads[0]] + [over_z(grads[d], -d) for d in (1, 2, 3)]
    dqs = [grads[4]] + [over_x(grads[4 + d], -d) for d in (1, 2, 3)]
    out_keep, out_send = call(
        gather_grads, [((3 * TILE, HD), BF16)] * 2, (*dkvs, *dqs), smem=0
    )
    out_recv = over_pair(out_send)
    grad_q, grad_k, grad_v = call(
        join_heads, [((TILE, 2 * HD), BF16)] * 3, (pos, out_keep, out_recv)
    )
    return (mixed[None], grad_q[None], grad_k[None], grad_v[None], grad_weight)


def solution(mesh):
    rows = P("dp", "tm", "tensor")
    blocks = P("dp", ("tm", "tensor"), None)
    weight = P("tensor", None)
    return jax.shard_map(
        on_device,
        mesh=mesh,
        in_specs=(rows, rows, rows, weight, blocks, P()),
        out_specs=(blocks, rows, rows, rows, weight),
        check_vma=False,
    )
```

time: 552 us -> 137 us (0.25)
  the two profiles are of different devices: /device:TPU:1 before, /device:TPU:6 now
where the time goes in v1:
time: 137 us
  waiting for transfers between devices  56.2 us (41%)
  starting transfers between devices  55.9 us (41%)
  Pallas kernels  19.1 us (14%)
  local copies, waits for them, and re-layouts  4.75 us (3%)
    ppermute x9, waiting for transfers between devices, over_z(): lax.ppermute(a, 'tm', [(i, i // 8 * 8 + (i + 2 * d) % 8) for i in range(3...  28.9 us
    ppermute x15, starting transfers between devices, over_x(): return lax.ppermute(a, 'tm', [(i, (i + 8 * d) % 32) for i in range(32)])  21.1 us
    ppermute x9, starting transfers between devices, over_z(): lax.ppermute(a, 'tm', [(i, i // 8 * 8 + (i + 2 * d) % 8) for i in range(3...  20.8 us
    pallas_call x15, Pallas kernels, call(): pl.pallas_call(body, out_shape=shapes, in_specs=specs, out_specs=[pl.Bloc...  19.1 us
    ppermute x15, waiting for transfers between devices, over_x(): return lax.ppermute(a, 'tm', [(i, (i + 8 * d) % 32) for i in range(32)])  16.4 us
    ppermute x6, starting transfers between devices, over_pair(): return lax.ppermute(a, 'tm', [(i, i ^ 1) for i in range(32)])  6.84 us
    ppermute x6, starting transfers between devices, over_y(): return lax.ppermute(a, 'tensor', [(i, (i + d) % 4) for i in range(4)])  6.29 us
    unnamed x14, local copies, waits for them, and re-layouts  4.65 us
  transfers between devices with their start and end apart: 39, of which 21 were waited for; matrix products, arithmetic and copies ran while one was open for 0% of the time, Pallas kernels for 10%

profile of v1, /device:TPU:6, one launch (start us, length us, event | category | flops | bytes accessed | tf_op | source)
XLA Modules:
  0.0 136.8 jit_solution(7937834634706978374)
XLA Ops:
  0.6 3.1 %collective-permute-start.6 = (bf16[32,2048]{1,0:T(8,128)(2,1)}, bf16[32,2048]{1,0:T(8,128)(2,1)S(1)}, u32[]{:S(2)}, u32[]{:S(2)}) collective-permute-start(bf16[32,2048]{1,0:T(8,128)(2,1)} %bitcast.13), channel_id=1, source_target_pairs={{0,6},{2,0},{4,2},{6,4},{1,7},{3,1},{5,3},{7,5},{8,14},{10,8},{12,... | collective-permute-start | bytes 393224 | tf_op jit(solution)/shard_map/ppermute | solution.py:289
  3.7 0.6 collective-permute-start.5
  4.4 1.0 collective-permute-start.4
  5.4 0.8 copy-done.3
  6.3 0.8 copy-done.4
  7.1 0.8 copy-done.5
  7.9 0.6 shard_map.101
  8.6 2.0 %collective-permute-start = (bf16[384,128]{1,0:T(8,128)(2,1)S(1)}, bf16[384,128]{1,0:T(8,128)(2,1)S(1)}, u32[]{:S(2)}, u32[]{:S(2)}) collective-permute-start(bf16[384,128]{1,0:T(8,128)(2,1)S(1)} %get-tuple-element.40), channel_id=1, source_target_pairs={{0,8},{8,0},{16,24},{24,16},{32,40},{40,32},{48,56},{56,48},{64,72... | collective-permute-start | bytes 294920 | tf_op jit(solution)/shard_map/ppermute | solution.py:285
  10.6 2.7 %collective-permute-done = bf16[384,128]{1,0:T(8,128)(2,1)S(1)} collective-permute-done((bf16[384,128]{1,0:T(8,128)(2,1)S(1)}, bf16[384,128]{1,0:T(8,128)(2,1)S(1)}, u32[]{:S(2)}, u32[]{:S(2)}) %collective-permute-start) | collective-permute-done | bytes 98336 | tf_op jit(solution)/shard_map/ppermute | solution.py:285
  13.3 1.2 copy-done
  14.5 0.9 copy-done.2
  15.4 1.0 shard_map.102
  16.4 2.0 %collective-permute-start.7 = (bf16[128,128]{1,0:T(8,128)(2,1)S(1)}, bf16[128,128]{1,0:T(8,128)(2,1)S(1)}, u32[]{:S(2)}, u32[]{:S(2)}) collective-permute-start(bf16[128,128]{1,0:T(8,128)(2,1)S(1)} %get-tuple-element.42), channel_id=1, source_target_pairs={{0,8},{8,0},{16,24},{24,16},{32,40},{40,32},{48,56},{56,48},{64,72... | collective-permute-start | bytes 98312 | tf_op jit(solution)/shard_map/ppermute | solution.py:285
  18.6 6.4 %collective-permute-start.3 = (bf16[512,128]{1,0:T(8,128)(2,1)S(1)}, bf16[512,128]{1,0:T(8,128)(2,1)S(1)}, u32[]{:S(2)}, u32[]{:S(2)}) collective-permute-start(bf16[512,128]{1,0:T(8,128)(2,1)S(1)} %pad_maximum_fusion.kv0), channel_id=1, source_target_pairs={{0,48},{8,56},{16,0},{24,8},{32,16},{40,24},{48,32},{56,40},{64,11... | collective-permute-start | bytes 393224 | tf_op jit(solution)/shard_map/ppermute | solution.py:281
  24.9 1.0 collective-permute-start.2
  25.9 2.8 %collective-permute-start.1 = (bf16[512,128]{1,0:T(8,128)(2,1)S(1)}, bf16[512,128]{1,0:T(8,128)(2,1)S(1)}, u32[]{:S(2)}, u32[]{:S(2)}) collective-permute-start(bf16[512,128]{1,0:T(8,128)(2,1)S(1)} %pad_maximum_fusion.kv0), channel_id=1, source_target_pairs={{0,16},{8,24},{16,32},{24,40},{32,48},{40,56},{48,0},{56,8},{64,80... | collective-permute-start | bytes 393224 | tf_op jit(solution)/shard_map/ppermute | solution.py:281
  28.8 0.9 collective-permute-start.10
  29.7 1.1 collective-permute-start.9
  30.8 16.2 %collective-permute-done.2.kv2 = bf16[512,128]{1,0:T(8,128)(2,1)S(1)} collective-permute-done((bf16[512,128]{1,0:T(8,128)(2,1)S(1)}, bf16[512,128]{1,0:T(8,128)(2,1)S(1)}, u32[]{:S(2)}, u32[]{:S(2)}) %collective-permute-start.2) | collective-permute-done | bytes 131104 | tf_op jit(solution)/shard_map/ppermute | solution.py:281
  47.0 0.5 collective-permute-start.8
  47.8 4.2 %collective-permute-done.8.qd1 = bf16[512,128]{1,0:T(8,128)(2,1)S(1)} collective-permute-done((bf16[512,128]{1,0:T(8,128)(2,1)S(1)}, bf16[512,128]{1,0:T(8,128)(2,1)S(1)}, u32[]{:S(2)}, u32[]{:S(2)}) %collective-permute-start.8) | collective-permute-done | bytes 131104 | tf_op jit(solution)/shard_map/ppermute | solution.py:277
  52.0 4.1 %shard_map.103 = (bf16[192,256]{1,0:T(8,128)(2,1)S(1)}, bf16[192,256]{1,0:T(8,128)(2,1)S(1)}, bf16[192,256]{1,0:T(8,128)(2,1)S(1)}, bf16[192,256]{1,0:T(8,128)(2,1)S(1)}) custom-call(s32[5]{0:T(128)S(1)} %stack.23.pos, s32[32,32]{1,0:T(8,128)S(1)} %copy-done.6, bf16[512,128]{1,0:T(8,128)(2,1)S(1)} %pad_maximum_fusion.kv0, ...), custom_call_target="tpu_custom_call" | custom-call | flops 536870912 | bytes 1445908 | tf_op jit(solution)/shard_map/pallas_call | solution.py:33
  56.0 0.9 collective-permute-start.11
  56.9 2.3 %collective-permute-start.12 = (bf16[192,256]{1,0:T(8,128)(2,1)S(1)}, bf16[192,256]{1,0:T(8,128)(2,1)S(1)}, u32[]{:S(2)}, u32[]{:S(2)}) collective-permute-start(bf16[192,256]{1,0:T(8,128)(2,1)S(1)} %get-tuple-element.45), channel_id=1, source_target_pairs={{0,128},{8,136},{16,144},{24,152},{32,160},{40,168},{48,176},{56,1... | collective-permute-start | bytes 294920 | tf_op jit(solution)/shard_map/ppermute | solution.py:277
  59.3 0.9 collective-permute-start.13
  60.1 1.8 %collective-permute-done.11.p1 = bf16[192,256]{1,0:T(8,128)(2,1)S(1)} collective-permute-done((bf16[192,256]{1,0:T(8,128)(2,1)S(1)}, bf16[192,256]{1,0:T(8,128)(2,1)S(1)}, u32[]{:S(2)}, u32[]{:S(2)}) %collective-permute-start.11) | collective-permute-done | bytes 98336 | tf_op jit(solution)/shard_map/ppermute | solution.py:277
  61.9 1.1 collective-permute-done.12.p2
  63.1 0.8 collective-permute-done.13.p3
  63.9 0.6 shard_map.104
  64.5 1.0 shard_map.110
  65.8 1.9 %collective-permute-done.26.other = f32[128,1024]{1,0:T(8,128)S(1)} collective-permute-done((f32[128,1024]{1,0:T(8,128)S(1)}, f32[128,1024]{1,0:T(8,128)S(1)}, u32[]{:S(2)}, u32[]{:S(2)}) %collective-permute-start.26) | collective-permute-done | bytes 524320 | tf_op jit(solution)/shard_map/ppermute | solution.py:293
  67.7 0.6 shard_map.111
  68.3 2.7 %collective-permute-start.27 = (bf16[128,256]{1,0:T(8,128)(2,1)S(1)}, bf16[128,256]{1,0:T(8,128)(2,1)S(1)}, u32[]{:S(2)}, u32[]{:S(2)}) collective-permute-start(bf16[128,256]{1,0:T(8,128)(2,1)S(1)} %get-tuple-element.70), channel_id=1, source_target_pairs={{0,64},{8,72},{16,80},{24,88},{32,96},{40,104},{48,112},{56,120},{... | collective-permute-start | bytes 196616 | tf_op jit(solution)/shard_map/ppermute | solution.py:277
  71.4 0.6 collective-permute-start.29
  72.0 2.1 %collective-permute-done.27.b = bf16[128,256]{1,0:T(8,128)(2,1)S(1)} collective-permute-done((bf16[128,256]{1,0:T(8,128)(2,1)S(1)}, bf16[128,256]{1,0:T(8,128)(2,1)S(1)}, u32[]{:S(2)}, u32[]{:S(2)}) %collective-permute-start.27) | collective-permute-done | bytes 65568 | tf_op jit(solution)/shard_map/ppermute | solution.py:277
  74.1 3.0 %collective-permute-done.28.c = bf16[128,256]{1,0:T(8,128)(2,1)S(1)} collective-permute-done((bf16[128,256]{1,0:T(8,128)(2,1)S(1)}, bf16[128,256]{1,0:T(8,128)(2,1)S(1)}, u32[]{:S(2)}, u32[]{:S(2)}) %collective-permute-start.28) | collective-permute-done | bytes 65568 | tf_op jit(solution)/shard_map/ppermute | solution.py:277
  77.2 0.4 collective-permute-done.29.d
  77.9 4.4 %collective-permute-start.31 = (bf16[128,256]{1,0:T(8,128)(2,1)S(1)}, bf16[128,256]{1,0:T(8,128)(2,1)S(1)}, u32[]{:S(2)}, u32[]{:S(2)}) collective-permute-start(bf16[128,256]{1,0:T(8,128)(2,1)S(1)} %shard_map.112.a), channel_id=1, source_target_pairs={{0,32},{8,40},{16,48},{24,56},{32,0},{40,8},{48,16},{56,24},{64,96... | collective-permute-start | bytes 196616 | tf_op jit(solution)/shard_map/ppermute | solution.py:281
  82.3 0.6 collective-permute-done.32.d
  82.9 4.5 %collective-permute-done.31.c = bf16[128,256]{1,0:T(8,128)(2,1)S(1)} collective-permute-done((bf16[128,256]{1,0:T(8,128)(2,1)S(1)}, bf16[128,256]{1,0:T(8,128)(2,1)S(1)}, u32[]{:S(2)}, u32[]{:S(2)}) %collective-permute-start.31) | collective-permute-done | bytes 65568 | tf_op jit(solution)/shard_map/ppermute | solution.py:281
  87.5 1.9 %collective-permute-done.30.b = bf16[128,256]{1,0:T(8,128)(2,1)S(1)} collective-permute-done((bf16[128,256]{1,0:T(8,128)(2,1)S(1)}, bf16[128,256]{1,0:T(8,128)(2,1)S(1)}, u32[]{:S(2)}, u32[]{:S(2)}) %collective-permute-start.30) | collective-permute-done | bytes 65568 | tf_op jit(solution)/shard_map/ppermute | solution.py:281
  89.5 2.6 %collective-permute-start.34 = (bf16[128,256]{1,0:T(8,128)(2,1)S(1)}, bf16[128,256]{1,0:T(8,128)(2,1)S(1)}, u32[]{:S(2)}, u32[]{:S(2)}) collective-permute-start(bf16[128,256]{1,0:T(8,128)(2,1)S(1)} %shard_map.113.f0), channel_id=1, source_target_pairs={{0,128},{8,136},{16,144},{24,152},{32,160},{40,168},{48,176},{56,1... | collective-permute-start | bytes 196616 | tf_op jit(solution)/shard_map/ppermute | solution.py:277
  92.1 1.6 %collective-permute-start.33 = (bf16[128,256]{1,0:T(8,128)(2,1)S(1)}, bf16[128,256]{1,0:T(8,128)(2,1)S(1)}, u32[]{:S(2)}, u32[]{:S(2)}) collective-permute-start(bf16[128,256]{1,0:T(8,128)(2,1)S(1)} %shard_map.113.f0), channel_id=1, source_target_pairs={{0,64},{8,72},{16,80},{24,88},{32,96},{40,104},{48,112},{56,120},{... | collective-permute-start | bytes 196616 | tf_op jit(solution)/shard_map/ppermute | solution.py:277
  93.7 2.0 %collective-permute-done.35.f3 = bf16[128,256]{1,0:T(8,128)(2,1)S(1)} collective-permute-done((bf16[128,256]{1,0:T(8,128)(2,1)S(1)}, bf16[128,256]{1,0:T(8,128)(2,1)S(1)}, u32[]{:S(2)}, u32[]{:S(2)}) %collective-permute-start.35) | collective-permute-done | bytes 65568 | tf_op jit(solution)/shard_map/ppermute | solution.py:277
  95.7 0.9 collective-permute-done.33.f1
  96.5 0.6 shard_map.114.here
  97.1 2.5 %collective-permute-start.36 = (bf16[128,1024]{1,0:T(8,128)(2,1)S(1)}, bf16[128,1024]{1,0:T(8,128)(2,1)S(1)}, u32[]{:S(2)}, u32[]{:S(2)}) collective-permute-start(bf16[128,1024]{1,0:T(8,128)(2,1)S(1)} %shard_map.114.here), channel_id=1, source_target_pairs={{0,8},{8,0},{16,24},{24,16},{32,40},{40,32},{48,56},{56,48},{64,72... | collective-permute-start | bytes 786440 | tf_op jit(solution)/shard_map/ppermute | solution.py:285
  99.7 5.4 %shard_map.107 = (bf16[512,128]{1,0:T(8,128)(2,1)S(1)}, bf16[512,128]{1,0:T(8,128)(2,1)S(1)}, bf16[512,128]{1,0:T(8,128)(2,1)S(1)}, bf16[512,128]{1,0:T(8,128)(2...) custom-call(s32[5]{0:T(128)S(1)} %stack.23.pos, ...), custom_call_target="tpu_custom_call" | custom-call | flops 1342177280 | bytes 2232340 | tf_op jit(solution)/shard_map/pallas_call | solution.py:33
  105.2 1.4 %collective-permute-start.21 = (bf16[128,256]{1,0:T(8,128)(2,1)S(1)}, bf16[128,256]{1,0:T(8,128)(2,1)S(1)}, u32[]{:S(2)}, u32[]{:S(2)}) collective-permute-start(bf16[128,256]{1,0:T(8,128)(2,1)S(1)} %get-tuple-element.58), channel_id=1, source_target_pairs={{0,192},{8,200},{16,208},{24,216},{32,224},{40,232},{48,240},{56,2... | collective-permute-start | bytes 196616 | tf_op jit(solution)/shard_map/ppermute | solution.py:277
  106.6 2.8 %collective-permute-start.22 = (bf16[128,256]{1,0:T(8,128)(2,1)S(1)}, bf16[128,256]{1,0:T(8,128)(2,1)S(1)}, u32[]{:S(2)}, u32[]{:S(2)}) collective-permute-start(bf16[128,256]{1,0:T(8,128)(2,1)S(1)} %get-tuple-element.59), channel_id=1, source_target_pairs={{0,128},{8,136},{16,144},{24,152},{32,160},{40,168},{48,176},{56,1... | collective-permute-start | bytes 196616 | tf_op jit(solution)/shard_map/ppermute | solution.py:277
  109.4 2.4 %collective-permute-start.23 = (bf16[128,256]{1,0:T(8,128)(2,1)S(1)}, bf16[128,256]{1,0:T(8,128)(2,1)S(1)}, u32[]{:S(2)}, u32[]{:S(2)}) collective-permute-start(bf16[128,256]{1,0:T(8,128)(2,1)S(1)} %get-tuple-element.60), channel_id=1, source_target_pairs={{0,64},{8,72},{16,80},{24,88},{32,96},{40,104},{48,112},{56,120},{... | collective-permute-start | bytes 196616 | tf_op jit(solution)/shard_map/ppermute | solution.py:277
  111.8 5.8 %collective-permute-start.19 = (bf16[512,128]{1,0:T(8,128)(2,1)S(1)}, bf16[512,128]{1,0:T(8,128)(2,1)S(1)}, u32[]{:S(2)}, u32[]{:S(2)}) collective-permute-start(bf16[512,128]{1,0:T(8,128)(2,1)S(1)} %get-tuple-element.55), channel_id=1, source_target_pairs={{0,32},{8,40},{16,48},{24,56},{32,0},{40,8},{48,16},{56,24},{64,96... | collective-permute-start | bytes 393224 | tf_op jit(solution)/shard_map/ppermute | solution.py:281
  117.8 0.5 collective-permute-start.38
  118.2 1.0 shard_map.105
  119.7 1.5 %collective-permute-done.19.k2 = bf16[512,128]{1,0:T(8,128)(2,1)S(1)} collective-permute-done((bf16[512,128]{1,0:T(8,128)(2,1)S(1)}, bf16[512,128]{1,0:T(8,128)(2,1)S(1)}, u32[]{:S(2)}, u32[]{:S(2)}) %collective-permute-start.19) | collective-permute-done | bytes 131104 | tf_op jit(solution)/shard_map/ppermute | solution.py:281
  121.2 0.9 collective-permute-start.16
  122.1 3.9 %collective-permute-done.20.k3 = bf16[512,128]{1,0:T(8,128)(2,1)S(1)} collective-permute-done((bf16[512,128]{1,0:T(8,128)(2,1)S(1)}, bf16[512,128]{1,0:T(8,128)(2,1)S(1)}, u32[]{:S(2)}, u32[]{:S(2)}) %collective-permute-start.20) | collective-permute-done | bytes 131104 | tf_op jit(solution)/shard_map/ppermute | solution.py:281
  125.9 0.4 collective-permute-start.17
  126.4 2.5 %collective-permute-done.15.b = bf16[32,2048]{1,0:T(8,128)(2,1)S(1)} collective-permute-done((bf16[32,2048]{1,0:T(8,128)(2,1)S(1)}, bf16[32,2048]{1,0:T(8,128)(2,1)S(1)}, u32[]{:S(2)}, u32[]{:S(2)}) %collective-permute-start.15) | collective-permute-done | bytes 131104 | tf_op jit(solution)/shard_map/ppermute | solution.py:289
  129.0 1.9 %collective-permute-done.17.d = bf16[32,2048]{1,0:T(8,128)(2,1)S(1)} collective-permute-done((bf16[32,2048]{1,0:T(8,128)(2,1)S(1)}, bf16[32,2048]{1,0:T(8,128)(2,1)S(1)}, u32[]{:S(2)}, u32[]{:S(2)}) %collective-permute-start.17) | collective-permute-done | bytes 131104 | tf_op jit(solution)/shard_map/ppermute | solution.py:289
  130.9 0.7 shard_map.106
  131.6 1.9 %collective-permute-done.24.other = bf16[384,128]{1,0:T(8,128)(2,1)S(1)} collective-permute-done((bf16[384,128]{1,0:T(8,128)(2,1)S(1)}, bf16[384,128]{1,0:T(8,128)(2,1)S(1)}, u32[]{:S(2)}, u32[]{:S(2)}) %collective-permute-start.24) | collective-permute-done | bytes 98336 | tf_op jit(solution)/shard_map/ppermute | solution.py:285
  133.5 1.3 shard_map.109
  134.8 2.0 %shard_map.115 = f32[256,2048]{1,0:T(8,128)} custom-call(s32[5]{0:T(128)S(1)} %stack.23.pos, bf16[128,1024]{1,0:T(8,128)(2,1)S(1)} %shard_map.114.here, bf16[128,1024]{1,0:T(8,128)(2,1)S(1)} %collective-permute-done.36.pair, bf16[128,1024]{1,0:T(8,128)(2,1)S(1)} %collective-permute-done.37.core, bf16[128,1024]{1,0:T(8,128)(2,1)S(1)} %collective-permute-done.38.both), custom_call_target="tpu_custom_call" | custom-call | bytes 3145748 | tf_op jit(solution)/shard_map/pallas_call | solution.py:33
  (48 shorter events, 2.5 us)
Async XLA Ops:
  0.6 51.3 %copy-start.6 = (s32[32,32]{1,0:T(8,128)S(1)}, s32[32,32]{1,0:T(8,128)}, u32[]{:S(2)}) copy-start(s32[32,32]{1,0:T(8,128)} %mask.3) | copy-start | bytes 12292
  0.6 12.6 %collective-permute-start.6 = (bf16[32,2048]{1,0:T(8,128)(2,1)}, bf16[32,2048]{1,0:T(8,128)(2,1)S(1)}, u32[]{:S(2)}, u32[]{:S(2)}) collective-permute-start(bf16[32,2048]{1,0:T(8,128)(2,1)} %bitcast.13), channel_id=1, source_target_pairs={{0,6},{2,0},{4,2},{6,4},{1,7},{3,1},{5,3},{7,5},{8,14},{10,8},{12,... | collective-permute-start | bytes 393224 | tf_op jit(solution)/shard_map/ppermute | solution.py:289
  3.7 9.6 %collective-permute-start.5 = (bf16[32,2048]{1,0:T(8,128)(2,1)}, bf16[32,2048]{1,0:T(8,128)(2,1)S(1)}, u32[]{:S(2)}, u32[]{:S(2)}) collective-permute-start(bf16[32,2048]{1,0:T(8,128)(2,1)} %bitcast.14), channel_id=1, source_target_pairs={{0,4},{2,6},{4,0},{6,2},{1,5},{3,7},{5,1},{7,3},{8,12},{10,14},{12... | collective-permute-start | bytes 393224 | tf_op jit(solution)/shard_map/ppermute | solution.py:289
  4.4 8.9 %collective-permute-start.4 = (bf16[32,2048]{1,0:T(8,128)(2,1)}, bf16[32,2048]{1,0:T(8,128)(2,1)S(1)}, u32[]{:S(2)}, u32[]{:S(2)}) collective-permute-start(bf16[32,2048]{1,0:T(8,128)(2,1)} %bitcast.15), channel_id=1, source_target_pairs={{0,2},{2,4},{4,6},{6,0},{1,3},{3,5},{5,7},{7,1},{8,10},{10,12},{12... | collective-permute-start | bytes 393224 | tf_op jit(solution)/shard_map/ppermute | solution.py:289
  5.4 0.8 copy-start.3
  6.3 0.8 copy-start.4
  7.1 0.8 copy-start.5
  8.6 4.7 %collective-permute-start = (bf16[384,128]{1,0:T(8,128)(2,1)S(1)}, bf16[384,128]{1,0:T(8,128)(2,1)S(1)}, u32[]{:S(2)}, u32[]{:S(2)}) collective-permute-start(bf16[384,128]{1,0:T(8,128)(2,1)S(1)} %get-tuple-element.40), channel_id=1, source_target_pairs={{0,8},{8,0},{16,24},{24,16},{32,40},{40,32},{48,56},{56,48},{64,72... | collective-permute-start | bytes 294920 | tf_op jit(solution)/shard_map/ppermute | solution.py:285
  13.3 1.2 copy-start
  14.5 0.9 copy-start.2
  16.4 12.3 %collective-permute-start.7 = (bf16[128,128]{1,0:T(8,128)(2,1)S(1)}, bf16[128,128]{1,0:T(8,128)(2,1)S(1)}, u32[]{:S(2)}, u32[]{:S(2)}) collective-permute-start(bf16[128,128]{1,0:T(8,128)(2,1)S(1)} %get-tuple-element.42), channel_id=1, source_target_pairs={{0,8},{8,0},{16,24},{24,16},{32,40},{40,32},{48,56},{56,48},{64,72... | collective-permute-start | bytes 98312 | tf_op jit(solution)/shard_map/ppermute | solution.py:285
  18.4 46.1 %collective-permute-start.25 = (bf16[128,2048]{1,0:T(8,128)(2,1)S(1)}, bf16[128,2048]{1,0:T(8,128)(2,1)S(1)}, u32[]{:S(2)}, u32[]{:S(2)}) collective-permute-start(bf16[128,2048]{1,0:T(8,128)(2,1)S(1)} %get-tuple-element.66.near), channel_id=1, source_target_pairs={{0,8},{8,0},{16,24},{24,16},{32,40},{40,32},{48,56},{56,48},{64,72... | collective-permute-start | bytes 1572872 | tf_op jit(solution)/shard_map/ppermute | solution.py:285
  18.6 11.1 %collective-permute-start.3 = (bf16[512,128]{1,0:T(8,128)(2,1)S(1)}, bf16[512,128]{1,0:T(8,128)(2,1)S(1)}, u32[]{:S(2)}, u32[]{:S(2)}) collective-permute-start(bf16[512,128]{1,0:T(8,128)(2,1)S(1)} %pad_maximum_fusion.kv0), channel_id=1, source_target_pairs={{0,48},{8,56},{16,0},{24,8},{32,16},{40,24},{48,32},{56,40},{64,11... | collective-permute-start | bytes 393224 | tf_op jit(solution)/shard_map/ppermute | solution.py:281
  24.9 22.1 %collective-permute-start.2 = (bf16[512,128]{1,0:T(8,128)(2,1)S(1)}, bf16[512,128]{1,0:T(8,128)(2,1)S(1)}, u32[]{:S(2)}, u32[]{:S(2)}) collective-permute-start(bf16[512,128]{1,0:T(8,128)(2,1)S(1)} %pad_maximum_fusion.kv0), channel_id=1, source_target_pairs={{0,32},{8,40},{16,48},{24,56},{32,0},{40,8},{48,16},{56,24},{64,96... | collective-permute-start | bytes 393224 | tf_op jit(solution)/shard_map/ppermute | solution.py:281
  25.9 21.8 %collective-permute-start.1 = (bf16[512,128]{1,0:T(8,128)(2,1)S(1)}, bf16[512,128]{1,0:T(8,128)(2,1)S(1)}, u32[]{:S(2)}, u32[]{:S(2)}) collective-permute-start(bf16[512,128]{1,0:T(8,128)(2,1)S(1)} %pad_maximum_fusion.kv0), channel_id=1, source_target_pairs={{0,16},{8,24},{16,32},{24,40},{32,48},{40,56},{48,0},{56,8},{64,80... | collective-permute-start | bytes 393224 | tf_op jit(solution)/shard_map/ppermute | solution.py:281
  28.8 19.0 %collective-permute-start.10 = (bf16[512,128]{1,0:T(8,128)(2,1)S(1)}, bf16[512,128]{1,0:T(8,128)(2,1)S(1)}, u32[]{:S(2)}, u32[]{:S(2)}) collective-permute-start(bf16[512,128]{1,0:T(8,128)(2,1)S(1)} %pad_maximum_fusion.1.qd0), channel_id=1, source_target_pairs={{0,192},{8,200},{16,208},{24,216},{32,224},{40,232},{48,240},{56,2... | collective-permute-start | bytes 393224 | tf_op jit(solution)/shard_map/ppermute | solution.py:277
  29.7 18.1 %collective-permute-start.9 = (bf16[512,128]{1,0:T(8,128)(2,1)S(1)}, bf16[512,128]{1,0:T(8,128)(2,1)S(1)}, u32[]{:S(2)}, u32[]{:S(2)}) collective-permute-start(bf16[512,128]{1,0:T(8,128)(2,1)S(1)} %pad_maximum_fusion.1.qd0), channel_id=1, source_target_pairs={{0,128},{8,136},{16,144},{24,152},{32,160},{40,168},{48,176},{56,1... | collective-permute-start | bytes 393224 | tf_op jit(solution)/shard_map/ppermute | solution.py:277
  47.0 5.0 %collective-permute-start.8 = (bf16[512,128]{1,0:T(8,128)(2,1)S(1)}, bf16[512,128]{1,0:T(8,128)(2,1)S(1)}, u32[]{:S(2)}, u32[]{:S(2)}) collective-permute-start(bf16[512,128]{1,0:T(8,128)(2,1)S(1)} %pad_maximum_fusion.1.qd0), channel_id=1, source_target_pairs={{0,64},{8,72},{16,80},{24,88},{32,96},{40,104},{48,112},{56,120},{... | collective-permute-start | bytes 393224 | tf_op jit(solution)/shard_map/ppermute | solution.py:277
  56.0 5.9 %collective-permute-start.11 = (bf16[192,256]{1,0:T(8,128)(2,1)S(1)}, bf16[192,256]{1,0:T(8,128)(2,1)S(1)}, u32[]{:S(2)}, u32[]{:S(2)}) collective-permute-start(bf16[192,256]{1,0:T(8,128)(2,1)S(1)} %get-tuple-element.44), channel_id=1, source_target_pairs={{0,192},{8,200},{16,208},{24,216},{32,224},{40,232},{48,240},{56,2... | collective-permute-start | bytes 294920 | tf_op jit(solution)/shard_map/ppermute | solution.py:277
  56.9 6.1 %collective-permute-start.12 = (bf16[192,256]{1,0:T(8,128)(2,1)S(1)}, bf16[192,256]{1,0:T(8,128)(2,1)S(1)}, u32[]{:S(2)}, u32[]{:S(2)}) collective-permute-start(bf16[192,256]{1,0:T(8,128)(2,1)S(1)} %get-tuple-element.45), channel_id=1, source_target_pairs={{0,128},{8,136},{16,144},{24,152},{32,160},{40,168},{48,176},{56,1... | collective-permute-start | bytes 294920 | tf_op jit(solution)/shard_map/ppermute | solution.py:277
  59.3 4.6 %collective-permute-start.13 = (bf16[192,256]{1,0:T(8,128)(2,1)S(1)}, bf16[192,256]{1,0:T(8,128)(2,1)S(1)}, u32[]{:S(2)}, u32[]{:S(2)}) collective-permute-start(bf16[192,256]{1,0:T(8,128)(2,1)S(1)} %get-tuple-element.46), channel_id=1, source_target_pairs={{0,64},{8,72},{16,80},{24,88},{32,96},{40,104},{48,112},{56,120},{... | collective-permute-start | bytes 294920 | tf_op jit(solution)/shard_map/ppermute | solution.py:277
  65.5 2.2 %collective-permute-start.26 = (f32[128,1024]{1,0:T(8,128)S(1)}, f32[128,1024]{1,0:T(8,128)S(1)}, u32[]{:S(2)}, u32[]{:S(2)}) collective-permute-start(f32[128,1024]{1,0:T(8,128)S(1)} %get-tuple-element.68), channel_id=1, source_target_pairs={{0,1},{1,0},{2,3},{3,2},{4,5},{5,4},{6,7},{7,6},{8,9},{9,8},{10,11... | collective-permute-start | bytes 1572872 | tf_op jit(solution)/shard_map/ppermute | solution.py:293
  68.3 5.8 %collective-permute-start.27 = (bf16[128,256]{1,0:T(8,128)(2,1)S(1)}, bf16[128,256]{1,0:T(8,128)(2,1)S(1)}, u32[]{:S(2)}, u32[]{:S(2)}) collective-permute-start(bf16[128,256]{1,0:T(8,128)(2,1)S(1)} %get-tuple-element.70), channel_id=1, source_target_pairs={{0,64},{8,72},{16,80},{24,88},{32,96},{40,104},{48,112},{56,120},{... | collective-permute-start | bytes 196616 | tf_op jit(solution)/shard_map/ppermute | solution.py:277
  71.1 6.1 %collective-permute-start.28 = (bf16[128,256]{1,0:T(8,128)(2,1)S(1)}, bf16[128,256]{1,0:T(8,128)(2,1)S(1)}, u32[]{:S(2)}, u32[]{:S(2)}) collective-permute-start(bf16[128,256]{1,0:T(8,128)(2,1)S(1)} %get-tuple-element.71), channel_id=1, source_target_pairs={{0,128},{8,136},{16,144},{24,152},{32,160},{40,168},{48,176},{56,1... | collective-permute-start | bytes 196616 | tf_op jit(solution)/shard_map/ppermute | solution.py:277
  71.4 6.2 %collective-permute-start.29 = (bf16[128,256]{1,0:T(8,128)(2,1)S(1)}, bf16[128,256]{1,0:T(8,128)(2,1)S(1)}, u32[]{:S(2)}, u32[]{:S(2)}) collective-permute-start(bf16[128,256]{1,0:T(8,128)(2,1)S(1)} %get-tuple-element.72), channel_id=1, source_target_pairs={{0,192},{8,200},{16,208},{24,216},{32,224},{40,232},{48,240},{56,2... | collective-permute-start | bytes 196616 | tf_op jit(solution)/shard_map/ppermute | solution.py:277
  77.6 5.3 %collective-permute-start.32 = (bf16[128,256]{1,0:T(8,128)(2,1)S(1)}, bf16[128,256]{1,0:T(8,128)(2,1)S(1)}, u32[]{:S(2)}, u32[]{:S(2)}) collective-permute-start(bf16[128,256]{1,0:T(8,128)(2,1)S(1)} %shard_map.112.a), channel_id=1, source_target_pairs={{0,48},{8,56},{16,0},{24,8},{32,16},{40,24},{48,32},{56,40},{64,11... | collective-permute-start | bytes 196616 | tf_op jit(solution)/shard_map/ppermute | solution.py:281
  77.9 9.5 %collective-permute-start.31 = (bf16[128,256]{1,0:T(8,128)(2,1)S(1)}, bf16[128,256]{1,0:T(8,128)(2,1)S(1)}, u32[]{:S(2)}, u32[]{:S(2)}) collective-permute-start(bf16[128,256]{1,0:T(8,128)(2,1)S(1)} %shard_map.112.a), channel_id=1, source_target_pairs={{0,32},{8,40},{16,48},{24,56},{32,0},{40,8},{48,16},{56,24},{64,96... | collective-permute-start | bytes 196616 | tf_op jit(solution)/shard_map/ppermute | solution.py:281
  82.3 7.0 %collective-permute-start.30 = (bf16[128,256]{1,0:T(8,128)(2,1)S(1)}, bf16[128,256]{1,0:T(8,128)(2,1)S(1)}, u32[]{:S(2)}, u32[]{:S(2)}) collective-permute-start(bf16[128,256]{1,0:T(8,128)(2,1)S(1)} %shard_map.112.a), channel_id=1, source_target_pairs={{0,16},{8,24},{16,32},{24,40},{32,48},{40,56},{48,0},{56,8},{64,80... | collective-permute-start | bytes 196616 | tf_op jit(solution)/shard_map/ppermute | solution.py:281
  89.4 6.3 %collective-permute-start.35 = (bf16[128,256]{1,0:T(8,128)(2,1)S(1)}, bf16[128,256]{1,0:T(8,128)(2,1)S(1)}, u32[]{:S(2)}, u32[]{:S(2)}) collective-permute-start(bf16[128,256]{1,0:T(8,128)(2,1)S(1)} %shard_map.113.f0), channel_id=1, source_target_pairs={{0,192},{8,200},{16,208},{24,216},{32,224},{40,232},{48,240},{56,2... | collective-permute-start | bytes 196616 | tf_op jit(solution)/shard_map/ppermute | solution.py:277
  89.5 6.2 %collective-permute-start.34 = (bf16[128,256]{1,0:T(8,128)(2,1)S(1)}, bf16[128,256]{1,0:T(8,128)(2,1)S(1)}, u32[]{:S(2)}, u32[]{:S(2)}) collective-permute-start(bf16[128,256]{1,0:T(8,128)(2,1)S(1)} %shard_map.113.f0), channel_id=1, source_target_pairs={{0,128},{8,136},{16,144},{24,152},{32,160},{40,168},{48,176},{56,1... | collective-permute-start | bytes 196616 | tf_op jit(solution)/shard_map/ppermute | solution.py:277
  92.1 4.4 %collective-permute-start.33 = (bf16[128,256]{1,0:T(8,128)(2,1)S(1)}, bf16[128,256]{1,0:T(8,128)(2,1)S(1)}, u32[]{:S(2)}, u32[]{:S(2)}) collective-permute-start(bf16[128,256]{1,0:T(8,128)(2,1)S(1)} %shard_map.113.f0), channel_id=1, source_target_pairs={{0,64},{8,72},{16,80},{24,88},{32,96},{40,104},{48,112},{56,120},{... | collective-permute-start | bytes 196616 | tf_op jit(solution)/shard_map/ppermute | solution.py:277
  97.1 21.1 %copy-start.1 = (bf16[256,2048]{1,0:T(8,128)(2,1)S(1)}, bf16[256,2048]{1,0:T(8,128)(2,1)}, u32[]{:S(2)}) copy-start(bf16[256,2048]{1,0:T(8,128)(2,1)} %w.3) | copy-start | bytes 3145732
  97.1 20.6 %collective-permute-start.36 = (bf16[128,1024]{1,0:T(8,128)(2,1)S(1)}, bf16[128,1024]{1,0:T(8,128)(2,1)S(1)}, u32[]{:S(2)}, u32[]{:S(2)}) collective-permute-start(bf16[128,1024]{1,0:T(8,128)(2,1)S(1)} %shard_map.114.here), channel_id=1, source_target_pairs={{0,8},{8,0},{16,24},{24,16},{32,40},{40,32},{48,56},{56,48},{64,72... | collective-permute-start | bytes 786440 | tf_op jit(solution)/shard_map/ppermute | solution.py:285
  105.0 14.3 %collective-permute-start.18 = (bf16[512,128]{1,0:T(8,128)(2,1)S(1)}, bf16[512,128]{1,0:T(8,128)(2,1)S(1)}, u32[]{:S(2)}, u32[]{:S(2)}) collective-permute-start(bf16[512,128]{1,0:T(8,128)(2,1)S(1)} %get-tuple-element.54), channel_id=1, source_target_pairs={{0,48},{8,56},{16,0},{24,8},{32,16},{40,24},{48,32},{56,40},{64,11... | collective-permute-start | bytes 393224 | tf_op jit(solution)/shard_map/ppermute | solution.py:281
  105.1 4.3 %collective-permute-start.14 = (bf16[128,128]{1,0:T(8,128)(2,1)S(1)}, bf16[128,128]{1,0:T(8,128)(2,1)S(1)}, u32[]{:S(2)}, u32[]{:S(2)}) collective-permute-start(bf16[128,128]{1,0:T(8,128)(2,1)S(1)} %get-tuple-element.48), channel_id=1, source_target_pairs={{0,8},{8,0},{16,24},{24,16},{32,40},{40,32},{48,56},{56,48},{64,72... | collective-permute-start | bytes 98312 | tf_op jit(solution)/shard_map/ppermute | solution.py:285
  105.2 6.6 %collective-permute-start.21 = (bf16[128,256]{1,0:T(8,128)(2,1)S(1)}, bf16[128,256]{1,0:T(8,128)(2,1)S(1)}, u32[]{:S(2)}, u32[]{:S(2)}) collective-permute-start(bf16[128,256]{1,0:T(8,128)(2,1)S(1)} %get-tuple-element.58), channel_id=1, source_target_pairs={{0,192},{8,200},{16,208},{24,216},{32,224},{40,232},{48,240},{56,2... | collective-permute-start | bytes 196616 | tf_op jit(solution)/shard_map/ppermute | solution.py:277
  106.6 11.0 %collective-permute-start.22 = (bf16[128,256]{1,0:T(8,128)(2,1)S(1)}, bf16[128,256]{1,0:T(8,128)(2,1)S(1)}, u32[]{:S(2)}, u32[]{:S(2)}) collective-permute-start(bf16[128,256]{1,0:T(8,128)(2,1)S(1)} %get-tuple-element.59), channel_id=1, source_target_pairs={{0,128},{8,136},{16,144},{24,152},{32,160},{40,168},{48,176},{56,1... | collective-permute-start | bytes 196616 | tf_op jit(solution)/shard_map/ppermute | solution.py:277
  109.4 8.2 %collective-permute-start.23 = (bf16[128,256]{1,0:T(8,128)(2,1)S(1)}, bf16[128,256]{1,0:T(8,128)(2,1)S(1)}, u32[]{:S(2)}, u32[]{:S(2)}) collective-permute-start(bf16[128,256]{1,0:T(8,128)(2,1)S(1)} %get-tuple-element.60), channel_id=1, source_target_pairs={{0,64},{8,72},{16,80},{24,88},{32,96},{40,104},{48,112},{56,120},{... | collective-permute-start | bytes 196616 | tf_op jit(solution)/shard_map/ppermute | solution.py:277
  111.8 9.4 %collective-permute-start.19 = (bf16[512,128]{1,0:T(8,128)(2,1)S(1)}, bf16[512,128]{1,0:T(8,128)(2,1)S(1)}, u32[]{:S(2)}, u32[]{:S(2)}) collective-permute-start(bf16[512,128]{1,0:T(8,128)(2,1)S(1)} %get-tuple-element.55), channel_id=1, source_target_pairs={{0,32},{8,40},{16,48},{24,56},{32,0},{40,8},{48,16},{56,24},{64,96... | collective-permute-start | bytes 393224 | tf_op jit(solution)/shard_map/ppermute | solution.py:281
  117.6 8.3 %collective-permute-start.20 = (bf16[512,128]{1,0:T(8,128)(2,1)S(1)}, bf16[512,128]{1,0:T(8,128)(2,1)S(1)}, u32[]{:S(2)}, u32[]{:S(2)}) collective-permute-start(bf16[512,128]{1,0:T(8,128)(2,1)S(1)} %get-tuple-element.56), channel_id=1, source_target_pairs={{0,16},{8,24},{16,32},{24,40},{32,48},{40,56},{48,0},{56,8},{64,80... | collective-permute-start | bytes 393224 | tf_op jit(solution)/shard_map/ppermute | solution.py:281
  117.6 17.2 %collective-permute-start.37 = (bf16[128,1024]{1,0:T(8,128)(2,1)S(1)}, bf16[128,1024]{1,0:T(8,128)(2,1)S(1)}, u32[]{:S(2)}, u32[]{:S(2)}) collective-permute-start(bf16[128,1024]{1,0:T(8,128)(2,1)S(1)} %shard_map.114.here), channel_id=1, source_target_pairs={{0,1},{1,0},{2,3},{3,2},{4,5},{5,4},{6,7},{7,6},{8,9},{9,8},{10,11... | collective-permute-start | bytes 786440 | tf_op jit(solution)/shard_map/ppermute | solution.py:293
  117.8 17.1 %collective-permute-start.38 = (bf16[128,1024]{1,0:T(8,128)(2,1)S(1)}, bf16[128,1024]{1,0:T(8,128)(2,1)S(1)}, u32[]{:S(2)}, u32[]{:S(2)}) collective-permute-start(bf16[128,1024]{1,0:T(8,128)(2,1)S(1)} %collective-permute-done.36.pair), channel_id=1, source_target_pairs={{0,1},{1,0},{2,3},{3,2},{4,5},{5,4},{6,7},{7,6},{8,9},{9,8},{10,11... | collective-permute-start | bytes 786440 | tf_op jit(solution)/shard_map/ppermute | solution.py:293
  119.3 9.6 %collective-permute-start.15 = (bf16[32,2048]{1,0:T(8,128)(2,1)S(1)}, bf16[32,2048]{1,0:T(8,128)(2,1)S(1)}, u32[]{:S(2)}, u32[]{:S(2)}) collective-permute-start(bf16[32,2048]{1,0:T(8,128)(2,1)S(1)} %get-tuple-element.50), channel_id=1, source_target_pairs={{0,2},{2,4},{4,6},{6,0},{1,3},{3,5},{5,7},{7,1},{8,10},{10,12},{12... | collective-permute-start | bytes 393224 | tf_op jit(solution)/shard_map/ppermute | solution.py:289
  121.2 7.8 %collective-permute-start.16 = (bf16[32,2048]{1,0:T(8,128)(2,1)S(1)}, bf16[32,2048]{1,0:T(8,128)(2,1)S(1)}, u32[]{:S(2)}, u32[]{:S(2)}) collective-permute-start(bf16[32,2048]{1,0:T(8,128)(2,1)S(1)} %get-tuple-element.51), channel_id=1, source_target_pairs={{0,4},{2,6},{4,0},{6,2},{1,5},{3,7},{5,1},{7,3},{8,12},{10,14},{12... | collective-permute-start | bytes 393224 | tf_op jit(solution)/shard_map/ppermute | solution.py:289
  125.9 5.0 %collective-permute-start.17 = (bf16[32,2048]{1,0:T(8,128)(2,1)S(1)}, bf16[32,2048]{1,0:T(8,128)(2,1)S(1)}, u32[]{:S(2)}, u32[]{:S(2)}) collective-permute-start(bf16[32,2048]{1,0:T(8,128)(2,1)S(1)} %get-tuple-element.52), channel_id=1, source_target_pairs={{0,6},{2,0},{4,2},{6,4},{1,7},{3,1},{5,3},{7,5},{8,14},{10,8},{12,... | collective-permute-start | bytes 393224 | tf_op jit(solution)/shard_map/ppermute | solution.py:289
  128.9 4.6 %collective-permute-start.24 = (bf16[384,128]{1,0:T(8,128)(2,1)S(1)}, bf16[384,128]{1,0:T(8,128)(2,1)S(1)}, u32[]{:S(2)}, u32[]{:S(2)}) collective-permute-start(bf16[384,128]{1,0:T(8,128)(2,1)S(1)} %get-tuple-element.62), channel_id=1, source_target_pairs={{0,8},{8,0},{16,24},{24,16},{32,40},{40,32},{48,56},{56,48},{64,72... | collective-permute-start | bytes 294920 | tf_op jit(solution)/shard_map/ppermute | solution.py:285

commit v2 on v1

v2 whole, which is shorter than its diff:
```python
import functools
import math

import jax
import jax.numpy as jnp
from jax import lax
from jax.experimental import pallas as pl
from jax.experimental.pallas import tpu as pltpu
from jax.sharding import Mesh
from jax.sharding import PartitionSpec as P

HD = 128
TILE = 128
BLK = 256
SCALE = HD ** (-0.5)
LOG2E = math.log2(math.e)
LOW = -1e30
F32 = jnp.float32
BF16 = jnp.bfloat16
AXES = ("x", "zh", "par", "y", "core")
X, ZH, PAR, Y, CORE = range(5)
ORDER = (0, 1, 3, 2)
NN = (((1,), (0,)), ((), ()))
NT = (((1,), (1,)), ((), ()))


def dot(a, b, dims=NN):
    return lax.dot_general(a, b, dims, preferred_element_type=F32)


def call(
    body, outs, ins, flops=0, scratch=(), smem=1, vmem=48, after=(), space=pltpu.VMEM,
    out_space=pltpu.VMEM,
):
    specs = [pl.BlockSpec(memory_space=pltpu.SMEM)] * smem
    specs += [pl.BlockSpec(memory_space=space)] * (len(ins) - smem)
    used = len(ins)
    if after:
        specs += [pl.BlockSpec(memory_space=pl.ANY)] * len(after)
        inner = body

        def body(*refs):
            inner(*refs[:used], *refs[used + len(after) :])

    shapes = [jax.ShapeDtypeStruct(s, d) for s, d in outs]
    moved = sum(math.prod(a.shape) * a.dtype.itemsize for a in list(ins) + shapes)
    ins = tuple(ins) + tuple(after)
    return pl.pallas_call(
        body,
        out_shape=shapes,
        in_specs=specs,
        out_specs=[pl.BlockSpec(memory_space=out_space)] * len(outs),
        scratch_shapes=list(scratch),
        compiler_params=pltpu.CompilerParams(vmem_limit_bytes=vmem * 2**20),
        cost_estimate=pl.CostEstimate(flops=flops, bytes_accessed=moved, transcendentals=0),
    )(*ins)


def split_heads(pos, q, k, v, keep, send, sems):
    mine = pl.ds(pl.multiple_of(pos[PAR] * HD, HD), HD)
    other = pl.ds(pl.multiple_of((1 - pos[PAR]) * HD, HD), HD)
    copies = []
    for n, ref in enumerate((q, k, v)):
        rows = pl.ds(n * TILE, TILE)
        for m, (columns, out) in enumerate(((other, send), (mine, keep))):
            copies.append(
                pltpu.make_async_copy(ref.at[:, columns], out.at[rows, :], sems.at[n, m])
            )
            copies[-1].start()
    for copy in copies:
        copy.wait()


def own_blocks(keep, recv, k, v, q):
    for n, ref in ((0, q), (1, k), (2, v)):
        rows = slice(n * TILE, (n + 1) * TILE)
        ref[:TILE, :] = keep[rows, :]
        ref[TILE:, :] = recv[rows, :]


def stack_two(a, b, out):
    rows = a.shape[0]
    out[:rows, :] = a[...]
    out[rows:, :] = b[...]


def stack_pairs(k0, k1, v0, v1, q0, q1, k, v, q):
    stack_two(k0, k1, k)
    stack_two(v0, v1, v)
    stack_two(q0, q1, q)


def join_rows(pos, pair, other, near, far):
    for n in range(4):
        ref = (pair, other)[n // 2]
        start = (n % 2) * 64
        rows = pl.ds(pl.multiple_of((pos[Y] ^ ORDER[n]) * 32, 32), 32)
        near[rows, :] = ref[start : start + 32, :]
        far[rows, :] = ref[start + 32 : start + 64, :]


def bias_rows(pos, mask, query_x):
    lane = lax.broadcasted_iota(jnp.int32, (1, BLK), 1)
    par = pos[PAR]
    query = (query_x * 4 + pos[ZH]) * 2
    rows = []
    for e in range(4):
        key = (pos[X] * 4 + (pos[ZH] ^ e)) * 2
        for tile in (par, 1 - par):
            near = jnp.where(mask[query + par, key + tile] > 0, 0.0, LOW)
            far = jnp.where(mask[query + 1 - par, key + tile] > 0, 0.0, LOW)
            rows.append(jnp.where(lane < TILE, near, far))
    return rows


def scores_of(keys, queries, rows, e):
    raw = dot(keys, queries, NT) * (SCALE * LOG2E)
    return jnp.concatenate([raw[:TILE] + rows[2 * e], raw[TILE:] + rows[2 * e + 1]], axis=0)


def split3(value):
    high = value.astype(BF16).astype(F32)
    rest = value - high
    middle = rest.astype(BF16).astype(F32)
    low = (rest - middle).astype(BF16).astype(F32)
    return high, middle, low


def pack_rows(values):
    row = lax.broadcasted_iota(jnp.int32, (16, BLK), 0)
    packed = jnp.zeros((16, BLK), F32)
    for n, value in enumerate(values):
        packed = jnp.where(row == n, value, packed)
    return packed.astype(BF16)


def halves(ref):
    rows = ref.shape[0] // 2
    return ref[:rows, :], ref[rows:, :]


def by_place(kp, kf, vp, vn):
    (k0, k1), (k3, k2) = halves(kp), halves(kf)
    (v0, v3), (v1, v2) = halves(vp), halves(vn)
    return (k0, k1, k2, k3), (v0, v1, v2, v3)


def forward(pos, mask, kp, kf, vp, vn, qp, qf, p0, p1, p2, p3, q, part):
    keys, values = by_place(kp, kf, vp, vn)
    values_t = [v.astype(F32).T.astype(BF16) for v in values]
    for n in range(4):
        start = (n % 2) * BLK
        q[pos[X] ^ ORDER[n]] = (qp, qf)[n // 2][start : start + BLK, :]

    def block(x, carry):
        rows = bias_rows(pos, mask, x)
        scores = [scores_of(keys[e], q[x], rows, e) for e in range(4)]
        largest = functools.reduce(
            jnp.maximum, [jnp.max(s, axis=0, keepdims=True) for s in scores]
        )
        largest = jnp.maximum(largest, 0.1 * LOW)
        total = jnp.zeros((1, BLK), F32)
        summed = jnp.zeros((HD, BLK), F32)
        for e in range(4):
            weights = jnp.exp2(scores[e] - largest)
            total = total + jnp.sum(weights, axis=0, keepdims=True)
            summed = summed + dot(values_t[e], weights.astype(BF16))
        some = total > 0.0
        safe = jnp.where(some, total, 1.0)
        part[x, :HD, :] = (summed / safe).astype(BF16)
        part[x, HD:, :] = pack_rows(split3(jnp.where(some, largest + jnp.log2(safe), LOW)))
        return carry

    lax.fori_loop(0, 4, block, 0)
    for n, ref in enumerate((p0, p1, p2, p3)):
        ref[...] = part[pos[X] ^ ORDER[n]]


def backward(
    pos, mask, kp, kf, vp, vn, qp, qf, s0, s1, s2, s3,
    dk, dk_far, dv, dv_near, dq, dq_far, q, g, stats, part, acc,
):
    keys, values = by_place(kp, kf, vp, vn)
    keys_t = [k.astype(F32).T.astype(BF16) for k in keys]
    for n, stat in enumerate((s0, s1, s2, s3)):
        x = pos[X] ^ ORDER[n]
        q[x] = (qp, qf)[n // 2][(n % 2) * BLK : (n % 2 + 1) * BLK, :]
        g[x] = stat[HD : 2 * HD, :]
        stats[x] = stat[2 * HD :, :]
    acc[...] = jnp.zeros_like(acc)

    def block(x, carry):
        rows = bias_rows(pos, mask, x)
        queries, grad_t = q[x], g[x]
        s = stats[x].astype(F32)
        lse = s[0:1] + s[1:2] + s[2:3]
        delta = s[3:4] + s[4:5] + s[5:6]
        grad_query = jnp.zeros((HD, BLK), F32)
        for e in range(4):
            probs = jnp.exp2(scores_of(keys[e], queries, rows, e) - lse)
            grad_probs = dot(values[e], grad_t)
            grad_scores = (probs * (grad_probs - delta)).astype(BF16)
            acc[e, BLK:, :] += dot(probs.astype(BF16), grad_t, NT)
            acc[e, :BLK, :] += dot(grad_scores, queries)
            grad_query = grad_query + dot(keys_t[e], grad_scores)
        part[x] = (grad_query * SCALE).astype(BF16)
        return carry

    lax.fori_loop(0, 4, block, 0)
    for n, (e, k, f, v) in enumerate(
        ((0, dk, 0, dv), (1, dk, 3, dv), (3, dk_far, 1, dv_near), (2, dk_far, 2, dv_near))
    ):
        rows = slice((n % 2) * BLK, (n % 2 + 1) * BLK)
        k[rows, :] = (acc[e, :BLK, :] * SCALE).astype(BF16)
        v[rows, :] = acc[f, BLK:, :].astype(BF16)
    for n in range(4):
        ref = (dq, dq_far)[n // 2]
        ref[(n % 2) * HD : (n % 2 + 1) * HD, :] = part[pos[X] ^ ORDER[n]]


def back_project(pos, w, near, far, grads):
    head = w[pl.ds(pl.multiple_of(pos[PAR] * HD, HD), HD), :]
    grads[:, :TILE] = dot(head, near[...], NT).astype(BF16)
    grads[:, TILE:] = dot(head, far[...], NT).astype(BF16)


def attend(pos, p0, p1, p2, p3, grads, near, far, att, stats, keep, send):
    lses, parts = [], []
    for pack in (p0, p1, p2, p3):
        parts.append(pack[:HD, :].astype(F32))
        s = pack[HD:, :].astype(F32)
        lses.append(s[0:1] + s[1:2] + s[2:3])
    largest = functools.reduce(jnp.maximum, lses)
    weights = [jnp.exp2(v - largest) for v in lses]
    total = sum(weights)
    out = sum((w / total) * p for w, p in zip(weights, parts)).astype(BF16)
    att[...] = out
    delta = jnp.sum(grads[...].astype(F32) * out.astype(F32), axis=0, keepdims=True)
    stats[...] = pack_rows(split3(largest + jnp.log2(total)) + split3(delta))
    both = dot(out[:, :TILE], near[...]) + dot(out[:, TILE:], far[...])

    @pl.when(pos[CORE] == 0)
    def _():
        keep[...] = both[:, :1024]
        send[...] = both[:, 1024:]

    @pl.when(pos[CORE] != 0)
    def _():
        keep[...] = both[:, 1024:]
        send[...] = both[:, :1024]


def weight_cut(pos, mine, other, grads, stats, b0, b1, b2, b3):
    for n, ref in enumerate((b0, b1, b2, b3)):
        columns = pl.ds(pl.multiple_of((pos[X] ^ ORDER[n]) * BLK, BLK), BLK)
        ref[:HD, :] = (mine[:, columns] + other[:, columns]).astype(BF16)
        ref[HD : 2 * HD, :] = grads[...]
        ref[2 * HD :, :] = stats[...]


def add(a, b):
    return a.astype(F32) + b.astype(F32)


def sum_cuts(a, b, c, d, out):
    out[...] = (add(a[:HD, :], b[:HD, :]) + add(c[:HD, :], d[:HD, :])).astype(BF16)


def sum_two(a, b, out):
    out[...] = add(a[...], b[...]).astype(BF16)


def sum_split(a, b, keep, send):
    total = add(a[...], b[...]).astype(BF16)
    rows = keep.shape[0]
    keep[...] = total[:rows]
    send[...] = total[rows:]


def weight_stack(pos, mine, other, out):
    out[pl.ds(pl.multiple_of(pos[PAR] * HD, HD), HD), :] = mine[...]
    out[pl.ds(pl.multiple_of((1 - pos[PAR]) * HD, HD), HD), :] = other[...]


def weight_row(pos, f0, f1, f2, f3, out):
    for n, ref in enumerate((f0, f1, f2, f3)):
        columns = pl.ds(pl.multiple_of((pos[X] ^ ORDER[n]) * BLK, BLK), BLK)
        out[:, columns] = ref[...]


def mix(pos, att, other, w, out, out_far, full):
    mine_rows = pl.ds(pl.multiple_of(pos[PAR] * HD, HD), HD)
    other_rows = pl.ds(pl.multiple_of((1 - pos[PAR]) * HD, HD), HD)
    mine_t = att[:, :TILE].astype(F32).T.astype(BF16)
    other_t = other[...].astype(F32).T.astype(BF16)
    full[...] = (dot(mine_t, w[mine_rows, :]) + dot(other_t, w[other_rows, :])).astype(BF16)
    for n in range(4):
        rows = pl.ds(pl.multiple_of((pos[Y] ^ ORDER[n]) * 32, 32), 32)
        (out, out_far)[n // 2][(n % 2) * 32 : (n % 2 + 1) * 32, :] = full[rows, :]


def gather_grads(k, k_near, v, v_far, q, q_near, keep, send):
    q = add(q[...], q_near[...])
    keep[:TILE, :] = q[:, :TILE].T.astype(BF16)
    send[:TILE, :] = q[:, TILE:].T.astype(BF16)
    for n, (mine, other) in enumerate(((k, k_near), (v, v_far))):
        total = add(mine[...], other[...]).astype(BF16)
        rows = slice((n + 1) * TILE, (n + 2) * TILE)
        keep[rows, :] = total[:TILE]
        send[rows, :] = total[TILE:]


def finish(pos, mine, other, here, core, q, k, v, weight):
    for half, ref in ((pos[CORE], here), (1 - pos[CORE], core)):
        columns = pl.ds(pl.multiple_of(half * 1024, 1024), 1024)
        weight[:, columns] = ref[...].astype(F32)
    for n, ref in enumerate((q, k, v)):
        rows = slice(n * TILE, (n + 1) * TILE)

        @pl.when(pos[PAR] == 0)
        def _():
            ref[:, :HD] = mine[rows, :]
            ref[:, HD:] = other[rows, :]

        @pl.when(pos[PAR] != 0)
        def _():
            ref[:, HD:] = mine[rows, :]
            ref[:, :HD] = other[rows, :]


def near(a, axis):
    return lax.ppermute(a, axis, [(0, 1), (1, 0), (2, 3), (3, 2)])


def far(a, axis):
    return lax.ppermute(a, axis, [(0, 3), (3, 0), (1, 2), (2, 1)])


def opposite(a, axis):
    return lax.ppermute(a, axis, [(0, 2), (2, 0), (1, 3), (3, 1)])


def over_pair(a):
    return lax.ppermute(a, "par", [(0, 1), (1, 0)])


def over_core(a):
    return lax.ppermute(a, "core", [(0, 1), (1, 0)])


def on_device(query_rows, key_rows, value_rows, out_weight, cotangent, tile_mask):
    pos = jnp.stack([lax.axis_index(name) for name in AXES]).astype(jnp.int32)
    kv_mm = 2 * 1024 * 1024 * HD

    keep, send = call(
        split_heads,
        [((3 * TILE, HD), BF16)] * 2,
        (pos, query_rows[0], key_rows[0], value_rows[0]),
        scratch=[pltpu.SemaphoreType.DMA((3, 2))],
        space=pltpu.HBM,
        out_space=pltpu.HBM,
    )
    recv = over_pair(send)
    rows_far = over_pair(cotangent[0])
    k, v, q = call(own_blocks, [((BLK, HD), BF16)] * 3, (keep, recv), smem=0)
    (rows,) = call(stack_two, [((64, 2048), BF16)], (cotangent[0], rows_far), smem=0, after=(recv,))
    kp, vp, qp = call(
        stack_pairs,
        [((2 * BLK, HD), BF16)] * 3,
        (k, near(k, "zh"), v, far(v, "zh"), q, near(q, "x")),
        smem=0,
    )
    (rows,) = call(stack_two, [((TILE, 2048), BF16)], (rows, near(rows, "y")), smem=0, after=(kp,))
    kf, vn, qf, rows_far = far(kp, "zh"), near(vp, "zh"), far(qp, "x"), far(rows, "y")

    packs = call(
        forward,
        [((HD + 16, BLK), BF16)] * 4,
        (pos, tile_mask, kp, kf, vp, vn, qp, qf),
        flops=2 * kv_mm,
        scratch=[pltpu.VMEM((4, BLK, HD), BF16), pltpu.VMEM((4, HD + 16, BLK), BF16)],
        smem=2,
    )
    packs = [packs[0], near(packs[1], "x"), far(packs[2], "x"), opposite(packs[3], "x")]

    cot, cot_far = call(join_rows, [((TILE, 2048), BF16)] * 2, (pos, rows, rows_far))
    (grads,) = call(
        back_project,
        [((HD, BLK), BF16)],
        (pos, out_weight, cot, cot_far),
        flops=2 * HD * BLK * 2048,
    )
    att, stats, gw_keep, gw_send = call(
        attend,
        [((HD, BLK), BF16), ((16, BLK), BF16)] + [((HD, 1024), F32)] * 2,
        (pos, *packs, grads, cot, cot_far),
        flops=2 * HD * BLK * 2048,
    )
    gw_recv = over_core(gw_send)
    cuts = call(
        weight_cut, [((2 * HD + 16, BLK), BF16)] * 4, (pos, gw_keep, gw_recv, grads, stats)
    )
    cuts = [cuts[0], near(cuts[1], "x"), far(cuts[2], "x"), opposite(cuts[3], "x")]
    (share,) = call(sum_cuts, [((HD, BLK), BF16)], cuts, smem=0)

    dk, dk_far, dv, dv_near, dq, dq_far = call(
        backward,
        [((2 * BLK, HD), BF16)] * 4 + [((2 * HD, BLK), BF16)] * 2,
        (pos, tile_mask, kp, kf, vp, vn, qp, qf, *cuts),
        flops=5 * kv_mm,
        scratch=[
            pltpu.VMEM((4, BLK, HD), BF16),
            pltpu.VMEM((4, HD, BLK), BF16),
            pltpu.VMEM((4, 16, BLK), BF16),
            pltpu.VMEM((4, HD, BLK), BF16),
            pltpu.VMEM((4, 2 * BLK, HD), F32),
        ],
        smem=2,
        after=(share,),
    )
    (near_sum,) = call(
        sum_two, [((HD, BLK), BF16)], (share, near(share, "zh")), smem=0, after=(dq,)
    )
    (done,) = call(sum_two, [((HD, BLK), BF16)], (near_sum, far(near_sum, "zh")), smem=0)
    dq_far = lax.optimization_barrier((dq_far, near_sum))[0]
    dk_far, dv_near, _ = lax.optimization_barrier((dk_far, dv_near, done))

    att_far = over_pair(att[:, TILE:])
    mixed, mixed_far = call(
        mix,
        [((64, 2048), BF16)] * 2,
        (pos, att, att_far, out_weight),
        flops=2 * TILE * 256 * 2048,
        scratch=[pltpu.VMEM((TILE, 2048), BF16)],
    )
    mixed, mixed_near = call(
        sum_split, [((32, 2048), BF16)] * 2, (mixed, far(mixed_far, "y")), smem=0
    )
    (mixed,) = call(sum_two, [((32, 2048), BF16)], (mixed, near(mixed_near, "y")), smem=0)

    dk, dk_near = call(
        sum_split, [((BLK, HD), BF16)] * 2, (dk, far(dk_far, "zh")), smem=0
    )
    dv, dv_far = call(
        sum_split, [((BLK, HD), BF16)] * 2, (dv, near(dv_near, "zh")), smem=0
    )
    dq, dq_near = call(sum_split, [((HD, BLK), BF16)] * 2, (dq, far(dq_far, "x")), smem=0)
    dq_near = lax.optimization_barrier((dq_near, dk_near))[0]
    out_keep, out_send = call(
        gather_grads,
        [((3 * TILE, HD), BF16)] * 2,
        (dk, near(dk_near, "zh"), dv, far(dv_far, "zh"), dq, near(dq_near, "x")),
        smem=0,
    )

    (stack,) = call(weight_stack, [((2 * HD, BLK), BF16)], (pos, done, over_pair(done)), after=(mixed,))
    stacks = [stack, near(stack, "x"), far(stack, "x"), opposite(stack, "x")]
    (here,) = call(
        weight_row, [((2 * HD, 1024), BF16)], (pos, *stacks), after=(out_send,)
    )
    grad_q, grad_k, grad_v, grad_weight = call(
        finish,
        [((TILE, 2 * HD), BF16)] * 3 + [((2 * HD, 2048), F32)],
        (pos, out_keep, over_pair(out_send), here, over_core(here)),
    )
    return (mixed[None], grad_q[None], grad_k[None], grad_v[None], grad_weight)


def solution(mesh):
    mesh = Mesh(mesh.devices.reshape(4, 4, 2, 4, 2), AXES)
    tokens = ("x", "zh", "par")
    rows = P("core", tokens, "y")
    blocks = P("core", (*tokens, "y"), None)
    weight = P("y", None)
    return jax.shard_map(
        on_device,
        mesh=mesh,
        in_specs=(rows, rows, rows, weight, blocks, P()),
        out_specs=(blocks, rows, rows, rows, weight),
        check_vma=False,
    )
```

time: 137 us -> 111 us (0.81)
  the two profiles are of different devices: /device:TPU:6 before, /device:TPU:1 now
where the time goes in v2:
time: 111 us
  starting transfers between devices  60.1 us (54%)
  waiting for transfers between devices  26.7 us (24%)
  Pallas kernels  18.8 us (17%)
  local copies, waits for them, and re-layouts  4.42 us (4%)
    ppermute x12, starting transfers between devices, far(): return lax.ppermute(a, axis, [(0, 3), (3, 0), (1, 2), (2, 1)])  21.2 us
    pallas_call x24, Pallas kernels, call(): pl.pallas_call(body, out_shape=shapes, in_specs=specs, out_specs=[pl.Bloc...  18.8 us
    ppermute x12, starting transfers between devices, near(): return lax.ppermute(a, axis, [(0, 1), (1, 0), (2, 3), (3, 2)])  16.6 us
    ppermute x12, waiting for transfers between devices, far(): return lax.ppermute(a, axis, [(0, 3), (3, 0), (1, 2), (2, 1)])  14 us
    ppermute x2, starting transfers between devices, over_core(): return lax.ppermute(a, 'core', [(0, 1), (1, 0)])  12.1 us
    ppermute x5, waiting for transfers between devices, over_pair(): return lax.ppermute(a, 'par', [(0, 1), (1, 0)])  10 us
    ppermute x5, starting transfers between devices, over_pair(): return lax.ppermute(a, 'par', [(0, 1), (1, 0)])  6.26 us
    unnamed x14, local copies, waits for them, and re-layouts  4.34 us
  transfers between devices with their start and end apart: 34, of which 14 were waited for; matrix products, arithmetic and copies ran while one was open for 0% of the time, Pallas kernels for 13%

profile of v2, /device:TPU:1, one launch (start us, length us, event | category | flops | bytes accessed | tf_op | source)
XLA Modules:
  0.0 111.0 jit_solution(1838858017365410027)
XLA Ops:
  0.6 2.6 %collective-permute-start.10 = (bf16[32,2048]{1,0:T(8,128)(2,1)}, bf16[32,2048]{1,0:T(8,128)(2,1)S(1)}, u32[]{:S(2)}, u32[]{:S(2)}) collective-permute-start(bf16[32,2048]{1,0:T(8,128)(2,1)} %bitcast.14), channel_id=1, source_target_pairs={{0,8},{8,0},{1,9},{9,1},{2,10},{10,2},{3,11},{11,3},{4,12},{12,4},... | collective-permute-start | bytes 393224 | tf_op jit(solution)/shard_map/ppermute | solution.py:344
  3.3 0.8 copy-done.3
  4.1 0.8 copy-done.4
  5.0 0.8 copy-done.5
  5.8 0.6 shard_map.101
  6.5 0.1 collective-permute-start
  6.6 3.4 %collective-permute-done.recv.refs_2_ = bf16[384,128]{1,0:T(8,128)(2,1)S(1)} collective-permute-done((bf16[384,128]{1,0:T(8,128)(2,1)S(1)}, bf16[384,128]{1,0:T(8,128)(2,1)S(1)}, u32[]{:S(2)}, u32[]{:S(2)}) %collective-permute-start) | collective-permute-done | bytes 98336 | tf_op jit(solution)/shard_map/ppermute | solution.py:344
  10.0 0.9 copy-done.2
  10.9 1.4 %collective-permute-start.11 = (bf16[64,2048]{1,0:T(8,128)(2,1)S(1)}, bf16[64,2048]{1,0:T(8,128)(2,1)S(1)}, u32[]{:S(2)}, u32[]{:S(2)}) collective-permute-start(bf16[64,2048]{1,0:T(8,128)(2,1)S(1)} %shard_map.105.refs_0_), channel_id=1, source_target_pairs={{0,2},{2,0},{4,6},{6,4},{1,3},{3,1},{5,7},{7,5},{8,10},{10,8},{12,... | collective-permute-start | bytes 786440 | tf_op jit(solution)/shard_map/ppermute | solution.py:332
  12.3 3.1 %collective-permute-start.1 = (bf16[256,128]{1,0:T(8,128)(2,1)S(1)}, bf16[256,128]{1,0:T(8,128)(2,1)S(1)}, u32[]{:S(2)}, u32[]{:S(2)}) collective-permute-start(bf16[256,128]{1,0:T(8,128)(2,1)S(1)} %get-tuple-element.55.k0), channel_id=1, source_target_pairs={{0,16},{16,0},{32,48},{48,32},{1,17},{17,1},{33,49},{49,33},{2,18}... | collective-permute-start | bytes 196616 | tf_op jit(solution)/shard_map/ppermute | solution.py:332
  15.4 3.3 %collective-permute-start.2 = (bf16[256,128]{1,0:T(8,128)(2,1)S(1)}, bf16[256,128]{1,0:T(8,128)(2,1)S(1)}, u32[]{:S(2)}, u32[]{:S(2)}) collective-permute-start(bf16[256,128]{1,0:T(8,128)(2,1)S(1)} %get-tuple-element.56.v0), channel_id=1, source_target_pairs={{0,48},{48,0},{16,32},{32,16},{1,49},{49,1},{17,33},{33,17},{2,50}... | collective-permute-start | bytes 196616 | tf_op jit(solution)/shard_map/ppermute | solution.py:336
  18.7 1.2 %collective-permute-start.3 = (bf16[256,128]{1,0:T(8,128)(2,1)S(1)}, bf16[256,128]{1,0:T(8,128)(2,1)S(1)}, u32[]{:S(2)}, u32[]{:S(2)}) collective-permute-start(bf16[256,128]{1,0:T(8,128)(2,1)S(1)} %get-tuple-element.57.q0), channel_id=1, source_target_pairs={{0,64},{64,0},{128,192},{192,128},{1,65},{65,1},{129,193},{193,129... | collective-permute-start | bytes 196616 | tf_op jit(solution)/shard_map/ppermute | solution.py:332
  19.9 1.3 %collective-permute-done.2.v1 = bf16[256,128]{1,0:T(8,128)(2,1)S(1)} collective-permute-done((bf16[256,128]{1,0:T(8,128)(2,1)S(1)}, bf16[256,128]{1,0:T(8,128)(2,1)S(1)}, u32[]{:S(2)}, u32[]{:S(2)}) %collective-permute-start.2) | collective-permute-done | bytes 65568 | tf_op jit(solution)/shard_map/ppermute | solution.py:336
  21.2 0.6 collective-permute-done.3.q1
  21.9 2.0 %collective-permute-start.12 = (bf16[128,2048]{1,0:T(8,128)(2,1)S(1)}, bf16[128,2048]{1,0:T(8,128)(2,1)S(1)}, u32[]{:S(2)}, u32[]{:S(2)}) collective-permute-start(bf16[128,2048]{1,0:T(8,128)(2,1)S(1)} %shard_map.106.pair), channel_id=1, source_target_pairs={{0,6},{6,0},{2,4},{4,2},{1,7},{7,1},{3,5},{5,3},{8,14},{14,8},{10,... | collective-permute-start | bytes 1572872 | tf_op jit(solution)/shard_map/ppermute | solution.py:336
  23.9 1.3 %collective-permute-start.5 = (bf16[512,128]{1,0:T(8,128)(2,1)S(1)}, bf16[512,128]{1,0:T(8,128)(2,1)S(1)}, u32[]{:S(2)}, u32[]{:S(2)}) collective-permute-start(bf16[512,128]{1,0:T(8,128)(2,1)S(1)} %get-tuple-element.59.vp.refs_4_), channel_id=1, source_target_pairs={{0,16},{16,0},{32,48},{48,32},{1,17},{17,1},{33,49},{49,33},{2,18}... | collective-permute-start | bytes 393224 | tf_op jit(solution)/shard_map/ppermute | solution.py:332
  25.3 2.5 %collective-permute-start.6 = (bf16[512,128]{1,0:T(8,128)(2,1)S(1)}, bf16[512,128]{1,0:T(8,128)(2,1)S(1)}, u32[]{:S(2)}, u32[]{:S(2)}) collective-permute-start(bf16[512,128]{1,0:T(8,128)(2,1)S(1)} %get-tuple-element.60.qp.refs_6_), channel_id=1, source_target_pairs={{0,192},{192,0},{64,128},{128,64},{1,193},{193,1},{65,129},{129,65... | collective-permute-start | bytes 393224 | tf_op jit(solution)/shard_map/ppermute | solution.py:336
  27.7 2.1 %collective-permute-start.4 = (bf16[512,128]{1,0:T(8,128)(2,1)S(1)}, bf16[512,128]{1,0:T(8,128)(2,1)S(1)}, u32[]{:S(2)}, u32[]{:S(2)}) collective-permute-start(bf16[512,128]{1,0:T(8,128)(2,1)S(1)} %get-tuple-element.58.kp.refs_2_), channel_id=1, source_target_pairs={{0,48},{48,0},{16,32},{32,16},{1,49},{49,1},{17,33},{33,17},{2,50}... | collective-permute-start | bytes 393224 | tf_op jit(solution)/shard_map/ppermute | solution.py:336
  29.8 0.2 collective-permute-done.5.vn.refs_5_
  30.0 0.5 collective-permute-done.6.qf.refs_7_
  30.6 4.5 %collective-permute-done.4.kf.refs_3_ = bf16[512,128]{1,0:T(8,128)(2,1)S(1)} collective-permute-done((bf16[512,128]{1,0:T(8,128)(2,1)S(1)}, bf16[512,128]{1,0:T(8,128)(2,1)S(1)}, u32[]{:S(2)}, u32[]{:S(2)}) %collective-permute-start.4) | collective-permute-done | bytes 131104 | tf_op jit(solution)/shard_map/ppermute | solution.py:336
  35.1 4.0 %shard_map.104 = (bf16[144,256]{1,0:T(8,128)(2,1)S(1)}, bf16[144,256]{1,0:T(8,128)(2,1)S(1)}, bf16[144,256]{1,0:T(8,128)(2,1)S(1)}, bf16[144,256]{1,0:T(8,128)(2,1)S(1)}) custom-call(s32[5]{0:T(128)S(1)} %stack.23.pos.refs_0_, s32[32,32]{1,0:T(8,128)S(1)} %copy-done.6, bf16[512,128]{1,0:T(8,128)(2,1)S(1)} %get-tuple-element.58.kp.refs_2_, ...), custom_call_target="tpu_custom_call" | custom-call | flops 536870912 | bytes 1085460 | tf_op jit(solution)/shard_map/pallas_call | solution.py:48
  39.2 0.1 collective-permute-start.7
  39.4 3.1 %collective-permute-start.9 = (bf16[144,256]{1,0:T(8,128)(2,1)S(1)}, bf16[144,256]{1,0:T(8,128)(2,1)S(1)}, u32[]{:S(2)}, u32[]{:S(2)}) collective-permute-start(bf16[144,256]{1,0:T(8,128)(2,1)S(1)} %get-tuple-element.64), channel_id=1, source_target_pairs={{0,128},{128,0},{64,192},{192,64},{1,129},{129,1},{65,193},{193,65... | collective-permute-start | bytes 221192 | tf_op jit(solution)/shard_map/ppermute | solution.py:340
  42.5 0.6 shard_map.107
  43.1 1.0 shard_map.108.grads
  44.1 0.4 collective-permute-done.8.p2
  44.6 1.1 shard_map.109
  45.6 6.7 %collective-permute-start.16 = (f32[128,1024]{1,0:T(8,128)S(1)}, f32[128,1024]{1,0:T(8,128)S(1)}, u32[]{:S(2)}, u32[]{:S(2)}) collective-permute-start(f32[128,1024]{1,0:T(8,128)S(1)} %get-tuple-element.73), channel_id=1, source_target_pairs={{0,1},{1,0},{2,3},{3,2},{4,5},{5,4},{6,7},{7,6},{8,9},{9,8},{10,11... | collective-permute-start | bytes 1572872 | tf_op jit(solution)/shard_map/ppermute | solution.py:348
  52.3 1.5 %collective-permute-done.16.other = f32[128,1024]{1,0:T(8,128)S(1)} collective-permute-done((f32[128,1024]{1,0:T(8,128)S(1)}, f32[128,1024]{1,0:T(8,128)S(1)}, u32[]{:S(2)}, u32[]{:S(2)}) %collective-permute-start.16) | collective-permute-done | bytes 524320 | tf_op jit(solution)/shard_map/ppermute | solution.py:348
  53.9 0.6 shard_map.113
  54.5 0.3 collective-permute-start.17
  54.8 2.3 %collective-permute-start.18 = (bf16[272,256]{1,0:T(8,128)(2,1)S(1)}, bf16[272,256]{1,0:T(8,128)(2,1)S(1)}, u32[]{:S(2)}, u32[]{:S(2)}) collective-permute-start(bf16[272,256]{1,0:T(8,128)(2,1)S(1)} %get-tuple-element.77), channel_id=1, source_target_pairs={{0,192},{192,0},{64,128},{128,64},{1,193},{193,1},{65,129},{129,65... | collective-permute-start | bytes 417800 | tf_op jit(solution)/shard_map/ppermute | solution.py:336
  57.2 0.7 collective-permute-start.19
  57.8 1.9 %collective-permute-start.13 = (bf16[128,128]{1,0:T(8,128)(2,1)S(1)}, bf16[128,128]{1,0:T(8,128)(2,1)S(1)}, u32[]{:S(2)}, u32[]{:S(2)}) collective-permute-start(bf16[128,128]{1,0:T(8,128)(2,1)S(1)} %slice.3), channel_id=1, source_target_pairs={{0,8},{8,0},{1,9},{9,1},{2,10},{10,2},{3,11},{11,3},{4,12},{12,4},... | collective-permute-start | bytes 98312 | tf_op jit(solution)/shard_map/ppermute | solution.py:344
  59.7 1.6 %collective-permute-done.13.other = bf16[128,128]{1,0:T(8,128)(2,1)S(1)} collective-permute-done((bf16[128,128]{1,0:T(8,128)(2,1)S(1)}, bf16[128,128]{1,0:T(8,128)(2,1)S(1)}, u32[]{:S(2)}, u32[]{:S(2)}) %collective-permute-start.13) | collective-permute-done | bytes 32800 | tf_op jit(solution)/shard_map/ppermute | solution.py:344
  61.3 1.1 shard_map.110
  62.4 0.9 collective-permute-start.14
  63.2 0.3 collective-permute-done.19.d.refs_11_
  63.5 2.5 %collective-permute-start.20 = (bf16[128,256]{1,0:T(8,128)(2,1)S(1)}, bf16[128,256]{1,0:T(8,128)(2,1)S(1)}, u32[]{:S(2)}, u32[]{:S(2)}) collective-permute-start(bf16[128,256]{1,0:T(8,128)(2,1)S(1)} %shard_map.114.refs_12_.refs_0_), channel_id=1, source_target_pairs={{0,16},{16,0},{32,48},{48,32},{1,17},{17,1},{33,49},{49,33},{2,18}... | collective-permute-start | bytes 196616 | tf_op jit(solution)/shard_map/ppermute | solution.py:332
  66.1 5.4 %shard_map.115 = (bf16[512,128]{1,0:T(8,128)(2,1)S(1)}, bf16[512,128]{1,0:T(8,128)(2,1)S(1)}, bf16[512,128]{1,0:T(8,128)(2,1)S(1)}, bf16[512,128]{1,0:T(8,128)(2...) custom-call(s32[5]{0:T(128)S(1)} %stack.23.pos.refs_0_, s32[32,32]{1,0:T(8,128)S(1)} %copy-done.6, ...), custom_call_target="tpu_custom_call" | custom-call | flops 1342177280 | bytes 2134036 | tf_op jit(solution)/shard_map/pallas_call | solution.py:48
  71.5 1.3 %collective-permute-start.21 = (bf16[128,256]{1,0:T(8,128)(2,1)S(1)}, bf16[128,256]{1,0:T(8,128)(2,1)S(1)}, u32[]{:S(2)}, u32[]{:S(2)}) collective-permute-start(bf16[128,256]{1,0:T(8,128)(2,1)S(1)} %shard_map.116.a), channel_id=1, source_target_pairs={{0,48},{48,0},{16,32},{32,16},{1,49},{49,1},{17,33},{33,17},{2,50}... | collective-permute-start | bytes 196616 | tf_op jit(solution)/shard_map/ppermute | solution.py:336
  72.9 4.0 %collective-permute-done.21.b = bf16[128,256]{1,0:T(8,128)(2,1)S(1)} collective-permute-done((bf16[128,256]{1,0:T(8,128)(2,1)S(1)}, bf16[128,256]{1,0:T(8,128)(2,1)S(1)}, u32[]{:S(2)}, u32[]{:S(2)}) %collective-permute-start.21) | collective-permute-done | bytes 65568 | tf_op jit(solution)/shard_map/ppermute | solution.py:336
  76.9 1.3 %collective-permute-start.22 = (bf16[512,128]{1,0:T(8,128)(2,1)S(1)}, bf16[512,128]{1,0:T(8,128)(2,1)S(1)}, u32[]{:S(2)}, u32[]{:S(2)}) collective-permute-start(bf16[512,128]{1,0:T(8,128)(2,1)S(1)} %get-tuple-element.83), channel_id=1, source_target_pairs={{0,48},{48,0},{16,32},{32,16},{1,49},{49,1},{17,33},{33,17},{2,50}... | collective-permute-start | bytes 393224 | tf_op jit(solution)/shard_map/ppermute | solution.py:336
  78.3 0.5 collective-permute-start.15
  78.8 2.7 %collective-permute-start.26 = (bf16[256,256]{1,0:T(8,128)(2,1)S(1)}, bf16[256,256]{1,0:T(8,128)(2,1)S(1)}, u32[]{:S(2)}, u32[]{:S(2)}) collective-permute-start(bf16[256,256]{1,0:T(8,128)(2,1)S(1)} %get-tuple-element.91), channel_id=1, source_target_pairs={{0,192},{192,0},{64,128},{128,64},{1,193},{193,1},{65,129},{129,65... | collective-permute-start | bytes 393224 | tf_op jit(solution)/shard_map/ppermute | solution.py:336
  81.5 1.9 %collective-permute-start.24 = (bf16[512,128]{1,0:T(8,128)(2,1)S(1)}, bf16[512,128]{1,0:T(8,128)(2,1)S(1)}, u32[]{:S(2)}, u32[]{:S(2)}) collective-permute-start(bf16[512,128]{1,0:T(8,128)(2,1)S(1)} %get-tuple-element.87), channel_id=1, source_target_pairs={{0,16},{16,0},{32,48},{48,32},{1,17},{17,1},{33,49},{49,33},{2,18}... | collective-permute-start | bytes 393224 | tf_op jit(solution)/shard_map/ppermute | solution.py:332
  83.4 2.0 %collective-permute-start.23 = (bf16[256,128]{1,0:T(8,128)(2,1)S(1)}, bf16[256,128]{1,0:T(8,128)(2,1)S(1)}, u32[]{:S(2)}, u32[]{:S(2)}) collective-permute-start(bf16[256,128]{1,0:T(8,128)(2,1)S(1)} %get-tuple-element.85), channel_id=1, source_target_pairs={{0,16},{16,0},{32,48},{48,32},{1,17},{17,1},{33,49},{49,33},{2,18}... | collective-permute-start | bytes 196616 | tf_op jit(solution)/shard_map/ppermute | solution.py:332
  85.4 0.7 shard_map.112.refs_3_
  86.1 1.9 %collective-permute-done.29.refs_2_ = bf16[128,256]{1,0:T(8,128)(2,1)S(1)} collective-permute-done((bf16[128,256]{1,0:T(8,128)(2,1)S(1)}, bf16[128,256]{1,0:T(8,128)(2,1)S(1)}, u32[]{:S(2)}, u32[]{:S(2)}) %collective-permute-start.29) | collective-permute-done | bytes 65568 | tf_op jit(solution)/shard_map/ppermute | solution.py:344
  88.0 0.9 copy-done.1
  88.9 0.6 shard_map.122.refs_1_
  89.4 0.1 collective-permute-start.32
  89.5 0.6 collective-permute-start.31
  90.2 2.0 %collective-permute-start.30 = (bf16[256,256]{1,0:T(8,128)(2,1)S(1)}, bf16[256,256]{1,0:T(8,128)(2,1)S(1)}, u32[]{:S(2)}, u32[]{:S(2)}) collective-permute-start(bf16[256,256]{1,0:T(8,128)(2,1)S(1)} %shard_map.122.refs_1_), channel_id=1, source_target_pairs={{0,64},{64,0},{128,192},{192,128},{1,65},{65,1},{129,193},{193,129... | collective-permute-start | bytes 393224 | tf_op jit(solution)/shard_map/ppermute | solution.py:332
  92.3 2.2 %collective-permute-start.25 = (bf16[256,128]{1,0:T(8,128)(2,1)S(1)}, bf16[256,128]{1,0:T(8,128)(2,1)S(1)}, u32[]{:S(2)}, u32[]{:S(2)}) collective-permute-start(bf16[256,128]{1,0:T(8,128)(2,1)S(1)} %get-tuple-element.89), channel_id=1, source_target_pairs={{0,48},{48,0},{16,32},{32,16},{1,49},{49,1},{17,33},{33,17},{2,50}... | collective-permute-start | bytes 196616 | tf_op jit(solution)/shard_map/ppermute | solution.py:336
  94.4 0.2 collective-permute-start.27
  94.6 3.3 %collective-permute-done.25.v_far = bf16[256,128]{1,0:T(8,128)(2,1)S(1)} collective-permute-done((bf16[256,128]{1,0:T(8,128)(2,1)S(1)}, bf16[256,128]{1,0:T(8,128)(2,1)S(1)}, u32[]{:S(2)}, u32[]{:S(2)}) %collective-permute-start.25) | collective-permute-done | bytes 65568 | tf_op jit(solution)/shard_map/ppermute | solution.py:336
  97.9 0.1 shard_map.121
  98.0 0.6 shard_map.123.here
  98.6 5.4 %collective-permute-start.33 = (bf16[256,1024]{1,0:T(8,128)(2,1)S(1)}, bf16[256,1024]{1,0:T(8,128)(2,1)S(1)}, u32[]{:S(2)}, u32[]{:S(2)}) collective-permute-start(bf16[256,1024]{1,0:T(8,128)(2,1)S(1)} %shard_map.123.here), channel_id=1, source_target_pairs={{0,1},{1,0},{2,3},{3,2},{4,5},{5,4},{6,7},{7,6},{8,9},{9,8},{10,11... | collective-permute-start | bytes 1572872 | tf_op jit(solution)/shard_map/ppermute | solution.py:348
  104.1 1.7 %collective-permute-start.28 = (bf16[384,128]{1,0:T(8,128)(2,1)S(1)}, bf16[384,128]{1,0:T(8,128)(2,1)S(1)}, u32[]{:S(2)}, u32[]{:S(2)}) collective-permute-start(bf16[384,128]{1,0:T(8,128)(2,1)S(1)} %get-tuple-element.96.refs_5_), channel_id=1, source_target_pairs={{0,8},{8,0},{1,9},{9,1},{2,10},{10,2},{3,11},{11,3},{4,12},{12,4},... | collective-permute-start | bytes 294920 | tf_op jit(solution)/shard_map/ppermute | solution.py:344
  105.8 3.1 %collective-permute-done.28.other = bf16[384,128]{1,0:T(8,128)(2,1)S(1)} collective-permute-done((bf16[384,128]{1,0:T(8,128)(2,1)S(1)}, bf16[384,128]{1,0:T(8,128)(2,1)S(1)}, u32[]{:S(2)}, u32[]{:S(2)}) %collective-permute-start.28) | collective-permute-done | bytes 98336 | tf_op jit(solution)/shard_map/ppermute | solution.py:344
  108.9 2.1 %shard_map.124 = (bf16[128,256]{1,0:T(8,128)(2,1)}, bf16[128,256]{1,0:T(8,128)(2,1)}, bf16[128,256]{1,0:T(8,128)(2,1)}, f32[256,2048]{1,0:T(8,128)}) custom-call(s32[5]{0:T(128)S(1)} %stack.23.pos.refs_0_, bf16[384,128]{1,0:T(8,128)(2,1)S(1)} %get-tuple-element.95.mine, bf16[384,128]{1,0:T(8,128)(2,1)S(1)} %collective-permute-done.28.other, ...), custom_call_target="tpu_custom_call" | custom-call | bytes 3538964 | tf_op jit(solution)/shard_map/pallas_call | solution.py:48
  (44 shorter events, 0.6 us)
Async XLA Ops:
  0.6 34.5 %copy-start.6 = (s32[32,32]{1,0:T(8,128)S(1)}, s32[32,32]{1,0:T(8,128)}, u32[]{:S(2)}) copy-start(s32[32,32]{1,0:T(8,128)} %refs_1_.1) | copy-start | bytes 12292
  0.6 9.4 %collective-permute-start.10 = (bf16[32,2048]{1,0:T(8,128)(2,1)}, bf16[32,2048]{1,0:T(8,128)(2,1)S(1)}, u32[]{:S(2)}, u32[]{:S(2)}) collective-permute-start(bf16[32,2048]{1,0:T(8,128)(2,1)} %bitcast.14), channel_id=1, source_target_pairs={{0,8},{8,0},{1,9},{9,1},{2,10},{10,2},{3,11},{11,3},{4,12},{12,4},... | collective-permute-start | bytes 393224 | tf_op jit(solution)/shard_map/ppermute | solution.py:344
  3.3 0.8 copy-start.3
  4.1 0.8 copy-start.4
  5.0 0.8 copy-start.5
  6.5 3.6 %collective-permute-start = (bf16[384,128]{1,0:T(8,128)(2,1)S(1)}, bf16[384,128]{1,0:T(8,128)(2,1)S(1)}, u32[]{:S(2)}, u32[]{:S(2)}) collective-permute-start(bf16[384,128]{1,0:T(8,128)(2,1)S(1)} %get-tuple-element.54), channel_id=1, source_target_pairs={{0,8},{8,0},{1,9},{9,1},{2,10},{10,2},{3,11},{11,3},{4,12},{12,4},... | collective-permute-start | bytes 294920 | tf_op jit(solution)/shard_map/ppermute | solution.py:344
  10.0 0.9 copy-start.2
  10.9 10.9 %collective-permute-start.11 = (bf16[64,2048]{1,0:T(8,128)(2,1)S(1)}, bf16[64,2048]{1,0:T(8,128)(2,1)S(1)}, u32[]{:S(2)}, u32[]{:S(2)}) collective-permute-start(bf16[64,2048]{1,0:T(8,128)(2,1)S(1)} %shard_map.105.refs_0_), channel_id=1, source_target_pairs={{0,2},{2,0},{4,6},{6,4},{1,3},{3,1},{5,7},{7,5},{8,10},{10,8},{12,... | collective-permute-start | bytes 786440 | tf_op jit(solution)/shard_map/ppermute | solution.py:332
  12.3 7.6 %collective-permute-start.1 = (bf16[256,128]{1,0:T(8,128)(2,1)S(1)}, bf16[256,128]{1,0:T(8,128)(2,1)S(1)}, u32[]{:S(2)}, u32[]{:S(2)}) collective-permute-start(bf16[256,128]{1,0:T(8,128)(2,1)S(1)} %get-tuple-element.55.k0), channel_id=1, source_target_pairs={{0,16},{16,0},{32,48},{48,32},{1,17},{17,1},{33,49},{49,33},{2,18}... | collective-permute-start | bytes 196616 | tf_op jit(solution)/shard_map/ppermute | solution.py:332
  15.4 5.8 %collective-permute-start.2 = (bf16[256,128]{1,0:T(8,128)(2,1)S(1)}, bf16[256,128]{1,0:T(8,128)(2,1)S(1)}, u32[]{:S(2)}, u32[]{:S(2)}) collective-permute-start(bf16[256,128]{1,0:T(8,128)(2,1)S(1)} %get-tuple-element.56.v0), channel_id=1, source_target_pairs={{0,48},{48,0},{16,32},{32,16},{1,49},{49,1},{17,33},{33,17},{2,50}... | collective-permute-start | bytes 196616 | tf_op jit(solution)/shard_map/ppermute | solution.py:336
  18.7 3.1 %collective-permute-start.3 = (bf16[256,128]{1,0:T(8,128)(2,1)S(1)}, bf16[256,128]{1,0:T(8,128)(2,1)S(1)}, u32[]{:S(2)}, u32[]{:S(2)}) collective-permute-start(bf16[256,128]{1,0:T(8,128)(2,1)S(1)} %get-tuple-element.57.q0), channel_id=1, source_target_pairs={{0,64},{64,0},{128,192},{192,128},{1,65},{65,1},{129,193},{193,129... | collective-permute-start | bytes 196616 | tf_op jit(solution)/shard_map/ppermute | solution.py:332
  21.9 21.3 %copy-start = (bf16[256,2048]{1,0:T(8,128)(2,1)S(1)}, bf16[256,2048]{1,0:T(8,128)(2,1)}, u32[]{:S(2)}) copy-start(bf16[256,2048]{1,0:T(8,128)(2,1)} %w.3) | copy-start | bytes 3145732
  21.9 20.6 %collective-permute-start.12 = (bf16[128,2048]{1,0:T(8,128)(2,1)S(1)}, bf16[128,2048]{1,0:T(8,128)(2,1)S(1)}, u32[]{:S(2)}, u32[]{:S(2)}) collective-permute-start(bf16[128,2048]{1,0:T(8,128)(2,1)S(1)} %shard_map.106.pair), channel_id=1, source_target_pairs={{0,6},{6,0},{2,4},{4,2},{1,7},{7,1},{3,5},{5,3},{8,14},{14,8},{10,... | collective-permute-start | bytes 1572872 | tf_op jit(solution)/shard_map/ppermute | solution.py:336
  23.9 6.1 %collective-permute-start.5 = (bf16[512,128]{1,0:T(8,128)(2,1)S(1)}, bf16[512,128]{1,0:T(8,128)(2,1)S(1)}, u32[]{:S(2)}, u32[]{:S(2)}) collective-permute-start(bf16[512,128]{1,0:T(8,128)(2,1)S(1)} %get-tuple-element.59.vp.refs_4_), channel_id=1, source_target_pairs={{0,16},{16,0},{32,48},{48,32},{1,17},{17,1},{33,49},{49,33},{2,18}... | collective-permute-start | bytes 393224 | tf_op jit(solution)/shard_map/ppermute | solution.py:332
  25.3 5.3 %collective-permute-start.6 = (bf16[512,128]{1,0:T(8,128)(2,1)S(1)}, bf16[512,128]{1,0:T(8,128)(2,1)S(1)}, u32[]{:S(2)}, u32[]{:S(2)}) collective-permute-start(bf16[512,128]{1,0:T(8,128)(2,1)S(1)} %get-tuple-element.60.qp.refs_6_), channel_id=1, source_target_pairs={{0,192},{192,0},{64,128},{128,64},{1,193},{193,1},{65,129},{129,65... | collective-permute-start | bytes 393224 | tf_op jit(solution)/shard_map/ppermute | solution.py:336
  27.7 7.4 %collective-permute-start.4 = (bf16[512,128]{1,0:T(8,128)(2,1)S(1)}, bf16[512,128]{1,0:T(8,128)(2,1)S(1)}, u32[]{:S(2)}, u32[]{:S(2)}) collective-permute-start(bf16[512,128]{1,0:T(8,128)(2,1)S(1)} %get-tuple-element.58.kp.refs_2_), channel_id=1, source_target_pairs={{0,48},{48,0},{16,32},{32,16},{1,49},{49,1},{17,33},{33,17},{2,50}... | collective-permute-start | bytes 393224 | tf_op jit(solution)/shard_map/ppermute | solution.py:336
  39.2 5.0 %collective-permute-start.7 = (bf16[144,256]{1,0:T(8,128)(2,1)S(1)}, bf16[144,256]{1,0:T(8,128)(2,1)S(1)}, u32[]{:S(2)}, u32[]{:S(2)}) collective-permute-start(bf16[144,256]{1,0:T(8,128)(2,1)S(1)} %get-tuple-element.62), channel_id=1, source_target_pairs={{0,64},{64,0},{128,192},{192,128},{1,65},{65,1},{129,193},{193,129... | collective-permute-start | bytes 221192 | tf_op jit(solution)/shard_map/ppermute | solution.py:332
  39.3 5.3 %collective-permute-start.8 = (bf16[144,256]{1,0:T(8,128)(2,1)S(1)}, bf16[144,256]{1,0:T(8,128)(2,1)S(1)}, u32[]{:S(2)}, u32[]{:S(2)}) collective-permute-start(bf16[144,256]{1,0:T(8,128)(2,1)S(1)} %get-tuple-element.63), channel_id=1, source_target_pairs={{0,192},{192,0},{64,128},{128,64},{1,193},{193,1},{65,129},{129,65... | collective-permute-start | bytes 221192 | tf_op jit(solution)/shard_map/ppermute | solution.py:336
  39.4 5.2 %collective-permute-start.9 = (bf16[144,256]{1,0:T(8,128)(2,1)S(1)}, bf16[144,256]{1,0:T(8,128)(2,1)S(1)}, u32[]{:S(2)}, u32[]{:S(2)}) collective-permute-start(bf16[144,256]{1,0:T(8,128)(2,1)S(1)} %get-tuple-element.64), channel_id=1, source_target_pairs={{0,128},{128,0},{64,192},{192,64},{1,129},{129,1},{65,193},{193,65... | collective-permute-start | bytes 221192 | tf_op jit(solution)/shard_map/ppermute | solution.py:340
  45.6 8.2 %collective-permute-start.16 = (f32[128,1024]{1,0:T(8,128)S(1)}, f32[128,1024]{1,0:T(8,128)S(1)}, u32[]{:S(2)}, u32[]{:S(2)}) collective-permute-start(f32[128,1024]{1,0:T(8,128)S(1)} %get-tuple-element.73), channel_id=1, source_target_pairs={{0,1},{1,0},{2,3},{3,2},{4,5},{5,4},{6,7},{7,6},{8,9},{9,8},{10,11... | collective-permute-start | bytes 1572872 | tf_op jit(solution)/shard_map/ppermute | solution.py:348
  54.5 8.8 %collective-permute-start.17 = (bf16[272,256]{1,0:T(8,128)(2,1)S(1)}, bf16[272,256]{1,0:T(8,128)(2,1)S(1)}, u32[]{:S(2)}, u32[]{:S(2)}) collective-permute-start(bf16[272,256]{1,0:T(8,128)(2,1)S(1)} %get-tuple-element.76), channel_id=1, source_target_pairs={{0,64},{64,0},{128,192},{192,128},{1,65},{65,1},{129,193},{193,129... | collective-permute-start | bytes 417800 | tf_op jit(solution)/shard_map/ppermute | solution.py:332
  54.8 8.4 %collective-permute-start.18 = (bf16[272,256]{1,0:T(8,128)(2,1)S(1)}, bf16[272,256]{1,0:T(8,128)(2,1)S(1)}, u32[]{:S(2)}, u32[]{:S(2)}) collective-permute-start(bf16[272,256]{1,0:T(8,128)(2,1)S(1)} %get-tuple-element.77), channel_id=1, source_target_pairs={{0,192},{192,0},{64,128},{128,64},{1,193},{193,1},{65,129},{129,65... | collective-permute-start | bytes 417800 | tf_op jit(solution)/shard_map/ppermute | solution.py:336
  57.2 6.3 %collective-permute-start.19 = (bf16[272,256]{1,0:T(8,128)(2,1)S(1)}, bf16[272,256]{1,0:T(8,128)(2,1)S(1)}, u32[]{:S(2)}, u32[]{:S(2)}) collective-permute-start(bf16[272,256]{1,0:T(8,128)(2,1)S(1)} %get-tuple-element.78), channel_id=1, source_target_pairs={{0,128},{128,0},{64,192},{192,64},{1,129},{129,1},{65,193},{193,65... | collective-permute-start | bytes 417800 | tf_op jit(solution)/shard_map/ppermute | solution.py:340
  57.8 3.5 %collective-permute-start.13 = (bf16[128,128]{1,0:T(8,128)(2,1)S(1)}, bf16[128,128]{1,0:T(8,128)(2,1)S(1)}, u32[]{:S(2)}, u32[]{:S(2)}) collective-permute-start(bf16[128,128]{1,0:T(8,128)(2,1)S(1)} %slice.3), channel_id=1, source_target_pairs={{0,8},{8,0},{1,9},{9,1},{2,10},{10,2},{3,11},{11,3},{4,12},{12,4},... | collective-permute-start | bytes 98312 | tf_op jit(solution)/shard_map/ppermute | solution.py:344
  62.4 15.8 %collective-permute-start.14 = (bf16[64,2048]{1,0:T(8,128)(2,1)S(1)}, bf16[64,2048]{1,0:T(8,128)(2,1)S(1)}, u32[]{:S(2)}, u32[]{:S(2)}) collective-permute-start(bf16[64,2048]{1,0:T(8,128)(2,1)S(1)} %get-tuple-element.69), channel_id=1, source_target_pairs={{0,6},{6,0},{2,4},{4,2},{1,7},{7,1},{3,5},{5,3},{8,14},{14,8},{10,... | collective-permute-start | bytes 786440 | tf_op jit(solution)/shard_map/ppermute | solution.py:336
  63.5 8.0 %collective-permute-start.20 = (bf16[128,256]{1,0:T(8,128)(2,1)S(1)}, bf16[128,256]{1,0:T(8,128)(2,1)S(1)}, u32[]{:S(2)}, u32[]{:S(2)}) collective-permute-start(bf16[128,256]{1,0:T(8,128)(2,1)S(1)} %shard_map.114.refs_12_.refs_0_), channel_id=1, source_target_pairs={{0,16},{16,0},{32,48},{48,32},{1,17},{17,1},{33,49},{49,33},{2,18}... | collective-permute-start | bytes 196616 | tf_op jit(solution)/shard_map/ppermute | solution.py:332
  71.5 5.3 %collective-permute-start.21 = (bf16[128,256]{1,0:T(8,128)(2,1)S(1)}, bf16[128,256]{1,0:T(8,128)(2,1)S(1)}, u32[]{:S(2)}, u32[]{:S(2)}) collective-permute-start(bf16[128,256]{1,0:T(8,128)(2,1)S(1)} %shard_map.116.a), channel_id=1, source_target_pairs={{0,48},{48,0},{16,32},{32,16},{1,49},{49,1},{17,33},{33,17},{2,50}... | collective-permute-start | bytes 196616 | tf_op jit(solution)/shard_map/ppermute | solution.py:336
  76.9 6.5 %collective-permute-start.22 = (bf16[512,128]{1,0:T(8,128)(2,1)S(1)}, bf16[512,128]{1,0:T(8,128)(2,1)S(1)}, u32[]{:S(2)}, u32[]{:S(2)}) collective-permute-start(bf16[512,128]{1,0:T(8,128)(2,1)S(1)} %get-tuple-element.83), channel_id=1, source_target_pairs={{0,48},{48,0},{16,32},{32,16},{1,49},{49,1},{17,33},{33,17},{2,50}... | collective-permute-start | bytes 393224 | tf_op jit(solution)/shard_map/ppermute | solution.py:336
  78.3 7.1 %collective-permute-start.15 = (bf16[32,2048]{1,0:T(8,128)(2,1)S(1)}, bf16[32,2048]{1,0:T(8,128)(2,1)S(1)}, u32[]{:S(2)}, u32[]{:S(2)}) collective-permute-start(bf16[32,2048]{1,0:T(8,128)(2,1)S(1)} %get-tuple-element.71), channel_id=1, source_target_pairs={{0,2},{2,0},{4,6},{6,4},{1,3},{3,1},{5,7},{7,5},{8,10},{10,8},{12,... | collective-permute-start | bytes 393224 | tf_op jit(solution)/shard_map/ppermute | solution.py:332
  78.8 11.4 %collective-permute-start.26 = (bf16[256,256]{1,0:T(8,128)(2,1)S(1)}, bf16[256,256]{1,0:T(8,128)(2,1)S(1)}, u32[]{:S(2)}, u32[]{:S(2)}) collective-permute-start(bf16[256,256]{1,0:T(8,128)(2,1)S(1)} %get-tuple-element.91), channel_id=1, source_target_pairs={{0,192},{192,0},{64,128},{128,64},{1,193},{193,1},{65,129},{129,65... | collective-permute-start | bytes 393224 | tf_op jit(solution)/shard_map/ppermute | solution.py:336
  81.5 10.8 %collective-permute-start.24 = (bf16[512,128]{1,0:T(8,128)(2,1)S(1)}, bf16[512,128]{1,0:T(8,128)(2,1)S(1)}, u32[]{:S(2)}, u32[]{:S(2)}) collective-permute-start(bf16[512,128]{1,0:T(8,128)(2,1)S(1)} %get-tuple-element.87), channel_id=1, source_target_pairs={{0,16},{16,0},{32,48},{48,32},{1,17},{17,1},{33,49},{49,33},{2,18}... | collective-permute-start | bytes 393224 | tf_op jit(solution)/shard_map/ppermute | solution.py:332
  83.4 4.6 %collective-permute-start.29 = (bf16[128,256]{1,0:T(8,128)(2,1)S(1)}, bf16[128,256]{1,0:T(8,128)(2,1)S(1)}, u32[]{:S(2)}, u32[]{:S(2)}) collective-permute-start(bf16[128,256]{1,0:T(8,128)(2,1)S(1)} %shard_map.117.refs_1_), channel_id=1, source_target_pairs={{0,8},{8,0},{1,9},{9,1},{2,10},{10,2},{3,11},{11,3},{4,12},{12,4},... | collective-permute-start | bytes 196616 | tf_op jit(solution)/shard_map/ppermute | solution.py:344
  83.4 11.0 %collective-permute-start.23 = (bf16[256,128]{1,0:T(8,128)(2,1)S(1)}, bf16[256,128]{1,0:T(8,128)(2,1)S(1)}, u32[]{:S(2)}, u32[]{:S(2)}) collective-permute-start(bf16[256,128]{1,0:T(8,128)(2,1)S(1)} %get-tuple-element.85), channel_id=1, source_target_pairs={{0,16},{16,0},{32,48},{48,32},{1,17},{17,1},{33,49},{49,33},{2,18}... | collective-permute-start | bytes 196616 | tf_op jit(solution)/shard_map/ppermute | solution.py:332
  88.0 0.9 copy-start.1
  89.4 8.6 %collective-permute-start.32 = (bf16[256,256]{1,0:T(8,128)(2,1)S(1)}, bf16[256,256]{1,0:T(8,128)(2,1)S(1)}, u32[]{:S(2)}, u32[]{:S(2)}) collective-permute-start(bf16[256,256]{1,0:T(8,128)(2,1)S(1)} %shard_map.122.refs_1_), channel_id=1, source_target_pairs={{0,128},{128,0},{64,192},{192,64},{1,129},{129,1},{65,193},{193,65... | collective-permute-start | bytes 393224 | tf_op jit(solution)/shard_map/ppermute | solution.py:340
  89.5 8.5 %collective-permute-start.31 = (bf16[256,256]{1,0:T(8,128)(2,1)S(1)}, bf16[256,256]{1,0:T(8,128)(2,1)S(1)}, u32[]{:S(2)}, u32[]{:S(2)}) collective-permute-start(bf16[256,256]{1,0:T(8,128)(2,1)S(1)} %shard_map.122.refs_1_), channel_id=1, source_target_pairs={{0,192},{192,0},{64,128},{128,64},{1,193},{193,1},{65,129},{129,65... | collective-permute-start | bytes 393224 | tf_op jit(solution)/shard_map/ppermute | solution.py:336
  90.2 7.9 %collective-permute-start.30 = (bf16[256,256]{1,0:T(8,128)(2,1)S(1)}, bf16[256,256]{1,0:T(8,128)(2,1)S(1)}, u32[]{:S(2)}, u32[]{:S(2)}) collective-permute-start(bf16[256,256]{1,0:T(8,128)(2,1)S(1)} %shard_map.122.refs_1_), channel_id=1, source_target_pairs={{0,64},{64,0},{128,192},{192,128},{1,65},{65,1},{129,193},{193,129... | collective-permute-start | bytes 393224 | tf_op jit(solution)/shard_map/ppermute | solution.py:332
  92.3 5.6 %collective-permute-start.25 = (bf16[256,128]{1,0:T(8,128)(2,1)S(1)}, bf16[256,128]{1,0:T(8,128)(2,1)S(1)}, u32[]{:S(2)}, u32[]{:S(2)}) collective-permute-start(bf16[256,128]{1,0:T(8,128)(2,1)S(1)} %get-tuple-element.89), channel_id=1, source_target_pairs={{0,48},{48,0},{16,32},{32,16},{1,49},{49,1},{17,33},{33,17},{2,50}... | collective-permute-start | bytes 196616 | tf_op jit(solution)/shard_map/ppermute | solution.py:336
  94.4 3.5 %collective-permute-start.27 = (bf16[128,256]{1,0:T(8,128)(2,1)S(1)}, bf16[128,256]{1,0:T(8,128)(2,1)S(1)}, u32[]{:S(2)}, u32[]{:S(2)}) collective-permute-start(bf16[128,256]{1,0:T(8,128)(2,1)S(1)} %get-tuple-element.94), channel_id=1, source_target_pairs={{0,64},{64,0},{128,192},{192,128},{1,65},{65,1},{129,193},{193,129... | collective-permute-start | bytes 196616 | tf_op jit(solution)/shard_map/ppermute | solution.py:332
  98.6 10.2 %collective-permute-start.33 = (bf16[256,1024]{1,0:T(8,128)(2,1)S(1)}, bf16[256,1024]{1,0:T(8,128)(2,1)S(1)}, u32[]{:S(2)}, u32[]{:S(2)}) collective-permute-start(bf16[256,1024]{1,0:T(8,128)(2,1)S(1)} %shard_map.123.here), channel_id=1, source_target_pairs={{0,1},{1,0},{2,3},{3,2},{4,5},{5,4},{6,7},{7,6},{8,9},{9,8},{10,11... | collective-permute-start | bytes 1572872 | tf_op jit(solution)/shard_map/ppermute | solution.py:348
  104.1 4.8 %collective-permute-start.28 = (bf16[384,128]{1,0:T(8,128)(2,1)S(1)}, bf16[384,128]{1,0:T(8,128)(2,1)S(1)}, u32[]{:S(2)}, u32[]{:S(2)}) collective-permute-start(bf16[384,128]{1,0:T(8,128)(2,1)S(1)} %get-tuple-element.96.refs_5_), channel_id=1, source_target_pairs={{0,8},{8,0},{1,9},{9,1},{2,10},{10,2},{3,11},{11,3},{4,12},{12,4},... | collective-permute-start | bytes 294920 | tf_op jit(solution)/shard_map/ppermute | solution.py:344

commit v3 on v2

--- a/solution.py
+++ b/solution.py
@@ -56,21 +56,6 @@
     )(*ins)
 
 
-def split_heads(pos, q, k, v, keep, send, sems):
-    mine = pl.ds(pl.multiple_of(pos[PAR] * HD, HD), HD)
-    other = pl.ds(pl.multiple_of((1 - pos[PAR]) * HD, HD), HD)
-    copies = []
-    for n, ref in enumerate((q, k, v)):
-        rows = pl.ds(n * TILE, TILE)
-        for m, (columns, out) in enumerate(((other, send), (mine, keep))):
-            copies.append(
-                pltpu.make_async_copy(ref.at[:, columns], out.at[rows, :], sems.at[n, m])
-            )
-            copies[-1].start()
-    for copy in copies:
-        copy.wait()
-
-
 def own_blocks(keep, recv, k, v, q):
     for n, ref in ((0, q), (1, k), (2, v)):
         rows = slice(n * TILE, (n + 1) * TILE)
@@ -104,7 +89,7 @@
     par = pos[PAR]
     query = (query_x * 4 + pos[ZH]) * 2
     rows = []
-    for e in range(4):
+    for e in ORDER:
         key = (pos[X] * 4 + (pos[ZH] ^ e)) * 2
         for tile in (par, 1 - par):
             near = jnp.where(mask[query + par, key + tile] > 0, 0.0, LOW)
@@ -113,9 +98,11 @@
     return rows
 
 
-def scores_of(keys, queries, rows, e):
+def scores_of(keys, queries, rows):
     raw = dot(keys, queries, NT) * (SCALE * LOG2E)
-    return jnp.concatenate([raw[:TILE] + rows[2 * e], raw[TILE:] + rows[2 * e + 1]], axis=0)
+    return jnp.concatenate(
+        [raw[t * TILE : (t + 1) * TILE] + row for t, row in enumerate(rows)], axis=0
+    )
 
 
 def split3(value):
@@ -134,29 +121,32 @@
     return packed.astype(BF16)
 
 
-def halves(ref):
-    rows = ref.shape[0] // 2
-    return ref[:rows, :], ref[rows:, :]
-
-
-def by_place(kp, kf, vp, vn):
-    (k0, k1), (k3, k2) = halves(kp), halves(kf)
-    (v0, v3), (v1, v2) = halves(vp), halves(vn)
-    return (k0, k1, k2, k3), (v0, v1, v2, v3)
-
-
-def forward(pos, mask, kp, kf, vp, vn, qp, qf, p0, p1, p2, p3, q, part):
-    keys, values = by_place(kp, kf, vp, vn)
-    values_t = [v.astype(F32).T.astype(BF16) for v in values]
-    for n in range(4):
-        start = (n % 2) * BLK
-        q[pos[X] ^ ORDER[n]] = (qp, qf)[n // 2][start : start + BLK, :]
-
-    def block(x, carry):
-        rows = bias_rows(pos, mask, x)
-        scores = [scores_of(keys[e], q[x], rows, e) for e in range(4)]
+def load_kv(kp, kf, vp, vn):
+    keys = jnp.concatenate([kp[...], kf[...]], axis=0)
+    values = [vp[:BLK, :], vn[:BLK, :], vp[BLK:, :], vn[BLK:, :]]
+    return keys, jnp.concatenate(values, axis=0)
+
+
+def transposed(a):
+    return a.astype(F32).T.astype(BF16)
+
+
+def query_block(qp, qf, n):
+    return (qp, qf)[n // 2][(n % 2) * BLK : (n % 2 + 1) * BLK, :]
+
+
+def forward(pos, mask, kp, kf, vp, vn, qp, qf, p0, p1, p2, p3):
+    keys, values = load_kv(kp, kf, vp, vn)
+    values_t = transposed(values)
+    for n, pack in enumerate((p0, p1, p2, p3)):
+        rows = bias_rows(pos, mask, pos[X] ^ ORDER[n])
+        queries = query_block(qp, qf, n)
+        scores = [
+            scores_of(keys[e * BLK : (e + 1) * BLK], queries, rows[2 * e : 2 * e + 2])
+            for e in range(4)
+        ]
         largest = functools.reduce(
-            jnp.maximum, [jnp.max(s, axis=0, keepdims=True) for s in scores]
+            jnp.maximum, [jnp.max(block, axis=0, keepdims=True) for block in scores]
         )
         largest = jnp.maximum(largest, 0.1 * LOW)
         total = jnp.zeros((1, BLK), F32)
@@ -164,58 +154,42 @@
         for e in range(4):
             weights = jnp.exp2(scores[e] - largest)
             total = total + jnp.sum(weights, axis=0, keepdims=True)
-            summed = summed + dot(values_t[e], weights.astype(BF16))
+            summed = summed + dot(values_t[:, e * BLK : (e + 1) * BLK], weights.astype(BF16))
         some = total > 0.0
         safe = jnp.where(some, total, 1.0)
-        part[x, :HD, :] = (summed / safe).astype(BF16)
-        part[x, HD:, :] = pack_rows(split3(jnp.where(some, largest + jnp.log2(safe), LOW)))
-        return carry
-
-    lax.fori_loop(0, 4, block, 0)
-    for n, ref in enumerate((p0, p1, p2, p3)):
-        ref[...] = part[pos[X] ^ ORDER[n]]
+        pack[:HD, :] = (summed / safe).astype(BF16)
+        pack[HD:, :] = pack_rows(split3(jnp.where(some, largest + jnp.log2(safe), LOW)))
 
 
 def backward(
     pos, mask, kp, kf, vp, vn, qp, qf, s0, s1, s2, s3,
-    dk, dk_far, dv, dv_near, dq, dq_far, q, g, stats, part, acc,
+    dk, dk_far, dv, dv_near, dq, dq_far, probs_of, scores_grad_of,
 ):
-    keys, values = by_place(kp, kf, vp, vn)
-    keys_t = [k.astype(F32).T.astype(BF16) for k in keys]
-    for n, stat in enumerate((s0, s1, s2, s3)):
-        x = pos[X] ^ ORDER[n]
-        q[x] = (qp, qf)[n // 2][(n % 2) * BLK : (n % 2 + 1) * BLK, :]
-        g[x] = stat[HD : 2 * HD, :]
-        stats[x] = stat[2 * HD :, :]
-    acc[...] = jnp.zeros_like(acc)
-
-    def block(x, carry):
-        rows = bias_rows(pos, mask, x)
-        queries, grad_t = q[x], g[x]
-        s = stats[x].astype(F32)
+    keys, values = load_kv(kp, kf, vp, vn)
+    keys_t = transposed(keys)
+    for n, ref in enumerate((s0, s1, s2, s3)):
+        rows = bias_rows(pos, mask, pos[X] ^ ORDER[n])
+        s = ref[2 * HD :, :].astype(F32)
         lse = s[0:1] + s[1:2] + s[2:3]
         delta = s[3:4] + s[4:5] + s[5:6]
-        grad_query = jnp.zeros((HD, BLK), F32)
-        for e in range(4):
-            probs = jnp.exp2(scores_of(keys[e], queries, rows, e) - lse)
-            grad_probs = dot(values[e], grad_t)
-            grad_scores = (probs * (grad_probs - delta)).astype(BF16)
-            acc[e, BLK:, :] += dot(probs.astype(BF16), grad_t, NT)
-            acc[e, :BLK, :] += dot(grad_scores, queries)
-            grad_query = grad_query + dot(keys_t[e], grad_scores)
-        part[x] = (grad_query * SCALE).astype(BF16)
-        return carry
-
-    lax.fori_loop(0, 4, block, 0)
-    for n, (e, k, f, v) in enumerate(
-        ((0, dk, 0, dv), (1, dk, 3, dv), (3, dk_far, 1, dv_near), (2, dk_far, 2, dv_near))
-    ):
-        rows = slice((n % 2) * BLK, (n % 2 + 1) * BLK)
-        k[rows, :] = (acc[e, :BLK, :] * SCALE).astype(BF16)
-        v[rows, :] = acc[f, BLK:, :].astype(BF16)
+        probs = jnp.exp2(scores_of(keys, query_block(qp, qf, n), rows) - lse)
+        grad_probs = dot(values, ref[HD : 2 * HD, :])
+        grad_scores = (probs * (grad_probs - delta)).astype(BF16)
+        columns = slice(n * BLK, (n + 1) * BLK)
+        probs_of[:, columns] = probs.astype(BF16)
+        scores_grad_of[:, columns] = grad_scores
+        out = (dq, dq_far)[n // 2]
+        out[(n % 2) * HD : (n % 2 + 1) * HD, :] = (dot(keys_t, grad_scores) * SCALE).astype(BF16)
+    queries = jnp.concatenate([qp[...], qf[...]], axis=0)
+    grads = jnp.concatenate([ref[HD : 2 * HD, :] for ref in (s0, s1, s2, s3)], axis=1)
     for n in range(4):
-        ref = (dq, dq_far)[n // 2]
-        ref[(n % 2) * HD : (n % 2 + 1) * HD, :] = part[pos[X] ^ ORDER[n]]
+        block = slice(n * BLK, (n + 1) * BLK)
+        half = slice((n % 2) * BLK, (n % 2 + 1) * BLK)
+        out = (dk, dk_far)[n // 2]
+        out[half, :] = (dot(scores_grad_of[block, :], queries) * SCALE).astype(BF16)
+        half = slice((n // 2) * BLK, (n // 2 + 1) * BLK)
+        out = (dv, dv_near)[n % 2]
+        out[half, :] = dot(probs_of[block, :], grads, NT).astype(BF16)
 
 
 def back_project(pos, w, near, far, grads):
@@ -352,14 +326,10 @@
     pos = jnp.stack([lax.axis_index(name) for name in AXES]).astype(jnp.int32)
     kv_mm = 2 * 1024 * 1024 * HD
 
-    keep, send = call(
-        split_heads,
-        [((3 * TILE, HD), BF16)] * 2,
-        (pos, query_rows[0], key_rows[0], value_rows[0]),
-        scratch=[pltpu.SemaphoreType.DMA((3, 2))],
-        space=pltpu.HBM,
-        out_space=pltpu.HBM,
-    )
+    inputs = (query_rows[0], key_rows[0], value_rows[0])
+    first = pos[PAR] == 0
+    send = jnp.concatenate([jnp.where(first, rows[:, HD:], rows[:, :HD]) for rows in inputs])
+    keep = jnp.concatenate([jnp.where(first, rows[:, :HD], rows[:, HD:]) for rows in inputs])
     recv = over_pair(send)
     rows_far = over_pair(cotangent[0])
     k, v, q = call(own_blocks, [((BLK, HD), BF16)] * 3, (keep, recv), smem=0)
@@ -378,7 +348,6 @@
         [((HD + 16, BLK), BF16)] * 4,
         (pos, tile_mask, kp, kf, vp, vn, qp, qf),
         flops=2 * kv_mm,
-        scratch=[pltpu.VMEM((4, BLK, HD), BF16), pltpu.VMEM((4, HD + 16, BLK), BF16)],
         smem=2,
     )
     packs = [packs[0], near(packs[1], "x"), far(packs[2], "x"), opposite(packs[3], "x")]
@@ -401,30 +370,6 @@
         weight_cut, [((2 * HD + 16, BLK), BF16)] * 4, (pos, gw_keep, gw_recv, grads, stats)
     )
     cuts = [cuts[0], near(cuts[1], "x"), far(cuts[2], "x"), opposite(cuts[3], "x")]
-    (share,) = call(sum_cuts, [((HD, BLK), BF16)], cuts, smem=0)
-
-    dk, dk_far, dv, dv_near, dq, dq_far = call(
-        backward,
-        [((2 * BLK, HD), BF16)] * 4 + [((2 * HD, BLK), BF16)] * 2,
-        (pos, tile_mask, kp, kf, vp, vn, qp, qf, *cuts),
-        flops=5 * kv_mm,
-        scratch=[
-            pltpu.VMEM((4, BLK, HD), BF16),
-            pltpu.VMEM((4, HD, BLK), BF16),
-            pltpu.VMEM((4, 16, BLK), BF16),
-            pltpu.VMEM((4, HD, BLK), BF16),
-            pltpu.VMEM((4, 2 * BLK, HD), F32),
-        ],
-        smem=2,
-        after=(share,),
-    )
-    (near_sum,) = call(
-        sum_two, [((HD, BLK), BF16)], (share, near(share, "zh")), smem=0, after=(dq,)
-    )
-    (done,) = call(sum_two, [((HD, BLK), BF16)], (near_sum, far(near_sum, "zh")), smem=0)
-    dq_far = lax.optimization_barrier((dq_far, near_sum))[0]
-    dk_far, dv_near, _ = lax.optimization_barrier((dk_far, dv_near, done))
-
     att_far = over_pair(att[:, TILE:])
     mixed, mixed_far = call(
         mix,
@@ -433,19 +378,39 @@
         flops=2 * TILE * 256 * 2048,
         scratch=[pltpu.VMEM((TILE, 2048), BF16)],
     )
+    (share,) = call(sum_cuts, [((HD, BLK), BF16)], cuts, smem=0, after=(mixed_far,))
+
+    dk, dk_far, dv, dv_near, dq, dq_far = call(
+        backward,
+        [((2 * BLK, HD), BF16)] * 4 + [((2 * HD, BLK), BF16)] * 2,
+        (pos, tile_mask, kp, kf, vp, vn, qp, qf, *cuts),
+        flops=5 * kv_mm,
+        scratch=[pltpu.VMEM((4 * BLK, 4 * BLK), BF16)] * 2,
+        smem=2,
+        after=(share,),
+    )
+    (near_sum,) = call(
+        sum_two, [((HD, BLK), BF16)], (share, near(share, "zh")), smem=0, after=(dq,)
+    )
+    (done,) = call(sum_two, [((HD, BLK), BF16)], (near_sum, far(near_sum, "zh")), smem=0)
+    done_far = over_pair(done)
+    dq_far = lax.optimization_barrier((dq_far, near_sum))[0]
+    dk_far, dv_near, _ = lax.optimization_barrier((dk_far, dv_near, done_far))
+
+    dq, dq_near = call(sum_split, [((HD, BLK), BF16)] * 2, (dq, far(dq_far, "x")), smem=0)
     mixed, mixed_near = call(
-        sum_split, [((32, 2048), BF16)] * 2, (mixed, far(mixed_far, "y")), smem=0
+        sum_split, [((32, 2048), BF16)] * 2, (mixed, far(mixed_far, "y")), smem=0, after=(done,)
     )
     (mixed,) = call(sum_two, [((32, 2048), BF16)], (mixed, near(mixed_near, "y")), smem=0)
-
+    (stack,) = call(weight_stack, [((2 * HD, BLK), BF16)], (pos, done, done_far), after=(dq_near,))
+    stacks = [stack, near(stack, "x"), far(stack, "x"), opposite(stack, "x")]
     dk, dk_near = call(
-        sum_split, [((BLK, HD), BF16)] * 2, (dk, far(dk_far, "zh")), smem=0
+        sum_split, [((BLK, HD), BF16)] * 2, (dk, far(dk_far, "zh")), smem=0, after=(stacks[1], mixed)
     )
     dv, dv_far = call(
-        sum_split, [((BLK, HD), BF16)] * 2, (dv, near(dv_near, "zh")), smem=0
-    )
-    dq, dq_near = call(sum_split, [((HD, BLK), BF16)] * 2, (dq, far(dq_far, "x")), smem=0)
-    dq_near = lax.optimization_barrier((dq_near, dk_near))[0]
+        sum_split, [((BLK, HD), BF16)] * 2, (dv, near(dv_near, "zh")), smem=0, after=(stacks[1],)
+    )
+    dq_near = lax.optimization_barrier((dq_near, stacks[1]))[0]
     out_keep, out_send = call(
         gather_grads,
         [((3 * TILE, HD), BF16)] * 2,
@@ -453,15 +418,19 @@
         smem=0,
     )
 
-    (stack,) = call(weight_stack, [((2 * HD, BLK), BF16)], (pos, done, over_pair(done)), after=(mixed,))
-    stacks = [stack, near(stack, "x"), far(stack, "x"), opposite(stack, "x")]
     (here,) = call(
         weight_row, [((2 * HD, 1024), BF16)], (pos, *stacks), after=(out_send,)
     )
     grad_q, grad_k, grad_v, grad_weight = call(
         finish,
         [((TILE, 2 * HD), BF16)] * 3 + [((2 * HD, 2048), F32)],
-        (pos, out_keep, over_pair(out_send), here, over_core(here)),
+        (
+            pos,
+            out_keep,
+            over_pair(out_send),
+            here,
+            over_core(here),
+        ),
     )
     return (mixed[None], grad_q[None], grad_k[None], grad_v[None], grad_weight)
 

time: 111 us -> 106 us (0.955)
  Pallas kernels: 18.8 us -> 15.8 us
  local copies, waits for them, and re-layouts: 4.42 us -> 1.91 us
  waiting for transfers between devices: 26.7 us -> 25 us
  other arithmetic: 0 us -> 1.62 us
    ppermute x12, waiting for transfers between devices: 14 us -> 9.97 us  [far(): return lax.ppermute(a, axis, [(0, 3), (3, 0), (1, 2), (2, 1)])]
    ppermute x12, starting transfers between devices: 16.6 us -> 13 us  [near(): return lax.ppermute(a, axis, [(0, 1), (1, 0), (2, 3), (3, 2)])]
    ppermute x3, starting transfers between devices: 3.9 us -> 7.02 us  [opposite(): return lax.ppermute(a, axis, [(0, 2), (2, 0), (1, 3), (3, 1)])]
    pallas_call x24 -> x23, Pallas kernels: 18.8 us -> 15.8 us  [call(): pl.pallas_call(body, out_shape=shapes, in_specs=specs, out_specs=[pl.Bloc...]
    unnamed x14 -> x8, local copies, waits for them, and re-layouts: 4.34 us -> 1.82 us
    ppermute x5, waiting for transfers between devices: 10 us -> 11.9 us  [over_pair(): return lax.ppermute(a, 'par', [(0, 1), (1, 0)])]
    select_n x0 -> x2, other arithmetic: none -> 1.6 us  [on_device(): jnp.where(first, rows[:, HD:], rows[:, :HD])]
  transfers between devices with their start and end apart: 34 -> 34, of which waited for: 14 -> 16; matrix products, arithmetic and copies ran while one was open for 0% -> 2% of each run, Pallas kernels for 13% -> 11%
where the time goes in v3:
time: 106 us
  starting transfers between devices  60.9 us (57%)
  waiting for transfers between devices  25 us (24%)
  Pallas kernels  15.8 us (15%)
  local copies, waits for them, and re-layouts  1.91 us (2%)
  other arithmetic  1.62 us (2%)
    ppermute x12, starting transfers between devices, far(): return lax.ppermute(a, axis, [(0, 3), (3, 0), (1, 2), (2, 1)])  21.5 us
    pallas_call x23, Pallas kernels, call(): pl.pallas_call(body, out_shape=shapes, in_specs=specs, out_specs=[pl.Bloc...  15.8 us
    ppermute x12, starting transfers between devices, near(): return lax.ppermute(a, axis, [(0, 1), (1, 0), (2, 3), (3, 2)])  13 us
    ppermute x2, starting transfers between devices, over_core(): return lax.ppermute(a, 'core', [(0, 1), (1, 0)])  12.5 us
    ppermute x5, waiting for transfers between devices, over_pair(): return lax.ppermute(a, 'par', [(0, 1), (1, 0)])  11.9 us
    ppermute x12, waiting for transfers between devices, far(): return lax.ppermute(a, axis, [(0, 3), (3, 0), (1, 2), (2, 1)])  9.97 us
    ppermute x3, starting transfers between devices, opposite(): return lax.ppermute(a, axis, [(0, 2), (2, 0), (1, 3), (3, 1)])  7.02 us
    ppermute x5, starting transfers between devices, over_pair(): return lax.ppermute(a, 'par', [(0, 1), (1, 0)])  6.91 us
  transfers between devices with their start and end apart: 34, of which 16 were waited for; matrix products, arithmetic and copies ran while one was open for 2% of the time, Pallas kernels for 11%

profile of v3, /device:TPU:1, one launch (start us, length us, event | category | flops | bytes accessed | tf_op | source)
XLA Modules:
  0.0 106.1 jit_solution(14621462843704178268)
XLA Ops:
  0.6 2.6 %collective-permute-start.10 = (bf16[32,2048]{1,0:T(8,128)(2,1)}, bf16[32,2048]{1,0:T(8,128)(2,1)S(1)}, u32[]{:S(2)}, u32[]{:S(2)}) collective-permute-start(bf16[32,2048]{1,0:T(8,128)(2,1)} %bitcast.14), channel_id=1, source_target_pairs={{0,8},{8,0},{1,9},{9,1},{2,10},{10,2},{3,11},{11,3},{4,12},{12,4},... | collective-permute-start | bytes 393224 | tf_op jit(solution)/shard_map/ppermute | solution.py:318
  3.2 0.8 broadcast_select_fusion.2
  4.0 0.8 broadcast_select_fusion
  4.8 0.1 collective-permute-start
  4.9 4.8 %collective-permute-done.recv.refs_2_ = bf16[384,128]{1,0:T(8,128)(2,1)S(1)} collective-permute-done((bf16[384,128]{1,0:T(8,128)(2,1)S(1)}, bf16[384,128]{1,0:T(8,128)(2,1)S(1)}, u32[]{:S(2)}, u32[]{:S(2)}) %collective-permute-start) | collective-permute-done | bytes 98336 | tf_op jit(solution)/shard_map/ppermute | solution.py:318
  9.7 0.9 copy-done.2
  10.6 0.1 collective-permute-start.11
  10.8 3.0 %collective-permute-start.1 = (bf16[256,128]{1,0:T(8,128)(2,1)S(1)}, bf16[256,128]{1,0:T(8,128)(2,1)S(1)}, u32[]{:S(2)}, u32[]{:S(2)}) collective-permute-start(bf16[256,128]{1,0:T(8,128)(2,1)S(1)} %get-tuple-element.51.k0), channel_id=1, source_target_pairs={{0,16},{16,0},{32,48},{48,32},{1,17},{17,1},{33,49},{49,33},{2,18}... | collective-permute-start | bytes 196616 | tf_op jit(solution)/shard_map/ppermute | solution.py:306
  13.8 4.3 %collective-permute-start.2 = (bf16[256,128]{1,0:T(8,128)(2,1)S(1)}, bf16[256,128]{1,0:T(8,128)(2,1)S(1)}, u32[]{:S(2)}, u32[]{:S(2)}) collective-permute-start(bf16[256,128]{1,0:T(8,128)(2,1)S(1)} %get-tuple-element.52.v0), channel_id=1, source_target_pairs={{0,48},{48,0},{16,32},{32,16},{1,49},{49,1},{17,33},{33,17},{2,50}... | collective-permute-start | bytes 196616 | tf_op jit(solution)/shard_map/ppermute | solution.py:310
  18.1 1.2 %collective-permute-start.3 = (bf16[256,128]{1,0:T(8,128)(2,1)S(1)}, bf16[256,128]{1,0:T(8,128)(2,1)S(1)}, u32[]{:S(2)}, u32[]{:S(2)}) collective-permute-start(bf16[256,128]{1,0:T(8,128)(2,1)S(1)} %get-tuple-element.53.q0), channel_id=1, source_target_pairs={{0,64},{64,0},{128,192},{192,128},{1,65},{65,1},{129,193},{193,129... | collective-permute-start | bytes 196616 | tf_op jit(solution)/shard_map/ppermute | solution.py:306
  19.3 1.0 collective-permute-done.2.v1
  20.3 0.9 collective-permute-done.3.q1
  21.3 2.0 %collective-permute-start.12 = (bf16[128,2048]{1,0:T(8,128)(2,1)S(1)}, bf16[128,2048]{1,0:T(8,128)(2,1)S(1)}, u32[]{:S(2)}, u32[]{:S(2)}) collective-permute-start(bf16[128,2048]{1,0:T(8,128)(2,1)S(1)} %shard_map.105.pair), channel_id=1, source_target_pairs={{0,6},{6,0},{2,4},{4,2},{1,7},{7,1},{3,5},{5,3},{8,14},{14,8},{10,... | collective-permute-start | bytes 1572872 | tf_op jit(solution)/shard_map/ppermute | solution.py:310
  23.3 1.5 %collective-permute-start.5 = (bf16[512,128]{1,0:T(8,128)(2,1)S(1)}, bf16[512,128]{1,0:T(8,128)(2,1)S(1)}, u32[]{:S(2)}, u32[]{:S(2)}) collective-permute-start(bf16[512,128]{1,0:T(8,128)(2,1)S(1)} %get-tuple-element.55.vp.refs_4_), channel_id=1, source_target_pairs={{0,16},{16,0},{32,48},{48,32},{1,17},{17,1},{33,49},{49,33},{2,18}... | collective-permute-start | bytes 393224 | tf_op jit(solution)/shard_map/ppermute | solution.py:306
  24.8 2.5 %collective-permute-start.6 = (bf16[512,128]{1,0:T(8,128)(2,1)S(1)}, bf16[512,128]{1,0:T(8,128)(2,1)S(1)}, u32[]{:S(2)}, u32[]{:S(2)}) collective-permute-start(bf16[512,128]{1,0:T(8,128)(2,1)S(1)} %get-tuple-element.56.qp.refs_6_), channel_id=1, source_target_pairs={{0,192},{192,0},{64,128},{128,64},{1,193},{193,1},{65,129},{129,65... | collective-permute-start | bytes 393224 | tf_op jit(solution)/shard_map/ppermute | solution.py:310
  27.3 2.2 %collective-permute-start.4 = (bf16[512,128]{1,0:T(8,128)(2,1)S(1)}, bf16[512,128]{1,0:T(8,128)(2,1)S(1)}, u32[]{:S(2)}, u32[]{:S(2)}) collective-permute-start(bf16[512,128]{1,0:T(8,128)(2,1)S(1)} %get-tuple-element.54.kp.refs_2_), channel_id=1, source_target_pairs={{0,48},{48,0},{16,32},{32,16},{1,49},{49,1},{17,33},{33,17},{2,50}... | collective-permute-start | bytes 393224 | tf_op jit(solution)/shard_map/ppermute | solution.py:310
  29.5 0.1 stack.23.pos.refs_0_
  29.6 0.2 collective-permute-done.5.vn.refs_5_
  29.7 0.4 collective-permute-done.6.qf.refs_7_
  30.1 4.5 %collective-permute-done.4.kf.refs_3_ = bf16[512,128]{1,0:T(8,128)(2,1)S(1)} collective-permute-done((bf16[512,128]{1,0:T(8,128)(2,1)S(1)}, bf16[512,128]{1,0:T(8,128)(2,1)S(1)}, u32[]{:S(2)}, u32[]{:S(2)}) %collective-permute-start.4) | collective-permute-done | bytes 131104 | tf_op jit(solution)/shard_map/ppermute | solution.py:310
  34.6 3.0 %shard_map.103 = (bf16[144,256]{1,0:T(8,128)(2,1)S(1)}, bf16[144,256]{1,0:T(8,128)(2,1)S(1)}, bf16[144,256]{1,0:T(8,128)(2,1)S(1)}, bf16[144,256]{1,0:T(8,128)(2,1)S(1)}) custom-call(s32[5]{0:T(128)S(1)} %stack.23.pos.refs_0_, s32[32,32]{1,0:T(8,128)S(1)} %copy-done.3, bf16[512,128]{1,0:T(8,128)(2,1)S(1)} %get-tuple-element.54.kp.refs_2_, ...), custom_call_target="tpu_custom_call" | custom-call | flops 536870912 | bytes 1085460 | tf_op jit(solution)/shard_map/pallas_call | solution.py:48
  37.6 0.3 collective-permute-start.7
  37.9 3.0 %collective-permute-start.9 = (bf16[144,256]{1,0:T(8,128)(2,1)S(1)}, bf16[144,256]{1,0:T(8,128)(2,1)S(1)}, u32[]{:S(2)}, u32[]{:S(2)}) collective-permute-start(bf16[144,256]{1,0:T(8,128)(2,1)S(1)} %get-tuple-element.60), channel_id=1, source_target_pairs={{0,128},{128,0},{64,192},{192,64},{1,129},{129,1},{65,193},{193,65... | collective-permute-start | bytes 221192 | tf_op jit(solution)/shard_map/ppermute | solution.py:314
  41.0 0.6 shard_map.106
  41.6 1.0 shard_map.107.grads
  42.6 0.5 collective-permute-done.8.p2
  43.1 1.1 shard_map.108
  44.2 5.5 %collective-permute-start.15 = (f32[128,1024]{1,0:T(8,128)S(1)}, f32[128,1024]{1,0:T(8,128)S(1)}, u32[]{:S(2)}, u32[]{:S(2)}) collective-permute-start(f32[128,1024]{1,0:T(8,128)S(1)} %get-tuple-element.67), channel_id=1, source_target_pairs={{0,1},{1,0},{2,3},{3,2},{4,5},{5,4},{6,7},{7,6},{8,9},{9,8},{10,11... | collective-permute-start | bytes 1572872 | tf_op jit(solution)/shard_map/ppermute | solution.py:322
  49.7 1.5 %collective-permute-done.15.other = f32[128,1024]{1,0:T(8,128)S(1)} collective-permute-done((f32[128,1024]{1,0:T(8,128)S(1)}, f32[128,1024]{1,0:T(8,128)S(1)}, u32[]{:S(2)}, u32[]{:S(2)}) %collective-permute-start.15) | collective-permute-done | bytes 524320 | tf_op jit(solution)/shard_map/ppermute | solution.py:322
  51.3 0.6 shard_map.110
  51.9 0.5 collective-permute-start.16
  52.4 2.4 %collective-permute-start.17 = (bf16[272,256]{1,0:T(8,128)(2,1)S(1)}, bf16[272,256]{1,0:T(8,128)(2,1)S(1)}, u32[]{:S(2)}, u32[]{:S(2)}) collective-permute-start(bf16[272,256]{1,0:T(8,128)(2,1)S(1)} %get-tuple-element.71), channel_id=1, source_target_pairs={{0,192},{192,0},{64,128},{128,64},{1,193},{193,1},{65,129},{129,65... | collective-permute-start | bytes 417800 | tf_op jit(solution)/shard_map/ppermute | solution.py:310
  54.7 0.5 collective-permute-start.18
  55.2 2.0 %collective-permute-start.13 = (bf16[128,128]{1,0:T(8,128)(2,1)S(1)}, bf16[128,128]{1,0:T(8,128)(2,1)S(1)}, u32[]{:S(2)}, u32[]{:S(2)}) collective-permute-start(bf16[128,128]{1,0:T(8,128)(2,1)S(1)} %slice.33), channel_id=1, source_target_pairs={{0,8},{8,0},{1,9},{9,1},{2,10},{10,2},{3,11},{11,3},{4,12},{12,4},... | collective-permute-start | bytes 98312 | tf_op jit(solution)/shard_map/ppermute | solution.py:318
  57.3 1.6 %collective-permute-done.13.other = bf16[128,128]{1,0:T(8,128)(2,1)S(1)} collective-permute-done((bf16[128,128]{1,0:T(8,128)(2,1)S(1)}, bf16[128,128]{1,0:T(8,128)(2,1)S(1)}, u32[]{:S(2)}, u32[]{:S(2)}) %collective-permute-start.13) | collective-permute-done | bytes 32800 | tf_op jit(solution)/shard_map/ppermute | solution.py:318
  58.9 1.1 shard_map.109
  59.9 0.9 collective-permute-start.14
  60.8 0.2 collective-permute-done.18.refs_3_.refs_11_
  61.1 2.6 %collective-permute-start.19 = (bf16[128,256]{1,0:T(8,128)(2,1)S(1)}, bf16[128,256]{1,0:T(8,128)(2,1)S(1)}, u32[]{:S(2)}, u32[]{:S(2)}) collective-permute-start(bf16[128,256]{1,0:T(8,128)(2,1)S(1)} %shard_map.111.refs_12_.refs_0_), channel_id=1, source_target_pairs={{0,16},{16,0},{32,48},{48,32},{1,17},{17,1},{33,49},{49,33},{2,18}... | collective-permute-start | bytes 196616 | tf_op jit(solution)/shard_map/ppermute | solution.py:306
  63.6 4.0 %shard_map.112 = (bf16[512,128]{1,0:T(8,128)(2,1)S(1)}, bf16[512,128]{1,0:T(8,128)(2,1)S(1)}, bf16[512,128]{1,0:T(8,128)(2,1)S(1)}, bf16[512,128]{1,0:T(8,128)(2...) custom-call(s32[5]{0:T(128)S(1)} %stack.23.pos.refs_0_, s32[32,32]{1,0:T(8,128)S(1)} %copy-done.3, ...), custom_call_target="tpu_custom_call" | custom-call | flops 1342177280 | bytes 2134036 | tf_op jit(solution)/shard_map/pallas_call | solution.py:48
  67.7 1.3 %collective-permute-start.20 = (bf16[128,256]{1,0:T(8,128)(2,1)S(1)}, bf16[128,256]{1,0:T(8,128)(2,1)S(1)}, u32[]{:S(2)}, u32[]{:S(2)}) collective-permute-start(bf16[128,256]{1,0:T(8,128)(2,1)S(1)} %shard_map.113.a), channel_id=1, source_target_pairs={{0,48},{48,0},{16,32},{32,16},{1,49},{49,1},{17,33},{33,17},{2,50}... | collective-permute-start | bytes 196616 | tf_op jit(solution)/shard_map/ppermute | solution.py:310
  69.0 2.7 %collective-permute-start.24 = (bf16[256,256]{1,0:T(8,128)(2,1)S(1)}, bf16[256,256]{1,0:T(8,128)(2,1)S(1)}, u32[]{:S(2)}, u32[]{:S(2)}) collective-permute-start(bf16[256,256]{1,0:T(8,128)(2,1)S(1)} %get-tuple-element.81), channel_id=1, source_target_pairs={{0,192},{192,0},{64,128},{128,64},{1,193},{193,1},{65,129},{129,65... | collective-permute-start | bytes 393224 | tf_op jit(solution)/shard_map/ppermute | solution.py:310
  71.7 1.3 %collective-permute-done.20.b = bf16[128,256]{1,0:T(8,128)(2,1)S(1)} collective-permute-done((bf16[128,256]{1,0:T(8,128)(2,1)S(1)}, bf16[128,256]{1,0:T(8,128)(2,1)S(1)}, u32[]{:S(2)}, u32[]{:S(2)}) %collective-permute-start.20) | collective-permute-done | bytes 65568 | tf_op jit(solution)/shard_map/ppermute | solution.py:310
  73.0 0.2 collective-permute-start.22
  73.3 0.5 collective-permute-start.21
  73.8 0.2 collective-permute-done.24.b
  74.1 2.4 %collective-permute-done.22.refs_2_ = bf16[128,256]{1,0:T(8,128)(2,1)S(1)} collective-permute-done((bf16[128,256]{1,0:T(8,128)(2,1)S(1)}, bf16[128,256]{1,0:T(8,128)(2,1)S(1)}, u32[]{:S(2)}, u32[]{:S(2)}) %collective-permute-start.22) | collective-permute-done | bytes 65568 | tf_op jit(solution)/shard_map/ppermute | solution.py:318
  76.5 0.6 shard_map.118.refs_1_
  77.1 0.5 collective-permute-start.25
  77.5 0.8 collective-permute-start.27
  78.3 2.3 %collective-permute-start.23 = (bf16[512,128]{1,0:T(8,128)(2,1)S(1)}, bf16[512,128]{1,0:T(8,128)(2,1)S(1)}, u32[]{:S(2)}, u32[]{:S(2)}) collective-permute-start(bf16[512,128]{1,0:T(8,128)(2,1)S(1)} %get-tuple-element.79), channel_id=1, source_target_pairs={{0,48},{48,0},{16,32},{32,16},{1,49},{49,1},{17,33},{33,17},{2,50}... | collective-permute-start | bytes 393224 | tf_op jit(solution)/shard_map/ppermute | solution.py:310
  80.7 3.5 %collective-permute-start.32 = (bf16[256,256]{1,0:T(8,128)(2,1)S(1)}, bf16[256,256]{1,0:T(8,128)(2,1)S(1)}, u32[]{:S(2)}, u32[]{:S(2)}) collective-permute-start(bf16[256,256]{1,0:T(8,128)(2,1)S(1)} %shard_map.118.refs_1_), channel_id=1, source_target_pairs={{0,128},{128,0},{64,192},{192,64},{1,129},{129,1},{65,193},{193,65... | collective-permute-start | bytes 393224 | tf_op jit(solution)/shard_map/ppermute | solution.py:314
  84.2 0.7 shard_map.116.refs_3_
  84.9 0.9 collective-permute-start.28
  85.8 0.9 copy-done.1
  86.8 2.1 %collective-permute-start.26 = (bf16[256,128]{1,0:T(8,128)(2,1)S(1)}, bf16[256,128]{1,0:T(8,128)(2,1)S(1)}, u32[]{:S(2)}, u32[]{:S(2)}) collective-permute-start(bf16[256,128]{1,0:T(8,128)(2,1)S(1)} %get-tuple-element.84), channel_id=1, source_target_pairs={{0,16},{16,0},{32,48},{48,32},{1,17},{17,1},{33,49},{49,33},{2,18}... | collective-permute-start | bytes 196616 | tf_op jit(solution)/shard_map/ppermute | solution.py:306
  88.9 2.0 %collective-permute-done.28.v_far = bf16[256,128]{1,0:T(8,128)(2,1)S(1)} collective-permute-done((bf16[256,128]{1,0:T(8,128)(2,1)S(1)}, bf16[256,128]{1,0:T(8,128)(2,1)S(1)}, u32[]{:S(2)}, u32[]{:S(2)}) %collective-permute-start.28) | collective-permute-done | bytes 65568 | tf_op jit(solution)/shard_map/ppermute | solution.py:310
  90.9 0.3 collective-permute-done.26.k_near
  91.2 0.1 shard_map.121
  91.3 0.6 shard_map.122.here
  91.9 7.0 %collective-permute-start.33 = (bf16[256,1024]{1,0:T(8,128)(2,1)S(1)}, bf16[256,1024]{1,0:T(8,128)(2,1)S(1)}, u32[]{:S(2)}, u32[]{:S(2)}) collective-permute-start(bf16[256,1024]{1,0:T(8,128)(2,1)S(1)} %shard_map.122.here), channel_id=1, source_target_pairs={{0,1},{1,0},{2,3},{3,2},{4,5},{5,4},{6,7},{7,6},{8,9},{9,8},{10,11... | collective-permute-start | bytes 1572872 | tf_op jit(solution)/shard_map/ppermute | solution.py:322
  98.9 2.0 %collective-permute-start.30 = (bf16[384,128]{1,0:T(8,128)(2,1)S(1)}, bf16[384,128]{1,0:T(8,128)(2,1)S(1)}, u32[]{:S(2)}, u32[]{:S(2)}) collective-permute-start(bf16[384,128]{1,0:T(8,128)(2,1)S(1)} %get-tuple-element.92.refs_5_), channel_id=1, source_target_pairs={{0,8},{8,0},{1,9},{9,1},{2,10},{10,2},{3,11},{11,3},{4,12},{12,4},... | collective-permute-start | bytes 294920 | tf_op jit(solution)/shard_map/ppermute | solution.py:318
  100.9 3.0 %collective-permute-done.30.other = bf16[384,128]{1,0:T(8,128)(2,1)S(1)} collective-permute-done((bf16[384,128]{1,0:T(8,128)(2,1)S(1)}, bf16[384,128]{1,0:T(8,128)(2,1)S(1)}, u32[]{:S(2)}, u32[]{:S(2)}) %collective-permute-start.30) | collective-permute-done | bytes 98336 | tf_op jit(solution)/shard_map/ppermute | solution.py:318
  104.0 2.1 %shard_map.123 = (bf16[128,256]{1,0:T(8,128)(2,1)}, bf16[128,256]{1,0:T(8,128)(2,1)}, bf16[128,256]{1,0:T(8,128)(2,1)}, f32[256,2048]{1,0:T(8,128)}) custom-call(s32[5]{0:T(128)S(1)} %stack.23.pos.refs_0_, bf16[384,128]{1,0:T(8,128)(2,1)S(1)} %get-tuple-element.91.mine, bf16[384,128]{1,0:T(8,128)(2,1)S(1)} %collective-permute-done.30.other, ...), custom_call_target="tpu_custom_call" | custom-call | bytes 3538964 | tf_op jit(solution)/shard_map/pallas_call | solution.py:48
  (41 shorter events, 0.5 us)
Async XLA Ops:
  0.6 34.0 %copy-start.3 = (s32[32,32]{1,0:T(8,128)S(1)}, s32[32,32]{1,0:T(8,128)}, u32[]{:S(2)}) copy-start(s32[32,32]{1,0:T(8,128)} %refs_1_.1) | copy-start | bytes 12292
  0.6 9.1 %collective-permute-start.10 = (bf16[32,2048]{1,0:T(8,128)(2,1)}, bf16[32,2048]{1,0:T(8,128)(2,1)S(1)}, u32[]{:S(2)}, u32[]{:S(2)}) collective-permute-start(bf16[32,2048]{1,0:T(8,128)(2,1)} %bitcast.14), channel_id=1, source_target_pairs={{0,8},{8,0},{1,9},{9,1},{2,10},{10,2},{3,11},{11,3},{4,12},{12,4},... | collective-permute-start | bytes 393224 | tf_op jit(solution)/shard_map/ppermute | solution.py:318
  4.8 4.9 %collective-permute-start = (bf16[384,128]{1,0:T(8,128)(2,1)S(1)}, bf16[384,128]{1,0:T(8,128)(2,1)S(1)}, u32[]{:S(2)}, u32[]{:S(2)}) collective-permute-start(bf16[384,128]{1,0:T(8,128)(2,1)S(1)} %pad_maximum_fusion.1), channel_id=1, source_target_pairs={{0,8},{8,0},{1,9},{9,1},{2,10},{10,2},{3,11},{11,3},{4,12},{12,4},... | collective-permute-start | bytes 294920 | tf_op jit(solution)/shard_map/ppermute | solution.py:318
  9.7 0.9 copy-start.2
  10.6 10.6 %collective-permute-start.11 = (bf16[64,2048]{1,0:T(8,128)(2,1)S(1)}, bf16[64,2048]{1,0:T(8,128)(2,1)S(1)}, u32[]{:S(2)}, u32[]{:S(2)}) collective-permute-start(bf16[64,2048]{1,0:T(8,128)(2,1)S(1)} %shard_map.104.refs_0_), channel_id=1, source_target_pairs={{0,2},{2,0},{4,6},{6,4},{1,3},{3,1},{5,7},{7,5},{8,10},{10,8},{12,... | collective-permute-start | bytes 786440 | tf_op jit(solution)/shard_map/ppermute | solution.py:306
  10.8 8.5 %collective-permute-start.1 = (bf16[256,128]{1,0:T(8,128)(2,1)S(1)}, bf16[256,128]{1,0:T(8,128)(2,1)S(1)}, u32[]{:S(2)}, u32[]{:S(2)}) collective-permute-start(bf16[256,128]{1,0:T(8,128)(2,1)S(1)} %get-tuple-element.51.k0), channel_id=1, source_target_pairs={{0,16},{16,0},{32,48},{48,32},{1,17},{17,1},{33,49},{49,33},{2,18}... | collective-permute-start | bytes 196616 | tf_op jit(solution)/shard_map/ppermute | solution.py:306
  13.8 6.5 %collective-permute-start.2 = (bf16[256,128]{1,0:T(8,128)(2,1)S(1)}, bf16[256,128]{1,0:T(8,128)(2,1)S(1)}, u32[]{:S(2)}, u32[]{:S(2)}) collective-permute-start(bf16[256,128]{1,0:T(8,128)(2,1)S(1)} %get-tuple-element.52.v0), channel_id=1, source_target_pairs={{0,48},{48,0},{16,32},{32,16},{1,49},{49,1},{17,33},{33,17},{2,50}... | collective-permute-start | bytes 196616 | tf_op jit(solution)/shard_map/ppermute | solution.py:310
  18.1 3.1 %collective-permute-start.3 = (bf16[256,128]{1,0:T(8,128)(2,1)S(1)}, bf16[256,128]{1,0:T(8,128)(2,1)S(1)}, u32[]{:S(2)}, u32[]{:S(2)}) collective-permute-start(bf16[256,128]{1,0:T(8,128)(2,1)S(1)} %get-tuple-element.53.q0), channel_id=1, source_target_pairs={{0,64},{64,0},{128,192},{192,128},{1,65},{65,1},{129,193},{193,129... | collective-permute-start | bytes 196616 | tf_op jit(solution)/shard_map/ppermute | solution.py:306
  21.3 20.3 %copy-start = (bf16[256,2048]{1,0:T(8,128)(2,1)S(1)}, bf16[256,2048]{1,0:T(8,128)(2,1)}, u32[]{:S(2)}) copy-start(bf16[256,2048]{1,0:T(8,128)(2,1)} %w.3) | copy-start | bytes 3145732
  21.3 19.7 %collective-permute-start.12 = (bf16[128,2048]{1,0:T(8,128)(2,1)S(1)}, bf16[128,2048]{1,0:T(8,128)(2,1)S(1)}, u32[]{:S(2)}, u32[]{:S(2)}) collective-permute-start(bf16[128,2048]{1,0:T(8,128)(2,1)S(1)} %shard_map.105.pair), channel_id=1, source_target_pairs={{0,6},{6,0},{2,4},{4,2},{1,7},{7,1},{3,5},{5,3},{8,14},{14,8},{10,... | collective-permute-start | bytes 1572872 | tf_op jit(solution)/shard_map/ppermute | solution.py:310
  23.3 6.4 %collective-permute-start.5 = (bf16[512,128]{1,0:T(8,128)(2,1)S(1)}, bf16[512,128]{1,0:T(8,128)(2,1)S(1)}, u32[]{:S(2)}, u32[]{:S(2)}) collective-permute-start(bf16[512,128]{1,0:T(8,128)(2,1)S(1)} %get-tuple-element.55.vp.refs_4_), channel_id=1, source_target_pairs={{0,16},{16,0},{32,48},{48,32},{1,17},{17,1},{33,49},{49,33},{2,18}... | collective-permute-start | bytes 393224 | tf_op jit(solution)/shard_map/ppermute | solution.py:306
  24.8 5.3 %collective-permute-start.6 = (bf16[512,128]{1,0:T(8,128)(2,1)S(1)}, bf16[512,128]{1,0:T(8,128)(2,1)S(1)}, u32[]{:S(2)}, u32[]{:S(2)}) collective-permute-start(bf16[512,128]{1,0:T(8,128)(2,1)S(1)} %get-tuple-element.56.qp.refs_6_), channel_id=1, source_target_pairs={{0,192},{192,0},{64,128},{128,64},{1,193},{193,1},{65,129},{129,65... | collective-permute-start | bytes 393224 | tf_op jit(solution)/shard_map/ppermute | solution.py:310
  27.3 7.3 %collective-permute-start.4 = (bf16[512,128]{1,0:T(8,128)(2,1)S(1)}, bf16[512,128]{1,0:T(8,128)(2,1)S(1)}, u32[]{:S(2)}, u32[]{:S(2)}) collective-permute-start(bf16[512,128]{1,0:T(8,128)(2,1)S(1)} %get-tuple-element.54.kp.refs_2_), channel_id=1, source_target_pairs={{0,48},{48,0},{16,32},{32,16},{1,49},{49,1},{17,33},{33,17},{2,50}... | collective-permute-start | bytes 393224 | tf_op jit(solution)/shard_map/ppermute | solution.py:310
  37.6 5.0 %collective-permute-start.7 = (bf16[144,256]{1,0:T(8,128)(2,1)S(1)}, bf16[144,256]{1,0:T(8,128)(2,1)S(1)}, u32[]{:S(2)}, u32[]{:S(2)}) collective-permute-start(bf16[144,256]{1,0:T(8,128)(2,1)S(1)} %get-tuple-element.58), channel_id=1, source_target_pairs={{0,64},{64,0},{128,192},{192,128},{1,65},{65,1},{129,193},{193,129... | collective-permute-start | bytes 221192 | tf_op jit(solution)/shard_map/ppermute | solution.py:306
  37.9 5.2 %collective-permute-start.8 = (bf16[144,256]{1,0:T(8,128)(2,1)S(1)}, bf16[144,256]{1,0:T(8,128)(2,1)S(1)}, u32[]{:S(2)}, u32[]{:S(2)}) collective-permute-start(bf16[144,256]{1,0:T(8,128)(2,1)S(1)} %get-tuple-element.59), channel_id=1, source_target_pairs={{0,192},{192,0},{64,128},{128,64},{1,193},{193,1},{65,129},{129,65... | collective-permute-start | bytes 221192 | tf_op jit(solution)/shard_map/ppermute | solution.py:310
  37.9 5.2 %collective-permute-start.9 = (bf16[144,256]{1,0:T(8,128)(2,1)S(1)}, bf16[144,256]{1,0:T(8,128)(2,1)S(1)}, u32[]{:S(2)}, u32[]{:S(2)}) collective-permute-start(bf16[144,256]{1,0:T(8,128)(2,1)S(1)} %get-tuple-element.60), channel_id=1, source_target_pairs={{0,128},{128,0},{64,192},{192,64},{1,129},{129,1},{65,193},{193,65... | collective-permute-start | bytes 221192 | tf_op jit(solution)/shard_map/ppermute | solution.py:314
  44.2 7.0 %collective-permute-start.15 = (f32[128,1024]{1,0:T(8,128)S(1)}, f32[128,1024]{1,0:T(8,128)S(1)}, u32[]{:S(2)}, u32[]{:S(2)}) collective-permute-start(f32[128,1024]{1,0:T(8,128)S(1)} %get-tuple-element.67), channel_id=1, source_target_pairs={{0,1},{1,0},{2,3},{3,2},{4,5},{5,4},{6,7},{7,6},{8,9},{9,8},{10,11... | collective-permute-start | bytes 1572872 | tf_op jit(solution)/shard_map/ppermute | solution.py:322
  51.9 8.9 %collective-permute-start.16 = (bf16[272,256]{1,0:T(8,128)(2,1)S(1)}, bf16[272,256]{1,0:T(8,128)(2,1)S(1)}, u32[]{:S(2)}, u32[]{:S(2)}) collective-permute-start(bf16[272,256]{1,0:T(8,128)(2,1)S(1)} %get-tuple-element.70), channel_id=1, source_target_pairs={{0,64},{64,0},{128,192},{192,128},{1,65},{65,1},{129,193},{193,129... | collective-permute-start | bytes 417800 | tf_op jit(solution)/shard_map/ppermute | solution.py:306
  52.4 8.4 %collective-permute-start.17 = (bf16[272,256]{1,0:T(8,128)(2,1)S(1)}, bf16[272,256]{1,0:T(8,128)(2,1)S(1)}, u32[]{:S(2)}, u32[]{:S(2)}) collective-permute-start(bf16[272,256]{1,0:T(8,128)(2,1)S(1)} %get-tuple-element.71), channel_id=1, source_target_pairs={{0,192},{192,0},{64,128},{128,64},{1,193},{193,1},{65,129},{129,65... | collective-permute-start | bytes 417800 | tf_op jit(solution)/shard_map/ppermute | solution.py:310
  54.7 6.3 %collective-permute-start.18 = (bf16[272,256]{1,0:T(8,128)(2,1)S(1)}, bf16[272,256]{1,0:T(8,128)(2,1)S(1)}, u32[]{:S(2)}, u32[]{:S(2)}) collective-permute-start(bf16[272,256]{1,0:T(8,128)(2,1)S(1)} %get-tuple-element.72), channel_id=1, source_target_pairs={{0,128},{128,0},{64,192},{192,64},{1,129},{129,1},{65,193},{193,65... | collective-permute-start | bytes 417800 | tf_op jit(solution)/shard_map/ppermute | solution.py:314
  55.2 3.6 %collective-permute-start.13 = (bf16[128,128]{1,0:T(8,128)(2,1)S(1)}, bf16[128,128]{1,0:T(8,128)(2,1)S(1)}, u32[]{:S(2)}, u32[]{:S(2)}) collective-permute-start(bf16[128,128]{1,0:T(8,128)(2,1)S(1)} %slice.33), channel_id=1, source_target_pairs={{0,8},{8,0},{1,9},{9,1},{2,10},{10,2},{3,11},{11,3},{4,12},{12,4},... | collective-permute-start | bytes 98312 | tf_op jit(solution)/shard_map/ppermute | solution.py:318
  59.9 13.3 %collective-permute-start.14 = (bf16[64,2048]{1,0:T(8,128)(2,1)S(1)}, bf16[64,2048]{1,0:T(8,128)(2,1)S(1)}, u32[]{:S(2)}, u32[]{:S(2)}) collective-permute-start(bf16[64,2048]{1,0:T(8,128)(2,1)S(1)} %get-tuple-element.65.refs_4_), channel_id=1, source_target_pairs={{0,6},{6,0},{2,4},{4,2},{1,7},{7,1},{3,5},{5,3},{8,14},{14,8},{10,... | collective-permute-start | bytes 786440 | tf_op jit(solution)/shard_map/ppermute | solution.py:310
  61.1 6.6 %collective-permute-start.19 = (bf16[128,256]{1,0:T(8,128)(2,1)S(1)}, bf16[128,256]{1,0:T(8,128)(2,1)S(1)}, u32[]{:S(2)}, u32[]{:S(2)}) collective-permute-start(bf16[128,256]{1,0:T(8,128)(2,1)S(1)} %shard_map.111.refs_12_.refs_0_), channel_id=1, source_target_pairs={{0,16},{16,0},{32,48},{48,32},{1,17},{17,1},{33,49},{49,33},{2,18}... | collective-permute-start | bytes 196616 | tf_op jit(solution)/shard_map/ppermute | solution.py:306
  67.7 5.3 %collective-permute-start.20 = (bf16[128,256]{1,0:T(8,128)(2,1)S(1)}, bf16[128,256]{1,0:T(8,128)(2,1)S(1)}, u32[]{:S(2)}, u32[]{:S(2)}) collective-permute-start(bf16[128,256]{1,0:T(8,128)(2,1)S(1)} %shard_map.113.a), channel_id=1, source_target_pairs={{0,48},{48,0},{16,32},{32,16},{1,49},{49,1},{17,33},{33,17},{2,50}... | collective-permute-start | bytes 196616 | tf_op jit(solution)/shard_map/ppermute | solution.py:310
  69.0 5.0 %collective-permute-start.24 = (bf16[256,256]{1,0:T(8,128)(2,1)S(1)}, bf16[256,256]{1,0:T(8,128)(2,1)S(1)}, u32[]{:S(2)}, u32[]{:S(2)}) collective-permute-start(bf16[256,256]{1,0:T(8,128)(2,1)S(1)} %get-tuple-element.81), channel_id=1, source_target_pairs={{0,192},{192,0},{64,128},{128,64},{1,193},{193,1},{65,129},{129,65... | collective-permute-start | bytes 393224 | tf_op jit(solution)/shard_map/ppermute | solution.py:310
  73.0 3.5 %collective-permute-start.22 = (bf16[128,256]{1,0:T(8,128)(2,1)S(1)}, bf16[128,256]{1,0:T(8,128)(2,1)S(1)}, u32[]{:S(2)}, u32[]{:S(2)}) collective-permute-start(bf16[128,256]{1,0:T(8,128)(2,1)S(1)} %shard_map.114.refs_2_.refs_1_), channel_id=1, source_target_pairs={{0,8},{8,0},{1,9},{9,1},{2,10},{10,2},{3,11},{11,3},{4,12},{12,4},... | collective-permute-start | bytes 196616 | tf_op jit(solution)/shard_map/ppermute | solution.py:318
  73.3 10.9 %collective-permute-start.21 = (bf16[32,2048]{1,0:T(8,128)(2,1)S(1)}, bf16[32,2048]{1,0:T(8,128)(2,1)S(1)}, u32[]{:S(2)}, u32[]{:S(2)}) collective-permute-start(bf16[32,2048]{1,0:T(8,128)(2,1)S(1)} %get-tuple-element.75), channel_id=1, source_target_pairs={{0,2},{2,0},{4,6},{6,4},{1,3},{3,1},{5,7},{7,5},{8,10},{10,8},{12,... | collective-permute-start | bytes 393224 | tf_op jit(solution)/shard_map/ppermute | solution.py:306
  77.1 7.8 %collective-permute-start.25 = (bf16[256,256]{1,0:T(8,128)(2,1)S(1)}, bf16[256,256]{1,0:T(8,128)(2,1)S(1)}, u32[]{:S(2)}, u32[]{:S(2)}) collective-permute-start(bf16[256,256]{1,0:T(8,128)(2,1)S(1)} %shard_map.118.refs_1_), channel_id=1, source_target_pairs={{0,64},{64,0},{128,192},{192,128},{1,65},{65,1},{129,193},{193,129... | collective-permute-start | bytes 393224 | tf_op jit(solution)/shard_map/ppermute | solution.py:306
  77.5 7.3 %collective-permute-start.27 = (bf16[512,128]{1,0:T(8,128)(2,1)S(1)}, bf16[512,128]{1,0:T(8,128)(2,1)S(1)}, u32[]{:S(2)}, u32[]{:S(2)}) collective-permute-start(bf16[512,128]{1,0:T(8,128)(2,1)S(1)} %get-tuple-element.86), channel_id=1, source_target_pairs={{0,16},{16,0},{32,48},{48,32},{1,17},{17,1},{33,49},{49,33},{2,18}... | collective-permute-start | bytes 393224 | tf_op jit(solution)/shard_map/ppermute | solution.py:306
  78.3 7.5 %collective-permute-start.23 = (bf16[512,128]{1,0:T(8,128)(2,1)S(1)}, bf16[512,128]{1,0:T(8,128)(2,1)S(1)}, u32[]{:S(2)}, u32[]{:S(2)}) collective-permute-start(bf16[512,128]{1,0:T(8,128)(2,1)S(1)} %get-tuple-element.79), channel_id=1, source_target_pairs={{0,48},{48,0},{16,32},{32,16},{1,49},{49,1},{17,33},{33,17},{2,50}... | collective-permute-start | bytes 393224 | tf_op jit(solution)/shard_map/ppermute | solution.py:310
  80.7 10.6 %collective-permute-start.32 = (bf16[256,256]{1,0:T(8,128)(2,1)S(1)}, bf16[256,256]{1,0:T(8,128)(2,1)S(1)}, u32[]{:S(2)}, u32[]{:S(2)}) collective-permute-start(bf16[256,256]{1,0:T(8,128)(2,1)S(1)} %shard_map.118.refs_1_), channel_id=1, source_target_pairs={{0,128},{128,0},{64,192},{192,64},{1,129},{129,1},{65,193},{193,65... | collective-permute-start | bytes 393224 | tf_op jit(solution)/shard_map/ppermute | solution.py:314
  84.2 7.1 %collective-permute-start.31 = (bf16[256,256]{1,0:T(8,128)(2,1)S(1)}, bf16[256,256]{1,0:T(8,128)(2,1)S(1)}, u32[]{:S(2)}, u32[]{:S(2)}) collective-permute-start(bf16[256,256]{1,0:T(8,128)(2,1)S(1)} %shard_map.118.refs_1_), channel_id=1, source_target_pairs={{0,192},{192,0},{64,128},{128,64},{1,193},{193,1},{65,129},{129,65... | collective-permute-start | bytes 393224 | tf_op jit(solution)/shard_map/ppermute | solution.py:310
  84.9 4.0 %collective-permute-start.29 = (bf16[128,256]{1,0:T(8,128)(2,1)S(1)}, bf16[128,256]{1,0:T(8,128)(2,1)S(1)}, u32[]{:S(2)}, u32[]{:S(2)}) collective-permute-start(bf16[128,256]{1,0:T(8,128)(2,1)S(1)} %get-tuple-element.90.refs_3_), channel_id=1, source_target_pairs={{0,64},{64,0},{128,192},{192,128},{1,65},{65,1},{129,193},{193,129... | collective-permute-start | bytes 196616 | tf_op jit(solution)/shard_map/ppermute | solution.py:306
  84.9 6.0 %collective-permute-start.28 = (bf16[256,128]{1,0:T(8,128)(2,1)S(1)}, bf16[256,128]{1,0:T(8,128)(2,1)S(1)}, u32[]{:S(2)}, u32[]{:S(2)}) collective-permute-start(bf16[256,128]{1,0:T(8,128)(2,1)S(1)} %get-tuple-element.88), channel_id=1, source_target_pairs={{0,48},{48,0},{16,32},{32,16},{1,49},{49,1},{17,33},{33,17},{2,50}... | collective-permute-start | bytes 196616 | tf_op jit(solution)/shard_map/ppermute | solution.py:310
  85.8 0.9 copy-start.1
  86.8 4.4 %collective-permute-start.26 = (bf16[256,128]{1,0:T(8,128)(2,1)S(1)}, bf16[256,128]{1,0:T(8,128)(2,1)S(1)}, u32[]{:S(2)}, u32[]{:S(2)}) collective-permute-start(bf16[256,128]{1,0:T(8,128)(2,1)S(1)} %get-tuple-element.84), channel_id=1, source_target_pairs={{0,16},{16,0},{32,48},{48,32},{1,17},{17,1},{33,49},{49,33},{2,18}... | collective-permute-start | bytes 196616 | tf_op jit(solution)/shard_map/ppermute | solution.py:306
  91.9 12.1 %collective-permute-start.33 = (bf16[256,1024]{1,0:T(8,128)(2,1)S(1)}, bf16[256,1024]{1,0:T(8,128)(2,1)S(1)}, u32[]{:S(2)}, u32[]{:S(2)}) collective-permute-start(bf16[256,1024]{1,0:T(8,128)(2,1)S(1)} %shard_map.122.here), channel_id=1, source_target_pairs={{0,1},{1,0},{2,3},{3,2},{4,5},{5,4},{6,7},{7,6},{8,9},{9,8},{10,11... | collective-permute-start | bytes 1572872 | tf_op jit(solution)/shard_map/ppermute | solution.py:322
  98.9 5.1 %collective-permute-start.30 = (bf16[384,128]{1,0:T(8,128)(2,1)S(1)}, bf16[384,128]{1,0:T(8,128)(2,1)S(1)}, u32[]{:S(2)}, u32[]{:S(2)}) collective-permute-start(bf16[384,128]{1,0:T(8,128)(2,1)S(1)} %get-tuple-element.92.refs_5_), channel_id=1, source_target_pairs={{0,8},{8,0},{1,9},{9,1},{2,10},{10,2},{3,11},{11,3},{4,12},{12,4},... | collective-permute-start | bytes 294920 | tf_op jit(solution)/shard_map/ppermute | solution.py:318

commit v4 on v3

--- a/solution.py
+++ b/solution.py
@@ -61,6 +61,10 @@
         rows = slice(n * TILE, (n + 1) * TILE)
         ref[:TILE, :] = keep[rows, :]
         ref[TILE:, :] = recv[rows, :]
+
+
+def copy_rows(rows, out):
+    out[...] = rows[...]
 
 
 def stack_two(a, b, out):
@@ -216,18 +220,18 @@
     @pl.when(pos[CORE] == 0)
     def _():
         keep[...] = both[:, :1024]
-        send[...] = both[:, 1024:]
+        send[...] = both[:, 1024:].astype(BF16)
 
     @pl.when(pos[CORE] != 0)
     def _():
         keep[...] = both[:, 1024:]
-        send[...] = both[:, :1024]
+        send[...] = both[:, :1024].astype(BF16)
 
 
 def weight_cut(pos, mine, other, grads, stats, b0, b1, b2, b3):
     for n, ref in enumerate((b0, b1, b2, b3)):
         columns = pl.ds(pl.multiple_of((pos[X] ^ ORDER[n]) * BLK, BLK), BLK)
-        ref[:HD, :] = (mine[:, columns] + other[:, columns]).astype(BF16)
+        ref[:HD, :] = (mine[:, columns] + other[:, columns].astype(F32)).astype(BF16)
         ref[HD : 2 * HD, :] = grads[...]
         ref[2 * HD :, :] = stats[...]
 
@@ -284,22 +288,29 @@
         send[rows, :] = total[TILE:]
 
 
-def finish(pos, mine, other, here, core, q, k, v, weight):
-    for half, ref in ((pos[CORE], here), (1 - pos[CORE], core)):
+def finish(
+    pos, mine, other, here, core, mix_mine, mix_other, q, k, v, weight, mixed,
+    heads, halves, rows_out, sems,
+):
+    copies = []
+    for n, (half, ref) in enumerate(((pos[CORE], here), (1 - pos[CORE], core))):
+        halves[n] = ref[...].astype(F32)
         columns = pl.ds(pl.multiple_of(half * 1024, 1024), 1024)
-        weight[:, columns] = ref[...].astype(F32)
+        copies.append(pltpu.make_async_copy(halves.at[n], weight.at[:, columns], sems.at[n]))
+        copies[-1].start()
+    left = pl.ds(pl.multiple_of(pos[PAR] * HD, HD), HD)
+    right = pl.ds(pl.multiple_of((1 - pos[PAR]) * HD, HD), HD)
     for n, ref in enumerate((q, k, v)):
         rows = slice(n * TILE, (n + 1) * TILE)
-
-        @pl.when(pos[PAR] == 0)
-        def _():
-            ref[:, :HD] = mine[rows, :]
-            ref[:, HD:] = other[rows, :]
-
-        @pl.when(pos[PAR] != 0)
-        def _():
-            ref[:, HD:] = mine[rows, :]
-            ref[:, :HD] = other[rows, :]
+        heads[n, :, left] = mine[rows, :]
+        heads[n, :, right] = other[rows, :]
+        copies.append(pltpu.make_async_copy(heads.at[n], ref, sems.at[2 + n]))
+        copies[-1].start()
+    rows_out[...] = add(mix_mine[...], mix_other[...]).astype(BF16)
+    copies.append(pltpu.make_async_copy(rows_out, mixed, sems.at[5]))
+    copies[-1].start()
+    for copy in copies:
+        copy.wait()
 
 
 def near(a, axis):
@@ -332,8 +343,9 @@
     keep = jnp.concatenate([jnp.where(first, rows[:, :HD], rows[:, HD:]) for rows in inputs])
     recv = over_pair(send)
     rows_far = over_pair(cotangent[0])
+    (rows,) = call(copy_rows, [((32, 2048), BF16)], (cotangent[0],), smem=0, after=(send,))
     k, v, q = call(own_blocks, [((BLK, HD), BF16)] * 3, (keep, recv), smem=0)
-    (rows,) = call(stack_two, [((64, 2048), BF16)], (cotangent[0], rows_far), smem=0, after=(recv,))
+    (rows,) = call(stack_two, [((64, 2048), BF16)], (rows, rows_far), smem=0, after=(recv,))
     kp, vp, qp = call(
         stack_pairs,
         [((2 * BLK, HD), BF16)] * 3,
@@ -361,7 +373,7 @@
     )
     att, stats, gw_keep, gw_send = call(
         attend,
-        [((HD, BLK), BF16), ((16, BLK), BF16)] + [((HD, 1024), F32)] * 2,
+        [((HD, BLK), BF16), ((16, BLK), BF16), ((HD, 1024), F32), ((HD, 1024), BF16)],
         (pos, *packs, grads, cot, cot_far),
         flops=2 * HD * BLK * 2048,
     )
@@ -395,20 +407,20 @@
     (done,) = call(sum_two, [((HD, BLK), BF16)], (near_sum, far(near_sum, "zh")), smem=0)
     done_far = over_pair(done)
     dq_far = lax.optimization_barrier((dq_far, near_sum))[0]
-    dk_far, dv_near, _ = lax.optimization_barrier((dk_far, dv_near, done_far))
+    dk_far, dv_near, _ = lax.optimization_barrier((dk_far, dv_near, done))
 
     dq, dq_near = call(sum_split, [((HD, BLK), BF16)] * 2, (dq, far(dq_far, "x")), smem=0)
     mixed, mixed_near = call(
         sum_split, [((32, 2048), BF16)] * 2, (mixed, far(mixed_far, "y")), smem=0, after=(done,)
     )
-    (mixed,) = call(sum_two, [((32, 2048), BF16)], (mixed, near(mixed_near, "y")), smem=0)
+    mixed_other = near(mixed_near, "y")
     (stack,) = call(weight_stack, [((2 * HD, BLK), BF16)], (pos, done, done_far), after=(dq_near,))
     stacks = [stack, near(stack, "x"), far(stack, "x"), opposite(stack, "x")]
     dk, dk_near = call(
-        sum_split, [((BLK, HD), BF16)] * 2, (dk, far(dk_far, "zh")), smem=0, after=(stacks[1], mixed)
+        sum_split, [((BLK, HD), BF16)] * 2, (dk, far(dk_far, "zh")), smem=0, after=(mixed_other,)
     )
     dv, dv_far = call(
-        sum_split, [((BLK, HD), BF16)] * 2, (dv, near(dv_near, "zh")), smem=0, after=(stacks[1],)
+        sum_split, [((BLK, HD), BF16)] * 2, (dv, near(dv_near, "zh")), smem=0
     )
     dq_near = lax.optimization_barrier((dq_near, stacks[1]))[0]
     out_keep, out_send = call(
@@ -421,16 +433,25 @@
     (here,) = call(
         weight_row, [((2 * HD, 1024), BF16)], (pos, *stacks), after=(out_send,)
     )
-    grad_q, grad_k, grad_v, grad_weight = call(
+    grad_q, grad_k, grad_v, grad_weight, mixed = call(
         finish,
-        [((TILE, 2 * HD), BF16)] * 3 + [((2 * HD, 2048), F32)],
+        [((TILE, 2 * HD), BF16)] * 3 + [((2 * HD, 2048), F32), ((32, 2048), BF16)],
         (
             pos,
             out_keep,
             over_pair(out_send),
             here,
             over_core(here),
+            mixed,
+            mixed_other,
         ),
+        scratch=[
+            pltpu.VMEM((3, TILE, 2 * HD), BF16),
+            pltpu.VMEM((2, 2 * HD, 1024), F32),
+            pltpu.VMEM((32, 2048), BF16),
+            pltpu.SemaphoreType.DMA((6,)),
+        ],
+        out_space=pl.ANY,
     )
     return (mixed[None], grad_q[None], grad_k[None], grad_v[None], grad_weight)
 

time: 106 us -> 102 us (0.962)
  waiting for transfers between devices: 25 us -> 22 us
    ppermute x5, waiting for transfers between devices: 11.9 us -> 9.19 us  [over_pair(): return lax.ppermute(a, 'par', [(0, 1), (1, 0)])]
    ppermute x12, starting transfers between devices: 13 us -> 15.1 us  [near(): return lax.ppermute(a, axis, [(0, 1), (1, 0), (2, 3), (3, 2)])]
    ppermute x12, waiting for transfers between devices: 9.97 us -> 8.33 us  [far(): return lax.ppermute(a, axis, [(0, 3), (3, 0), (1, 2), (2, 1)])]
    ppermute x12, waiting for transfers between devices: 1.42 us -> 3.05 us  [near(): return lax.ppermute(a, axis, [(0, 1), (1, 0), (2, 3), (3, 2)])]
    ppermute x5, starting transfers between devices: 6.91 us -> 5.58 us  [over_pair(): return lax.ppermute(a, 'par', [(0, 1), (1, 0)])]
    ppermute x2, starting transfers between devices: 12.5 us -> 11.3 us  [over_core(): return lax.ppermute(a, 'core', [(0, 1), (1, 0)])]
  transfers between devices with their start and end apart: 34 -> 34, of which waited for: 16 -> 15; matrix products, arithmetic and copies ran while one was open for 2% -> 2% of each run, Pallas kernels for 11% -> 10%
where the time goes in v4:
time: 102 us; the launch traced here: 101 us
  starting transfers between devices  60.7 us (60%)
  waiting for transfers between devices  22 us (22%)
  Pallas kernels  15 us (15%)
  other arithmetic  1.62 us (2%)
  between operations  1.05 us (1%)
    ppermute x12, starting transfers between devices, far(): return lax.ppermute(a, axis, [(0, 3), (3, 0), (1, 2), (2, 1)])  21.9 us
    ppermute x12, starting transfers between devices, near(): return lax.ppermute(a, axis, [(0, 1), (1, 0), (2, 3), (3, 2)])  15.1 us
    pallas_call x23, Pallas kernels, call(): pl.pallas_call(body, out_shape=shapes, in_specs=specs, out_specs=[pl.Bloc...  15 us
    ppermute x2, starting transfers between devices, over_core(): return lax.ppermute(a, 'core', [(0, 1), (1, 0)])  11.3 us
    ppermute x5, waiting for transfers between devices, over_pair(): return lax.ppermute(a, 'par', [(0, 1), (1, 0)])  9.19 us
    ppermute x12, waiting for transfers between devices, far(): return lax.ppermute(a, axis, [(0, 3), (3, 0), (1, 2), (2, 1)])  8.33 us
    ppermute x3, starting transfers between devices, opposite(): return lax.ppermute(a, axis, [(0, 2), (2, 0), (1, 3), (3, 1)])  6.75 us
    ppermute x5, starting transfers between devices, over_pair(): return lax.ppermute(a, 'par', [(0, 1), (1, 0)])  5.58 us
  transfers between devices with their start and end apart: 34, of which 15 were waited for; matrix products, arithmetic and copies ran while one was open for 2% of the time, Pallas kernels for 10%

profile of v4, /device:TPU:1, one launch (start us, length us, event | category | flops | bytes accessed | tf_op | source)
XLA Modules:
  0.0 101.3 jit_solution(15701997859668263133)
XLA Ops:
  0.6 2.6 %collective-permute-start.10 = (bf16[32,2048]{1,0:T(8,128)(2,1)}, bf16[32,2048]{1,0:T(8,128)(2,1)S(1)}, u32[]{:S(2)}, u32[]{:S(2)}) collective-permute-start(bf16[32,2048]{1,0:T(8,128)(2,1)} %bitcast.13), channel_id=1, source_target_pairs={{0,8},{8,0},{1,9},{9,1},{2,10},{10,2},{3,11},{11,3},{4,12},{12,4},... | collective-permute-start | bytes 393224 | tf_op jit(solution)/shard_map/ppermute | solution.py:329
  3.2 0.8 broadcast_select_fusion.2
  4.0 0.8 broadcast_select_fusion
  4.8 0.1 collective-permute-start
  4.9 0.9 copy-done.1
  5.8 3.9 %collective-permute-done.recv.refs_2_ = bf16[384,128]{1,0:T(8,128)(2,1)S(1)} collective-permute-done((bf16[384,128]{1,0:T(8,128)(2,1)S(1)}, bf16[384,128]{1,0:T(8,128)(2,1)S(1)}, u32[]{:S(2)}, u32[]{:S(2)}) %collective-permute-start) | collective-permute-done | bytes 98336 | tf_op jit(solution)/shard_map/ppermute | solution.py:329
  9.7 0.1 collective-permute-start.11
  9.9 3.0 %collective-permute-start.1 = (bf16[256,128]{1,0:T(8,128)(2,1)S(1)}, bf16[256,128]{1,0:T(8,128)(2,1)S(1)}, u32[]{:S(2)}, u32[]{:S(2)}) collective-permute-start(bf16[256,128]{1,0:T(8,128)(2,1)S(1)} %get-tuple-element.52.k0), channel_id=1, source_target_pairs={{0,16},{16,0},{32,48},{48,32},{1,17},{17,1},{33,49},{49,33},{2,18}... | collective-permute-start | bytes 196616 | tf_op jit(solution)/shard_map/ppermute | solution.py:317
  12.9 4.3 %collective-permute-start.2 = (bf16[256,128]{1,0:T(8,128)(2,1)S(1)}, bf16[256,128]{1,0:T(8,128)(2,1)S(1)}, u32[]{:S(2)}, u32[]{:S(2)}) collective-permute-start(bf16[256,128]{1,0:T(8,128)(2,1)S(1)} %get-tuple-element.53.v0), channel_id=1, source_target_pairs={{0,48},{48,0},{16,32},{32,16},{1,49},{49,1},{17,33},{33,17},{2,50}... | collective-permute-start | bytes 196616 | tf_op jit(solution)/shard_map/ppermute | solution.py:321
  17.2 1.2 %collective-permute-start.3 = (bf16[256,128]{1,0:T(8,128)(2,1)S(1)}, bf16[256,128]{1,0:T(8,128)(2,1)S(1)}, u32[]{:S(2)}, u32[]{:S(2)}) collective-permute-start(bf16[256,128]{1,0:T(8,128)(2,1)S(1)} %get-tuple-element.54.q0), channel_id=1, source_target_pairs={{0,64},{64,0},{128,192},{192,128},{1,65},{65,1},{129,193},{193,129... | collective-permute-start | bytes 196616 | tf_op jit(solution)/shard_map/ppermute | solution.py:317
  18.4 1.0 collective-permute-done.2.v1
  19.4 0.9 collective-permute-done.3.q1
  20.4 2.0 %collective-permute-start.12 = (bf16[128,2048]{1,0:T(8,128)(2,1)S(1)}, bf16[128,2048]{1,0:T(8,128)(2,1)S(1)}, u32[]{:S(2)}, u32[]{:S(2)}) collective-permute-start(bf16[128,2048]{1,0:T(8,128)(2,1)S(1)} %shard_map.106.pair), channel_id=1, source_target_pairs={{0,6},{6,0},{2,4},{4,2},{1,7},{7,1},{3,5},{5,3},{8,14},{14,8},{10,... | collective-permute-start | bytes 1572872 | tf_op jit(solution)/shard_map/ppermute | solution.py:321
  22.4 1.5 %collective-permute-start.5 = (bf16[512,128]{1,0:T(8,128)(2,1)S(1)}, bf16[512,128]{1,0:T(8,128)(2,1)S(1)}, u32[]{:S(2)}, u32[]{:S(2)}) collective-permute-start(bf16[512,128]{1,0:T(8,128)(2,1)S(1)} %get-tuple-element.56.vp.refs_4_), channel_id=1, source_target_pairs={{0,16},{16,0},{32,48},{48,32},{1,17},{17,1},{33,49},{49,33},{2,18}... | collective-permute-start | bytes 393224 | tf_op jit(solution)/shard_map/ppermute | solution.py:317
  23.9 2.5 %collective-permute-start.6 = (bf16[512,128]{1,0:T(8,128)(2,1)S(1)}, bf16[512,128]{1,0:T(8,128)(2,1)S(1)}, u32[]{:S(2)}, u32[]{:S(2)}) collective-permute-start(bf16[512,128]{1,0:T(8,128)(2,1)S(1)} %get-tuple-element.57.qp.refs_6_), channel_id=1, source_target_pairs={{0,192},{192,0},{64,128},{128,64},{1,193},{193,1},{65,129},{129,65... | collective-permute-start | bytes 393224 | tf_op jit(solution)/shard_map/ppermute | solution.py:321
  26.4 2.2 %collective-permute-start.4 = (bf16[512,128]{1,0:T(8,128)(2,1)S(1)}, bf16[512,128]{1,0:T(8,128)(2,1)S(1)}, u32[]{:S(2)}, u32[]{:S(2)}) collective-permute-start(bf16[512,128]{1,0:T(8,128)(2,1)S(1)} %get-tuple-element.55.kp.refs_2_), channel_id=1, source_target_pairs={{0,48},{48,0},{16,32},{32,16},{1,49},{49,1},{17,33},{33,17},{2,50}... | collective-permute-start | bytes 393224 | tf_op jit(solution)/shard_map/ppermute | solution.py:321
  28.6 0.1 stack.23.pos.refs_0_
  28.6 0.2 collective-permute-done.5.vn.refs_5_
  28.8 0.4 collective-permute-done.6.qf.refs_7_
  29.2 4.5 %collective-permute-done.4.kf.refs_3_ = bf16[512,128]{1,0:T(8,128)(2,1)S(1)} collective-permute-done((bf16[512,128]{1,0:T(8,128)(2,1)S(1)}, bf16[512,128]{1,0:T(8,128)(2,1)S(1)}, u32[]{:S(2)}, u32[]{:S(2)}) %collective-permute-start.4) | collective-permute-done | bytes 131104 | tf_op jit(solution)/shard_map/ppermute | solution.py:321
  33.7 3.0 %shard_map.103 = (bf16[144,256]{1,0:T(8,128)(2,1)S(1)}, bf16[144,256]{1,0:T(8,128)(2,1)S(1)}, bf16[144,256]{1,0:T(8,128)(2,1)S(1)}, bf16[144,256]{1,0:T(8,128)(2,1)S(1)}) custom-call(s32[5]{0:T(128)S(1)} %stack.23.pos.refs_0_, s32[32,32]{1,0:T(8,128)S(1)} %copy-done.2, bf16[512,128]{1,0:T(8,128)(2,1)S(1)} %get-tuple-element.55.kp.refs_2_, ...), custom_call_target="tpu_custom_call" | custom-call | flops 536870912 | bytes 1085460 | tf_op jit(solution)/shard_map/pallas_call | solution.py:48
  36.7 0.3 collective-permute-start.7
  37.0 3.0 %collective-permute-start.9 = (bf16[144,256]{1,0:T(8,128)(2,1)S(1)}, bf16[144,256]{1,0:T(8,128)(2,1)S(1)}, u32[]{:S(2)}, u32[]{:S(2)}) collective-permute-start(bf16[144,256]{1,0:T(8,128)(2,1)S(1)} %get-tuple-element.61), channel_id=1, source_target_pairs={{0,128},{128,0},{64,192},{192,64},{1,129},{129,1},{65,193},{193,65... | collective-permute-start | bytes 221192 | tf_op jit(solution)/shard_map/ppermute | solution.py:325
  40.1 0.6 shard_map.107
  40.7 1.0 shard_map.108.grads
  41.7 0.5 collective-permute-done.8.p2
  42.2 1.0 %shard_map.109 = (bf16[128,256]{1,0:T(8,128)(2,1)S(1)}, bf16[16,256]{1,0:T(8,128)(2,1)S(1)}, f32[128,1024]{1,0:T(8,128)S(1)}, bf16[128,1024]{1,0:T(8,128)(2,1)S(1)}) custom-call(s32[5]{0:T(128)S(1)} %stack.23.pos.refs_0_, bf16[144,256]{1,0:T(8,128)(2,1)S(1)} %get-tuple-element.58.p0, bf16[144,256]{1,0:T(8,128)(2,1)S(1)} %collective-permute-done.7.p1, ...), custom_call_target="tpu_custom_call" | custom-call | flops 134217728 | bytes 2269204 | tf_op jit(solution)/shard_map/pallas_call | solution.py:48
  43.3 5.5 %collective-permute-start.13 = (bf16[128,1024]{1,0:T(8,128)(2,1)S(1)}, bf16[128,1024]{1,0:T(8,128)(2,1)S(1)}, u32[]{:S(2)}, u32[]{:S(2)}) collective-permute-start(bf16[128,1024]{1,0:T(8,128)(2,1)S(1)} %get-tuple-element.65), channel_id=1, source_target_pairs={{0,1},{1,0},{2,3},{3,2},{4,5},{5,4},{6,7},{7,6},{8,9},{9,8},{10,11... | collective-permute-start | bytes 786440 | tf_op jit(solution)/shard_map/ppermute | solution.py:333
  48.8 1.2 %collective-permute-done.13.other = bf16[128,1024]{1,0:T(8,128)(2,1)S(1)} collective-permute-done((bf16[128,1024]{1,0:T(8,128)(2,1)S(1)}, bf16[128,1024]{1,0:T(8,128)(2,1)S(1)}, u32[]{:S(2)}, u32[]{:S(2)}) %collective-permute-start.13) | collective-permute-done | bytes 262176 | tf_op jit(solution)/shard_map/ppermute | solution.py:333
  50.0 0.6 shard_map.110
  50.6 0.5 collective-permute-start.14
  51.1 2.3 %collective-permute-start.15 = (bf16[272,256]{1,0:T(8,128)(2,1)S(1)}, bf16[272,256]{1,0:T(8,128)(2,1)S(1)}, u32[]{:S(2)}, u32[]{:S(2)}) collective-permute-start(bf16[272,256]{1,0:T(8,128)(2,1)S(1)} %get-tuple-element.69), channel_id=1, source_target_pairs={{0,192},{192,0},{64,128},{128,64},{1,193},{193,1},{65,129},{129,65... | collective-permute-start | bytes 417800 | tf_op jit(solution)/shard_map/ppermute | solution.py:321
  53.4 0.5 collective-permute-start.16
  54.0 2.0 %collective-permute-start.17 = (bf16[128,128]{1,0:T(8,128)(2,1)S(1)}, bf16[128,128]{1,0:T(8,128)(2,1)S(1)}, u32[]{:S(2)}, u32[]{:S(2)}) collective-permute-start(bf16[128,128]{1,0:T(8,128)(2,1)S(1)} %slice.33), channel_id=1, source_target_pairs={{0,8},{8,0},{1,9},{9,1},{2,10},{10,2},{3,11},{11,3},{4,12},{12,4},... | collective-permute-start | bytes 98312 | tf_op jit(solution)/shard_map/ppermute | solution.py:329
  56.0 1.6 %collective-permute-done.17.other = bf16[128,128]{1,0:T(8,128)(2,1)S(1)} collective-permute-done((bf16[128,128]{1,0:T(8,128)(2,1)S(1)}, bf16[128,128]{1,0:T(8,128)(2,1)S(1)}, u32[]{:S(2)}, u32[]{:S(2)}) %collective-permute-start.17) | collective-permute-done | bytes 32800 | tf_op jit(solution)/shard_map/ppermute | solution.py:329
  57.6 1.1 %shard_map.111 = (bf16[64,2048]{1,0:T(8,128)(2,1)S(1)}, bf16[64,2048]{1,0:T(8,128)(2,1)S(1)}) custom-call(s32[5]{0:T(128)S(1)} %stack.23.pos.refs_0_, bf16[128,256]{1,0:T(8,128)(2,1)S(1)} %get-tuple-element.71.att, bf16[128,128]{1,0:T(8,128)(2,1)S(1)} %collective-permute-done.17.other, bf16[256,2048]{1,0:T(8,128)(2,1)S(1)} %copy-done), custom_call_target="tpu_custom_call" | custom-call | flops 134217728 | bytes 1671188 | tf_op jit(solution)/shard_map/pallas_call | solution.py:48
  58.7 0.9 collective-permute-start.21
  59.5 0.2 collective-permute-done.16.refs_3_.refs_11_
  59.8 2.6 %collective-permute-start.18 = (bf16[128,256]{1,0:T(8,128)(2,1)S(1)}, bf16[128,256]{1,0:T(8,128)(2,1)S(1)}, u32[]{:S(2)}, u32[]{:S(2)}) collective-permute-start(bf16[128,256]{1,0:T(8,128)(2,1)S(1)} %shard_map.112.refs_12_.refs_0_), channel_id=1, source_target_pairs={{0,16},{16,0},{32,48},{48,32},{1,17},{17,1},{33,49},{49,33},{2,18}... | collective-permute-start | bytes 196616 | tf_op jit(solution)/shard_map/ppermute | solution.py:317
  62.3 4.0 %shard_map.113 = (bf16[512,128]{1,0:T(8,128)(2,1)S(1)}, bf16[512,128]{1,0:T(8,128)(2,1)S(1)}, bf16[512,128]{1,0:T(8,128)(2,1)S(1)}, bf16[512,128]{1,0:T(8,128)(2...) custom-call(s32[5]{0:T(128)S(1)} %stack.23.pos.refs_0_, s32[32,32]{1,0:T(8,128)S(1)} %copy-done.2, ...), custom_call_target="tpu_custom_call" | custom-call | flops 1342177280 | bytes 2134036 | tf_op jit(solution)/shard_map/pallas_call | solution.py:48
  66.4 1.3 %collective-permute-start.19 = (bf16[128,256]{1,0:T(8,128)(2,1)S(1)}, bf16[128,256]{1,0:T(8,128)(2,1)S(1)}, u32[]{:S(2)}, u32[]{:S(2)}) collective-permute-start(bf16[128,256]{1,0:T(8,128)(2,1)S(1)} %shard_map.114.a), channel_id=1, source_target_pairs={{0,48},{48,0},{16,32},{32,16},{1,49},{49,1},{17,33},{33,17},{2,50}... | collective-permute-start | bytes 196616 | tf_op jit(solution)/shard_map/ppermute | solution.py:321
  67.7 2.7 %collective-permute-start.26 = (bf16[256,256]{1,0:T(8,128)(2,1)S(1)}, bf16[256,256]{1,0:T(8,128)(2,1)S(1)}, u32[]{:S(2)}, u32[]{:S(2)}) collective-permute-start(bf16[256,256]{1,0:T(8,128)(2,1)S(1)} %get-tuple-element.87), channel_id=1, source_target_pairs={{0,192},{192,0},{64,128},{128,64},{1,193},{193,1},{65,129},{129,65... | collective-permute-start | bytes 393224 | tf_op jit(solution)/shard_map/ppermute | solution.py:321
  70.4 1.3 %collective-permute-done.19.b = bf16[128,256]{1,0:T(8,128)(2,1)S(1)} collective-permute-done((bf16[128,256]{1,0:T(8,128)(2,1)S(1)}, bf16[128,256]{1,0:T(8,128)(2,1)S(1)}, u32[]{:S(2)}, u32[]{:S(2)}) %collective-permute-start.19) | collective-permute-done | bytes 65568 | tf_op jit(solution)/shard_map/ppermute | solution.py:321
  71.7 0.2 collective-permute-start.27
  72.0 1.8 %collective-permute-start.24 = (bf16[512,128]{1,0:T(8,128)(2,1)S(1)}, bf16[512,128]{1,0:T(8,128)(2,1)S(1)}, u32[]{:S(2)}, u32[]{:S(2)}) collective-permute-start(bf16[512,128]{1,0:T(8,128)(2,1)S(1)} %get-tuple-element.83), channel_id=1, source_target_pairs={{0,16},{16,0},{32,48},{48,32},{1,17},{17,1},{33,49},{49,33},{2,18}... | collective-permute-start | bytes 393224 | tf_op jit(solution)/shard_map/ppermute | solution.py:317
  73.8 1.3 %collective-permute-start.20 = (bf16[512,128]{1,0:T(8,128)(2,1)S(1)}, bf16[512,128]{1,0:T(8,128)(2,1)S(1)}, u32[]{:S(2)}, u32[]{:S(2)}) collective-permute-start(bf16[512,128]{1,0:T(8,128)(2,1)S(1)} %get-tuple-element.77), channel_id=1, source_target_pairs={{0,48},{48,0},{16,32},{32,16},{1,49},{49,1},{17,33},{33,17},{2,50}... | collective-permute-start | bytes 393224 | tf_op jit(solution)/shard_map/ppermute | solution.py:321
  75.1 0.1 shard_map.116
  75.1 0.5 collective-permute-start.22
  75.7 0.6 shard_map.120.refs_1_
  76.2 0.8 collective-permute-start.28
  77.0 3.2 %collective-permute-start.32 = (bf16[256,256]{1,0:T(8,128)(2,1)S(1)}, bf16[256,256]{1,0:T(8,128)(2,1)S(1)}, u32[]{:S(2)}, u32[]{:S(2)}) collective-permute-start(bf16[256,256]{1,0:T(8,128)(2,1)S(1)} %shard_map.120.refs_1_), channel_id=1, source_target_pairs={{0,128},{128,0},{64,192},{192,64},{1,129},{129,1},{65,193},{193,65... | collective-permute-start | bytes 393224 | tf_op jit(solution)/shard_map/ppermute | solution.py:325
  80.2 0.7 collective-permute-start.31
  80.9 1.7 %collective-permute-start.25 = (bf16[256,128]{1,0:T(8,128)(2,1)S(1)}, bf16[256,128]{1,0:T(8,128)(2,1)S(1)}, u32[]{:S(2)}, u32[]{:S(2)}) collective-permute-start(bf16[256,128]{1,0:T(8,128)(2,1)S(1)} %get-tuple-element.85), channel_id=1, source_target_pairs={{0,48},{48,0},{16,32},{32,16},{1,49},{49,1},{17,33},{33,17},{2,50}... | collective-permute-start | bytes 196616 | tf_op jit(solution)/shard_map/ppermute | solution.py:321
  82.7 2.2 %collective-permute-start.23 = (bf16[256,128]{1,0:T(8,128)(2,1)S(1)}, bf16[256,128]{1,0:T(8,128)(2,1)S(1)}, u32[]{:S(2)}, u32[]{:S(2)}) collective-permute-start(bf16[256,128]{1,0:T(8,128)(2,1)S(1)} %get-tuple-element.81), channel_id=1, source_target_pairs={{0,16},{16,0},{32,48},{48,32},{1,17},{17,1},{33,49},{49,33},{2,18}... | collective-permute-start | bytes 196616 | tf_op jit(solution)/shard_map/ppermute | solution.py:317
  84.8 0.8 collective-permute-start.29
  85.6 0.7 collective-permute-done.25.v_far
  86.3 0.5 collective-permute-done.23.k_near
  86.8 1.5 %collective-permute-done.29.q_near = bf16[128,256]{1,0:T(8,128)(2,1)S(1)} collective-permute-done((bf16[128,256]{1,0:T(8,128)(2,1)S(1)}, bf16[128,256]{1,0:T(8,128)(2,1)S(1)}, u32[]{:S(2)}, u32[]{:S(2)}) %collective-permute-start.29) | collective-permute-done | bytes 65568 | tf_op jit(solution)/shard_map/ppermute | solution.py:317
  88.2 0.1 shard_map.121
  88.4 0.6 shard_map.122.here
  89.0 5.8 %collective-permute-start.33 = (bf16[256,1024]{1,0:T(8,128)(2,1)S(1)}, bf16[256,1024]{1,0:T(8,128)(2,1)S(1)}, u32[]{:S(2)}, u32[]{:S(2)}) collective-permute-start(bf16[256,1024]{1,0:T(8,128)(2,1)S(1)} %shard_map.122.here), channel_id=1, source_target_pairs={{0,1},{1,0},{2,3},{3,2},{4,5},{5,4},{6,7},{7,6},{8,9},{9,8},{10,11... | collective-permute-start | bytes 1572872 | tf_op jit(solution)/shard_map/ppermute | solution.py:333
  94.7 0.6 collective-permute-start.30
  95.4 3.7 %collective-permute-done.30.other = bf16[384,128]{1,0:T(8,128)(2,1)S(1)} collective-permute-done((bf16[384,128]{1,0:T(8,128)(2,1)S(1)}, bf16[384,128]{1,0:T(8,128)(2,1)S(1)}, u32[]{:S(2)}, u32[]{:S(2)}) %collective-permute-start.30) | collective-permute-done | bytes 98336 | tf_op jit(solution)/shard_map/ppermute | solution.py:329
  99.1 2.1 %shard_map.123 = (bf16[128,256]{1,0:T(8,128)(2,1)}, bf16[128,256]{1,0:T(8,128)(2,1)}, bf16[128,256]{1,0:T(8,128)(2,1)}, f32[256,2048]{1,0:T(8,128)}, bf16[32,2048]{1,0:T(8,128)(2,1)}) custom-call(s32[5]{0:T(128)S(1)} %stack.23.pos.refs_0_, bf16[384,128]{1,0:T(8,128)(2,1)S(1)} %get-tuple-element.91.mine, bf16[384,128]{1,0:T(8,128)(2,1)S(1)} %collective-permute-done.30.other, ...), custom_call_target="tpu_custom_call" | custom-call | bytes 3932180 | tf_op jit(solution)/shard_map/pallas_call | solution.py:48
  (39 shorter events, 0.4 us)
Async XLA Ops:
  0.6 33.1 %copy-start.2 = (s32[32,32]{1,0:T(8,128)S(1)}, s32[32,32]{1,0:T(8,128)}, u32[]{:S(2)}) copy-start(s32[32,32]{1,0:T(8,128)} %refs_1_.1) | copy-start | bytes 12292
  0.6 9.1 %collective-permute-start.10 = (bf16[32,2048]{1,0:T(8,128)(2,1)}, bf16[32,2048]{1,0:T(8,128)(2,1)S(1)}, u32[]{:S(2)}, u32[]{:S(2)}) collective-permute-start(bf16[32,2048]{1,0:T(8,128)(2,1)} %bitcast.13), channel_id=1, source_target_pairs={{0,8},{8,0},{1,9},{9,1},{2,10},{10,2},{3,11},{11,3},{4,12},{12,4},... | collective-permute-start | bytes 393224 | tf_op jit(solution)/shard_map/ppermute | solution.py:329
  4.8 4.9 %collective-permute-start = (bf16[384,128]{1,0:T(8,128)(2,1)S(1)}, bf16[384,128]{1,0:T(8,128)(2,1)S(1)}, u32[]{:S(2)}, u32[]{:S(2)}) collective-permute-start(bf16[384,128]{1,0:T(8,128)(2,1)S(1)} %pad_maximum_fusion.1.refs_1_), channel_id=1, source_target_pairs={{0,8},{8,0},{1,9},{9,1},{2,10},{10,2},{3,11},{11,3},{4,12},{12,4},... | collective-permute-start | bytes 294920 | tf_op jit(solution)/shard_map/ppermute | solution.py:329
  4.9 0.9 copy-start.1
  9.7 10.6 %collective-permute-start.11 = (bf16[64,2048]{1,0:T(8,128)(2,1)S(1)}, bf16[64,2048]{1,0:T(8,128)(2,1)S(1)}, u32[]{:S(2)}, u32[]{:S(2)}) collective-permute-start(bf16[64,2048]{1,0:T(8,128)(2,1)S(1)} %shard_map.105.refs_0_), channel_id=1, source_target_pairs={{0,2},{2,0},{4,6},{6,4},{1,3},{3,1},{5,7},{7,5},{8,10},{10,8},{12,... | collective-permute-start | bytes 786440 | tf_op jit(solution)/shard_map/ppermute | solution.py:317
  9.9 8.5 %collective-permute-start.1 = (bf16[256,128]{1,0:T(8,128)(2,1)S(1)}, bf16[256,128]{1,0:T(8,128)(2,1)S(1)}, u32[]{:S(2)}, u32[]{:S(2)}) collective-permute-start(bf16[256,128]{1,0:T(8,128)(2,1)S(1)} %get-tuple-element.52.k0), channel_id=1, source_target_pairs={{0,16},{16,0},{32,48},{48,32},{1,17},{17,1},{33,49},{49,33},{2,18}... | collective-permute-start | bytes 196616 | tf_op jit(solution)/shard_map/ppermute | solution.py:317
  12.9 6.5 %collective-permute-start.2 = (bf16[256,128]{1,0:T(8,128)(2,1)S(1)}, bf16[256,128]{1,0:T(8,128)(2,1)S(1)}, u32[]{:S(2)}, u32[]{:S(2)}) collective-permute-start(bf16[256,128]{1,0:T(8,128)(2,1)S(1)} %get-tuple-element.53.v0), channel_id=1, source_target_pairs={{0,48},{48,0},{16,32},{32,16},{1,49},{49,1},{17,33},{33,17},{2,50}... | collective-permute-start | bytes 196616 | tf_op jit(solution)/shard_map/ppermute | solution.py:321
  17.2 3.1 %collective-permute-start.3 = (bf16[256,128]{1,0:T(8,128)(2,1)S(1)}, bf16[256,128]{1,0:T(8,128)(2,1)S(1)}, u32[]{:S(2)}, u32[]{:S(2)}) collective-permute-start(bf16[256,128]{1,0:T(8,128)(2,1)S(1)} %get-tuple-element.54.q0), channel_id=1, source_target_pairs={{0,64},{64,0},{128,192},{192,128},{1,65},{65,1},{129,193},{193,129... | collective-permute-start | bytes 196616 | tf_op jit(solution)/shard_map/ppermute | solution.py:317
  20.4 20.3 %copy-start = (bf16[256,2048]{1,0:T(8,128)(2,1)S(1)}, bf16[256,2048]{1,0:T(8,128)(2,1)}, u32[]{:S(2)}) copy-start(bf16[256,2048]{1,0:T(8,128)(2,1)} %w.3) | copy-start | bytes 3145732
  20.4 19.7 %collective-permute-start.12 = (bf16[128,2048]{1,0:T(8,128)(2,1)S(1)}, bf16[128,2048]{1,0:T(8,128)(2,1)S(1)}, u32[]{:S(2)}, u32[]{:S(2)}) collective-permute-start(bf16[128,2048]{1,0:T(8,128)(2,1)S(1)} %shard_map.106.pair), channel_id=1, source_target_pairs={{0,6},{6,0},{2,4},{4,2},{1,7},{7,1},{3,5},{5,3},{8,14},{14,8},{10,... | collective-permute-start | bytes 1572872 | tf_op jit(solution)/shard_map/ppermute | solution.py:321
  22.4 6.4 %collective-permute-start.5 = (bf16[512,128]{1,0:T(8,128)(2,1)S(1)}, bf16[512,128]{1,0:T(8,128)(2,1)S(1)}, u32[]{:S(2)}, u32[]{:S(2)}) collective-permute-start(bf16[512,128]{1,0:T(8,128)(2,1)S(1)} %get-tuple-element.56.vp.refs_4_), channel_id=1, source_target_pairs={{0,16},{16,0},{32,48},{48,32},{1,17},{17,1},{33,49},{49,33},{2,18}... | collective-permute-start | bytes 393224 | tf_op jit(solution)/shard_map/ppermute | solution.py:317
  23.9 5.3 %collective-permute-start.6 = (bf16[512,128]{1,0:T(8,128)(2,1)S(1)}, bf16[512,128]{1,0:T(8,128)(2,1)S(1)}, u32[]{:S(2)}, u32[]{:S(2)}) collective-permute-start(bf16[512,128]{1,0:T(8,128)(2,1)S(1)} %get-tuple-element.57.qp.refs_6_), channel_id=1, source_target_pairs={{0,192},{192,0},{64,128},{128,64},{1,193},{193,1},{65,129},{129,65... | collective-permute-start | bytes 393224 | tf_op jit(solution)/shard_map/ppermute | solution.py:321
  26.4 7.3 %collective-permute-start.4 = (bf16[512,128]{1,0:T(8,128)(2,1)S(1)}, bf16[512,128]{1,0:T(8,128)(2,1)S(1)}, u32[]{:S(2)}, u32[]{:S(2)}) collective-permute-start(bf16[512,128]{1,0:T(8,128)(2,1)S(1)} %get-tuple-element.55.kp.refs_2_), channel_id=1, source_target_pairs={{0,48},{48,0},{16,32},{32,16},{1,49},{49,1},{17,33},{33,17},{2,50}... | collective-permute-start | bytes 393224 | tf_op jit(solution)/shard_map/ppermute | solution.py:321
  36.7 5.0 %collective-permute-start.7 = (bf16[144,256]{1,0:T(8,128)(2,1)S(1)}, bf16[144,256]{1,0:T(8,128)(2,1)S(1)}, u32[]{:S(2)}, u32[]{:S(2)}) collective-permute-start(bf16[144,256]{1,0:T(8,128)(2,1)S(1)} %get-tuple-element.59), channel_id=1, source_target_pairs={{0,64},{64,0},{128,192},{192,128},{1,65},{65,1},{129,193},{193,129... | collective-permute-start | bytes 221192 | tf_op jit(solution)/shard_map/ppermute | solution.py:317
  37.0 5.2 %collective-permute-start.8 = (bf16[144,256]{1,0:T(8,128)(2,1)S(1)}, bf16[144,256]{1,0:T(8,128)(2,1)S(1)}, u32[]{:S(2)}, u32[]{:S(2)}) collective-permute-start(bf16[144,256]{1,0:T(8,128)(2,1)S(1)} %get-tuple-element.60), channel_id=1, source_target_pairs={{0,192},{192,0},{64,128},{128,64},{1,193},{193,1},{65,129},{129,65... | collective-permute-start | bytes 221192 | tf_op jit(solution)/shard_map/ppermute | solution.py:321
  37.0 5.2 %collective-permute-start.9 = (bf16[144,256]{1,0:T(8,128)(2,1)S(1)}, bf16[144,256]{1,0:T(8,128)(2,1)S(1)}, u32[]{:S(2)}, u32[]{:S(2)}) collective-permute-start(bf16[144,256]{1,0:T(8,128)(2,1)S(1)} %get-tuple-element.61), channel_id=1, source_target_pairs={{0,128},{128,0},{64,192},{192,64},{1,129},{129,1},{65,193},{193,65... | collective-permute-start | bytes 221192 | tf_op jit(solution)/shard_map/ppermute | solution.py:325
  43.3 6.7 %collective-permute-start.13 = (bf16[128,1024]{1,0:T(8,128)(2,1)S(1)}, bf16[128,1024]{1,0:T(8,128)(2,1)S(1)}, u32[]{:S(2)}, u32[]{:S(2)}) collective-permute-start(bf16[128,1024]{1,0:T(8,128)(2,1)S(1)} %get-tuple-element.65), channel_id=1, source_target_pairs={{0,1},{1,0},{2,3},{3,2},{4,5},{5,4},{6,7},{7,6},{8,9},{9,8},{10,11... | collective-permute-start | bytes 786440 | tf_op jit(solution)/shard_map/ppermute | solution.py:333
  50.6 8.9 %collective-permute-start.14 = (bf16[272,256]{1,0:T(8,128)(2,1)S(1)}, bf16[272,256]{1,0:T(8,128)(2,1)S(1)}, u32[]{:S(2)}, u32[]{:S(2)}) collective-permute-start(bf16[272,256]{1,0:T(8,128)(2,1)S(1)} %get-tuple-element.68), channel_id=1, source_target_pairs={{0,64},{64,0},{128,192},{192,128},{1,65},{65,1},{129,193},{193,129... | collective-permute-start | bytes 417800 | tf_op jit(solution)/shard_map/ppermute | solution.py:317
  51.1 8.5 %collective-permute-start.15 = (bf16[272,256]{1,0:T(8,128)(2,1)S(1)}, bf16[272,256]{1,0:T(8,128)(2,1)S(1)}, u32[]{:S(2)}, u32[]{:S(2)}) collective-permute-start(bf16[272,256]{1,0:T(8,128)(2,1)S(1)} %get-tuple-element.69), channel_id=1, source_target_pairs={{0,192},{192,0},{64,128},{128,64},{1,193},{193,1},{65,129},{129,65... | collective-permute-start | bytes 417800 | tf_op jit(solution)/shard_map/ppermute | solution.py:321
  53.4 6.3 %collective-permute-start.16 = (bf16[272,256]{1,0:T(8,128)(2,1)S(1)}, bf16[272,256]{1,0:T(8,128)(2,1)S(1)}, u32[]{:S(2)}, u32[]{:S(2)}) collective-permute-start(bf16[272,256]{1,0:T(8,128)(2,1)S(1)} %get-tuple-element.70), channel_id=1, source_target_pairs={{0,128},{128,0},{64,192},{192,64},{1,129},{129,1},{65,193},{193,65... | collective-permute-start | bytes 417800 | tf_op jit(solution)/shard_map/ppermute | solution.py:325
  54.0 3.6 %collective-permute-start.17 = (bf16[128,128]{1,0:T(8,128)(2,1)S(1)}, bf16[128,128]{1,0:T(8,128)(2,1)S(1)}, u32[]{:S(2)}, u32[]{:S(2)}) collective-permute-start(bf16[128,128]{1,0:T(8,128)(2,1)S(1)} %slice.33), channel_id=1, source_target_pairs={{0,8},{8,0},{1,9},{9,1},{2,10},{10,2},{3,11},{11,3},{4,12},{12,4},... | collective-permute-start | bytes 98312 | tf_op jit(solution)/shard_map/ppermute | solution.py:329
  58.7 16.4 %collective-permute-start.21 = (bf16[64,2048]{1,0:T(8,128)(2,1)S(1)}, bf16[64,2048]{1,0:T(8,128)(2,1)S(1)}, u32[]{:S(2)}, u32[]{:S(2)}) collective-permute-start(bf16[64,2048]{1,0:T(8,128)(2,1)S(1)} %get-tuple-element.72.refs_4_), channel_id=1, source_target_pairs={{0,6},{6,0},{2,4},{4,2},{1,7},{7,1},{3,5},{5,3},{8,14},{14,8},{10,... | collective-permute-start | bytes 786440 | tf_op jit(solution)/shard_map/ppermute | solution.py:321
  59.8 6.6 %collective-permute-start.18 = (bf16[128,256]{1,0:T(8,128)(2,1)S(1)}, bf16[128,256]{1,0:T(8,128)(2,1)S(1)}, u32[]{:S(2)}, u32[]{:S(2)}) collective-permute-start(bf16[128,256]{1,0:T(8,128)(2,1)S(1)} %shard_map.112.refs_12_.refs_0_), channel_id=1, source_target_pairs={{0,16},{16,0},{32,48},{48,32},{1,17},{17,1},{33,49},{49,33},{2,18}... | collective-permute-start | bytes 196616 | tf_op jit(solution)/shard_map/ppermute | solution.py:317
  66.4 5.3 %collective-permute-start.19 = (bf16[128,256]{1,0:T(8,128)(2,1)S(1)}, bf16[128,256]{1,0:T(8,128)(2,1)S(1)}, u32[]{:S(2)}, u32[]{:S(2)}) collective-permute-start(bf16[128,256]{1,0:T(8,128)(2,1)S(1)} %shard_map.114.a), channel_id=1, source_target_pairs={{0,48},{48,0},{16,32},{32,16},{1,49},{49,1},{17,33},{33,17},{2,50}... | collective-permute-start | bytes 196616 | tf_op jit(solution)/shard_map/ppermute | solution.py:321
  67.7 7.9 %collective-permute-start.26 = (bf16[256,256]{1,0:T(8,128)(2,1)S(1)}, bf16[256,256]{1,0:T(8,128)(2,1)S(1)}, u32[]{:S(2)}, u32[]{:S(2)}) collective-permute-start(bf16[256,256]{1,0:T(8,128)(2,1)S(1)} %get-tuple-element.87), channel_id=1, source_target_pairs={{0,192},{192,0},{64,128},{128,64},{1,193},{193,1},{65,129},{129,65... | collective-permute-start | bytes 393224 | tf_op jit(solution)/shard_map/ppermute | solution.py:321
  71.7 3.9 %collective-permute-start.27 = (bf16[128,256]{1,0:T(8,128)(2,1)S(1)}, bf16[128,256]{1,0:T(8,128)(2,1)S(1)}, u32[]{:S(2)}, u32[]{:S(2)}) collective-permute-start(bf16[128,256]{1,0:T(8,128)(2,1)S(1)} %shard_map.115.refs_2_.refs_1_), channel_id=1, source_target_pairs={{0,8},{8,0},{1,9},{9,1},{2,10},{10,2},{3,11},{11,3},{4,12},{12,4},... | collective-permute-start | bytes 196616 | tf_op jit(solution)/shard_map/ppermute | solution.py:329
  72.0 8.2 %collective-permute-start.24 = (bf16[512,128]{1,0:T(8,128)(2,1)S(1)}, bf16[512,128]{1,0:T(8,128)(2,1)S(1)}, u32[]{:S(2)}, u32[]{:S(2)}) collective-permute-start(bf16[512,128]{1,0:T(8,128)(2,1)S(1)} %get-tuple-element.83), channel_id=1, source_target_pairs={{0,16},{16,0},{32,48},{48,32},{1,17},{17,1},{33,49},{49,33},{2,18}... | collective-permute-start | bytes 393224 | tf_op jit(solution)/shard_map/ppermute | solution.py:317
  73.8 7.1 %collective-permute-start.20 = (bf16[512,128]{1,0:T(8,128)(2,1)S(1)}, bf16[512,128]{1,0:T(8,128)(2,1)S(1)}, u32[]{:S(2)}, u32[]{:S(2)}) collective-permute-start(bf16[512,128]{1,0:T(8,128)(2,1)S(1)} %get-tuple-element.77), channel_id=1, source_target_pairs={{0,48},{48,0},{16,32},{32,16},{1,49},{49,1},{17,33},{33,17},{2,50}... | collective-permute-start | bytes 393224 | tf_op jit(solution)/shard_map/ppermute | solution.py:321
  75.1 7.5 %collective-permute-start.22 = (bf16[32,2048]{1,0:T(8,128)(2,1)S(1)}, bf16[32,2048]{1,0:T(8,128)(2,1)S(1)}, u32[]{:S(2)}, u32[]{:S(2)}) collective-permute-start(bf16[32,2048]{1,0:T(8,128)(2,1)S(1)} %get-tuple-element.79), channel_id=1, source_target_pairs={{0,2},{2,0},{4,6},{6,4},{1,3},{3,1},{5,7},{7,5},{8,10},{10,8},{12,... | collective-permute-start | bytes 393224 | tf_op jit(solution)/shard_map/ppermute | solution.py:317
  76.2 8.6 %collective-permute-start.28 = (bf16[256,256]{1,0:T(8,128)(2,1)S(1)}, bf16[256,256]{1,0:T(8,128)(2,1)S(1)}, u32[]{:S(2)}, u32[]{:S(2)}) collective-permute-start(bf16[256,256]{1,0:T(8,128)(2,1)S(1)} %shard_map.120.refs_1_), channel_id=1, source_target_pairs={{0,64},{64,0},{128,192},{192,128},{1,65},{65,1},{129,193},{193,129... | collective-permute-start | bytes 393224 | tf_op jit(solution)/shard_map/ppermute | solution.py:317
  77.0 11.3 %collective-permute-start.32 = (bf16[256,256]{1,0:T(8,128)(2,1)S(1)}, bf16[256,256]{1,0:T(8,128)(2,1)S(1)}, u32[]{:S(2)}, u32[]{:S(2)}) collective-permute-start(bf16[256,256]{1,0:T(8,128)(2,1)S(1)} %shard_map.120.refs_1_), channel_id=1, source_target_pairs={{0,128},{128,0},{64,192},{192,64},{1,129},{129,1},{65,193},{193,65... | collective-permute-start | bytes 393224 | tf_op jit(solution)/shard_map/ppermute | solution.py:325
  80.2 8.2 %collective-permute-start.31 = (bf16[256,256]{1,0:T(8,128)(2,1)S(1)}, bf16[256,256]{1,0:T(8,128)(2,1)S(1)}, u32[]{:S(2)}, u32[]{:S(2)}) collective-permute-start(bf16[256,256]{1,0:T(8,128)(2,1)S(1)} %shard_map.120.refs_1_), channel_id=1, source_target_pairs={{0,192},{192,0},{64,128},{128,64},{1,193},{193,1},{65,129},{129,65... | collective-permute-start | bytes 393224 | tf_op jit(solution)/shard_map/ppermute | solution.py:321
  80.9 5.4 %collective-permute-start.25 = (bf16[256,128]{1,0:T(8,128)(2,1)S(1)}, bf16[256,128]{1,0:T(8,128)(2,1)S(1)}, u32[]{:S(2)}, u32[]{:S(2)}) collective-permute-start(bf16[256,128]{1,0:T(8,128)(2,1)S(1)} %get-tuple-element.85), channel_id=1, source_target_pairs={{0,48},{48,0},{16,32},{32,16},{1,49},{49,1},{17,33},{33,17},{2,50}... | collective-permute-start | bytes 196616 | tf_op jit(solution)/shard_map/ppermute | solution.py:321
  82.7 4.1 %collective-permute-start.23 = (bf16[256,128]{1,0:T(8,128)(2,1)S(1)}, bf16[256,128]{1,0:T(8,128)(2,1)S(1)}, u32[]{:S(2)}, u32[]{:S(2)}) collective-permute-start(bf16[256,128]{1,0:T(8,128)(2,1)S(1)} %get-tuple-element.81), channel_id=1, source_target_pairs={{0,16},{16,0},{32,48},{48,32},{1,17},{17,1},{33,49},{49,33},{2,18}... | collective-permute-start | bytes 196616 | tf_op jit(solution)/shard_map/ppermute | solution.py:317
  84.8 3.4 %collective-permute-start.29 = (bf16[128,256]{1,0:T(8,128)(2,1)S(1)}, bf16[128,256]{1,0:T(8,128)(2,1)S(1)}, u32[]{:S(2)}, u32[]{:S(2)}) collective-permute-start(bf16[128,256]{1,0:T(8,128)(2,1)S(1)} %get-tuple-element.90.refs_3_), channel_id=1, source_target_pairs={{0,64},{64,0},{128,192},{192,128},{1,65},{65,1},{129,193},{193,129... | collective-permute-start | bytes 196616 | tf_op jit(solution)/shard_map/ppermute | solution.py:317
  89.0 10.1 %collective-permute-start.33 = (bf16[256,1024]{1,0:T(8,128)(2,1)S(1)}, bf16[256,1024]{1,0:T(8,128)(2,1)S(1)}, u32[]{:S(2)}, u32[]{:S(2)}) collective-permute-start(bf16[256,1024]{1,0:T(8,128)(2,1)S(1)} %shard_map.122.here), channel_id=1, source_target_pairs={{0,1},{1,0},{2,3},{3,2},{4,5},{5,4},{6,7},{7,6},{8,9},{9,8},{10,11... | collective-permute-start | bytes 1572872 | tf_op jit(solution)/shard_map/ppermute | solution.py:333
  94.7 4.4 %collective-permute-start.30 = (bf16[384,128]{1,0:T(8,128)(2,1)S(1)}, bf16[384,128]{1,0:T(8,128)(2,1)S(1)}, u32[]{:S(2)}, u32[]{:S(2)}) collective-permute-start(bf16[384,128]{1,0:T(8,128)(2,1)S(1)} %get-tuple-element.92.refs_5_), channel_id=1, source_target_pairs={{0,8},{8,0},{1,9},{9,1},{2,10},{10,2},{3,11},{11,3},{4,12},{12,4},... | collective-permute-start | bytes 294920 | tf_op jit(solution)/shard_map/ppermute | solution.py:329

commit v5 on v4

--- a/solution.py
+++ b/solution.py
@@ -35,6 +35,7 @@
     specs = [pl.BlockSpec(memory_space=pltpu.SMEM)] * smem
     specs += [pl.BlockSpec(memory_space=space)] * (len(ins) - smem)
     used = len(ins)
+    out_spaces = out_space if isinstance(out_space, list) else [out_space] * len(outs)
     if after:
         specs += [pl.BlockSpec(memory_space=pl.ANY)] * len(after)
         inner = body
@@ -49,7 +50,7 @@
         body,
         out_shape=shapes,
         in_specs=specs,
-        out_specs=[pl.BlockSpec(memory_space=out_space)] * len(outs),
+        out_specs=[pl.BlockSpec(memory_space=place) for place in out_spaces],
         scratch_shapes=list(scratch),
         compiler_params=pltpu.CompilerParams(vmem_limit_bytes=vmem * 2**20),
         cost_estimate=pl.CostEstimate(flops=flops, bytes_accessed=moved, transcendentals=0),
@@ -288,27 +289,31 @@
         send[rows, :] = total[TILE:]
 
 
-def finish(
-    pos, mine, other, here, core, mix_mine, mix_other, q, k, v, weight, mixed,
-    heads, halves, rows_out, sems,
-):
+def weight_out(pos, here, core, mix_mine, mix_other, weight, mixed, flag, halves, rows_out, sems):
     copies = []
+    flag[...] = jnp.zeros_like(flag)
     for n, (half, ref) in enumerate(((pos[CORE], here), (1 - pos[CORE], core))):
         halves[n] = ref[...].astype(F32)
         columns = pl.ds(pl.multiple_of(half * 1024, 1024), 1024)
         copies.append(pltpu.make_async_copy(halves.at[n], weight.at[:, columns], sems.at[n]))
         copies[-1].start()
+    rows_out[...] = add(mix_mine[...], mix_other[...]).astype(BF16)
+    copies.append(pltpu.make_async_copy(rows_out, mixed, sems.at[2]))
+    copies[-1].start()
+    for copy in copies:
+        copy.wait()
+
+
+def join_heads(pos, mine, other, q, k, v, heads, sems):
     left = pl.ds(pl.multiple_of(pos[PAR] * HD, HD), HD)
     right = pl.ds(pl.multiple_of((1 - pos[PAR]) * HD, HD), HD)
+    copies = []
     for n, ref in enumerate((q, k, v)):
         rows = slice(n * TILE, (n + 1) * TILE)
         heads[n, :, left] = mine[rows, :]
         heads[n, :, right] = other[rows, :]
-        copies.append(pltpu.make_async_copy(heads.at[n], ref, sems.at[2 + n]))
+        copies.append(pltpu.make_async_copy(heads.at[n], ref, sems.at[n]))
         copies[-1].start()
-    rows_out[...] = add(mix_mine[...], mix_other[...]).astype(BF16)
-    copies.append(pltpu.make_async_copy(rows_out, mixed, sems.at[5]))
-    copies[-1].start()
     for copy in copies:
         copy.wait()
 
@@ -433,25 +438,25 @@
     (here,) = call(
         weight_row, [((2 * HD, 1024), BF16)], (pos, *stacks), after=(out_send,)
     )
-    grad_q, grad_k, grad_v, grad_weight, mixed = call(
-        finish,
-        [((TILE, 2 * HD), BF16)] * 3 + [((2 * HD, 2048), F32), ((32, 2048), BF16)],
-        (
-            pos,
-            out_keep,
-            over_pair(out_send),
-            here,
-            over_core(here),
-            mixed,
-            mixed_other,
-        ),
+    out_recv = over_pair(out_send)
+    grad_weight, mixed, written = call(
+        weight_out,
+        [((2 * HD, 2048), F32), ((32, 2048), BF16), ((8, HD), F32)],
+        (pos, here, over_core(here), mixed, mixed_other),
         scratch=[
-            pltpu.VMEM((3, TILE, 2 * HD), BF16),
             pltpu.VMEM((2, 2 * HD, 1024), F32),
             pltpu.VMEM((32, 2048), BF16),
-            pltpu.SemaphoreType.DMA((6,)),
+            pltpu.SemaphoreType.DMA((3,)),
         ],
+        out_space=[pl.ANY, pl.ANY, pltpu.VMEM],
+    )
+    grad_q, grad_k, grad_v = call(
+        join_heads,
+        [((TILE, 2 * HD), BF16)] * 3,
+        (pos, out_keep, out_recv),
+        scratch=[pltpu.VMEM((3, TILE, 2 * HD), BF16), pltpu.SemaphoreType.DMA((3,))],
         out_space=pl.ANY,
+        after=(written,),
     )
     return (mixed[None], grad_q[None], grad_k[None], grad_v[None], grad_weight)
 

time: 102 us -> 101 us (level)
  waiting for transfers between devices: 22 us -> 20 us
  Pallas kernels: 15 us -> 16.2 us
    ppermute x5, waiting for transfers between devices: 9.19 us -> 6.3 us  [over_pair(): return lax.ppermute(a, 'par', [(0, 1), (1, 0)])]
    pallas_call x23 -> x24, Pallas kernels: 15 us -> 16.2 us  [call(): pl.pallas_call(body, out_shape=shapes, in_specs=specs, out_specs=[pl.Bloc...]
  transfers between devices with their start and end apart: 34 -> 34, of which waited for: 15 -> 16; matrix products, arithmetic and copies ran while one was open for 2% -> 2% of each run, Pallas kernels for 10% -> 13%
where the time goes in v5:
time: 101 us; the launch traced here: 100 us
  starting transfers between devices  60.7 us (60%)
  waiting for transfers between devices  20 us (20%)
  Pallas kernels  16.2 us (16%)
  other arithmetic  1.62 us (2%)
  between operations  1.06 us (1%)
    ppermute x12, starting transfers between devices, far(): return lax.ppermute(a, axis, [(0, 3), (3, 0), (1, 2), (2, 1)])  21.9 us
    pallas_call x24, Pallas kernels, call(): pl.pallas_call(body, out_shape=shapes, in_specs=specs, out_specs=[pl.Bloc...  16.2 us
    ppermute x12, starting transfers between devices, near(): return lax.ppermute(a, axis, [(0, 1), (1, 0), (2, 3), (3, 2)])  15.1 us
    ppermute x2, starting transfers between devices, over_core(): return lax.ppermute(a, 'core', [(0, 1), (1, 0)])  11.3 us
    ppermute x12, waiting for transfers between devices, far(): return lax.ppermute(a, axis, [(0, 3), (3, 0), (1, 2), (2, 1)])  8.33 us
    ppermute x3, starting transfers between devices, opposite(): return lax.ppermute(a, axis, [(0, 2), (2, 0), (1, 3), (3, 1)])  6.75 us
    ppermute x5, waiting for transfers between devices, over_pair(): return lax.ppermute(a, 'par', [(0, 1), (1, 0)])  6.3 us
    ppermute x5, starting transfers between devices, over_pair(): return lax.ppermute(a, 'par', [(0, 1), (1, 0)])  5.58 us
  transfers between devices with their start and end apart: 34, of which 16 were waited for; matrix products, arithmetic and copies ran while one was open for 2% of the time, Pallas kernels for 13%

profile of v5, /device:TPU:1, one launch (start us, length us, event | category | flops | bytes accessed | tf_op | source)
XLA Modules:
  0.0 100.5 jit_solution(6825518665521669392)
XLA Ops:
  0.6 2.6 %collective-permute-start.10 = (bf16[32,2048]{1,0:T(8,128)(2,1)}, bf16[32,2048]{1,0:T(8,128)(2,1)S(1)}, u32[]{:S(2)}, u32[]{:S(2)}) collective-permute-start(bf16[32,2048]{1,0:T(8,128)(2,1)} %bitcast.13), channel_id=1, source_target_pairs={{0,8},{8,0},{1,9},{9,1},{2,10},{10,2},{3,11},{11,3},{4,12},{12,4},... | collective-permute-start | bytes 393224 | tf_op jit(solution)/shard_map/ppermute | solution.py:334
  3.2 0.8 broadcast_select_fusion.2
  4.0 0.8 broadcast_select_fusion
  4.8 0.1 collective-permute-start
  4.9 0.9 copy-done.1
  5.8 3.9 %collective-permute-done.recv.refs_2_ = bf16[384,128]{1,0:T(8,128)(2,1)S(1)} collective-permute-done((bf16[384,128]{1,0:T(8,128)(2,1)S(1)}, bf16[384,128]{1,0:T(8,128)(2,1)S(1)}, u32[]{:S(2)}, u32[]{:S(2)}) %collective-permute-start) | collective-permute-done | bytes 98336 | tf_op jit(solution)/shard_map/ppermute | solution.py:334
  9.7 0.1 collective-permute-start.11
  9.9 3.0 %collective-permute-start.1 = (bf16[256,128]{1,0:T(8,128)(2,1)S(1)}, bf16[256,128]{1,0:T(8,128)(2,1)S(1)}, u32[]{:S(2)}, u32[]{:S(2)}) collective-permute-start(bf16[256,128]{1,0:T(8,128)(2,1)S(1)} %get-tuple-element.53.k0), channel_id=1, source_target_pairs={{0,16},{16,0},{32,48},{48,32},{1,17},{17,1},{33,49},{49,33},{2,18}... | collective-permute-start | bytes 196616 | tf_op jit(solution)/shard_map/ppermute | solution.py:322
  12.9 4.3 %collective-permute-start.2 = (bf16[256,128]{1,0:T(8,128)(2,1)S(1)}, bf16[256,128]{1,0:T(8,128)(2,1)S(1)}, u32[]{:S(2)}, u32[]{:S(2)}) collective-permute-start(bf16[256,128]{1,0:T(8,128)(2,1)S(1)} %get-tuple-element.54.v0), channel_id=1, source_target_pairs={{0,48},{48,0},{16,32},{32,16},{1,49},{49,1},{17,33},{33,17},{2,50}... | collective-permute-start | bytes 196616 | tf_op jit(solution)/shard_map/ppermute | solution.py:326
  17.2 1.2 %collective-permute-start.3 = (bf16[256,128]{1,0:T(8,128)(2,1)S(1)}, bf16[256,128]{1,0:T(8,128)(2,1)S(1)}, u32[]{:S(2)}, u32[]{:S(2)}) collective-permute-start(bf16[256,128]{1,0:T(8,128)(2,1)S(1)} %get-tuple-element.55.q0), channel_id=1, source_target_pairs={{0,64},{64,0},{128,192},{192,128},{1,65},{65,1},{129,193},{193,129... | collective-permute-start | bytes 196616 | tf_op jit(solution)/shard_map/ppermute | solution.py:322
  18.4 1.0 collective-permute-done.2.v1
  19.4 0.9 collective-permute-done.3.q1
  20.4 2.0 %collective-permute-start.12 = (bf16[128,2048]{1,0:T(8,128)(2,1)S(1)}, bf16[128,2048]{1,0:T(8,128)(2,1)S(1)}, u32[]{:S(2)}, u32[]{:S(2)}) collective-permute-start(bf16[128,2048]{1,0:T(8,128)(2,1)S(1)} %shard_map.106.pair), channel_id=1, source_target_pairs={{0,6},{6,0},{2,4},{4,2},{1,7},{7,1},{3,5},{5,3},{8,14},{14,8},{10,... | collective-permute-start | bytes 1572872 | tf_op jit(solution)/shard_map/ppermute | solution.py:326
  22.4 1.5 %collective-permute-start.5 = (bf16[512,128]{1,0:T(8,128)(2,1)S(1)}, bf16[512,128]{1,0:T(8,128)(2,1)S(1)}, u32[]{:S(2)}, u32[]{:S(2)}) collective-permute-start(bf16[512,128]{1,0:T(8,128)(2,1)S(1)} %get-tuple-element.57.vp.refs_4_), channel_id=1, source_target_pairs={{0,16},{16,0},{32,48},{48,32},{1,17},{17,1},{33,49},{49,33},{2,18}... | collective-permute-start | bytes 393224 | tf_op jit(solution)/shard_map/ppermute | solution.py:322
  23.9 2.5 %collective-permute-start.6 = (bf16[512,128]{1,0:T(8,128)(2,1)S(1)}, bf16[512,128]{1,0:T(8,128)(2,1)S(1)}, u32[]{:S(2)}, u32[]{:S(2)}) collective-permute-start(bf16[512,128]{1,0:T(8,128)(2,1)S(1)} %get-tuple-element.58.qp.refs_6_), channel_id=1, source_target_pairs={{0,192},{192,0},{64,128},{128,64},{1,193},{193,1},{65,129},{129,65... | collective-permute-start | bytes 393224 | tf_op jit(solution)/shard_map/ppermute | solution.py:326
  26.4 2.2 %collective-permute-start.4 = (bf16[512,128]{1,0:T(8,128)(2,1)S(1)}, bf16[512,128]{1,0:T(8,128)(2,1)S(1)}, u32[]{:S(2)}, u32[]{:S(2)}) collective-permute-start(bf16[512,128]{1,0:T(8,128)(2,1)S(1)} %get-tuple-element.56.kp.refs_2_), channel_id=1, source_target_pairs={{0,48},{48,0},{16,32},{32,16},{1,49},{49,1},{17,33},{33,17},{2,50}... | collective-permute-start | bytes 393224 | tf_op jit(solution)/shard_map/ppermute | solution.py:326
  28.6 0.2 collective-permute-done.5.vn.refs_5_
  28.8 0.4 collective-permute-done.6.qf.refs_7_
  29.2 4.5 %collective-permute-done.4.kf.refs_3_ = bf16[512,128]{1,0:T(8,128)(2,1)S(1)} collective-permute-done((bf16[512,128]{1,0:T(8,128)(2,1)S(1)}, bf16[512,128]{1,0:T(8,128)(2,1)S(1)}, u32[]{:S(2)}, u32[]{:S(2)}) %collective-permute-start.4) | collective-permute-done | bytes 131104 | tf_op jit(solution)/shard_map/ppermute | solution.py:326
  33.7 3.0 %shard_map.103 = (bf16[144,256]{1,0:T(8,128)(2,1)S(1)}, bf16[144,256]{1,0:T(8,128)(2,1)S(1)}, bf16[144,256]{1,0:T(8,128)(2,1)S(1)}, bf16[144,256]{1,0:T(8,128)(2,1)S(1)}) custom-call(s32[5]{0:T(128)S(1)} %stack.23.pos.refs_0_, s32[32,32]{1,0:T(8,128)S(1)} %copy-done.2, bf16[512,128]{1,0:T(8,128)(2,1)S(1)} %get-tuple-element.56.kp.refs_2_, ...), custom_call_target="tpu_custom_call" | custom-call | flops 536870912 | bytes 1085460 | tf_op jit(solution)/shard_map/pallas_call | solution.py:49
  36.7 0.3 collective-permute-start.7
  37.0 3.0 %collective-permute-start.9 = (bf16[144,256]{1,0:T(8,128)(2,1)S(1)}, bf16[144,256]{1,0:T(8,128)(2,1)S(1)}, u32[]{:S(2)}, u32[]{:S(2)}) collective-permute-start(bf16[144,256]{1,0:T(8,128)(2,1)S(1)} %get-tuple-element.62), channel_id=1, source_target_pairs={{0,128},{128,0},{64,192},{192,64},{1,129},{129,1},{65,193},{193,65... | collective-permute-start | bytes 221192 | tf_op jit(solution)/shard_map/ppermute | solution.py:330
  40.1 0.6 shard_map.107
  40.7 1.0 shard_map.108.grads
  41.7 0.5 collective-permute-done.8.p2
  42.2 1.0 %shard_map.109 = (bf16[128,256]{1,0:T(8,128)(2,1)S(1)}, bf16[16,256]{1,0:T(8,128)(2,1)S(1)}, f32[128,1024]{1,0:T(8,128)S(1)}, bf16[128,1024]{1,0:T(8,128)(2,1)S(1)}) custom-call(s32[5]{0:T(128)S(1)} %stack.23.pos.refs_0_, bf16[144,256]{1,0:T(8,128)(2,1)S(1)} %get-tuple-element.59.p0, bf16[144,256]{1,0:T(8,128)(2,1)S(1)} %collective-permute-done.7.p1, ...), custom_call_target="tpu_custom_call" | custom-call | flops 134217728 | bytes 2269204 | tf_op jit(solution)/shard_map/pallas_call | solution.py:49
  43.3 5.5 %collective-permute-start.13 = (bf16[128,1024]{1,0:T(8,128)(2,1)S(1)}, bf16[128,1024]{1,0:T(8,128)(2,1)S(1)}, u32[]{:S(2)}, u32[]{:S(2)}) collective-permute-start(bf16[128,1024]{1,0:T(8,128)(2,1)S(1)} %get-tuple-element.66), channel_id=1, source_target_pairs={{0,1},{1,0},{2,3},{3,2},{4,5},{5,4},{6,7},{7,6},{8,9},{9,8},{10,11... | collective-permute-start | bytes 786440 | tf_op jit(solution)/shard_map/ppermute | solution.py:338
  48.8 1.2 %collective-permute-done.13.other = bf16[128,1024]{1,0:T(8,128)(2,1)S(1)} collective-permute-done((bf16[128,1024]{1,0:T(8,128)(2,1)S(1)}, bf16[128,1024]{1,0:T(8,128)(2,1)S(1)}, u32[]{:S(2)}, u32[]{:S(2)}) %collective-permute-start.13) | collective-permute-done | bytes 262176 | tf_op jit(solution)/shard_map/ppermute | solution.py:338
  50.0 0.6 shard_map.110
  50.6 0.5 collective-permute-start.14
  51.1 2.3 %collective-permute-start.15 = (bf16[272,256]{1,0:T(8,128)(2,1)S(1)}, bf16[272,256]{1,0:T(8,128)(2,1)S(1)}, u32[]{:S(2)}, u32[]{:S(2)}) collective-permute-start(bf16[272,256]{1,0:T(8,128)(2,1)S(1)} %get-tuple-element.70), channel_id=1, source_target_pairs={{0,192},{192,0},{64,128},{128,64},{1,193},{193,1},{65,129},{129,65... | collective-permute-start | bytes 417800 | tf_op jit(solution)/shard_map/ppermute | solution.py:326
  53.4 0.5 collective-permute-start.16
  54.0 2.0 %collective-permute-start.17 = (bf16[128,128]{1,0:T(8,128)(2,1)S(1)}, bf16[128,128]{1,0:T(8,128)(2,1)S(1)}, u32[]{:S(2)}, u32[]{:S(2)}) collective-permute-start(bf16[128,128]{1,0:T(8,128)(2,1)S(1)} %slice.33), channel_id=1, source_target_pairs={{0,8},{8,0},{1,9},{9,1},{2,10},{10,2},{3,11},{11,3},{4,12},{12,4},... | collective-permute-start | bytes 98312 | tf_op jit(solution)/shard_map/ppermute | solution.py:334
  56.0 1.6 %collective-permute-done.17.other = bf16[128,128]{1,0:T(8,128)(2,1)S(1)} collective-permute-done((bf16[128,128]{1,0:T(8,128)(2,1)S(1)}, bf16[128,128]{1,0:T(8,128)(2,1)S(1)}, u32[]{:S(2)}, u32[]{:S(2)}) %collective-permute-start.17) | collective-permute-done | bytes 32800 | tf_op jit(solution)/shard_map/ppermute | solution.py:334
  57.6 1.1 %shard_map.111 = (bf16[64,2048]{1,0:T(8,128)(2,1)S(1)}, bf16[64,2048]{1,0:T(8,128)(2,1)S(1)}) custom-call(s32[5]{0:T(128)S(1)} %stack.23.pos.refs_0_, bf16[128,256]{1,0:T(8,128)(2,1)S(1)} %get-tuple-element.72.att, bf16[128,128]{1,0:T(8,128)(2,1)S(1)} %collective-permute-done.17.other, bf16[256,2048]{1,0:T(8,128)(2,1)S(1)} %copy-done), custom_call_target="tpu_custom_call" | custom-call | flops 134217728 | bytes 1671188 | tf_op jit(solution)/shard_map/pallas_call | solution.py:49
  58.7 0.9 collective-permute-start.26
  59.5 0.2 collective-permute-done.16.refs_3_.refs_11_
  59.8 2.6 %collective-permute-start.18 = (bf16[128,256]{1,0:T(8,128)(2,1)S(1)}, bf16[128,256]{1,0:T(8,128)(2,1)S(1)}, u32[]{:S(2)}, u32[]{:S(2)}) collective-permute-start(bf16[128,256]{1,0:T(8,128)(2,1)S(1)} %shard_map.112.refs_12_.refs_0_), channel_id=1, source_target_pairs={{0,16},{16,0},{32,48},{48,32},{1,17},{17,1},{33,49},{49,33},{2,18}... | collective-permute-start | bytes 196616 | tf_op jit(solution)/shard_map/ppermute | solution.py:322
  62.3 4.0 %shard_map.113 = (bf16[512,128]{1,0:T(8,128)(2,1)S(1)}, bf16[512,128]{1,0:T(8,128)(2,1)S(1)}, bf16[512,128]{1,0:T(8,128)(2,1)S(1)}, bf16[512,128]{1,0:T(8,128)(2...) custom-call(s32[5]{0:T(128)S(1)} %stack.23.pos.refs_0_, s32[32,32]{1,0:T(8,128)S(1)} %copy-done.2, ...), custom_call_target="tpu_custom_call" | custom-call | flops 1342177280 | bytes 2134036 | tf_op jit(solution)/shard_map/pallas_call | solution.py:49
  66.4 1.3 %collective-permute-start.19 = (bf16[128,256]{1,0:T(8,128)(2,1)S(1)}, bf16[128,256]{1,0:T(8,128)(2,1)S(1)}, u32[]{:S(2)}, u32[]{:S(2)}) collective-permute-start(bf16[128,256]{1,0:T(8,128)(2,1)S(1)} %shard_map.114.a), channel_id=1, source_target_pairs={{0,48},{48,0},{16,32},{32,16},{1,49},{49,1},{17,33},{33,17},{2,50}... | collective-permute-start | bytes 196616 | tf_op jit(solution)/shard_map/ppermute | solution.py:326
  67.7 2.7 %collective-permute-start.21 = (bf16[256,256]{1,0:T(8,128)(2,1)S(1)}, bf16[256,256]{1,0:T(8,128)(2,1)S(1)}, u32[]{:S(2)}, u32[]{:S(2)}) collective-permute-start(bf16[256,256]{1,0:T(8,128)(2,1)S(1)} %get-tuple-element.76), channel_id=1, source_target_pairs={{0,192},{192,0},{64,128},{128,64},{1,193},{193,1},{65,129},{129,65... | collective-permute-start | bytes 393224 | tf_op jit(solution)/shard_map/ppermute | solution.py:326
  70.4 1.3 %collective-permute-done.19.b = bf16[128,256]{1,0:T(8,128)(2,1)S(1)} collective-permute-done((bf16[128,256]{1,0:T(8,128)(2,1)S(1)}, bf16[128,256]{1,0:T(8,128)(2,1)S(1)}, u32[]{:S(2)}, u32[]{:S(2)}) %collective-permute-start.19) | collective-permute-done | bytes 65568 | tf_op jit(solution)/shard_map/ppermute | solution.py:326
  71.7 0.2 collective-permute-start.20
  72.0 1.8 %collective-permute-start.29 = (bf16[512,128]{1,0:T(8,128)(2,1)S(1)}, bf16[512,128]{1,0:T(8,128)(2,1)S(1)}, u32[]{:S(2)}, u32[]{:S(2)}) collective-permute-start(bf16[512,128]{1,0:T(8,128)(2,1)S(1)} %get-tuple-element.87), channel_id=1, source_target_pairs={{0,16},{16,0},{32,48},{48,32},{1,17},{17,1},{33,49},{49,33},{2,18}... | collective-permute-start | bytes 393224 | tf_op jit(solution)/shard_map/ppermute | solution.py:322
  73.8 1.3 %collective-permute-start.25 = (bf16[512,128]{1,0:T(8,128)(2,1)S(1)}, bf16[512,128]{1,0:T(8,128)(2,1)S(1)}, u32[]{:S(2)}, u32[]{:S(2)}) collective-permute-start(bf16[512,128]{1,0:T(8,128)(2,1)S(1)} %get-tuple-element.81), channel_id=1, source_target_pairs={{0,48},{48,0},{16,32},{32,16},{1,49},{49,1},{17,33},{33,17},{2,50}... | collective-permute-start | bytes 393224 | tf_op jit(solution)/shard_map/ppermute | solution.py:326
  75.1 0.5 collective-permute-start.27
  75.7 0.6 shard_map.117.refs_1_
  76.2 0.8 collective-permute-start.22
  77.0 3.2 %collective-permute-start.24 = (bf16[256,256]{1,0:T(8,128)(2,1)S(1)}, bf16[256,256]{1,0:T(8,128)(2,1)S(1)}, u32[]{:S(2)}, u32[]{:S(2)}) collective-permute-start(bf16[256,256]{1,0:T(8,128)(2,1)S(1)} %shard_map.117.refs_1_), channel_id=1, source_target_pairs={{0,128},{128,0},{64,192},{192,64},{1,129},{129,1},{65,193},{193,65... | collective-permute-start | bytes 393224 | tf_op jit(solution)/shard_map/ppermute | solution.py:330
  80.2 0.7 collective-permute-start.23
  80.9 1.7 %collective-permute-start.30 = (bf16[256,128]{1,0:T(8,128)(2,1)S(1)}, bf16[256,128]{1,0:T(8,128)(2,1)S(1)}, u32[]{:S(2)}, u32[]{:S(2)}) collective-permute-start(bf16[256,128]{1,0:T(8,128)(2,1)S(1)} %get-tuple-element.89), channel_id=1, source_target_pairs={{0,48},{48,0},{16,32},{32,16},{1,49},{49,1},{17,33},{33,17},{2,50}... | collective-permute-start | bytes 196616 | tf_op jit(solution)/shard_map/ppermute | solution.py:326
  82.7 2.2 %collective-permute-start.28 = (bf16[256,128]{1,0:T(8,128)(2,1)S(1)}, bf16[256,128]{1,0:T(8,128)(2,1)S(1)}, u32[]{:S(2)}, u32[]{:S(2)}) collective-permute-start(bf16[256,128]{1,0:T(8,128)(2,1)S(1)} %get-tuple-element.85), channel_id=1, source_target_pairs={{0,16},{16,0},{32,48},{48,32},{1,17},{17,1},{33,49},{49,33},{2,18}... | collective-permute-start | bytes 196616 | tf_op jit(solution)/shard_map/ppermute | solution.py:322
  84.8 0.8 collective-permute-start.31
  85.6 0.7 collective-permute-done.30.v_far
  86.3 0.5 collective-permute-done.28.k_near
  86.8 1.5 %collective-permute-done.31.q_near = bf16[128,256]{1,0:T(8,128)(2,1)S(1)} collective-permute-done((bf16[128,256]{1,0:T(8,128)(2,1)S(1)}, bf16[128,256]{1,0:T(8,128)(2,1)S(1)}, u32[]{:S(2)}, u32[]{:S(2)}) %collective-permute-start.31) | collective-permute-done | bytes 65568 | tf_op jit(solution)/shard_map/ppermute | solution.py:322
  88.2 0.1 shard_map.121
  88.4 0.6 shard_map.122.here
  89.0 5.8 %collective-permute-start.32 = (bf16[256,1024]{1,0:T(8,128)(2,1)S(1)}, bf16[256,1024]{1,0:T(8,128)(2,1)S(1)}, u32[]{:S(2)}, u32[]{:S(2)}) collective-permute-start(bf16[256,1024]{1,0:T(8,128)(2,1)S(1)} %shard_map.122.here), channel_id=1, source_target_pairs={{0,1},{1,0},{2,3},{3,2},{4,5},{5,4},{6,7},{7,6},{8,9},{9,8},{10,11... | collective-permute-start | bytes 1572872 | tf_op jit(solution)/shard_map/ppermute | solution.py:338
  94.7 0.6 collective-permute-start.33
  95.4 0.9 collective-permute-done.32.core
  96.3 2.0 %shard_map.123 = (f32[256,2048]{1,0:T(8,128)}, bf16[32,2048]{1,0:T(8,128)(2,1)}, f32[8,128]{1,0:T(8,128)S(1)}) custom-call(s32[5]{0:T(128)S(1)} %stack.23.pos.refs_0_, bf16[256,1024]{1,0:T(8,128)(2,1)S(1)} %shard_map.122.here, bf16[256,1024]{1,0:T(8,128)(2,1)S(1)} %collective-permute-done.32.core, bf16[32,2048]{1,0:T(8,128)(2,1)S(1)} %get-tuple-element.93.mix_mine, ...), custom_call_target="tpu_custom_call" | custom-call | bytes 3543060 | tf_op jit(solution)/shard_map/pallas_call | solution.py:49
  98.3 0.8 collective-permute-done.33.refs_2_
  99.1 1.2 %shard_map.124 = (bf16[128,256]{1,0:T(8,128)(2,1)}, bf16[128,256]{1,0:T(8,128)(2,1)}, bf16[128,256]{1,0:T(8,128)(2,1)}) custom-call(s32[5]{0:T(128)S(1)} %stack.23.pos.refs_0_, bf16[384,128]{1,0:T(8,128)(2,1)S(1)} %get-tuple-element.95.refs_1_, bf16[384,128]{1,0:T(8,128)(2,1)S(1)} %collective-permute-done.33.refs_2_, f32[8,128]{1,0:T(8,128)S(1)} %get-tuple-element.96.refs_3_), custom_call_target="tpu_custom_call" | custom-call | bytes 393236 | tf_op jit(solution)/shard_map/pallas_call | solution.py:49
  (40 shorter events, 0.5 us)
Async XLA Ops:
  0.6 33.1 %copy-start.2 = (s32[32,32]{1,0:T(8,128)S(1)}, s32[32,32]{1,0:T(8,128)}, u32[]{:S(2)}) copy-start(s32[32,32]{1,0:T(8,128)} %refs_1_.1) | copy-start | bytes 12292
  0.6 9.1 %collective-permute-start.10 = (bf16[32,2048]{1,0:T(8,128)(2,1)}, bf16[32,2048]{1,0:T(8,128)(2,1)S(1)}, u32[]{:S(2)}, u32[]{:S(2)}) collective-permute-start(bf16[32,2048]{1,0:T(8,128)(2,1)} %bitcast.13), channel_id=1, source_target_pairs={{0,8},{8,0},{1,9},{9,1},{2,10},{10,2},{3,11},{11,3},{4,12},{12,4},... | collective-permute-start | bytes 393224 | tf_op jit(solution)/shard_map/ppermute | solution.py:334
  4.8 4.9 %collective-permute-start = (bf16[384,128]{1,0:T(8,128)(2,1)S(1)}, bf16[384,128]{1,0:T(8,128)(2,1)S(1)}, u32[]{:S(2)}, u32[]{:S(2)}) collective-permute-start(bf16[384,128]{1,0:T(8,128)(2,1)S(1)} %pad_maximum_fusion.1.refs_1_), channel_id=1, source_target_pairs={{0,8},{8,0},{1,9},{9,1},{2,10},{10,2},{3,11},{11,3},{4,12},{12,4},... | collective-permute-start | bytes 294920 | tf_op jit(solution)/shard_map/ppermute | solution.py:334
  4.9 0.9 copy-start.1
  9.7 10.6 %collective-permute-start.11 = (bf16[64,2048]{1,0:T(8,128)(2,1)S(1)}, bf16[64,2048]{1,0:T(8,128)(2,1)S(1)}, u32[]{:S(2)}, u32[]{:S(2)}) collective-permute-start(bf16[64,2048]{1,0:T(8,128)(2,1)S(1)} %shard_map.105.refs_0_), channel_id=1, source_target_pairs={{0,2},{2,0},{4,6},{6,4},{1,3},{3,1},{5,7},{7,5},{8,10},{10,8},{12,... | collective-permute-start | bytes 786440 | tf_op jit(solution)/shard_map/ppermute | solution.py:322
  9.9 8.5 %collective-permute-start.1 = (bf16[256,128]{1,0:T(8,128)(2,1)S(1)}, bf16[256,128]{1,0:T(8,128)(2,1)S(1)}, u32[]{:S(2)}, u32[]{:S(2)}) collective-permute-start(bf16[256,128]{1,0:T(8,128)(2,1)S(1)} %get-tuple-element.53.k0), channel_id=1, source_target_pairs={{0,16},{16,0},{32,48},{48,32},{1,17},{17,1},{33,49},{49,33},{2,18}... | collective-permute-start | bytes 196616 | tf_op jit(solution)/shard_map/ppermute | solution.py:322
  12.9 6.5 %collective-permute-start.2 = (bf16[256,128]{1,0:T(8,128)(2,1)S(1)}, bf16[256,128]{1,0:T(8,128)(2,1)S(1)}, u32[]{:S(2)}, u32[]{:S(2)}) collective-permute-start(bf16[256,128]{1,0:T(8,128)(2,1)S(1)} %get-tuple-element.54.v0), channel_id=1, source_target_pairs={{0,48},{48,0},{16,32},{32,16},{1,49},{49,1},{17,33},{33,17},{2,50}... | collective-permute-start | bytes 196616 | tf_op jit(solution)/shard_map/ppermute | solution.py:326
  17.2 3.1 %collective-permute-start.3 = (bf16[256,128]{1,0:T(8,128)(2,1)S(1)}, bf16[256,128]{1,0:T(8,128)(2,1)S(1)}, u32[]{:S(2)}, u32[]{:S(2)}) collective-permute-start(bf16[256,128]{1,0:T(8,128)(2,1)S(1)} %get-tuple-element.55.q0), channel_id=1, source_target_pairs={{0,64},{64,0},{128,192},{192,128},{1,65},{65,1},{129,193},{193,129... | collective-permute-start | bytes 196616 | tf_op jit(solution)/shard_map/ppermute | solution.py:322
  20.4 20.3 %copy-start = (bf16[256,2048]{1,0:T(8,128)(2,1)S(1)}, bf16[256,2048]{1,0:T(8,128)(2,1)}, u32[]{:S(2)}) copy-start(bf16[256,2048]{1,0:T(8,128)(2,1)} %w.3) | copy-start | bytes 3145732
  20.4 19.7 %collective-permute-start.12 = (bf16[128,2048]{1,0:T(8,128)(2,1)S(1)}, bf16[128,2048]{1,0:T(8,128)(2,1)S(1)}, u32[]{:S(2)}, u32[]{:S(2)}) collective-permute-start(bf16[128,2048]{1,0:T(8,128)(2,1)S(1)} %shard_map.106.pair), channel_id=1, source_target_pairs={{0,6},{6,0},{2,4},{4,2},{1,7},{7,1},{3,5},{5,3},{8,14},{14,8},{10,... | collective-permute-start | bytes 1572872 | tf_op jit(solution)/shard_map/ppermute | solution.py:326
  22.4 6.4 %collective-permute-start.5 = (bf16[512,128]{1,0:T(8,128)(2,1)S(1)}, bf16[512,128]{1,0:T(8,128)(2,1)S(1)}, u32[]{:S(2)}, u32[]{:S(2)}) collective-permute-start(bf16[512,128]{1,0:T(8,128)(2,1)S(1)} %get-tuple-element.57.vp.refs_4_), channel_id=1, source_target_pairs={{0,16},{16,0},{32,48},{48,32},{1,17},{17,1},{33,49},{49,33},{2,18}... | collective-permute-start | bytes 393224 | tf_op jit(solution)/shard_map/ppermute | solution.py:322
  23.9 5.3 %collective-permute-start.6 = (bf16[512,128]{1,0:T(8,128)(2,1)S(1)}, bf16[512,128]{1,0:T(8,128)(2,1)S(1)}, u32[]{:S(2)}, u32[]{:S(2)}) collective-permute-start(bf16[512,128]{1,0:T(8,128)(2,1)S(1)} %get-tuple-element.58.qp.refs_6_), channel_id=1, source_target_pairs={{0,192},{192,0},{64,128},{128,64},{1,193},{193,1},{65,129},{129,65... | collective-permute-start | bytes 393224 | tf_op jit(solution)/shard_map/ppermute | solution.py:326
  26.4 7.3 %collective-permute-start.4 = (bf16[512,128]{1,0:T(8,128)(2,1)S(1)}, bf16[512,128]{1,0:T(8,128)(2,1)S(1)}, u32[]{:S(2)}, u32[]{:S(2)}) collective-permute-start(bf16[512,128]{1,0:T(8,128)(2,1)S(1)} %get-tuple-element.56.kp.refs_2_), channel_id=1, source_target_pairs={{0,48},{48,0},{16,32},{32,16},{1,49},{49,1},{17,33},{33,17},{2,50}... | collective-permute-start | bytes 393224 | tf_op jit(solution)/shard_map/ppermute | solution.py:326
  36.7 5.0 %collective-permute-start.7 = (bf16[144,256]{1,0:T(8,128)(2,1)S(1)}, bf16[144,256]{1,0:T(8,128)(2,1)S(1)}, u32[]{:S(2)}, u32[]{:S(2)}) collective-permute-start(bf16[144,256]{1,0:T(8,128)(2,1)S(1)} %get-tuple-element.60), channel_id=1, source_target_pairs={{0,64},{64,0},{128,192},{192,128},{1,65},{65,1},{129,193},{193,129... | collective-permute-start | bytes 221192 | tf_op jit(solution)/shard_map/ppermute | solution.py:322
  37.0 5.2 %collective-permute-start.8 = (bf16[144,256]{1,0:T(8,128)(2,1)S(1)}, bf16[144,256]{1,0:T(8,128)(2,1)S(1)}, u32[]{:S(2)}, u32[]{:S(2)}) collective-permute-start(bf16[144,256]{1,0:T(8,128)(2,1)S(1)} %get-tuple-element.61), channel_id=1, source_target_pairs={{0,192},{192,0},{64,128},{128,64},{1,193},{193,1},{65,129},{129,65... | collective-permute-start | bytes 221192 | tf_op jit(solution)/shard_map/ppermute | solution.py:326
  37.0 5.2 %collective-permute-start.9 = (bf16[144,256]{1,0:T(8,128)(2,1)S(1)}, bf16[144,256]{1,0:T(8,128)(2,1)S(1)}, u32[]{:S(2)}, u32[]{:S(2)}) collective-permute-start(bf16[144,256]{1,0:T(8,128)(2,1)S(1)} %get-tuple-element.62), channel_id=1, source_target_pairs={{0,128},{128,0},{64,192},{192,64},{1,129},{129,1},{65,193},{193,65... | collective-permute-start | bytes 221192 | tf_op jit(solution)/shard_map/ppermute | solution.py:330
  43.3 6.7 %collective-permute-start.13 = (bf16[128,1024]{1,0:T(8,128)(2,1)S(1)}, bf16[128,1024]{1,0:T(8,128)(2,1)S(1)}, u32[]{:S(2)}, u32[]{:S(2)}) collective-permute-start(bf16[128,1024]{1,0:T(8,128)(2,1)S(1)} %get-tuple-element.66), channel_id=1, source_target_pairs={{0,1},{1,0},{2,3},{3,2},{4,5},{5,4},{6,7},{7,6},{8,9},{9,8},{10,11... | collective-permute-start | bytes 786440 | tf_op jit(solution)/shard_map/ppermute | solution.py:338
  50.6 8.9 %collective-permute-start.14 = (bf16[272,256]{1,0:T(8,128)(2,1)S(1)}, bf16[272,256]{1,0:T(8,128)(2,1)S(1)}, u32[]{:S(2)}, u32[]{:S(2)}) collective-permute-start(bf16[272,256]{1,0:T(8,128)(2,1)S(1)} %get-tuple-element.69), channel_id=1, source_target_pairs={{0,64},{64,0},{128,192},{192,128},{1,65},{65,1},{129,193},{193,129... | collective-permute-start | bytes 417800 | tf_op jit(solution)/shard_map/ppermute | solution.py:322
  51.1 8.5 %collective-permute-start.15 = (bf16[272,256]{1,0:T(8,128)(2,1)S(1)}, bf16[272,256]{1,0:T(8,128)(2,1)S(1)}, u32[]{:S(2)}, u32[]{:S(2)}) collective-permute-start(bf16[272,256]{1,0:T(8,128)(2,1)S(1)} %get-tuple-element.70), channel_id=1, source_target_pairs={{0,192},{192,0},{64,128},{128,64},{1,193},{193,1},{65,129},{129,65... | collective-permute-start | bytes 417800 | tf_op jit(solution)/shard_map/ppermute | solution.py:326
  53.4 6.3 %collective-permute-start.16 = (bf16[272,256]{1,0:T(8,128)(2,1)S(1)}, bf16[272,256]{1,0:T(8,128)(2,1)S(1)}, u32[]{:S(2)}, u32[]{:S(2)}) collective-permute-start(bf16[272,256]{1,0:T(8,128)(2,1)S(1)} %get-tuple-element.71), channel_id=1, source_target_pairs={{0,128},{128,0},{64,192},{192,64},{1,129},{129,1},{65,193},{193,65... | collective-permute-start | bytes 417800 | tf_op jit(solution)/shard_map/ppermute | solution.py:330
  54.0 3.6 %collective-permute-start.17 = (bf16[128,128]{1,0:T(8,128)(2,1)S(1)}, bf16[128,128]{1,0:T(8,128)(2,1)S(1)}, u32[]{:S(2)}, u32[]{:S(2)}) collective-permute-start(bf16[128,128]{1,0:T(8,128)(2,1)S(1)} %slice.33), channel_id=1, source_target_pairs={{0,8},{8,0},{1,9},{9,1},{2,10},{10,2},{3,11},{11,3},{4,12},{12,4},... | collective-permute-start | bytes 98312 | tf_op jit(solution)/shard_map/ppermute | solution.py:334
  58.7 16.4 %collective-permute-start.26 = (bf16[64,2048]{1,0:T(8,128)(2,1)S(1)}, bf16[64,2048]{1,0:T(8,128)(2,1)S(1)}, u32[]{:S(2)}, u32[]{:S(2)}) collective-permute-start(bf16[64,2048]{1,0:T(8,128)(2,1)S(1)} %get-tuple-element.73.refs_4_), channel_id=1, source_target_pairs={{0,6},{6,0},{2,4},{4,2},{1,7},{7,1},{3,5},{5,3},{8,14},{14,8},{10,... | collective-permute-start | bytes 786440 | tf_op jit(solution)/shard_map/ppermute | solution.py:326
  59.8 6.6 %collective-permute-start.18 = (bf16[128,256]{1,0:T(8,128)(2,1)S(1)}, bf16[128,256]{1,0:T(8,128)(2,1)S(1)}, u32[]{:S(2)}, u32[]{:S(2)}) collective-permute-start(bf16[128,256]{1,0:T(8,128)(2,1)S(1)} %shard_map.112.refs_12_.refs_0_), channel_id=1, source_target_pairs={{0,16},{16,0},{32,48},{48,32},{1,17},{17,1},{33,49},{49,33},{2,18}... | collective-permute-start | bytes 196616 | tf_op jit(solution)/shard_map/ppermute | solution.py:322
  66.4 5.3 %collective-permute-start.19 = (bf16[128,256]{1,0:T(8,128)(2,1)S(1)}, bf16[128,256]{1,0:T(8,128)(2,1)S(1)}, u32[]{:S(2)}, u32[]{:S(2)}) collective-permute-start(bf16[128,256]{1,0:T(8,128)(2,1)S(1)} %shard_map.114.a), channel_id=1, source_target_pairs={{0,48},{48,0},{16,32},{32,16},{1,49},{49,1},{17,33},{33,17},{2,50}... | collective-permute-start | bytes 196616 | tf_op jit(solution)/shard_map/ppermute | solution.py:326
  67.7 7.9 %collective-permute-start.21 = (bf16[256,256]{1,0:T(8,128)(2,1)S(1)}, bf16[256,256]{1,0:T(8,128)(2,1)S(1)}, u32[]{:S(2)}, u32[]{:S(2)}) collective-permute-start(bf16[256,256]{1,0:T(8,128)(2,1)S(1)} %get-tuple-element.76), channel_id=1, source_target_pairs={{0,192},{192,0},{64,128},{128,64},{1,193},{193,1},{65,129},{129,65... | collective-permute-start | bytes 393224 | tf_op jit(solution)/shard_map/ppermute | solution.py:326
  71.7 3.9 %collective-permute-start.20 = (bf16[128,256]{1,0:T(8,128)(2,1)S(1)}, bf16[128,256]{1,0:T(8,128)(2,1)S(1)}, u32[]{:S(2)}, u32[]{:S(2)}) collective-permute-start(bf16[128,256]{1,0:T(8,128)(2,1)S(1)} %shard_map.115.refs_1_.refs_2_), channel_id=1, source_target_pairs={{0,8},{8,0},{1,9},{9,1},{2,10},{10,2},{3,11},{11,3},{4,12},{12,4},... | collective-permute-start | bytes 196616 | tf_op jit(solution)/shard_map/ppermute | solution.py:334
  72.0 8.2 %collective-permute-start.29 = (bf16[512,128]{1,0:T(8,128)(2,1)S(1)}, bf16[512,128]{1,0:T(8,128)(2,1)S(1)}, u32[]{:S(2)}, u32[]{:S(2)}) collective-permute-start(bf16[512,128]{1,0:T(8,128)(2,1)S(1)} %get-tuple-element.87), channel_id=1, source_target_pairs={{0,16},{16,0},{32,48},{48,32},{1,17},{17,1},{33,49},{49,33},{2,18}... | collective-permute-start | bytes 393224 | tf_op jit(solution)/shard_map/ppermute | solution.py:322
  73.8 7.1 %collective-permute-start.25 = (bf16[512,128]{1,0:T(8,128)(2,1)S(1)}, bf16[512,128]{1,0:T(8,128)(2,1)S(1)}, u32[]{:S(2)}, u32[]{:S(2)}) collective-permute-start(bf16[512,128]{1,0:T(8,128)(2,1)S(1)} %get-tuple-element.81), channel_id=1, source_target_pairs={{0,48},{48,0},{16,32},{32,16},{1,49},{49,1},{17,33},{33,17},{2,50}... | collective-permute-start | bytes 393224 | tf_op jit(solution)/shard_map/ppermute | solution.py:326
  75.1 7.5 %collective-permute-start.27 = (bf16[32,2048]{1,0:T(8,128)(2,1)S(1)}, bf16[32,2048]{1,0:T(8,128)(2,1)S(1)}, u32[]{:S(2)}, u32[]{:S(2)}) collective-permute-start(bf16[32,2048]{1,0:T(8,128)(2,1)S(1)} %get-tuple-element.83), channel_id=1, source_target_pairs={{0,2},{2,0},{4,6},{6,4},{1,3},{3,1},{5,7},{7,5},{8,10},{10,8},{12,... | collective-permute-start | bytes 393224 | tf_op jit(solution)/shard_map/ppermute | solution.py:322
  76.2 8.6 %collective-permute-start.22 = (bf16[256,256]{1,0:T(8,128)(2,1)S(1)}, bf16[256,256]{1,0:T(8,128)(2,1)S(1)}, u32[]{:S(2)}, u32[]{:S(2)}) collective-permute-start(bf16[256,256]{1,0:T(8,128)(2,1)S(1)} %shard_map.117.refs_1_), channel_id=1, source_target_pairs={{0,64},{64,0},{128,192},{192,128},{1,65},{65,1},{129,193},{193,129... | collective-permute-start | bytes 393224 | tf_op jit(solution)/shard_map/ppermute | solution.py:322
  77.0 11.3 %collective-permute-start.24 = (bf16[256,256]{1,0:T(8,128)(2,1)S(1)}, bf16[256,256]{1,0:T(8,128)(2,1)S(1)}, u32[]{:S(2)}, u32[]{:S(2)}) collective-permute-start(bf16[256,256]{1,0:T(8,128)(2,1)S(1)} %shard_map.117.refs_1_), channel_id=1, source_target_pairs={{0,128},{128,0},{64,192},{192,64},{1,129},{129,1},{65,193},{193,65... | collective-permute-start | bytes 393224 | tf_op jit(solution)/shard_map/ppermute | solution.py:330
  80.2 8.2 %collective-permute-start.23 = (bf16[256,256]{1,0:T(8,128)(2,1)S(1)}, bf16[256,256]{1,0:T(8,128)(2,1)S(1)}, u32[]{:S(2)}, u32[]{:S(2)}) collective-permute-start(bf16[256,256]{1,0:T(8,128)(2,1)S(1)} %shard_map.117.refs_1_), channel_id=1, source_target_pairs={{0,192},{192,0},{64,128},{128,64},{1,193},{193,1},{65,129},{129,65... | collective-permute-start | bytes 393224 | tf_op jit(solution)/shard_map/ppermute | solution.py:326
  80.9 5.4 %collective-permute-start.30 = (bf16[256,128]{1,0:T(8,128)(2,1)S(1)}, bf16[256,128]{1,0:T(8,128)(2,1)S(1)}, u32[]{:S(2)}, u32[]{:S(2)}) collective-permute-start(bf16[256,128]{1,0:T(8,128)(2,1)S(1)} %get-tuple-element.89), channel_id=1, source_target_pairs={{0,48},{48,0},{16,32},{32,16},{1,49},{49,1},{17,33},{33,17},{2,50}... | collective-permute-start | bytes 196616 | tf_op jit(solution)/shard_map/ppermute | solution.py:326
  82.7 4.1 %collective-permute-start.28 = (bf16[256,128]{1,0:T(8,128)(2,1)S(1)}, bf16[256,128]{1,0:T(8,128)(2,1)S(1)}, u32[]{:S(2)}, u32[]{:S(2)}) collective-permute-start(bf16[256,128]{1,0:T(8,128)(2,1)S(1)} %get-tuple-element.85), channel_id=1, source_target_pairs={{0,16},{16,0},{32,48},{48,32},{1,17},{17,1},{33,49},{49,33},{2,18}... | collective-permute-start | bytes 196616 | tf_op jit(solution)/shard_map/ppermute | solution.py:322
  84.8 3.4 %collective-permute-start.31 = (bf16[128,256]{1,0:T(8,128)(2,1)S(1)}, bf16[128,256]{1,0:T(8,128)(2,1)S(1)}, u32[]{:S(2)}, u32[]{:S(2)}) collective-permute-start(bf16[128,256]{1,0:T(8,128)(2,1)S(1)} %get-tuple-element.91.refs_3_), channel_id=1, source_target_pairs={{0,64},{64,0},{128,192},{192,128},{1,65},{65,1},{129,193},{193,129... | collective-permute-start | bytes 196616 | tf_op jit(solution)/shard_map/ppermute | solution.py:322
  89.0 7.3 %collective-permute-start.32 = (bf16[256,1024]{1,0:T(8,128)(2,1)S(1)}, bf16[256,1024]{1,0:T(8,128)(2,1)S(1)}, u32[]{:S(2)}, u32[]{:S(2)}) collective-permute-start(bf16[256,1024]{1,0:T(8,128)(2,1)S(1)} %shard_map.122.here), channel_id=1, source_target_pairs={{0,1},{1,0},{2,3},{3,2},{4,5},{5,4},{6,7},{7,6},{8,9},{9,8},{10,11... | collective-permute-start | bytes 1572872 | tf_op jit(solution)/shard_map/ppermute | solution.py:338
  94.7 4.4 %collective-permute-start.33 = (bf16[384,128]{1,0:T(8,128)(2,1)S(1)}, bf16[384,128]{1,0:T(8,128)(2,1)S(1)}, u32[]{:S(2)}, u32[]{:S(2)}) collective-permute-start(bf16[384,128]{1,0:T(8,128)(2,1)S(1)} %get-tuple-element.92.refs_5_), channel_id=1, source_target_pairs={{0,8},{8,0},{1,9},{9,1},{2,10},{10,2},{3,11},{11,3},{4,12},{12,4},... | collective-permute-start | bytes 294920 | tf_op jit(solution)/shard_map/ppermute | solution.py:334

commit v6 on v5

--- a/solution.py
+++ b/solution.py
@@ -28,10 +28,22 @@
     return lax.dot_general(a, b, dims, preferred_element_type=F32)
 
 
+class Position:
+    def __getitem__(self, n):
+        return lax.axis_index(AXES[n])
+
+
 def call(
     body, outs, ins, flops=0, scratch=(), smem=1, vmem=48, after=(), space=pltpu.VMEM,
     out_space=pltpu.VMEM,
 ):
+    if isinstance(ins[0], Position):
+        place, placed = ins[0], body
+        ins, smem = ins[1:], smem - 1
+
+        def body(*refs):
+            placed(place, *refs)
+
     specs = [pl.BlockSpec(memory_space=pltpu.SMEM)] * smem
     specs += [pl.BlockSpec(memory_space=space)] * (len(ins) - smem)
     used = len(ins)
@@ -339,7 +351,7 @@
 
 
 def on_device(query_rows, key_rows, value_rows, out_weight, cotangent, tile_mask):
-    pos = jnp.stack([lax.axis_index(name) for name in AXES]).astype(jnp.int32)
+    pos = Position()
     kv_mm = 2 * 1024 * 1024 * HD
 
     inputs = (query_rows[0], key_rows[0], value_rows[0])

time: 101 us -> 98.5 us (0.975)
  Pallas kernels: 16.2 us -> 11.3 us
  waiting for transfers between devices: 20 us -> 22.3 us
    pallas_call x24, Pallas kernels: 16.2 us -> 11.3 us  [call(): pl.pallas_call(body, out_shape=shapes, in_specs=specs, out_specs=[pl.Bloc...]
    ppermute x12, waiting for transfers between devices: 8.33 us -> 9.37 us  [far(): return lax.ppermute(a, axis, [(0, 3), (3, 0), (1, 2), (2, 1)])]
  transfers between devices with their start and end apart: 34 -> 34, of which waited for: 16 -> 16; matrix products, arithmetic and copies ran while one was open for 2% -> 2% of each run, Pallas kernels for 13% -> 10%
where the time goes in v6:
time: 98.5 us; the launch traced here: 98.2 us
  starting transfers between devices  61 us (62%)
  waiting for transfers between devices  22.3 us (23%)
  Pallas kernels  11.3 us (11%)
  other arithmetic  1.62 us (2%)
  between operations  1.05 us (1%)
    ppermute x12, starting transfers between devices, far(): return lax.ppermute(a, axis, [(0, 3), (3, 0), (1, 2), (2, 1)])  22 us
    ppermute x12, starting transfers between devices, near(): return lax.ppermute(a, axis, [(0, 1), (1, 0), (2, 3), (3, 2)])  15.5 us
    pallas_call x24, Pallas kernels, call(): pl.pallas_call(body, out_shape=shapes, in_specs=specs, out_specs=[pl.Bloc...  11.3 us
    ppermute x2, starting transfers between devices, over_core(): return lax.ppermute(a, 'core', [(0, 1), (1, 0)])  11.2 us
    ppermute x12, waiting for transfers between devices, far(): return lax.ppermute(a, axis, [(0, 3), (3, 0), (1, 2), (2, 1)])  9.37 us
    ppermute x5, waiting for transfers between devices, over_pair(): return lax.ppermute(a, 'par', [(0, 1), (1, 0)])  6.85 us
    ppermute x3, starting transfers between devices, opposite(): return lax.ppermute(a, axis, [(0, 2), (2, 0), (1, 3), (3, 1)])  6.75 us
    ppermute x5, starting transfers between devices, over_pair(): return lax.ppermute(a, 'par', [(0, 1), (1, 0)])  5.57 us
  transfers between devices with their start and end apart: 34, of which 16 were waited for; matrix products, arithmetic and copies ran while one was open for 2% of the time, Pallas kernels for 10%

profile of v6, /device:TPU:1, one launch (start us, length us, event | category | flops | bytes accessed | tf_op | source)
XLA Modules:
  0.0 98.2 jit_solution(17194325120764915653)
XLA Ops:
  0.6 2.6 %collective-permute-start.10 = (bf16[32,2048]{1,0:T(8,128)(2,1)}, bf16[32,2048]{1,0:T(8,128)(2,1)S(1)}, u32[]{:S(2)}, u32[]{:S(2)}) collective-permute-start(bf16[32,2048]{1,0:T(8,128)(2,1)} %bitcast.8), channel_id=1, source_target_pairs={{0,8},{8,0},{1,9},{9,1},{2,10},{10,2},{3,11},{11,3},{4,12},{12,4},... | collective-permute-start | bytes 393224 | tf_op jit(solution)/shard_map/ppermute | solution.py:346
  3.2 0.8 broadcast_select_fusion.2
  4.0 0.8 broadcast_select_fusion
  4.8 0.1 collective-permute-start
  4.9 0.9 copy-done.1
  5.8 3.9 %collective-permute-done.recv.refs_2_ = bf16[384,128]{1,0:T(8,128)(2,1)S(1)} collective-permute-done((bf16[384,128]{1,0:T(8,128)(2,1)S(1)}, bf16[384,128]{1,0:T(8,128)(2,1)S(1)}, u32[]{:S(2)}, u32[]{:S(2)}) %collective-permute-start) | collective-permute-done | bytes 98336 | tf_op jit(solution)/shard_map/ppermute | solution.py:346
  9.7 0.1 collective-permute-start.11
  9.9 3.0 %collective-permute-start.1 = (bf16[256,128]{1,0:T(8,128)(2,1)S(1)}, bf16[256,128]{1,0:T(8,128)(2,1)S(1)}, u32[]{:S(2)}, u32[]{:S(2)}) collective-permute-start(bf16[256,128]{1,0:T(8,128)(2,1)S(1)} %get-tuple-element.53.k0), channel_id=1, source_target_pairs={{0,16},{16,0},{32,48},{48,32},{1,17},{17,1},{33,49},{49,33},{2,18}... | collective-permute-start | bytes 196616 | tf_op jit(solution)/shard_map/ppermute | solution.py:334
  12.9 4.3 %collective-permute-start.2 = (bf16[256,128]{1,0:T(8,128)(2,1)S(1)}, bf16[256,128]{1,0:T(8,128)(2,1)S(1)}, u32[]{:S(2)}, u32[]{:S(2)}) collective-permute-start(bf16[256,128]{1,0:T(8,128)(2,1)S(1)} %get-tuple-element.54.v0), channel_id=1, source_target_pairs={{0,48},{48,0},{16,32},{32,16},{1,49},{49,1},{17,33},{33,17},{2,50}... | collective-permute-start | bytes 196616 | tf_op jit(solution)/shard_map/ppermute | solution.py:338
  17.2 1.2 %collective-permute-start.3 = (bf16[256,128]{1,0:T(8,128)(2,1)S(1)}, bf16[256,128]{1,0:T(8,128)(2,1)S(1)}, u32[]{:S(2)}, u32[]{:S(2)}) collective-permute-start(bf16[256,128]{1,0:T(8,128)(2,1)S(1)} %get-tuple-element.55.q0), channel_id=1, source_target_pairs={{0,64},{64,0},{128,192},{192,128},{1,65},{65,1},{129,193},{193,129... | collective-permute-start | bytes 196616 | tf_op jit(solution)/shard_map/ppermute | solution.py:334
  18.4 1.0 collective-permute-done.2.v1
  19.4 0.9 collective-permute-done.3.q1
  20.4 2.0 %collective-permute-start.12 = (bf16[128,2048]{1,0:T(8,128)(2,1)S(1)}, bf16[128,2048]{1,0:T(8,128)(2,1)S(1)}, u32[]{:S(2)}, u32[]{:S(2)}) collective-permute-start(bf16[128,2048]{1,0:T(8,128)(2,1)S(1)} %shard_map.106.refs_0_), channel_id=1, source_target_pairs={{0,6},{6,0},{2,4},{4,2},{1,7},{7,1},{3,5},{5,3},{8,14},{14,8},{10,... | collective-permute-start | bytes 1572872 | tf_op jit(solution)/shard_map/ppermute | solution.py:338
  22.4 1.5 %collective-permute-start.5 = (bf16[512,128]{1,0:T(8,128)(2,1)S(1)}, bf16[512,128]{1,0:T(8,128)(2,1)S(1)}, u32[]{:S(2)}, u32[]{:S(2)}) collective-permute-start(bf16[512,128]{1,0:T(8,128)(2,1)S(1)} %get-tuple-element.57.refs_3_), channel_id=1, source_target_pairs={{0,16},{16,0},{32,48},{48,32},{1,17},{17,1},{33,49},{49,33},{2,18}... | collective-permute-start | bytes 393224 | tf_op jit(solution)/shard_map/ppermute | solution.py:334
  23.9 2.5 %collective-permute-start.6 = (bf16[512,128]{1,0:T(8,128)(2,1)S(1)}, bf16[512,128]{1,0:T(8,128)(2,1)S(1)}, u32[]{:S(2)}, u32[]{:S(2)}) collective-permute-start(bf16[512,128]{1,0:T(8,128)(2,1)S(1)} %get-tuple-element.58.refs_5_), channel_id=1, source_target_pairs={{0,192},{192,0},{64,128},{128,64},{1,193},{193,1},{65,129},{129,65... | collective-permute-start | bytes 393224 | tf_op jit(solution)/shard_map/ppermute | solution.py:338
  26.4 2.2 %collective-permute-start.4 = (bf16[512,128]{1,0:T(8,128)(2,1)S(1)}, bf16[512,128]{1,0:T(8,128)(2,1)S(1)}, u32[]{:S(2)}, u32[]{:S(2)}) collective-permute-start(bf16[512,128]{1,0:T(8,128)(2,1)S(1)} %get-tuple-element.56.refs_1_.refs_2_), channel_id=1, source_target_pairs={{0,48},{48,0},{16,32},{32,16},{1,49},{49,1},{17,33},{33,17},{2,50}... | collective-permute-start | bytes 393224 | tf_op jit(solution)/shard_map/ppermute | solution.py:338
  28.6 0.3 collective-permute-done.5.refs_4_
  28.8 0.4 collective-permute-done.6.refs_6_
  29.2 4.5 %collective-permute-done.4.refs_2_ = bf16[512,128]{1,0:T(8,128)(2,1)S(1)} collective-permute-done((bf16[512,128]{1,0:T(8,128)(2,1)S(1)}, bf16[512,128]{1,0:T(8,128)(2,1)S(1)}, u32[]{:S(2)}, u32[]{:S(2)}) %collective-permute-start.4) | collective-permute-done | bytes 131104 | tf_op jit(solution)/shard_map/ppermute | solution.py:338
  33.7 3.0 %shard_map.103 = (bf16[144,256]{1,0:T(8,128)(2,1)S(1)}, bf16[144,256]{1,0:T(8,128)(2,1)S(1)}, bf16[144,256]{1,0:T(8,128)(2,1)S(1)}, bf16[144,256]{1,0:T(8,128)(2,1)S(1)}) custom-call(s32[32,32]{1,0:T(8,128)S(1)} %copy-done.2, bf16[512,128]{1,0:T(8,128)(2,1)S(1)} %get-tuple-element.56.refs_1_.refs_2_, bf16[512,128]{1,0:T(8,128)(2,1)S(1)} %collective-permute-done.4.refs_2_, ...), custom_call_target="tpu_custom_call" | custom-call | flops 536870912 | bytes 1085440 | tf_op jit(solution)/shard_map/pallas_call | solution.py:61
  36.7 0.3 collective-permute-start.7
  37.0 3.0 %collective-permute-start.9 = (bf16[144,256]{1,0:T(8,128)(2,1)S(1)}, bf16[144,256]{1,0:T(8,128)(2,1)S(1)}, u32[]{:S(2)}, u32[]{:S(2)}) collective-permute-start(bf16[144,256]{1,0:T(8,128)(2,1)S(1)} %get-tuple-element.62), channel_id=1, source_target_pairs={{0,128},{128,0},{64,192},{192,64},{1,129},{129,1},{65,193},{193,65... | collective-permute-start | bytes 221192 | tf_op jit(solution)/shard_map/ppermute | solution.py:342
  40.1 0.1 shard_map.107
  40.2 0.4 shard_map.108.refs_4_.refs_2_
  40.6 1.6 %collective-permute-done.8.refs_2_ = bf16[144,256]{1,0:T(8,128)(2,1)S(1)} collective-permute-done((bf16[144,256]{1,0:T(8,128)(2,1)S(1)}, bf16[144,256]{1,0:T(8,128)(2,1)S(1)}, u32[]{:S(2)}, u32[]{:S(2)}) %collective-permute-start.8) | collective-permute-done | bytes 73760 | tf_op jit(solution)/shard_map/ppermute | solution.py:338
  42.2 0.5 shard_map.109
  42.7 5.5 %collective-permute-start.13 = (bf16[128,1024]{1,0:T(8,128)(2,1)S(1)}, bf16[128,1024]{1,0:T(8,128)(2,1)S(1)}, u32[]{:S(2)}, u32[]{:S(2)}) collective-permute-start(bf16[128,1024]{1,0:T(8,128)(2,1)S(1)} %get-tuple-element.66), channel_id=1, source_target_pairs={{0,1},{1,0},{2,3},{3,2},{4,5},{5,4},{6,7},{7,6},{8,9},{9,8},{10,11... | collective-permute-start | bytes 786440 | tf_op jit(solution)/shard_map/ppermute | solution.py:350
  48.3 1.2 %collective-permute-done.13.refs_1_ = bf16[128,1024]{1,0:T(8,128)(2,1)S(1)} collective-permute-done((bf16[128,1024]{1,0:T(8,128)(2,1)S(1)}, bf16[128,1024]{1,0:T(8,128)(2,1)S(1)}, u32[]{:S(2)}, u32[]{:S(2)}) %collective-permute-start.13) | collective-permute-done | bytes 262176 | tf_op jit(solution)/shard_map/ppermute | solution.py:350
  49.5 0.1 shard_map.110
  49.5 0.5 collective-permute-start.14
  50.0 2.4 %collective-permute-start.15 = (bf16[272,256]{1,0:T(8,128)(2,1)S(1)}, bf16[272,256]{1,0:T(8,128)(2,1)S(1)}, u32[]{:S(2)}, u32[]{:S(2)}) collective-permute-start(bf16[272,256]{1,0:T(8,128)(2,1)S(1)} %get-tuple-element.70), channel_id=1, source_target_pairs={{0,192},{192,0},{64,128},{128,64},{1,193},{193,1},{65,129},{129,65... | collective-permute-start | bytes 417800 | tf_op jit(solution)/shard_map/ppermute | solution.py:338
  52.4 0.5 collective-permute-start.16
  52.9 2.0 %collective-permute-start.17 = (bf16[128,128]{1,0:T(8,128)(2,1)S(1)}, bf16[128,128]{1,0:T(8,128)(2,1)S(1)}, u32[]{:S(2)}, u32[]{:S(2)}) collective-permute-start(bf16[128,128]{1,0:T(8,128)(2,1)S(1)} %slice.33), channel_id=1, source_target_pairs={{0,8},{8,0},{1,9},{9,1},{2,10},{10,2},{3,11},{11,3},{4,12},{12,4},... | collective-permute-start | bytes 98312 | tf_op jit(solution)/shard_map/ppermute | solution.py:346
  54.9 1.6 %collective-permute-done.17.refs_1_ = bf16[128,128]{1,0:T(8,128)(2,1)S(1)} collective-permute-done((bf16[128,128]{1,0:T(8,128)(2,1)S(1)}, bf16[128,128]{1,0:T(8,128)(2,1)S(1)}, u32[]{:S(2)}, u32[]{:S(2)}) %collective-permute-start.17) | collective-permute-done | bytes 32800 | tf_op jit(solution)/shard_map/ppermute | solution.py:346
  56.5 0.5 shard_map.111
  57.0 0.9 collective-permute-start.26
  57.9 0.8 collective-permute-done.16.refs_3_.refs_10_
  58.7 2.6 %collective-permute-start.18 = (bf16[128,256]{1,0:T(8,128)(2,1)S(1)}, bf16[128,256]{1,0:T(8,128)(2,1)S(1)}, u32[]{:S(2)}, u32[]{:S(2)}) collective-permute-start(bf16[128,256]{1,0:T(8,128)(2,1)S(1)} %shard_map.112.refs_11_.refs_0_), channel_id=1, source_target_pairs={{0,16},{16,0},{32,48},{48,32},{1,17},{17,1},{33,49},{49,33},{2,18}... | collective-permute-start | bytes 196616 | tf_op jit(solution)/shard_map/ppermute | solution.py:334
  61.3 4.0 %shard_map.113 = (bf16[512,128]{1,0:T(8,128)(2,1)S(1)}, bf16[512,128]{1,0:T(8,128)(2,1)S(1)}, bf16[512,128]{1,0:T(8,128)(2,1)S(1)}, bf16[512,128]{1,0:T(8,128)(2...) custom-call(s32[32,32]{1,0:T(8,128)S(1)} %copy-done.2, ...), custom_call_target="tpu_custom_call" | custom-call | flops 1342177280 | bytes 2134016 | tf_op jit(solution)/shard_map/pallas_call | solution.py:61
  65.3 1.3 %collective-permute-start.19 = (bf16[128,256]{1,0:T(8,128)(2,1)S(1)}, bf16[128,256]{1,0:T(8,128)(2,1)S(1)}, u32[]{:S(2)}, u32[]{:S(2)}) collective-permute-start(bf16[128,256]{1,0:T(8,128)(2,1)S(1)} %shard_map.114.a), channel_id=1, source_target_pairs={{0,48},{48,0},{16,32},{32,16},{1,49},{49,1},{17,33},{33,17},{2,50}... | collective-permute-start | bytes 196616 | tf_op jit(solution)/shard_map/ppermute | solution.py:338
  66.6 2.7 %collective-permute-start.21 = (bf16[256,256]{1,0:T(8,128)(2,1)S(1)}, bf16[256,256]{1,0:T(8,128)(2,1)S(1)}, u32[]{:S(2)}, u32[]{:S(2)}) collective-permute-start(bf16[256,256]{1,0:T(8,128)(2,1)S(1)} %get-tuple-element.76), channel_id=1, source_target_pairs={{0,192},{192,0},{64,128},{128,64},{1,193},{193,1},{65,129},{129,65... | collective-permute-start | bytes 393224 | tf_op jit(solution)/shard_map/ppermute | solution.py:338
  69.3 1.3 %collective-permute-done.19.b = bf16[128,256]{1,0:T(8,128)(2,1)S(1)} collective-permute-done((bf16[128,256]{1,0:T(8,128)(2,1)S(1)}, bf16[128,256]{1,0:T(8,128)(2,1)S(1)}, u32[]{:S(2)}, u32[]{:S(2)}) %collective-permute-start.19) | collective-permute-done | bytes 65568 | tf_op jit(solution)/shard_map/ppermute | solution.py:338
  70.6 0.2 collective-permute-start.20
  70.9 1.8 %collective-permute-start.29 = (bf16[512,128]{1,0:T(8,128)(2,1)S(1)}, bf16[512,128]{1,0:T(8,128)(2,1)S(1)}, u32[]{:S(2)}, u32[]{:S(2)}) collective-permute-start(bf16[512,128]{1,0:T(8,128)(2,1)S(1)} %get-tuple-element.87), channel_id=1, source_target_pairs={{0,16},{16,0},{32,48},{48,32},{1,17},{17,1},{33,49},{49,33},{2,18}... | collective-permute-start | bytes 393224 | tf_op jit(solution)/shard_map/ppermute | solution.py:334
  72.7 1.3 %collective-permute-start.25 = (bf16[512,128]{1,0:T(8,128)(2,1)S(1)}, bf16[512,128]{1,0:T(8,128)(2,1)S(1)}, u32[]{:S(2)}, u32[]{:S(2)}) collective-permute-start(bf16[512,128]{1,0:T(8,128)(2,1)S(1)} %get-tuple-element.81), channel_id=1, source_target_pairs={{0,48},{48,0},{16,32},{32,16},{1,49},{49,1},{17,33},{33,17},{2,50}... | collective-permute-start | bytes 393224 | tf_op jit(solution)/shard_map/ppermute | solution.py:338
  74.0 0.1 shard_map.118
  74.0 0.5 collective-permute-start.27
  74.6 0.8 collective-permute-start.22
  75.4 3.2 %collective-permute-start.24 = (bf16[256,256]{1,0:T(8,128)(2,1)S(1)}, bf16[256,256]{1,0:T(8,128)(2,1)S(1)}, u32[]{:S(2)}, u32[]{:S(2)}) collective-permute-start(bf16[256,256]{1,0:T(8,128)(2,1)S(1)} %shard_map.117.refs_0_), channel_id=1, source_target_pairs={{0,128},{128,0},{64,192},{192,64},{1,129},{129,1},{65,193},{193,65... | collective-permute-start | bytes 393224 | tf_op jit(solution)/shard_map/ppermute | solution.py:342
  78.6 1.2 %collective-permute-start.23 = (bf16[256,256]{1,0:T(8,128)(2,1)S(1)}, bf16[256,256]{1,0:T(8,128)(2,1)S(1)}, u32[]{:S(2)}, u32[]{:S(2)}) collective-permute-start(bf16[256,256]{1,0:T(8,128)(2,1)S(1)} %shard_map.117.refs_0_), channel_id=1, source_target_pairs={{0,192},{192,0},{64,128},{128,64},{1,193},{193,1},{65,129},{129,65... | collective-permute-start | bytes 393224 | tf_op jit(solution)/shard_map/ppermute | solution.py:338
  79.8 1.3 %collective-permute-start.30 = (bf16[256,128]{1,0:T(8,128)(2,1)S(1)}, bf16[256,128]{1,0:T(8,128)(2,1)S(1)}, u32[]{:S(2)}, u32[]{:S(2)}) collective-permute-start(bf16[256,128]{1,0:T(8,128)(2,1)S(1)} %get-tuple-element.89), channel_id=1, source_target_pairs={{0,48},{48,0},{16,32},{32,16},{1,49},{49,1},{17,33},{33,17},{2,50}... | collective-permute-start | bytes 196616 | tf_op jit(solution)/shard_map/ppermute | solution.py:338
  81.1 2.6 %collective-permute-start.28 = (bf16[256,128]{1,0:T(8,128)(2,1)S(1)}, bf16[256,128]{1,0:T(8,128)(2,1)S(1)}, u32[]{:S(2)}, u32[]{:S(2)}) collective-permute-start(bf16[256,128]{1,0:T(8,128)(2,1)S(1)} %get-tuple-element.85), channel_id=1, source_target_pairs={{0,16},{16,0},{32,48},{48,32},{1,17},{17,1},{33,49},{49,33},{2,18}... | collective-permute-start | bytes 196616 | tf_op jit(solution)/shard_map/ppermute | solution.py:334
  83.7 0.8 collective-permute-start.31
  84.5 0.6 collective-permute-done.30.v_far
  85.1 0.4 collective-permute-done.28.k_near
  85.5 1.7 %collective-permute-done.31.q_near = bf16[128,256]{1,0:T(8,128)(2,1)S(1)} collective-permute-done((bf16[128,256]{1,0:T(8,128)(2,1)S(1)}, bf16[128,256]{1,0:T(8,128)(2,1)S(1)}, u32[]{:S(2)}, u32[]{:S(2)}) %collective-permute-start.31) | collective-permute-done | bytes 65568 | tf_op jit(solution)/shard_map/ppermute | solution.py:334
  87.1 0.1 shard_map.121
  87.3 0.1 shard_map.122.refs_0_
  87.4 5.6 %collective-permute-start.32 = (bf16[256,1024]{1,0:T(8,128)(2,1)S(1)}, bf16[256,1024]{1,0:T(8,128)(2,1)S(1)}, u32[]{:S(2)}, u32[]{:S(2)}) collective-permute-start(bf16[256,1024]{1,0:T(8,128)(2,1)S(1)} %shard_map.122.refs_0_), channel_id=1, source_target_pairs={{0,1},{1,0},{2,3},{3,2},{4,5},{5,4},{6,7},{7,6},{8,9},{9,8},{10,11... | collective-permute-start | bytes 1572872 | tf_op jit(solution)/shard_map/ppermute | solution.py:350
  93.0 0.6 collective-permute-start.33
  93.6 0.9 collective-permute-done.32.refs_1_
  94.5 1.4 %shard_map.123 = (f32[256,2048]{1,0:T(8,128)}, bf16[32,2048]{1,0:T(8,128)(2,1)}, f32[8,128]{1,0:T(8,128)S(1)}) custom-call(bf16[256,1024]{1,0:T(8,128)(2,1)S(1)} %shard_map.122.refs_0_, bf16[256,1024]{1,0:T(8,128)(2,1)S(1)} %collective-permute-done.32.refs_1_, bf16[32,2048]{1,0:T(8,128)(2,1)S(1)} %get-tuple-element.93.refs_2_, ...), custom_call_target="tpu_custom_call" | custom-call | bytes 3543040 | tf_op jit(solution)/shard_map/pallas_call | solution.py:61
  96.0 1.4 %collective-permute-done.33.refs_1_ = bf16[384,128]{1,0:T(8,128)(2,1)S(1)} collective-permute-done((bf16[384,128]{1,0:T(8,128)(2,1)S(1)}, bf16[384,128]{1,0:T(8,128)(2,1)S(1)}, u32[]{:S(2)}, u32[]{:S(2)}) %collective-permute-start.33) | collective-permute-done | bytes 98336 | tf_op jit(solution)/shard_map/ppermute | solution.py:346
  97.4 0.7 shard_map.124
  (39 shorter events, 0.4 us)
Async XLA Ops:
  0.6 33.1 %copy-start.2 = (s32[32,32]{1,0:T(8,128)S(1)}, s32[32,32]{1,0:T(8,128)}, u32[]{:S(2)}) copy-start(s32[32,32]{1,0:T(8,128)} %refs_0_.5) | copy-start | bytes 12292
  0.6 9.1 %collective-permute-start.10 = (bf16[32,2048]{1,0:T(8,128)(2,1)}, bf16[32,2048]{1,0:T(8,128)(2,1)S(1)}, u32[]{:S(2)}, u32[]{:S(2)}) collective-permute-start(bf16[32,2048]{1,0:T(8,128)(2,1)} %bitcast.8), channel_id=1, source_target_pairs={{0,8},{8,0},{1,9},{9,1},{2,10},{10,2},{3,11},{11,3},{4,12},{12,4},... | collective-permute-start | bytes 393224 | tf_op jit(solution)/shard_map/ppermute | solution.py:346
  4.8 4.9 %collective-permute-start = (bf16[384,128]{1,0:T(8,128)(2,1)S(1)}, bf16[384,128]{1,0:T(8,128)(2,1)S(1)}, u32[]{:S(2)}, u32[]{:S(2)}) collective-permute-start(bf16[384,128]{1,0:T(8,128)(2,1)S(1)} %pad_maximum_fusion.1.refs_1_), channel_id=1, source_target_pairs={{0,8},{8,0},{1,9},{9,1},{2,10},{10,2},{3,11},{11,3},{4,12},{12,4},... | collective-permute-start | bytes 294920 | tf_op jit(solution)/shard_map/ppermute | solution.py:346
  4.9 0.9 copy-start.1
  9.7 10.6 %collective-permute-start.11 = (bf16[64,2048]{1,0:T(8,128)(2,1)S(1)}, bf16[64,2048]{1,0:T(8,128)(2,1)S(1)}, u32[]{:S(2)}, u32[]{:S(2)}) collective-permute-start(bf16[64,2048]{1,0:T(8,128)(2,1)S(1)} %shard_map.105.refs_0_), channel_id=1, source_target_pairs={{0,2},{2,0},{4,6},{6,4},{1,3},{3,1},{5,7},{7,5},{8,10},{10,8},{12,... | collective-permute-start | bytes 786440 | tf_op jit(solution)/shard_map/ppermute | solution.py:334
  9.9 8.5 %collective-permute-start.1 = (bf16[256,128]{1,0:T(8,128)(2,1)S(1)}, bf16[256,128]{1,0:T(8,128)(2,1)S(1)}, u32[]{:S(2)}, u32[]{:S(2)}) collective-permute-start(bf16[256,128]{1,0:T(8,128)(2,1)S(1)} %get-tuple-element.53.k0), channel_id=1, source_target_pairs={{0,16},{16,0},{32,48},{48,32},{1,17},{17,1},{33,49},{49,33},{2,18}... | collective-permute-start | bytes 196616 | tf_op jit(solution)/shard_map/ppermute | solution.py:334
  12.9 6.5 %collective-permute-start.2 = (bf16[256,128]{1,0:T(8,128)(2,1)S(1)}, bf16[256,128]{1,0:T(8,128)(2,1)S(1)}, u32[]{:S(2)}, u32[]{:S(2)}) collective-permute-start(bf16[256,128]{1,0:T(8,128)(2,1)S(1)} %get-tuple-element.54.v0), channel_id=1, source_target_pairs={{0,48},{48,0},{16,32},{32,16},{1,49},{49,1},{17,33},{33,17},{2,50}... | collective-permute-start | bytes 196616 | tf_op jit(solution)/shard_map/ppermute | solution.py:338
  17.2 3.1 %collective-permute-start.3 = (bf16[256,128]{1,0:T(8,128)(2,1)S(1)}, bf16[256,128]{1,0:T(8,128)(2,1)S(1)}, u32[]{:S(2)}, u32[]{:S(2)}) collective-permute-start(bf16[256,128]{1,0:T(8,128)(2,1)S(1)} %get-tuple-element.55.q0), channel_id=1, source_target_pairs={{0,64},{64,0},{128,192},{192,128},{1,65},{65,1},{129,193},{193,129... | collective-permute-start | bytes 196616 | tf_op jit(solution)/shard_map/ppermute | solution.py:334
  20.4 19.8 %copy-start = (bf16[256,2048]{1,0:T(8,128)(2,1)S(1)}, bf16[256,2048]{1,0:T(8,128)(2,1)}, u32[]{:S(2)}) copy-start(bf16[256,2048]{1,0:T(8,128)(2,1)} %refs_2_.1) | copy-start | bytes 3145732
  20.4 19.6 %collective-permute-start.12 = (bf16[128,2048]{1,0:T(8,128)(2,1)S(1)}, bf16[128,2048]{1,0:T(8,128)(2,1)S(1)}, u32[]{:S(2)}, u32[]{:S(2)}) collective-permute-start(bf16[128,2048]{1,0:T(8,128)(2,1)S(1)} %shard_map.106.refs_0_), channel_id=1, source_target_pairs={{0,6},{6,0},{2,4},{4,2},{1,7},{7,1},{3,5},{5,3},{8,14},{14,8},{10,... | collective-permute-start | bytes 1572872 | tf_op jit(solution)/shard_map/ppermute | solution.py:338
  22.4 6.4 %collective-permute-start.5 = (bf16[512,128]{1,0:T(8,128)(2,1)S(1)}, bf16[512,128]{1,0:T(8,128)(2,1)S(1)}, u32[]{:S(2)}, u32[]{:S(2)}) collective-permute-start(bf16[512,128]{1,0:T(8,128)(2,1)S(1)} %get-tuple-element.57.refs_3_), channel_id=1, source_target_pairs={{0,16},{16,0},{32,48},{48,32},{1,17},{17,1},{33,49},{49,33},{2,18}... | collective-permute-start | bytes 393224 | tf_op jit(solution)/shard_map/ppermute | solution.py:334
  23.9 5.3 %collective-permute-start.6 = (bf16[512,128]{1,0:T(8,128)(2,1)S(1)}, bf16[512,128]{1,0:T(8,128)(2,1)S(1)}, u32[]{:S(2)}, u32[]{:S(2)}) collective-permute-start(bf16[512,128]{1,0:T(8,128)(2,1)S(1)} %get-tuple-element.58.refs_5_), channel_id=1, source_target_pairs={{0,192},{192,0},{64,128},{128,64},{1,193},{193,1},{65,129},{129,65... | collective-permute-start | bytes 393224 | tf_op jit(solution)/shard_map/ppermute | solution.py:338
  26.4 7.3 %collective-permute-start.4 = (bf16[512,128]{1,0:T(8,128)(2,1)S(1)}, bf16[512,128]{1,0:T(8,128)(2,1)S(1)}, u32[]{:S(2)}, u32[]{:S(2)}) collective-permute-start(bf16[512,128]{1,0:T(8,128)(2,1)S(1)} %get-tuple-element.56.refs_1_.refs_2_), channel_id=1, source_target_pairs={{0,48},{48,0},{16,32},{32,16},{1,49},{49,1},{17,33},{33,17},{2,50}... | collective-permute-start | bytes 393224 | tf_op jit(solution)/shard_map/ppermute | solution.py:338
  36.7 3.9 %collective-permute-start.7 = (bf16[144,256]{1,0:T(8,128)(2,1)S(1)}, bf16[144,256]{1,0:T(8,128)(2,1)S(1)}, u32[]{:S(2)}, u32[]{:S(2)}) collective-permute-start(bf16[144,256]{1,0:T(8,128)(2,1)S(1)} %get-tuple-element.60), channel_id=1, source_target_pairs={{0,64},{64,0},{128,192},{192,128},{1,65},{65,1},{129,193},{193,129... | collective-permute-start | bytes 221192 | tf_op jit(solution)/shard_map/ppermute | solution.py:334
  37.0 5.2 %collective-permute-start.8 = (bf16[144,256]{1,0:T(8,128)(2,1)S(1)}, bf16[144,256]{1,0:T(8,128)(2,1)S(1)}, u32[]{:S(2)}, u32[]{:S(2)}) collective-permute-start(bf16[144,256]{1,0:T(8,128)(2,1)S(1)} %get-tuple-element.61), channel_id=1, source_target_pairs={{0,192},{192,0},{64,128},{128,64},{1,193},{193,1},{65,129},{129,65... | collective-permute-start | bytes 221192 | tf_op jit(solution)/shard_map/ppermute | solution.py:338
  37.0 5.2 %collective-permute-start.9 = (bf16[144,256]{1,0:T(8,128)(2,1)S(1)}, bf16[144,256]{1,0:T(8,128)(2,1)S(1)}, u32[]{:S(2)}, u32[]{:S(2)}) collective-permute-start(bf16[144,256]{1,0:T(8,128)(2,1)S(1)} %get-tuple-element.62), channel_id=1, source_target_pairs={{0,128},{128,0},{64,192},{192,64},{1,129},{129,1},{65,193},{193,65... | collective-permute-start | bytes 221192 | tf_op jit(solution)/shard_map/ppermute | solution.py:342
  42.7 6.7 %collective-permute-start.13 = (bf16[128,1024]{1,0:T(8,128)(2,1)S(1)}, bf16[128,1024]{1,0:T(8,128)(2,1)S(1)}, u32[]{:S(2)}, u32[]{:S(2)}) collective-permute-start(bf16[128,1024]{1,0:T(8,128)(2,1)S(1)} %get-tuple-element.66), channel_id=1, source_target_pairs={{0,1},{1,0},{2,3},{3,2},{4,5},{5,4},{6,7},{7,6},{8,9},{9,8},{10,11... | collective-permute-start | bytes 786440 | tf_op jit(solution)/shard_map/ppermute | solution.py:350
  49.5 8.4 %collective-permute-start.14 = (bf16[272,256]{1,0:T(8,128)(2,1)S(1)}, bf16[272,256]{1,0:T(8,128)(2,1)S(1)}, u32[]{:S(2)}, u32[]{:S(2)}) collective-permute-start(bf16[272,256]{1,0:T(8,128)(2,1)S(1)} %get-tuple-element.69), channel_id=1, source_target_pairs={{0,64},{64,0},{128,192},{192,128},{1,65},{65,1},{129,193},{193,129... | collective-permute-start | bytes 417800 | tf_op jit(solution)/shard_map/ppermute | solution.py:334
  50.0 7.9 %collective-permute-start.15 = (bf16[272,256]{1,0:T(8,128)(2,1)S(1)}, bf16[272,256]{1,0:T(8,128)(2,1)S(1)}, u32[]{:S(2)}, u32[]{:S(2)}) collective-permute-start(bf16[272,256]{1,0:T(8,128)(2,1)S(1)} %get-tuple-element.70), channel_id=1, source_target_pairs={{0,192},{192,0},{64,128},{128,64},{1,193},{193,1},{65,129},{129,65... | collective-permute-start | bytes 417800 | tf_op jit(solution)/shard_map/ppermute | solution.py:338
  52.4 6.3 %collective-permute-start.16 = (bf16[272,256]{1,0:T(8,128)(2,1)S(1)}, bf16[272,256]{1,0:T(8,128)(2,1)S(1)}, u32[]{:S(2)}, u32[]{:S(2)}) collective-permute-start(bf16[272,256]{1,0:T(8,128)(2,1)S(1)} %get-tuple-element.71), channel_id=1, source_target_pairs={{0,128},{128,0},{64,192},{192,64},{1,129},{129,1},{65,193},{193,65... | collective-permute-start | bytes 417800 | tf_op jit(solution)/shard_map/ppermute | solution.py:342
  52.9 3.6 %collective-permute-start.17 = (bf16[128,128]{1,0:T(8,128)(2,1)S(1)}, bf16[128,128]{1,0:T(8,128)(2,1)S(1)}, u32[]{:S(2)}, u32[]{:S(2)}) collective-permute-start(bf16[128,128]{1,0:T(8,128)(2,1)S(1)} %slice.33), channel_id=1, source_target_pairs={{0,8},{8,0},{1,9},{9,1},{2,10},{10,2},{3,11},{11,3},{4,12},{12,4},... | collective-permute-start | bytes 98312 | tf_op jit(solution)/shard_map/ppermute | solution.py:346
  57.0 16.9 %collective-permute-start.26 = (bf16[64,2048]{1,0:T(8,128)(2,1)S(1)}, bf16[64,2048]{1,0:T(8,128)(2,1)S(1)}, u32[]{:S(2)}, u32[]{:S(2)}) collective-permute-start(bf16[64,2048]{1,0:T(8,128)(2,1)S(1)} %get-tuple-element.73.refs_4_), channel_id=1, source_target_pairs={{0,6},{6,0},{2,4},{4,2},{1,7},{7,1},{3,5},{5,3},{8,14},{14,8},{10,... | collective-permute-start | bytes 786440 | tf_op jit(solution)/shard_map/ppermute | solution.py:338
  58.7 6.6 %collective-permute-start.18 = (bf16[128,256]{1,0:T(8,128)(2,1)S(1)}, bf16[128,256]{1,0:T(8,128)(2,1)S(1)}, u32[]{:S(2)}, u32[]{:S(2)}) collective-permute-start(bf16[128,256]{1,0:T(8,128)(2,1)S(1)} %shard_map.112.refs_11_.refs_0_), channel_id=1, source_target_pairs={{0,16},{16,0},{32,48},{48,32},{1,17},{17,1},{33,49},{49,33},{2,18}... | collective-permute-start | bytes 196616 | tf_op jit(solution)/shard_map/ppermute | solution.py:334
  65.3 5.3 %collective-permute-start.19 = (bf16[128,256]{1,0:T(8,128)(2,1)S(1)}, bf16[128,256]{1,0:T(8,128)(2,1)S(1)}, u32[]{:S(2)}, u32[]{:S(2)}) collective-permute-start(bf16[128,256]{1,0:T(8,128)(2,1)S(1)} %shard_map.114.a), channel_id=1, source_target_pairs={{0,48},{48,0},{16,32},{32,16},{1,49},{49,1},{17,33},{33,17},{2,50}... | collective-permute-start | bytes 196616 | tf_op jit(solution)/shard_map/ppermute | solution.py:338
  66.6 7.9 %collective-permute-start.21 = (bf16[256,256]{1,0:T(8,128)(2,1)S(1)}, bf16[256,256]{1,0:T(8,128)(2,1)S(1)}, u32[]{:S(2)}, u32[]{:S(2)}) collective-permute-start(bf16[256,256]{1,0:T(8,128)(2,1)S(1)} %get-tuple-element.76), channel_id=1, source_target_pairs={{0,192},{192,0},{64,128},{128,64},{1,193},{193,1},{65,129},{129,65... | collective-permute-start | bytes 393224 | tf_op jit(solution)/shard_map/ppermute | solution.py:338
  70.6 3.9 %collective-permute-start.20 = (bf16[128,256]{1,0:T(8,128)(2,1)S(1)}, bf16[128,256]{1,0:T(8,128)(2,1)S(1)}, u32[]{:S(2)}, u32[]{:S(2)}) collective-permute-start(bf16[128,256]{1,0:T(8,128)(2,1)S(1)} %shard_map.115.refs_0_.refs_2_), channel_id=1, source_target_pairs={{0,8},{8,0},{1,9},{9,1},{2,10},{10,2},{3,11},{11,3},{4,12},{12,4},... | collective-permute-start | bytes 196616 | tf_op jit(solution)/shard_map/ppermute | solution.py:346
  70.9 7.7 %collective-permute-start.29 = (bf16[512,128]{1,0:T(8,128)(2,1)S(1)}, bf16[512,128]{1,0:T(8,128)(2,1)S(1)}, u32[]{:S(2)}, u32[]{:S(2)}) collective-permute-start(bf16[512,128]{1,0:T(8,128)(2,1)S(1)} %get-tuple-element.87), channel_id=1, source_target_pairs={{0,16},{16,0},{32,48},{48,32},{1,17},{17,1},{33,49},{49,33},{2,18}... | collective-permute-start | bytes 393224 | tf_op jit(solution)/shard_map/ppermute | solution.py:334
  72.7 7.1 %collective-permute-start.25 = (bf16[512,128]{1,0:T(8,128)(2,1)S(1)}, bf16[512,128]{1,0:T(8,128)(2,1)S(1)}, u32[]{:S(2)}, u32[]{:S(2)}) collective-permute-start(bf16[512,128]{1,0:T(8,128)(2,1)S(1)} %get-tuple-element.81), channel_id=1, source_target_pairs={{0,48},{48,0},{16,32},{32,16},{1,49},{49,1},{17,33},{33,17},{2,50}... | collective-permute-start | bytes 393224 | tf_op jit(solution)/shard_map/ppermute | solution.py:338
  74.0 7.0 %collective-permute-start.27 = (bf16[32,2048]{1,0:T(8,128)(2,1)S(1)}, bf16[32,2048]{1,0:T(8,128)(2,1)S(1)}, u32[]{:S(2)}, u32[]{:S(2)}) collective-permute-start(bf16[32,2048]{1,0:T(8,128)(2,1)S(1)} %get-tuple-element.83), channel_id=1, source_target_pairs={{0,2},{2,0},{4,6},{6,4},{1,3},{3,1},{5,7},{7,5},{8,10},{10,8},{12,... | collective-permute-start | bytes 393224 | tf_op jit(solution)/shard_map/ppermute | solution.py:334
  74.6 9.1 %collective-permute-start.22 = (bf16[256,256]{1,0:T(8,128)(2,1)S(1)}, bf16[256,256]{1,0:T(8,128)(2,1)S(1)}, u32[]{:S(2)}, u32[]{:S(2)}) collective-permute-start(bf16[256,256]{1,0:T(8,128)(2,1)S(1)} %shard_map.117.refs_0_), channel_id=1, source_target_pairs={{0,64},{64,0},{128,192},{192,128},{1,65},{65,1},{129,193},{193,129... | collective-permute-start | bytes 393224 | tf_op jit(solution)/shard_map/ppermute | solution.py:334
  75.4 11.9 %collective-permute-start.24 = (bf16[256,256]{1,0:T(8,128)(2,1)S(1)}, bf16[256,256]{1,0:T(8,128)(2,1)S(1)}, u32[]{:S(2)}, u32[]{:S(2)}) collective-permute-start(bf16[256,256]{1,0:T(8,128)(2,1)S(1)} %shard_map.117.refs_0_), channel_id=1, source_target_pairs={{0,128},{128,0},{64,192},{192,64},{1,129},{129,1},{65,193},{193,65... | collective-permute-start | bytes 393224 | tf_op jit(solution)/shard_map/ppermute | solution.py:342
  78.6 8.7 %collective-permute-start.23 = (bf16[256,256]{1,0:T(8,128)(2,1)S(1)}, bf16[256,256]{1,0:T(8,128)(2,1)S(1)}, u32[]{:S(2)}, u32[]{:S(2)}) collective-permute-start(bf16[256,256]{1,0:T(8,128)(2,1)S(1)} %shard_map.117.refs_0_), channel_id=1, source_target_pairs={{0,192},{192,0},{64,128},{128,64},{1,193},{193,1},{65,129},{129,65... | collective-permute-start | bytes 393224 | tf_op jit(solution)/shard_map/ppermute | solution.py:338
  79.8 5.3 %collective-permute-start.30 = (bf16[256,128]{1,0:T(8,128)(2,1)S(1)}, bf16[256,128]{1,0:T(8,128)(2,1)S(1)}, u32[]{:S(2)}, u32[]{:S(2)}) collective-permute-start(bf16[256,128]{1,0:T(8,128)(2,1)S(1)} %get-tuple-element.89), channel_id=1, source_target_pairs={{0,48},{48,0},{16,32},{32,16},{1,49},{49,1},{17,33},{33,17},{2,50}... | collective-permute-start | bytes 196616 | tf_op jit(solution)/shard_map/ppermute | solution.py:338
  81.1 4.4 %collective-permute-start.28 = (bf16[256,128]{1,0:T(8,128)(2,1)S(1)}, bf16[256,128]{1,0:T(8,128)(2,1)S(1)}, u32[]{:S(2)}, u32[]{:S(2)}) collective-permute-start(bf16[256,128]{1,0:T(8,128)(2,1)S(1)} %get-tuple-element.85), channel_id=1, source_target_pairs={{0,16},{16,0},{32,48},{48,32},{1,17},{17,1},{33,49},{49,33},{2,18}... | collective-permute-start | bytes 196616 | tf_op jit(solution)/shard_map/ppermute | solution.py:334
  83.7 3.4 %collective-permute-start.31 = (bf16[128,256]{1,0:T(8,128)(2,1)S(1)}, bf16[128,256]{1,0:T(8,128)(2,1)S(1)}, u32[]{:S(2)}, u32[]{:S(2)}) collective-permute-start(bf16[128,256]{1,0:T(8,128)(2,1)S(1)} %get-tuple-element.91.refs_2_), channel_id=1, source_target_pairs={{0,64},{64,0},{128,192},{192,128},{1,65},{65,1},{129,193},{193,129... | collective-permute-start | bytes 196616 | tf_op jit(solution)/shard_map/ppermute | solution.py:334
  87.4 7.2 %collective-permute-start.32 = (bf16[256,1024]{1,0:T(8,128)(2,1)S(1)}, bf16[256,1024]{1,0:T(8,128)(2,1)S(1)}, u32[]{:S(2)}, u32[]{:S(2)}) collective-permute-start(bf16[256,1024]{1,0:T(8,128)(2,1)S(1)} %shard_map.122.refs_0_), channel_id=1, source_target_pairs={{0,1},{1,0},{2,3},{3,2},{4,5},{5,4},{6,7},{7,6},{8,9},{9,8},{10,11... | collective-permute-start | bytes 1572872 | tf_op jit(solution)/shard_map/ppermute | solution.py:350
  93.0 4.4 %collective-permute-start.33 = (bf16[384,128]{1,0:T(8,128)(2,1)S(1)}, bf16[384,128]{1,0:T(8,128)(2,1)S(1)}, u32[]{:S(2)}, u32[]{:S(2)}) collective-permute-start(bf16[384,128]{1,0:T(8,128)(2,1)S(1)} %get-tuple-element.92.refs_4_), channel_id=1, source_target_pairs={{0,8},{8,0},{1,9},{9,1},{2,10},{10,2},{3,11},{11,3},{4,12},{12,4},... | collective-permute-start | bytes 294920 | tf_op jit(solution)/shard_map/ppermute | solution.py:346

commit v7 on v6

--- a/solution.py
+++ b/solution.py
@@ -76,8 +76,11 @@
         ref[TILE:, :] = recv[rows, :]
 
 
-def copy_rows(rows, out):
+def early_rows(pos, mask, rows, out, bias):
     out[...] = rows[...]
+    for n in range(4):
+        for t, row in enumerate(bias_rows(pos, mask, pos[X] ^ ORDER[n])):
+            bias[n * 8 + t : n * 8 + t + 1, :] = row
 
 
 def stack_two(a, b, out):
@@ -152,11 +155,11 @@
     return (qp, qf)[n // 2][(n % 2) * BLK : (n % 2 + 1) * BLK, :]
 
 
-def forward(pos, mask, kp, kf, vp, vn, qp, qf, p0, p1, p2, p3):
+def forward(bias, kp, kf, vp, vn, qp, qf, p0, p1, p2, p3):
     keys, values = load_kv(kp, kf, vp, vn)
     values_t = transposed(values)
     for n, pack in enumerate((p0, p1, p2, p3)):
-        rows = bias_rows(pos, mask, pos[X] ^ ORDER[n])
+        rows = [bias[n * 8 + t : n * 8 + t + 1, :] for t in range(8)]
         queries = query_block(qp, qf, n)
         scores = [
             scores_of(keys[e * BLK : (e + 1) * BLK], queries, rows[2 * e : 2 * e + 2])
@@ -179,13 +182,13 @@
 
 
 def backward(
-    pos, mask, kp, kf, vp, vn, qp, qf, s0, s1, s2, s3,
+    bias, kp, kf, vp, vn, qp, qf, s0, s1, s2, s3,
     dk, dk_far, dv, dv_near, dq, dq_far, probs_of, scores_grad_of,
 ):
     keys, values = load_kv(kp, kf, vp, vn)
     keys_t = transposed(keys)
     for n, ref in enumerate((s0, s1, s2, s3)):
-        rows = bias_rows(pos, mask, pos[X] ^ ORDER[n])
+        rows = [bias[n * 8 + t : n * 8 + t + 1, :] for t in range(8)]
         s = ref[2 * HD :, :].astype(F32)
         lse = s[0:1] + s[1:2] + s[2:3]
         delta = s[3:4] + s[4:5] + s[5:6]
@@ -360,7 +363,13 @@
     keep = jnp.concatenate([jnp.where(first, rows[:, :HD], rows[:, HD:]) for rows in inputs])
     recv = over_pair(send)
     rows_far = over_pair(cotangent[0])
-    (rows,) = call(copy_rows, [((32, 2048), BF16)], (cotangent[0],), smem=0, after=(send,))
+    rows, bias = call(
+        early_rows,
+        [((32, 2048), BF16), ((32, BLK), F32)],
+        (pos, tile_mask, cotangent[0]),
+        smem=2,
+        after=(send,),
+    )
     k, v, q = call(own_blocks, [((BLK, HD), BF16)] * 3, (keep, recv), smem=0)
     (rows,) = call(stack_two, [((64, 2048), BF16)], (rows, rows_far), smem=0, after=(recv,))
     kp, vp, qp = call(
@@ -375,9 +384,9 @@
     packs = call(
         forward,
         [((HD + 16, BLK), BF16)] * 4,
-        (pos, tile_mask, kp, kf, vp, vn, qp, qf),
+        (bias, kp, kf, vp, vn, qp, qf),
         flops=2 * kv_mm,
-        smem=2,
+        smem=0,
     )
     packs = [packs[0], near(packs[1], "x"), far(packs[2], "x"), opposite(packs[3], "x")]
 
@@ -412,10 +421,10 @@
     dk, dk_far, dv, dv_near, dq, dq_far = call(
         backward,
         [((2 * BLK, HD), BF16)] * 4 + [((2 * HD, BLK), BF16)] * 2,
-        (pos, tile_mask, kp, kf, vp, vn, qp, qf, *cuts),
+        (bias, kp, kf, vp, vn, qp, qf, *cuts),
         flops=5 * kv_mm,
         scratch=[pltpu.VMEM((4 * BLK, 4 * BLK), BF16)] * 2,
-        smem=2,
+        smem=0,
         after=(share,),
     )
     (near_sum,) = call(

time: 98.5 us -> 98.9 us (level)
  starting transfers between devices: 61 us -> 64.1 us
  waiting for transfers between devices: 22.3 us -> 19.5 us
    ppermute x12, starting transfers between devices: 22 us -> 23.7 us  [far(): return lax.ppermute(a, axis, [(0, 3), (3, 0), (1, 2), (2, 1)])]
    ppermute x5, waiting for transfers between devices: 6.85 us -> 5.17 us  [over_pair(): return lax.ppermute(a, 'par', [(0, 1), (1, 0)])]
    ppermute x12, waiting for transfers between devices: 9.37 us -> 8.29 us  [far(): return lax.ppermute(a, axis, [(0, 3), (3, 0), (1, 2), (2, 1)])]
    ppermute x5, starting transfers between devices: 5.57 us -> 6.63 us  [over_pair(): return lax.ppermute(a, 'par', [(0, 1), (1, 0)])]
  transfers between devices with their start and end apart: 34 -> 34, of which waited for: 16 -> 14; matrix products, arithmetic and copies ran while one was open for 2% -> 2% of each run, Pallas kernels for 10% -> 9%
where the time goes in v7:
time: 98.9 us; the launch traced here: 98.6 us
  starting transfers between devices  64.1 us (65%)
  waiting for transfers between devices  19.5 us (20%)
  Pallas kernels  10.7 us (11%)
  local copies, waits for them, and re-layouts  1.63 us (2%)
  other arithmetic  1.62 us (2%)
  between operations  1.06 us (1%)
    ppermute x12, starting transfers between devices, far(): return lax.ppermute(a, axis, [(0, 3), (3, 0), (1, 2), (2, 1)])  23.7 us
    ppermute x12, starting transfers between devices, near(): return lax.ppermute(a, axis, [(0, 1), (1, 0), (2, 3), (3, 2)])  15.2 us
    ppermute x2, starting transfers between devices, over_core(): return lax.ppermute(a, 'core', [(0, 1), (1, 0)])  11.9 us
    pallas_call x24, Pallas kernels, call(): pl.pallas_call(body, out_shape=shapes, in_specs=specs, out_specs=[pl.Bloc...  10.7 us
    ppermute x12, waiting for transfers between devices, far(): return lax.ppermute(a, axis, [(0, 3), (3, 0), (1, 2), (2, 1)])  8.29 us
    ppermute x3, starting transfers between devices, opposite(): return lax.ppermute(a, axis, [(0, 2), (2, 0), (1, 3), (3, 1)])  6.72 us
    ppermute x5, starting transfers between devices, over_pair(): return lax.ppermute(a, 'par', [(0, 1), (1, 0)])  6.63 us
    ppermute x5, waiting for transfers between devices, over_pair(): return lax.ppermute(a, 'par', [(0, 1), (1, 0)])  5.17 us
  transfers between devices with their start and end apart: 34, of which 14 were waited for; matrix products, arithmetic and copies ran while one was open for 2% of the time, Pallas kernels for 9%

profile of v7, /device:TPU:1, one launch (start us, length us, event | category | flops | bytes accessed | tf_op | source)
XLA Modules:
  0.0 98.6 jit_solution(17384514887432992486)
XLA Ops:
  0.6 2.6 %collective-permute-start.10 = (bf16[32,2048]{1,0:T(8,128)(2,1)}, bf16[32,2048]{1,0:T(8,128)(2,1)S(1)}, u32[]{:S(2)}, u32[]{:S(2)}) collective-permute-start(bf16[32,2048]{1,0:T(8,128)(2,1)} %bitcast.8), channel_id=1, source_target_pairs={{0,8},{8,0},{1,9},{9,1},{2,10},{10,2},{3,11},{11,3},{4,12},{12,4},... | collective-permute-start | bytes 393224 | tf_op jit(solution)/shard_map/ppermute | solution.py:349
  3.2 0.8 broadcast_select_fusion.2
  4.0 0.8 broadcast_select_fusion
  4.8 0.1 collective-permute-start
  4.9 0.9 copy-done.1
  5.8 0.7 copy-done.2
  6.5 1.0 shard_map.101
  7.5 2.2 %collective-permute-done.recv.refs_2_ = bf16[384,128]{1,0:T(8,128)(2,1)S(1)} collective-permute-done((bf16[384,128]{1,0:T(8,128)(2,1)S(1)}, bf16[384,128]{1,0:T(8,128)(2,1)S(1)}, u32[]{:S(2)}, u32[]{:S(2)}) %collective-permute-start) | collective-permute-done | bytes 98336 | tf_op jit(solution)/shard_map/ppermute | solution.py:349
  9.7 0.1 collective-permute-start.11
  9.9 3.0 %collective-permute-start.1 = (bf16[256,128]{1,0:T(8,128)(2,1)S(1)}, bf16[256,128]{1,0:T(8,128)(2,1)S(1)}, u32[]{:S(2)}, u32[]{:S(2)}) collective-permute-start(bf16[256,128]{1,0:T(8,128)(2,1)S(1)} %get-tuple-element.56.k0), channel_id=1, source_target_pairs={{0,16},{16,0},{32,48},{48,32},{1,17},{17,1},{33,49},{49,33},{2,18}... | collective-permute-start | bytes 196616 | tf_op jit(solution)/shard_map/ppermute | solution.py:337
  12.9 4.3 %collective-permute-start.2 = (bf16[256,128]{1,0:T(8,128)(2,1)S(1)}, bf16[256,128]{1,0:T(8,128)(2,1)S(1)}, u32[]{:S(2)}, u32[]{:S(2)}) collective-permute-start(bf16[256,128]{1,0:T(8,128)(2,1)S(1)} %get-tuple-element.57.v0), channel_id=1, source_target_pairs={{0,48},{48,0},{16,32},{32,16},{1,49},{49,1},{17,33},{33,17},{2,50}... | collective-permute-start | bytes 196616 | tf_op jit(solution)/shard_map/ppermute | solution.py:341
  17.2 1.2 %collective-permute-start.3 = (bf16[256,128]{1,0:T(8,128)(2,1)S(1)}, bf16[256,128]{1,0:T(8,128)(2,1)S(1)}, u32[]{:S(2)}, u32[]{:S(2)}) collective-permute-start(bf16[256,128]{1,0:T(8,128)(2,1)S(1)} %get-tuple-element.58.q0), channel_id=1, source_target_pairs={{0,64},{64,0},{128,192},{192,128},{1,65},{65,1},{129,193},{193,129... | collective-permute-start | bytes 196616 | tf_op jit(solution)/shard_map/ppermute | solution.py:337
  18.4 1.0 collective-permute-done.2.v1
  19.4 0.9 collective-permute-done.3.q1
  20.4 2.0 %collective-permute-start.12 = (bf16[128,2048]{1,0:T(8,128)(2,1)S(1)}, bf16[128,2048]{1,0:T(8,128)(2,1)S(1)}, u32[]{:S(2)}, u32[]{:S(2)}) collective-permute-start(bf16[128,2048]{1,0:T(8,128)(2,1)S(1)} %shard_map.106.refs_0_), channel_id=1, source_target_pairs={{0,6},{6,0},{2,4},{4,2},{1,7},{7,1},{3,5},{5,3},{8,14},{14,8},{10,... | collective-permute-start | bytes 1572872 | tf_op jit(solution)/shard_map/ppermute | solution.py:341
  22.4 1.5 %collective-permute-start.5 = (bf16[512,128]{1,0:T(8,128)(2,1)S(1)}, bf16[512,128]{1,0:T(8,128)(2,1)S(1)}, u32[]{:S(2)}, u32[]{:S(2)}) collective-permute-start(bf16[512,128]{1,0:T(8,128)(2,1)S(1)} %get-tuple-element.60.vp.refs_3_), channel_id=1, source_target_pairs={{0,16},{16,0},{32,48},{48,32},{1,17},{17,1},{33,49},{49,33},{2,18}... | collective-permute-start | bytes 393224 | tf_op jit(solution)/shard_map/ppermute | solution.py:337
  23.9 2.5 %collective-permute-start.6 = (bf16[512,128]{1,0:T(8,128)(2,1)S(1)}, bf16[512,128]{1,0:T(8,128)(2,1)S(1)}, u32[]{:S(2)}, u32[]{:S(2)}) collective-permute-start(bf16[512,128]{1,0:T(8,128)(2,1)S(1)} %get-tuple-element.61.qp.refs_5_), channel_id=1, source_target_pairs={{0,192},{192,0},{64,128},{128,64},{1,193},{193,1},{65,129},{129,65... | collective-permute-start | bytes 393224 | tf_op jit(solution)/shard_map/ppermute | solution.py:341
  26.4 2.2 %collective-permute-start.4 = (bf16[512,128]{1,0:T(8,128)(2,1)S(1)}, bf16[512,128]{1,0:T(8,128)(2,1)S(1)}, u32[]{:S(2)}, u32[]{:S(2)}) collective-permute-start(bf16[512,128]{1,0:T(8,128)(2,1)S(1)} %get-tuple-element.59.kp.refs_2_.refs_1_), channel_id=1, source_target_pairs={{0,48},{48,0},{16,32},{32,16},{1,49},{49,1},{17,33},{33,17},{2,50}... | collective-permute-start | bytes 393224 | tf_op jit(solution)/shard_map/ppermute | solution.py:341
  28.6 0.3 collective-permute-done.5.vn.refs_4_
  28.8 0.4 collective-permute-done.6.qf.refs_6_
  29.2 4.5 %collective-permute-done.4.kf.refs_2_ = bf16[512,128]{1,0:T(8,128)(2,1)S(1)} collective-permute-done((bf16[512,128]{1,0:T(8,128)(2,1)S(1)}, bf16[512,128]{1,0:T(8,128)(2,1)S(1)}, u32[]{:S(2)}, u32[]{:S(2)}) %collective-permute-start.4) | collective-permute-done | bytes 131104 | tf_op jit(solution)/shard_map/ppermute | solution.py:341
  33.7 2.2 %shard_map.104 = (bf16[144,256]{1,0:T(8,128)(2,1)S(1)}, bf16[144,256]{1,0:T(8,128)(2,1)S(1)}, bf16[144,256]{1,0:T(8,128)(2,1)S(1)}, bf16[144,256]{1,0:T(8,128)(2,1)S(1)}) custom-call(f32[32,256]{1,0:T(8,128)S(1)} %get-tuple-element.55.bias.refs_0_, bf16[512,128]{1,0:T(8,128)(2,1)S(1)} %get-tuple-element.59.kp.refs_2_.refs_1_, ...), custom_call_target="tpu_custom_call" | custom-call | flops 536870912 | bytes 1114112 | tf_op jit(solution)/shard_map/pallas_call | solution.py:61
  35.9 0.3 collective-permute-start.7
  36.2 3.0 %collective-permute-start.9 = (bf16[144,256]{1,0:T(8,128)(2,1)S(1)}, bf16[144,256]{1,0:T(8,128)(2,1)S(1)}, u32[]{:S(2)}, u32[]{:S(2)}) collective-permute-start(bf16[144,256]{1,0:T(8,128)(2,1)S(1)} %get-tuple-element.65), channel_id=1, source_target_pairs={{0,128},{128,0},{64,192},{192,64},{1,129},{129,1},{65,193},{193,65... | collective-permute-start | bytes 221192 | tf_op jit(solution)/shard_map/ppermute | solution.py:345
  39.3 0.1 shard_map.107
  39.3 0.4 shard_map.108.refs_4_.refs_2_
  39.8 1.6 %collective-permute-done.8.refs_2_ = bf16[144,256]{1,0:T(8,128)(2,1)S(1)} collective-permute-done((bf16[144,256]{1,0:T(8,128)(2,1)S(1)}, bf16[144,256]{1,0:T(8,128)(2,1)S(1)}, u32[]{:S(2)}, u32[]{:S(2)}) %collective-permute-start.8) | collective-permute-done | bytes 73760 | tf_op jit(solution)/shard_map/ppermute | solution.py:341
  41.4 0.5 shard_map.109
  41.9 5.5 %collective-permute-start.13 = (bf16[128,1024]{1,0:T(8,128)(2,1)S(1)}, bf16[128,1024]{1,0:T(8,128)(2,1)S(1)}, u32[]{:S(2)}, u32[]{:S(2)}) collective-permute-start(bf16[128,1024]{1,0:T(8,128)(2,1)S(1)} %get-tuple-element.70), channel_id=1, source_target_pairs={{0,1},{1,0},{2,3},{3,2},{4,5},{5,4},{6,7},{7,6},{8,9},{9,8},{10,11... | collective-permute-start | bytes 786440 | tf_op jit(solution)/shard_map/ppermute | solution.py:353
  47.5 1.2 %collective-permute-done.13.refs_1_ = bf16[128,1024]{1,0:T(8,128)(2,1)S(1)} collective-permute-done((bf16[128,1024]{1,0:T(8,128)(2,1)S(1)}, bf16[128,1024]{1,0:T(8,128)(2,1)S(1)}, u32[]{:S(2)}, u32[]{:S(2)}) %collective-permute-start.13) | collective-permute-done | bytes 262176 | tf_op jit(solution)/shard_map/ppermute | solution.py:353
  48.6 0.1 shard_map.110
  48.7 0.5 collective-permute-start.14
  49.2 2.4 %collective-permute-start.15 = (bf16[272,256]{1,0:T(8,128)(2,1)S(1)}, bf16[272,256]{1,0:T(8,128)(2,1)S(1)}, u32[]{:S(2)}, u32[]{:S(2)}) collective-permute-start(bf16[272,256]{1,0:T(8,128)(2,1)S(1)} %get-tuple-element.74), channel_id=1, source_target_pairs={{0,192},{192,0},{64,128},{128,64},{1,193},{193,1},{65,129},{129,65... | collective-permute-start | bytes 417800 | tf_op jit(solution)/shard_map/ppermute | solution.py:341
  51.6 0.5 collective-permute-start.16
  52.1 2.0 %collective-permute-start.17 = (bf16[128,128]{1,0:T(8,128)(2,1)S(1)}, bf16[128,128]{1,0:T(8,128)(2,1)S(1)}, u32[]{:S(2)}, u32[]{:S(2)}) collective-permute-start(bf16[128,128]{1,0:T(8,128)(2,1)S(1)} %slice.33), channel_id=1, source_target_pairs={{0,8},{8,0},{1,9},{9,1},{2,10},{10,2},{3,11},{11,3},{4,12},{12,4},... | collective-permute-start | bytes 98312 | tf_op jit(solution)/shard_map/ppermute | solution.py:349
  54.1 1.6 %collective-permute-done.17.refs_1_ = bf16[128,128]{1,0:T(8,128)(2,1)S(1)} collective-permute-done((bf16[128,128]{1,0:T(8,128)(2,1)S(1)}, bf16[128,128]{1,0:T(8,128)(2,1)S(1)}, u32[]{:S(2)}, u32[]{:S(2)}) %collective-permute-start.17) | collective-permute-done | bytes 32800 | tf_op jit(solution)/shard_map/ppermute | solution.py:349
  55.7 0.5 shard_map.111
  56.2 0.9 collective-permute-start.26
  57.1 0.8 collective-permute-done.16.refs_3_.refs_10_
  57.9 2.6 %collective-permute-start.18 = (bf16[128,256]{1,0:T(8,128)(2,1)S(1)}, bf16[128,256]{1,0:T(8,128)(2,1)S(1)}, u32[]{:S(2)}, u32[]{:S(2)}) collective-permute-start(bf16[128,256]{1,0:T(8,128)(2,1)S(1)} %shard_map.112.refs_11_.refs_0_), channel_id=1, source_target_pairs={{0,16},{16,0},{32,48},{48,32},{1,17},{17,1},{33,49},{49,33},{2,18}... | collective-permute-start | bytes 196616 | tf_op jit(solution)/shard_map/ppermute | solution.py:337
  60.5 3.2 %shard_map.113 = (bf16[512,128]{1,0:T(8,128)(2,1)S(1)}, bf16[512,128]{1,0:T(8,128)(2,1)S(1)}, bf16[512,128]{1,0:T(8,128)(2,1)S(1)}, bf16[512,128]{1,0:T(8,128)(2...) custom-call(f32[32,256]{1,0:T(8,128)S(1)} %get-tuple-element.55.bias.refs_0_, ...), custom_call_target="tpu_custom_call" | custom-call | flops 1342177280 | bytes 2162688 | tf_op jit(solution)/shard_map/pallas_call | solution.py:61
  63.7 1.9 %collective-permute-start.19 = (bf16[128,256]{1,0:T(8,128)(2,1)S(1)}, bf16[128,256]{1,0:T(8,128)(2,1)S(1)}, u32[]{:S(2)}, u32[]{:S(2)}) collective-permute-start(bf16[128,256]{1,0:T(8,128)(2,1)S(1)} %shard_map.114.a), channel_id=1, source_target_pairs={{0,48},{48,0},{16,32},{32,16},{1,49},{49,1},{17,33},{33,17},{2,50}... | collective-permute-start | bytes 196616 | tf_op jit(solution)/shard_map/ppermute | solution.py:341
  65.6 2.7 %collective-permute-start.21 = (bf16[256,256]{1,0:T(8,128)(2,1)S(1)}, bf16[256,256]{1,0:T(8,128)(2,1)S(1)}, u32[]{:S(2)}, u32[]{:S(2)}) collective-permute-start(bf16[256,256]{1,0:T(8,128)(2,1)S(1)} %get-tuple-element.80), channel_id=1, source_target_pairs={{0,192},{192,0},{64,128},{128,64},{1,193},{193,1},{65,129},{129,65... | collective-permute-start | bytes 393224 | tf_op jit(solution)/shard_map/ppermute | solution.py:341
  68.3 0.8 collective-permute-done.19.b
  69.1 1.3 %collective-permute-start.20 = (bf16[128,256]{1,0:T(8,128)(2,1)S(1)}, bf16[128,256]{1,0:T(8,128)(2,1)S(1)}, u32[]{:S(2)}, u32[]{:S(2)}) collective-permute-start(bf16[128,256]{1,0:T(8,128)(2,1)S(1)} %shard_map.115.refs_0_.refs_2_), channel_id=1, source_target_pairs={{0,8},{8,0},{1,9},{9,1},{2,10},{10,2},{3,11},{11,3},{4,12},{12,4},... | collective-permute-start | bytes 196616 | tf_op jit(solution)/shard_map/ppermute | solution.py:349
  70.5 0.7 collective-permute-start.29
  71.1 2.4 %collective-permute-start.25 = (bf16[512,128]{1,0:T(8,128)(2,1)S(1)}, bf16[512,128]{1,0:T(8,128)(2,1)S(1)}, u32[]{:S(2)}, u32[]{:S(2)}) collective-permute-start(bf16[512,128]{1,0:T(8,128)(2,1)S(1)} %get-tuple-element.85), channel_id=1, source_target_pairs={{0,48},{48,0},{16,32},{32,16},{1,49},{49,1},{17,33},{33,17},{2,50}... | collective-permute-start | bytes 393224 | tf_op jit(solution)/shard_map/ppermute | solution.py:341
  73.6 0.1 shard_map.118
  73.6 0.1 collective-permute-start.27
  73.8 0.8 collective-permute-start.22
  74.6 3.2 %collective-permute-start.24 = (bf16[256,256]{1,0:T(8,128)(2,1)S(1)}, bf16[256,256]{1,0:T(8,128)(2,1)S(1)}, u32[]{:S(2)}, u32[]{:S(2)}) collective-permute-start(bf16[256,256]{1,0:T(8,128)(2,1)S(1)} %shard_map.117.refs_0_), channel_id=1, source_target_pairs={{0,128},{128,0},{64,192},{192,64},{1,129},{129,1},{65,193},{193,65... | collective-permute-start | bytes 393224 | tf_op jit(solution)/shard_map/ppermute | solution.py:345
  77.8 1.6 %collective-permute-start.23 = (bf16[256,256]{1,0:T(8,128)(2,1)S(1)}, bf16[256,256]{1,0:T(8,128)(2,1)S(1)}, u32[]{:S(2)}, u32[]{:S(2)}) collective-permute-start(bf16[256,256]{1,0:T(8,128)(2,1)S(1)} %shard_map.117.refs_0_), channel_id=1, source_target_pairs={{0,192},{192,0},{64,128},{128,64},{1,193},{193,1},{65,129},{129,65... | collective-permute-start | bytes 393224 | tf_op jit(solution)/shard_map/ppermute | solution.py:341
  79.4 0.9 collective-permute-start.30
  80.4 2.4 %collective-permute-start.28 = (bf16[256,128]{1,0:T(8,128)(2,1)S(1)}, bf16[256,128]{1,0:T(8,128)(2,1)S(1)}, u32[]{:S(2)}, u32[]{:S(2)}) collective-permute-start(bf16[256,128]{1,0:T(8,128)(2,1)S(1)} %get-tuple-element.89), channel_id=1, source_target_pairs={{0,16},{16,0},{32,48},{48,32},{1,17},{17,1},{33,49},{49,33},{2,18}... | collective-permute-start | bytes 196616 | tf_op jit(solution)/shard_map/ppermute | solution.py:337
  82.8 2.1 %collective-permute-start.31 = (bf16[128,256]{1,0:T(8,128)(2,1)S(1)}, bf16[128,256]{1,0:T(8,128)(2,1)S(1)}, u32[]{:S(2)}, u32[]{:S(2)}) collective-permute-start(bf16[128,256]{1,0:T(8,128)(2,1)S(1)} %get-tuple-element.95.refs_2_), channel_id=1, source_target_pairs={{0,64},{64,0},{128,192},{192,128},{1,65},{65,1},{129,193},{193,129... | collective-permute-start | bytes 196616 | tf_op jit(solution)/shard_map/ppermute | solution.py:337
  84.9 1.9 %collective-permute-done.31.q_near = bf16[128,256]{1,0:T(8,128)(2,1)S(1)} collective-permute-done((bf16[128,256]{1,0:T(8,128)(2,1)S(1)}, bf16[128,256]{1,0:T(8,128)(2,1)S(1)}, u32[]{:S(2)}, u32[]{:S(2)}) %collective-permute-start.31) | collective-permute-done | bytes 65568 | tf_op jit(solution)/shard_map/ppermute | solution.py:337
  86.8 0.1 shard_map.121
  86.9 0.1 shard_map.122.refs_0_
  87.0 6.4 %collective-permute-start.32 = (bf16[256,1024]{1,0:T(8,128)(2,1)S(1)}, bf16[256,1024]{1,0:T(8,128)(2,1)S(1)}, u32[]{:S(2)}, u32[]{:S(2)}) collective-permute-start(bf16[256,1024]{1,0:T(8,128)(2,1)S(1)} %shard_map.122.refs_0_), channel_id=1, source_target_pairs={{0,1},{1,0},{2,3},{3,2},{4,5},{5,4},{6,7},{7,6},{8,9},{9,8},{10,11... | collective-permute-start | bytes 1572872 | tf_op jit(solution)/shard_map/ppermute | solution.py:353
  93.4 0.6 collective-permute-start.33
  94.0 0.9 collective-permute-done.32.refs_1_
  94.9 1.4 %shard_map.123 = (f32[256,2048]{1,0:T(8,128)}, bf16[32,2048]{1,0:T(8,128)(2,1)}, f32[8,128]{1,0:T(8,128)S(1)}) custom-call(bf16[256,1024]{1,0:T(8,128)(2,1)S(1)} %shard_map.122.refs_0_, bf16[256,1024]{1,0:T(8,128)(2,1)S(1)} %collective-permute-done.32.refs_1_, bf16[32,2048]{1,0:T(8,128)(2,1)S(1)} %get-tuple-element.97.refs_2_, ...), custom_call_target="tpu_custom_call" | custom-call | bytes 3543040 | tf_op jit(solution)/shard_map/pallas_call | solution.py:61
  96.4 1.4 %collective-permute-done.33.refs_1_ = bf16[384,128]{1,0:T(8,128)(2,1)S(1)} collective-permute-done((bf16[384,128]{1,0:T(8,128)(2,1)S(1)}, bf16[384,128]{1,0:T(8,128)(2,1)S(1)}, u32[]{:S(2)}, u32[]{:S(2)}) %collective-permute-start.33) | collective-permute-done | bytes 98336 | tf_op jit(solution)/shard_map/ppermute | solution.py:349
  97.7 0.7 shard_map.124
  (39 shorter events, 0.4 us)
Async XLA Ops:
  0.6 9.1 %collective-permute-start.10 = (bf16[32,2048]{1,0:T(8,128)(2,1)}, bf16[32,2048]{1,0:T(8,128)(2,1)S(1)}, u32[]{:S(2)}, u32[]{:S(2)}) collective-permute-start(bf16[32,2048]{1,0:T(8,128)(2,1)} %bitcast.8), channel_id=1, source_target_pairs={{0,8},{8,0},{1,9},{9,1},{2,10},{10,2},{3,11},{11,3},{4,12},{12,4},... | collective-permute-start | bytes 393224 | tf_op jit(solution)/shard_map/ppermute | solution.py:349
  4.8 4.9 %collective-permute-start = (bf16[384,128]{1,0:T(8,128)(2,1)S(1)}, bf16[384,128]{1,0:T(8,128)(2,1)S(1)}, u32[]{:S(2)}, u32[]{:S(2)}) collective-permute-start(bf16[384,128]{1,0:T(8,128)(2,1)S(1)} %pad_maximum_fusion.refs_2_), channel_id=1, source_target_pairs={{0,8},{8,0},{1,9},{9,1},{2,10},{10,2},{3,11},{11,3},{4,12},{12,4},... | collective-permute-start | bytes 294920 | tf_op jit(solution)/shard_map/ppermute | solution.py:349
  4.9 0.9 copy-start.1
  5.8 0.7 copy-start.2
  9.7 10.6 %collective-permute-start.11 = (bf16[64,2048]{1,0:T(8,128)(2,1)S(1)}, bf16[64,2048]{1,0:T(8,128)(2,1)S(1)}, u32[]{:S(2)}, u32[]{:S(2)}) collective-permute-start(bf16[64,2048]{1,0:T(8,128)(2,1)S(1)} %shard_map.105.refs_0_), channel_id=1, source_target_pairs={{0,2},{2,0},{4,6},{6,4},{1,3},{3,1},{5,7},{7,5},{8,10},{10,8},{12,... | collective-permute-start | bytes 786440 | tf_op jit(solution)/shard_map/ppermute | solution.py:337
  9.9 8.5 %collective-permute-start.1 = (bf16[256,128]{1,0:T(8,128)(2,1)S(1)}, bf16[256,128]{1,0:T(8,128)(2,1)S(1)}, u32[]{:S(2)}, u32[]{:S(2)}) collective-permute-start(bf16[256,128]{1,0:T(8,128)(2,1)S(1)} %get-tuple-element.56.k0), channel_id=1, source_target_pairs={{0,16},{16,0},{32,48},{48,32},{1,17},{17,1},{33,49},{49,33},{2,18}... | collective-permute-start | bytes 196616 | tf_op jit(solution)/shard_map/ppermute | solution.py:337
  12.9 6.5 %collective-permute-start.2 = (bf16[256,128]{1,0:T(8,128)(2,1)S(1)}, bf16[256,128]{1,0:T(8,128)(2,1)S(1)}, u32[]{:S(2)}, u32[]{:S(2)}) collective-permute-start(bf16[256,128]{1,0:T(8,128)(2,1)S(1)} %get-tuple-element.57.v0), channel_id=1, source_target_pairs={{0,48},{48,0},{16,32},{32,16},{1,49},{49,1},{17,33},{33,17},{2,50}... | collective-permute-start | bytes 196616 | tf_op jit(solution)/shard_map/ppermute | solution.py:341
  17.2 3.1 %collective-permute-start.3 = (bf16[256,128]{1,0:T(8,128)(2,1)S(1)}, bf16[256,128]{1,0:T(8,128)(2,1)S(1)}, u32[]{:S(2)}, u32[]{:S(2)}) collective-permute-start(bf16[256,128]{1,0:T(8,128)(2,1)S(1)} %get-tuple-element.58.q0), channel_id=1, source_target_pairs={{0,64},{64,0},{128,192},{192,128},{1,65},{65,1},{129,193},{193,129... | collective-permute-start | bytes 196616 | tf_op jit(solution)/shard_map/ppermute | solution.py:337
  20.4 19.0 %copy-start = (bf16[256,2048]{1,0:T(8,128)(2,1)S(1)}, bf16[256,2048]{1,0:T(8,128)(2,1)}, u32[]{:S(2)}) copy-start(bf16[256,2048]{1,0:T(8,128)(2,1)} %refs_2_.1) | copy-start | bytes 3145732
  20.4 18.8 %collective-permute-start.12 = (bf16[128,2048]{1,0:T(8,128)(2,1)S(1)}, bf16[128,2048]{1,0:T(8,128)(2,1)S(1)}, u32[]{:S(2)}, u32[]{:S(2)}) collective-permute-start(bf16[128,2048]{1,0:T(8,128)(2,1)S(1)} %shard_map.106.refs_0_), channel_id=1, source_target_pairs={{0,6},{6,0},{2,4},{4,2},{1,7},{7,1},{3,5},{5,3},{8,14},{14,8},{10,... | collective-permute-start | bytes 1572872 | tf_op jit(solution)/shard_map/ppermute | solution.py:341
  22.4 6.4 %collective-permute-start.5 = (bf16[512,128]{1,0:T(8,128)(2,1)S(1)}, bf16[512,128]{1,0:T(8,128)(2,1)S(1)}, u32[]{:S(2)}, u32[]{:S(2)}) collective-permute-start(bf16[512,128]{1,0:T(8,128)(2,1)S(1)} %get-tuple-element.60.vp.refs_3_), channel_id=1, source_target_pairs={{0,16},{16,0},{32,48},{48,32},{1,17},{17,1},{33,49},{49,33},{2,18}... | collective-permute-start | bytes 393224 | tf_op jit(solution)/shard_map/ppermute | solution.py:337
  23.9 5.3 %collective-permute-start.6 = (bf16[512,128]{1,0:T(8,128)(2,1)S(1)}, bf16[512,128]{1,0:T(8,128)(2,1)S(1)}, u32[]{:S(2)}, u32[]{:S(2)}) collective-permute-start(bf16[512,128]{1,0:T(8,128)(2,1)S(1)} %get-tuple-element.61.qp.refs_5_), channel_id=1, source_target_pairs={{0,192},{192,0},{64,128},{128,64},{1,193},{193,1},{65,129},{129,65... | collective-permute-start | bytes 393224 | tf_op jit(solution)/shard_map/ppermute | solution.py:341
  26.4 7.3 %collective-permute-start.4 = (bf16[512,128]{1,0:T(8,128)(2,1)S(1)}, bf16[512,128]{1,0:T(8,128)(2,1)S(1)}, u32[]{:S(2)}, u32[]{:S(2)}) collective-permute-start(bf16[512,128]{1,0:T(8,128)(2,1)S(1)} %get-tuple-element.59.kp.refs_2_.refs_1_), channel_id=1, source_target_pairs={{0,48},{48,0},{16,32},{32,16},{1,49},{49,1},{17,33},{33,17},{2,50}... | collective-permute-start | bytes 393224 | tf_op jit(solution)/shard_map/ppermute | solution.py:341
  35.9 3.9 %collective-permute-start.7 = (bf16[144,256]{1,0:T(8,128)(2,1)S(1)}, bf16[144,256]{1,0:T(8,128)(2,1)S(1)}, u32[]{:S(2)}, u32[]{:S(2)}) collective-permute-start(bf16[144,256]{1,0:T(8,128)(2,1)S(1)} %get-tuple-element.63), channel_id=1, source_target_pairs={{0,64},{64,0},{128,192},{192,128},{1,65},{65,1},{129,193},{193,129... | collective-permute-start | bytes 221192 | tf_op jit(solution)/shard_map/ppermute | solution.py:337
  36.2 5.2 %collective-permute-start.8 = (bf16[144,256]{1,0:T(8,128)(2,1)S(1)}, bf16[144,256]{1,0:T(8,128)(2,1)S(1)}, u32[]{:S(2)}, u32[]{:S(2)}) collective-permute-start(bf16[144,256]{1,0:T(8,128)(2,1)S(1)} %get-tuple-element.64), channel_id=1, source_target_pairs={{0,192},{192,0},{64,128},{128,64},{1,193},{193,1},{65,129},{129,65... | collective-permute-start | bytes 221192 | tf_op jit(solution)/shard_map/ppermute | solution.py:341
  36.2 5.2 %collective-permute-start.9 = (bf16[144,256]{1,0:T(8,128)(2,1)S(1)}, bf16[144,256]{1,0:T(8,128)(2,1)S(1)}, u32[]{:S(2)}, u32[]{:S(2)}) collective-permute-start(bf16[144,256]{1,0:T(8,128)(2,1)S(1)} %get-tuple-element.65), channel_id=1, source_target_pairs={{0,128},{128,0},{64,192},{192,64},{1,129},{129,1},{65,193},{193,65... | collective-permute-start | bytes 221192 | tf_op jit(solution)/shard_map/ppermute | solution.py:345
  41.9 6.7 %collective-permute-start.13 = (bf16[128,1024]{1,0:T(8,128)(2,1)S(1)}, bf16[128,1024]{1,0:T(8,128)(2,1)S(1)}, u32[]{:S(2)}, u32[]{:S(2)}) collective-permute-start(bf16[128,1024]{1,0:T(8,128)(2,1)S(1)} %get-tuple-element.70), channel_id=1, source_target_pairs={{0,1},{1,0},{2,3},{3,2},{4,5},{5,4},{6,7},{7,6},{8,9},{9,8},{10,11... | collective-permute-start | bytes 786440 | tf_op jit(solution)/shard_map/ppermute | solution.py:353
  48.7 8.4 %collective-permute-start.14 = (bf16[272,256]{1,0:T(8,128)(2,1)S(1)}, bf16[272,256]{1,0:T(8,128)(2,1)S(1)}, u32[]{:S(2)}, u32[]{:S(2)}) collective-permute-start(bf16[272,256]{1,0:T(8,128)(2,1)S(1)} %get-tuple-element.73), channel_id=1, source_target_pairs={{0,64},{64,0},{128,192},{192,128},{1,65},{65,1},{129,193},{193,129... | collective-permute-start | bytes 417800 | tf_op jit(solution)/shard_map/ppermute | solution.py:337
  49.2 7.9 %collective-permute-start.15 = (bf16[272,256]{1,0:T(8,128)(2,1)S(1)}, bf16[272,256]{1,0:T(8,128)(2,1)S(1)}, u32[]{:S(2)}, u32[]{:S(2)}) collective-permute-start(bf16[272,256]{1,0:T(8,128)(2,1)S(1)} %get-tuple-element.74), channel_id=1, source_target_pairs={{0,192},{192,0},{64,128},{128,64},{1,193},{193,1},{65,129},{129,65... | collective-permute-start | bytes 417800 | tf_op jit(solution)/shard_map/ppermute | solution.py:341
  51.6 6.3 %collective-permute-start.16 = (bf16[272,256]{1,0:T(8,128)(2,1)S(1)}, bf16[272,256]{1,0:T(8,128)(2,1)S(1)}, u32[]{:S(2)}, u32[]{:S(2)}) collective-permute-start(bf16[272,256]{1,0:T(8,128)(2,1)S(1)} %get-tuple-element.75), channel_id=1, source_target_pairs={{0,128},{128,0},{64,192},{192,64},{1,129},{129,1},{65,193},{193,65... | collective-permute-start | bytes 417800 | tf_op jit(solution)/shard_map/ppermute | solution.py:345
  52.1 3.6 %collective-permute-start.17 = (bf16[128,128]{1,0:T(8,128)(2,1)S(1)}, bf16[128,128]{1,0:T(8,128)(2,1)S(1)}, u32[]{:S(2)}, u32[]{:S(2)}) collective-permute-start(bf16[128,128]{1,0:T(8,128)(2,1)S(1)} %slice.33), channel_id=1, source_target_pairs={{0,8},{8,0},{1,9},{9,1},{2,10},{10,2},{3,11},{11,3},{4,12},{12,4},... | collective-permute-start | bytes 98312 | tf_op jit(solution)/shard_map/ppermute | solution.py:349
  56.2 17.4 %collective-permute-start.26 = (bf16[64,2048]{1,0:T(8,128)(2,1)S(1)}, bf16[64,2048]{1,0:T(8,128)(2,1)S(1)}, u32[]{:S(2)}, u32[]{:S(2)}) collective-permute-start(bf16[64,2048]{1,0:T(8,128)(2,1)S(1)} %get-tuple-element.77.refs_4_), channel_id=1, source_target_pairs={{0,6},{6,0},{2,4},{4,2},{1,7},{7,1},{3,5},{5,3},{8,14},{14,8},{10,... | collective-permute-start | bytes 786440 | tf_op jit(solution)/shard_map/ppermute | solution.py:341
  57.9 5.8 %collective-permute-start.18 = (bf16[128,256]{1,0:T(8,128)(2,1)S(1)}, bf16[128,256]{1,0:T(8,128)(2,1)S(1)}, u32[]{:S(2)}, u32[]{:S(2)}) collective-permute-start(bf16[128,256]{1,0:T(8,128)(2,1)S(1)} %shard_map.112.refs_11_.refs_0_), channel_id=1, source_target_pairs={{0,16},{16,0},{32,48},{48,32},{1,17},{17,1},{33,49},{49,33},{2,18}... | collective-permute-start | bytes 196616 | tf_op jit(solution)/shard_map/ppermute | solution.py:337
  63.7 5.4 %collective-permute-start.19 = (bf16[128,256]{1,0:T(8,128)(2,1)S(1)}, bf16[128,256]{1,0:T(8,128)(2,1)S(1)}, u32[]{:S(2)}, u32[]{:S(2)}) collective-permute-start(bf16[128,256]{1,0:T(8,128)(2,1)S(1)} %shard_map.114.a), channel_id=1, source_target_pairs={{0,48},{48,0},{16,32},{32,16},{1,49},{49,1},{17,33},{33,17},{2,50}... | collective-permute-start | bytes 196616 | tf_op jit(solution)/shard_map/ppermute | solution.py:341
  65.6 8.1 %collective-permute-start.21 = (bf16[256,256]{1,0:T(8,128)(2,1)S(1)}, bf16[256,256]{1,0:T(8,128)(2,1)S(1)}, u32[]{:S(2)}, u32[]{:S(2)}) collective-permute-start(bf16[256,256]{1,0:T(8,128)(2,1)S(1)} %get-tuple-element.80), channel_id=1, source_target_pairs={{0,192},{192,0},{64,128},{128,64},{1,193},{193,1},{65,129},{129,65... | collective-permute-start | bytes 393224 | tf_op jit(solution)/shard_map/ppermute | solution.py:341
  69.1 4.7 %collective-permute-start.20 = (bf16[128,256]{1,0:T(8,128)(2,1)S(1)}, bf16[128,256]{1,0:T(8,128)(2,1)S(1)}, u32[]{:S(2)}, u32[]{:S(2)}) collective-permute-start(bf16[128,256]{1,0:T(8,128)(2,1)S(1)} %shard_map.115.refs_0_.refs_2_), channel_id=1, source_target_pairs={{0,8},{8,0},{1,9},{9,1},{2,10},{10,2},{3,11},{11,3},{4,12},{12,4},... | collective-permute-start | bytes 196616 | tf_op jit(solution)/shard_map/ppermute | solution.py:349
  70.5 7.3 %collective-permute-start.29 = (bf16[512,128]{1,0:T(8,128)(2,1)S(1)}, bf16[512,128]{1,0:T(8,128)(2,1)S(1)}, u32[]{:S(2)}, u32[]{:S(2)}) collective-permute-start(bf16[512,128]{1,0:T(8,128)(2,1)S(1)} %get-tuple-element.91), channel_id=1, source_target_pairs={{0,16},{16,0},{32,48},{48,32},{1,17},{17,1},{33,49},{49,33},{2,18}... | collective-permute-start | bytes 393224 | tf_op jit(solution)/shard_map/ppermute | solution.py:337
  71.1 8.3 %collective-permute-start.25 = (bf16[512,128]{1,0:T(8,128)(2,1)S(1)}, bf16[512,128]{1,0:T(8,128)(2,1)S(1)}, u32[]{:S(2)}, u32[]{:S(2)}) collective-permute-start(bf16[512,128]{1,0:T(8,128)(2,1)S(1)} %get-tuple-element.85), channel_id=1, source_target_pairs={{0,48},{48,0},{16,32},{32,16},{1,49},{49,1},{17,33},{33,17},{2,50}... | collective-permute-start | bytes 393224 | tf_op jit(solution)/shard_map/ppermute | solution.py:341
  73.6 6.7 %collective-permute-start.27 = (bf16[32,2048]{1,0:T(8,128)(2,1)S(1)}, bf16[32,2048]{1,0:T(8,128)(2,1)S(1)}, u32[]{:S(2)}, u32[]{:S(2)}) collective-permute-start(bf16[32,2048]{1,0:T(8,128)(2,1)S(1)} %get-tuple-element.87), channel_id=1, source_target_pairs={{0,2},{2,0},{4,6},{6,4},{1,3},{3,1},{5,7},{7,5},{8,10},{10,8},{12,... | collective-permute-start | bytes 393224 | tf_op jit(solution)/shard_map/ppermute | solution.py:337
  73.8 8.9 %collective-permute-start.22 = (bf16[256,256]{1,0:T(8,128)(2,1)S(1)}, bf16[256,256]{1,0:T(8,128)(2,1)S(1)}, u32[]{:S(2)}, u32[]{:S(2)}) collective-permute-start(bf16[256,256]{1,0:T(8,128)(2,1)S(1)} %shard_map.117.refs_0_), channel_id=1, source_target_pairs={{0,64},{64,0},{128,192},{192,128},{1,65},{65,1},{129,193},{193,129... | collective-permute-start | bytes 393224 | tf_op jit(solution)/shard_map/ppermute | solution.py:337
  74.6 12.3 %collective-permute-start.24 = (bf16[256,256]{1,0:T(8,128)(2,1)S(1)}, bf16[256,256]{1,0:T(8,128)(2,1)S(1)}, u32[]{:S(2)}, u32[]{:S(2)}) collective-permute-start(bf16[256,256]{1,0:T(8,128)(2,1)S(1)} %shard_map.117.refs_0_), channel_id=1, source_target_pairs={{0,128},{128,0},{64,192},{192,64},{1,129},{129,1},{65,193},{193,65... | collective-permute-start | bytes 393224 | tf_op jit(solution)/shard_map/ppermute | solution.py:345
  77.8 9.1 %collective-permute-start.23 = (bf16[256,256]{1,0:T(8,128)(2,1)S(1)}, bf16[256,256]{1,0:T(8,128)(2,1)S(1)}, u32[]{:S(2)}, u32[]{:S(2)}) collective-permute-start(bf16[256,256]{1,0:T(8,128)(2,1)S(1)} %shard_map.117.refs_0_), channel_id=1, source_target_pairs={{0,192},{192,0},{64,128},{128,64},{1,193},{193,1},{65,129},{129,65... | collective-permute-start | bytes 393224 | tf_op jit(solution)/shard_map/ppermute | solution.py:341
  79.4 5.4 %collective-permute-start.30 = (bf16[256,128]{1,0:T(8,128)(2,1)S(1)}, bf16[256,128]{1,0:T(8,128)(2,1)S(1)}, u32[]{:S(2)}, u32[]{:S(2)}) collective-permute-start(bf16[256,128]{1,0:T(8,128)(2,1)S(1)} %get-tuple-element.93), channel_id=1, source_target_pairs={{0,48},{48,0},{16,32},{32,16},{1,49},{49,1},{17,33},{33,17},{2,50}... | collective-permute-start | bytes 196616 | tf_op jit(solution)/shard_map/ppermute | solution.py:341
  80.4 4.5 %collective-permute-start.28 = (bf16[256,128]{1,0:T(8,128)(2,1)S(1)}, bf16[256,128]{1,0:T(8,128)(2,1)S(1)}, u32[]{:S(2)}, u32[]{:S(2)}) collective-permute-start(bf16[256,128]{1,0:T(8,128)(2,1)S(1)} %get-tuple-element.89), channel_id=1, source_target_pairs={{0,16},{16,0},{32,48},{48,32},{1,17},{17,1},{33,49},{49,33},{2,18}... | collective-permute-start | bytes 196616 | tf_op jit(solution)/shard_map/ppermute | solution.py:337
  82.8 4.1 %collective-permute-start.31 = (bf16[128,256]{1,0:T(8,128)(2,1)S(1)}, bf16[128,256]{1,0:T(8,128)(2,1)S(1)}, u32[]{:S(2)}, u32[]{:S(2)}) collective-permute-start(bf16[128,256]{1,0:T(8,128)(2,1)S(1)} %get-tuple-element.95.refs_2_), channel_id=1, source_target_pairs={{0,64},{64,0},{128,192},{192,128},{1,65},{65,1},{129,193},{193,129... | collective-permute-start | bytes 196616 | tf_op jit(solution)/shard_map/ppermute | solution.py:337
  87.0 7.9 %collective-permute-start.32 = (bf16[256,1024]{1,0:T(8,128)(2,1)S(1)}, bf16[256,1024]{1,0:T(8,128)(2,1)S(1)}, u32[]{:S(2)}, u32[]{:S(2)}) collective-permute-start(bf16[256,1024]{1,0:T(8,128)(2,1)S(1)} %shard_map.122.refs_0_), channel_id=1, source_target_pairs={{0,1},{1,0},{2,3},{3,2},{4,5},{5,4},{6,7},{7,6},{8,9},{9,8},{10,11... | collective-permute-start | bytes 1572872 | tf_op jit(solution)/shard_map/ppermute | solution.py:353
  93.4 4.4 %collective-permute-start.33 = (bf16[384,128]{1,0:T(8,128)(2,1)S(1)}, bf16[384,128]{1,0:T(8,128)(2,1)S(1)}, u32[]{:S(2)}, u32[]{:S(2)}) collective-permute-start(bf16[384,128]{1,0:T(8,128)(2,1)S(1)} %get-tuple-element.96.refs_4_), channel_id=1, source_target_pairs={{0,8},{8,0},{1,9},{9,1},{2,10},{10,2},{3,11},{11,3},{4,12},{12,4},... | collective-permute-start | bytes 294920 | tf_op jit(solution)/shard_map/ppermute | solution.py:349
